TPU v7x, 32 devices: a whole 2x2x4 slice. The times are simulated.
32 devices in a mesh: grp: 4 (over y, x), sub: 8 (over z, core).
Axes of the slice: x: 2, y: 2, z: 4, core: 2. Of those that a mesh axis runs over, the one named last changes fastest.
Arguments:
- loads: float32 [4, 8, 32, 768], P('grp', 'sub'), may hold values from -6 to 6, as said below
- stiffness: bfloat16 [4, 8, 768, 768], P('grp', 'sub'), as said below
- flexibility: bfloat16 [4, 8, 768, 768], P('grp', 'sub'), as said below
- coarse_inverse: float32 [4, 96, 96], P('grp'), as said below
- face_nodes: int32 [4, 8, 4], P('grp', 'sub'), may hold values from 16 to 64, as said below
- corner_index: int32 [4, 8, 12], P('grp', 'sub'), may hold values from 0 to 767, as said below
Outputs:
- multipliers: float32 [4, 8, 32, 768], P('grp', 'sub')
- direction: float32 [4, 8, 32, 768], P('grp', 'sub')
Inputs may be any that keep to these rules, and one draw needn't show every extreme that they name: `face_nodes`: matched subdomains hold the same value for the face they share; at least 16. `corner_index`: distinct within a subdomain. `stiffness`: symmetric positive definite for every subdomain. `flexibility`: symmetric positive definite for every subdomain. `coarse_inverse`: symmetric positive definite for every group. `loads`: A jump: equal on both copies of each face, zero at nodes not below face_nodes.
All inputs are finite; a program needn't handle non-finite values.
Results may differ from a plain program's by a relative error of at most 0.012.
The roundings to bfloat16 on the way count: a program that leaves them out, or rounds other values in their place, can miss the bound.
Values sent between devices are 32-bit elements; how exact they have to be, the bound alone decides.
No kernel may reach another device: no remote copies, remote signals or barrier semaphores. Data moves between devices by JAX's collectives and lax.ppermute only.
A program may use at most 64 MiB of HBM per device.

v0:
```python
import jax
import jax.numpy as jnp
from jax import lax
from jax.sharding import PartitionSpec as P

ITERS = 2


def partner(block, axis, distance):
    count = lax.axis_size(axis)
    route = []
    for low in range(count):
        high = low | 1 << distance
        if high != low and high < count:
            route += [(low, high), (high, low)]
    return lax.ppermute(block, axis, route)


def jump_faces(values, sign_vec, mask_vec):
    face_dofs = values.shape[1] // 4
    pieces = []
    for face_index in range(4):
        block = values[:, face_index * face_dofs : (face_index + 1) * face_dofs]
        if face_index < 3:
            across = partner(block, "sub", face_index)
        else:
            across = partner(block, "grp", 0)
        pieces.append(block - across)
    return jnp.concatenate(pieces, axis=1) * sign_vec * mask_vec


def global_total(local_terms):
    return lax.psum(local_terms, ("grp", "sub"))


def body(loads, stiffness, flexibility, coarse_inverse, face_nodes, corner_index):
    start_rhs = loads[0, 0]
    stiff_matrix = stiffness[0, 0]
    flex_matrix = flexibility[0, 0]
    group_inverse = coarse_inverse[0]
    live_nodes = face_nodes[0, 0]
    corner_ids = corner_index[0, 0]
    dof_count = start_rhs.shape[1]
    face_dofs = dof_count // 4
    node_count = face_dofs // 3
    corner_count = corner_ids.shape[0]
    sub_pos = lax.axis_index("sub")
    grp_pos = lax.axis_index("grp")
    bit_list = jnp.stack([sub_pos >> 0 & 1, sub_pos >> 1 & 1, sub_pos >> 2 & 1, grp_pos & 1])
    face_sign = 1.0 - 2.0 * bit_list.astype(jnp.float32)
    positions = jnp.arange(dof_count)
    face_match = (positions // face_dofs)[:, None] == jnp.arange(4)[None, :]
    sign_vec = jnp.sum(jnp.where(face_match, face_sign[None, :], 0.0), axis=1)[None, :]
    live_here = jnp.sum(jnp.where(face_match, live_nodes[None, :], 0), axis=1)
    mask_vec = (positions % node_count < live_here).astype(jnp.float32)[None, :]
    onehot = (corner_ids[:, None] == positions[None, :]).astype(jnp.float32)
    own_start = sub_pos * corner_count

    def coarse_solve(corner_vals):
        piece = lax.all_gather(corner_vals, "sub", axis=1, tiled=True)
        block = lax.dynamic_slice(group_inverse, (0, own_start), (piece.shape[1], corner_count))
        return jnp.dot(
            piece, block, precision=lax.Precision.HIGHEST, preferred_element_type=jnp.float32
        )

    def precondition(residual):
        scaled = 0.5 * sign_vec * residual
        local = jnp.dot(
            scaled.astype(jnp.bfloat16), stiff_matrix, preferred_element_type=jnp.float32
        )
        coarse = coarse_solve(scaled[:, corner_ids])
        local = local + jnp.dot(
            coarse, onehot, precision=lax.Precision.HIGHEST, preferred_element_type=jnp.float32
        )
        result = jump_faces(local, sign_vec, mask_vec)
        partial_sum = jnp.sum(residual * result, axis=1)
        return (result, global_total(partial_sum))

    residual = start_rhs * mask_vec
    multipliers = jnp.zeros_like(residual)
    zvector, rz_now = precondition(residual)
    direction = zvector
    for iteration in range(ITERS):
        signed = sign_vec * direction
        image = jnp.dot(
            signed.astype(jnp.bfloat16), flex_matrix, preferred_element_type=jnp.float32
        )
        apply_result = jump_faces(image, sign_vec, mask_vec)
        apply_partial_sum = jnp.sum(direction * apply_result, axis=1)
        image = apply_result
        curvature = global_total(apply_partial_sum)
        alpha = (rz_now / curvature)[:, None]
        multipliers = multipliers + alpha * direction
        residual = residual - alpha * image
        zvector, rz_next = precondition(residual)
        direction = zvector + (rz_next / rz_now)[:, None] * direction
        rz_now = rz_next
    return (multipliers[None, None], direction[None, None])


def solution(mesh):
    in_specs = (
        P("grp", "sub", None, None),
        P("grp", "sub", None, None),
        P("grp", "sub", None, None),
        P("grp", None, None),
        P("grp", "sub", None),
        P("grp", "sub", None),
    )
    out_specs = (P("grp", "sub", None, None), P("grp", "sub", None, None))
    return jax.shard_map(body, mesh=mesh, in_specs=in_specs, out_specs=out_specs, check_vma=False)
```

profile of v0, /device:TPU:0, one launch (start us, length us, event | category | flops | bytes accessed | tf_op | source)
XLA Modules:
  0.0 248.4 jit_solution(15780607372051609526)
XLA Ops:
  0.9 0.9 select_reduce_fusion.1
  1.7 0.9 fusion.30
  2.7 0.2 copy.17
  2.8 0.7 fusion.65
  3.5 0.6 gather_fusion
  4.1 15.7 %all-gather.3 = f32[8,12,32]{2,1,0:T(8,128)S(1)} all-gather(f32[1,12,32]{2,1,0:T(8,128)S(1)} %bitcast.109), channel_id=2, replica_groups=mesh['grp'=4,'sub'=8] {'sub'}, dimensions={0}, use_global_device_ids=true | all-gather | bytes 13824 | tf_op jit(solution)/shard_map/all_gather | solution.py:60
  19.8 0.3 fusion.8
  20.1 0.3 fusion.40
  20.4 0.3 convolution_add_fusion.2
  20.7 0.4 collective-permute-start
  21.1 1.6 collective-permute-start.1
  22.7 2.4 collective-permute-start.2
  25.0 1.5 collective-permute-start.3
  26.5 1.2 collective-permute-done.2
  27.7 1.2 collective-permute-done.3
  29.0 0.4 fusion.2
  29.4 0.1 fusion.79
  29.6 1.0 collective-permute-start.6
  30.6 1.5 collective-permute-start.7
  32.1 1.4 collective-permute-done.5
  33.5 1.0 collective-permute-done.6
  34.6 0.2 multiply_reduce_fusion.2
  34.9 40.6 %all-reduce = (f32[32]{0:T(128)S(1)}, f32[32]{0:T(128)S(1)}) all-reduce(f32[32]{0:T(128)S(1)} %get-tuple-element.3, f32[32]{0:T(128)S(1)} %get-tuple-element.2), channel_id=1, replica_groups=mesh['grp'=4,'sub'=8] {'grp','sub'}, use_global_device_ids=true, to_apply=%region_3.4 | all-reduce | flops 64 | bytes 512 | tf_op jit(solution)/shard_map/psum | solution.py:33
  75.5 0.1 broadcast_multiply_fusion.1
  75.6 0.2 copy.18
  75.8 0.6 gather_fusion.1
  76.3 14.0 %all-gather.4 = f32[8,12,32]{2,1,0:T(8,128)S(1)} all-gather(f32[1,12,32]{2,1,0:T(8,128)S(1)} %bitcast.110), channel_id=3, replica_groups=mesh['grp'=4,'sub'=8] {'sub'}, dimensions={0}, use_global_device_ids=true | all-gather | bytes 13824 | tf_op jit(solution)/shard_map/all_gather | solution.py:60
  90.3 0.3 fusion.38
  90.6 0.4 fusion.6
  91.0 0.3 convolution_add_fusion.1
  91.4 0.6 collective-permute-start.10
  92.0 2.3 collective-permute-start.11
  94.3 1.5 collective-permute-start.9
  95.8 0.4 collective-permute-done.10
  96.2 1.9 collective-permute-done.9
  98.2 0.1 slice_subtract_fusion.11
  98.3 0.2 multiply_reduce_fusion.1
  98.5 39.3 %psum.37 = f32[32]{0:T(128)S(1)} all-reduce(f32[32]{0:T(128)S(1)} %multiply_reduce_fusion.1), channel_id=1, replica_groups=mesh['grp'=4,'sub'=8] {'grp','sub'}, use_global_device_ids=true, to_apply=%region_7.8 | all-reduce | flops 32 | bytes 256 | tf_op jit(solution)/shard_map/psum | solution.py:33
  137.7 0.4 fusion
  138.1 0.1 fusion.77
  138.2 0.6 collective-permute-start.13
  138.8 2.3 collective-permute-start.14
  141.1 2.3 collective-permute-start.15
  143.4 0.6 collective-permute-done.14
  144.0 1.3 collective-permute-done.15
  145.3 0.1 slice_subtract_fusion.7
  145.4 0.2 multiply_reduce_fusion
  145.6 38.8 %psum.38 = f32[32]{0:T(128)S(1)} all-reduce(f32[32]{0:T(128)S(1)} %multiply_reduce_fusion), channel_id=1, replica_groups=mesh['grp'=4,'sub'=8] {'grp','sub'}, use_global_device_ids=true, to_apply=%region_9.10 | all-reduce | flops 32 | bytes 256 | tf_op jit(solution)/shard_map/psum | solution.py:33
  184.5 0.1 broadcast_multiply_fusion
  184.6 0.2 copy.19
  184.8 0.6 gather_fusion.2
  185.3 14.0 %all-gather.5 = f32[8,12,32]{2,1,0:T(8,128)S(1)} all-gather(f32[1,12,32]{2,1,0:T(8,128)S(1)} %bitcast.108), channel_id=4, replica_groups=mesh['grp'=4,'sub'=8] {'sub'}, dimensions={0}, use_global_device_ids=true | all-gather | bytes 13824 | tf_op jit(solution)/shard_map/all_gather | solution.py:60
  199.3 0.3 fusion.36
  199.6 0.4 fusion.4
  200.0 0.3 convolution_add_fusion
  200.3 0.4 collective-permute-start.16
  200.8 2.4 collective-permute-start.18
  203.1 2.3 collective-permute-start.19
  205.4 0.2 collective-permute-done.18
  205.6 1.7 collective-permute-done.19
  207.4 0.2 fusion.29
  207.6 0.8 multiply_add_fusion
  208.4 39.2 %psum.39 = f32[32]{0:T(128)S(1)} all-reduce(f32[32]{0:T(128)S(1)} %fusion.29), channel_id=1, replica_groups=mesh['grp'=4,'sub'=8] {'grp','sub'}, use_global_device_ids=true, to_apply=%region_11.12 | all-reduce | flops 32 | bytes 256 | tf_op jit(solution)/shard_map/psum | solution.py:33
  247.6 0.8 fusion.26
  (44 shorter events, 1.0 us)
Async XLA Ops:
  0.6 19.1 %copy-start = (bf16[1,1,768,768]{3,2,1,0:T(8,128)(2,1)S(1)}, bf16[1,1,768,768]{3,2,1,0:T(8,128)(2,1)}, u32[]{:S(2)}) copy-start(bf16[1,1,768,768]{3,2,1,0:T(8,128)(2,1)} %param.7) | copy-start | bytes 3538948
  0.6 19.1 %copy-start.2 = (f32[1,1,32,768]{3,2,1,0:T(8,128)S(1)}, f32[1,1,32,768]{3,2,1,0:T(8,128)}, u32[]{:S(2)}) copy-start(f32[1,1,32,768]{3,2,1,0:T(8,128)} %param.6) | copy-start | bytes 294916
  1.7 18.3 %copy-start.3 = (f32[1,96,96]{2,1,0:T(8,128)S(1)}, f32[1,96,96]{2,1,0:T(8,128)}, u32[]{:S(2)}) copy-start(f32[1,96,96]{2,1,0:T(8,128)} %param.9) | copy-start | bytes 110596
  2.7 17.7 %copy-start.4 = (s32[1,1,12]{2,1,0:T(1,128)S(1)}, s32[1,1,12]{2,1,0:T(1,128)}, u32[]{:S(2)}) copy-start(s32[1,1,12]{2,1,0:T(1,128)} %param.11) | copy-start | bytes 148
  19.7 9.3 %copy-start.1 = (bf16[1,1,768,768]{3,2,1,0:T(8,128)(2,1)S(1)}, bf16[1,1,768,768]{3,2,1,0:T(8,128)(2,1)}, u32[]{:S(2)}) copy-start(bf16[1,1,768,768]{3,2,1,0:T(8,128)(2,1)} %param.8) | copy-start | bytes 3538948
  20.7 5.8 %collective-permute-start = (f32[32,192]{1,0:T(8,128)S(1)}, f32[32,192]{1,0:T(8,128)S(1)}, u32[]{:S(2)}, u32[]{:S(2)}) collective-permute-start(f32[32,192]{1,0:T(8,128)S(1)} %get-tuple-element.44), channel_id=1, source_target_pairs={{0,1},{1,0},{2,3},{3,2},{4,5},{5,4},{6,7},{7,6},{8,9},{9,8},{10,11... | collective-permute-start | bytes 73736 | tf_op jit(solution)/shard_map/ppermute | solution.py:16
  21.1 5.4 %collective-permute-start.1 = (f32[32,192]{1,0:T(8,128)S(1)}, f32[32,192]{1,0:T(8,128)S(1)}, u32[]{:S(2)}, u32[]{:S(2)}) collective-permute-start(f32[32,192]{1,0:T(8,128)S(1)} %get-tuple-element.47), channel_id=1, source_target_pairs={{0,2},{2,0},{1,3},{3,1},{4,6},{6,4},{5,7},{7,5},{8,10},{10,8},{9,1... | collective-permute-start | bytes 73736 | tf_op jit(solution)/shard_map/ppermute | solution.py:16
  22.7 5.1 %collective-permute-start.2 = (f32[32,192]{1,0:T(8,128)S(1)}, f32[32,192]{1,0:T(8,128)S(1)}, u32[]{:S(2)}, u32[]{:S(2)}) collective-permute-start(f32[32,192]{1,0:T(8,128)S(1)} %get-tuple-element.46), channel_id=1, source_target_pairs={{0,4},{4,0},{1,5},{5,1},{2,6},{6,2},{3,7},{7,3},{8,12},{12,8},{9,1... | collective-permute-start | bytes 73736 | tf_op jit(solution)/shard_map/ppermute | solution.py:16
  25.0 3.9 %collective-permute-start.3 = (f32[32,192]{1,0:T(8,128)S(1)}, f32[32,192]{1,0:T(8,128)S(1)}, u32[]{:S(2)}, u32[]{:S(2)}) collective-permute-start(f32[32,192]{1,0:T(8,128)S(1)} %get-tuple-element.45), channel_id=1, source_target_pairs={{0,8},{8,0},{16,24},{24,16},{1,9},{9,1},{17,25},{25,17},{2,10},{10... | collective-permute-start | bytes 73736 | tf_op jit(solution)/shard_map/ppermute | solution.py:16
  29.5 2.6 %collective-permute-start.4 = (f32[32,192]{1,0:T(8,128)S(1)}, f32[32,192]{1,0:T(8,128)S(1)}, u32[]{:S(2)}, u32[]{:S(2)}) collective-permute-start(f32[32,192]{1,0:T(8,128)S(1)} %get-tuple-element.36), channel_id=1, source_target_pairs={{0,1},{1,0},{2,3},{3,2},{4,5},{5,4},{6,7},{7,6},{8,9},{9,8},{10,11... | collective-permute-start | bytes 73736 | tf_op jit(solution)/shard_map/ppermute | solution.py:16
  29.5 4.0 %collective-permute-start.5 = (f32[32,192]{1,0:T(8,128)S(1)}, f32[32,192]{1,0:T(8,128)S(1)}, u32[]{:S(2)}, u32[]{:S(2)}) collective-permute-start(f32[32,192]{1,0:T(8,128)S(1)} %get-tuple-element.39), channel_id=1, source_target_pairs={{0,2},{2,0},{1,3},{3,1},{4,6},{6,4},{5,7},{7,5},{8,10},{10,8},{9,1... | collective-permute-start | bytes 73736 | tf_op jit(solution)/shard_map/ppermute | solution.py:16
  29.6 4.9 %collective-permute-start.6 = (f32[32,192]{1,0:T(8,128)S(1)}, f32[32,192]{1,0:T(8,128)S(1)}, u32[]{:S(2)}, u32[]{:S(2)}) collective-permute-start(f32[32,192]{1,0:T(8,128)S(1)} %get-tuple-element.38), channel_id=1, source_target_pairs={{0,4},{4,0},{1,5},{5,1},{2,6},{6,2},{3,7},{7,3},{8,12},{12,8},{9,1... | collective-permute-start | bytes 73736 | tf_op jit(solution)/shard_map/ppermute | solution.py:16
  30.6 3.9 %collective-permute-start.7 = (f32[32,192]{1,0:T(8,128)S(1)}, f32[32,192]{1,0:T(8,128)S(1)}, u32[]{:S(2)}, u32[]{:S(2)}) collective-permute-start(f32[32,192]{1,0:T(8,128)S(1)} %get-tuple-element.37), channel_id=1, source_target_pairs={{0,8},{8,0},{16,24},{24,16},{1,9},{9,1},{17,25},{25,17},{2,10},{10... | collective-permute-start | bytes 73736 | tf_op jit(solution)/shard_map/ppermute | solution.py:16
  91.4 4.9 %collective-permute-start.10 = (f32[32,192]{1,0:T(8,128)S(1)}, f32[32,192]{1,0:T(8,128)S(1)}, u32[]{:S(2)}, u32[]{:S(2)}) collective-permute-start(f32[32,192]{1,0:T(8,128)S(1)} %get-tuple-element.30), channel_id=1, source_target_pairs={{0,4},{4,0},{1,5},{5,1},{2,6},{6,2},{3,7},{7,3},{8,12},{12,8},{9,1... | collective-permute-start | bytes 73736 | tf_op jit(solution)/shard_map/ppermute | solution.py:16
  92.0 4.2 %collective-permute-start.11 = (f32[32,192]{1,0:T(8,128)S(1)}, f32[32,192]{1,0:T(8,128)S(1)}, u32[]{:S(2)}, u32[]{:S(2)}) collective-permute-start(f32[32,192]{1,0:T(8,128)S(1)} %get-tuple-element.29), channel_id=1, source_target_pairs={{0,8},{8,0},{16,24},{24,16},{1,9},{9,1},{17,25},{25,17},{2,10},{10... | collective-permute-start | bytes 73736 | tf_op jit(solution)/shard_map/ppermute | solution.py:16
  94.2 2.0 collective-permute-start.8
  94.3 3.9 %collective-permute-start.9 = (f32[32,192]{1,0:T(8,128)S(1)}, f32[32,192]{1,0:T(8,128)S(1)}, u32[]{:S(2)}, u32[]{:S(2)}) collective-permute-start(f32[32,192]{1,0:T(8,128)S(1)} %get-tuple-element.31), channel_id=1, source_target_pairs={{0,2},{2,0},{1,3},{3,1},{4,6},{6,4},{5,7},{7,5},{8,10},{10,8},{9,1... | collective-permute-start | bytes 73736 | tf_op jit(solution)/shard_map/ppermute | solution.py:16
  138.2 5.2 %collective-permute-start.12 = (f32[32,192]{1,0:T(8,128)S(1)}, f32[32,192]{1,0:T(8,128)S(1)}, u32[]{:S(2)}, u32[]{:S(2)}) collective-permute-start(f32[32,192]{1,0:T(8,128)S(1)} %get-tuple-element.20), channel_id=1, source_target_pairs={{0,1},{1,0},{2,3},{3,2},{4,5},{5,4},{6,7},{7,6},{8,9},{9,8},{10,11... | collective-permute-start | bytes 73736 | tf_op jit(solution)/shard_map/ppermute | solution.py:16
  138.2 5.2 %collective-permute-start.13 = (f32[32,192]{1,0:T(8,128)S(1)}, f32[32,192]{1,0:T(8,128)S(1)}, u32[]{:S(2)}, u32[]{:S(2)}) collective-permute-start(f32[32,192]{1,0:T(8,128)S(1)} %get-tuple-element.23), channel_id=1, source_target_pairs={{0,2},{2,0},{1,3},{3,1},{4,6},{6,4},{5,7},{7,5},{8,10},{10,8},{9,1... | collective-permute-start | bytes 73736 | tf_op jit(solution)/shard_map/ppermute | solution.py:16
  138.8 5.2 %collective-permute-start.14 = (f32[32,192]{1,0:T(8,128)S(1)}, f32[32,192]{1,0:T(8,128)S(1)}, u32[]{:S(2)}, u32[]{:S(2)}) collective-permute-start(f32[32,192]{1,0:T(8,128)S(1)} %get-tuple-element.22), channel_id=1, source_target_pairs={{0,4},{4,0},{1,5},{5,1},{2,6},{6,2},{3,7},{7,3},{8,12},{12,8},{9,1... | collective-permute-start | bytes 73736 | tf_op jit(solution)/shard_map/ppermute | solution.py:16
  141.1 4.2 %collective-permute-start.15 = (f32[32,192]{1,0:T(8,128)S(1)}, f32[32,192]{1,0:T(8,128)S(1)}, u32[]{:S(2)}, u32[]{:S(2)}) collective-permute-start(f32[32,192]{1,0:T(8,128)S(1)} %get-tuple-element.21), channel_id=1, source_target_pairs={{0,8},{8,0},{16,24},{24,16},{1,9},{9,1},{17,25},{25,17},{2,10},{10... | collective-permute-start | bytes 73736 | tf_op jit(solution)/shard_map/ppermute | solution.py:16
  200.3 5.1 %collective-permute-start.16 = (f32[32,192]{1,0:T(8,128)S(1)}, f32[32,192]{1,0:T(8,128)S(1)}, u32[]{:S(2)}, u32[]{:S(2)}) collective-permute-start(f32[32,192]{1,0:T(8,128)S(1)} %get-tuple-element.12), channel_id=1, source_target_pairs={{0,1},{1,0},{2,3},{3,2},{4,5},{5,4},{6,7},{7,6},{8,9},{9,8},{10,11... | collective-permute-start | bytes 73736 | tf_op jit(solution)/shard_map/ppermute | solution.py:16
  200.7 4.7 %collective-permute-start.17 = (f32[32,192]{1,0:T(8,128)S(1)}, f32[32,192]{1,0:T(8,128)S(1)}, u32[]{:S(2)}, u32[]{:S(2)}) collective-permute-start(f32[32,192]{1,0:T(8,128)S(1)} %get-tuple-element.15), channel_id=1, source_target_pairs={{0,2},{2,0},{1,3},{3,1},{4,6},{6,4},{5,7},{7,5},{8,10},{10,8},{9,1... | collective-permute-start | bytes 73736 | tf_op jit(solution)/shard_map/ppermute | solution.py:16
  200.8 4.8 %collective-permute-start.18 = (f32[32,192]{1,0:T(8,128)S(1)}, f32[32,192]{1,0:T(8,128)S(1)}, u32[]{:S(2)}, u32[]{:S(2)}) collective-permute-start(f32[32,192]{1,0:T(8,128)S(1)} %get-tuple-element.14), channel_id=1, source_target_pairs={{0,4},{4,0},{1,5},{5,1},{2,6},{6,2},{3,7},{7,3},{8,12},{12,8},{9,1... | collective-permute-start | bytes 73736 | tf_op jit(solution)/shard_map/ppermute | solution.py:16
  203.1 4.2 %collective-permute-start.19 = (f32[32,192]{1,0:T(8,128)S(1)}, f32[32,192]{1,0:T(8,128)S(1)}, u32[]{:S(2)}, u32[]{:S(2)}) collective-permute-start(f32[32,192]{1,0:T(8,128)S(1)} %get-tuple-element.13), channel_id=1, source_target_pairs={{0,8},{8,0},{16,24},{24,16},{1,9},{9,1},{17,25},{25,17},{2,10},{10... | collective-permute-start | bytes 73736 | tf_op jit(solution)/shard_map/ppermute | solution.py:16
where the time goes:
time: 249 us; the launch traced here: 248 us
  blocking collectives  202 us (81%)
  starting transfers between devices  23.1 us (9%)
  waiting for transfers between devices  11 us (4%)
  other arithmetic  5.73 us (2%)
  matrix products  3.47 us (1%)
  local copies, waits for them, and re-layouts  2.63 us (1%)
    psum x4, blocking collectives, global_total(): return lax.psum(local_terms, ('grp', 'sub'))  158 us
    all_gather x3, blocking collectives, coarse_solve(): piece = lax.all_gather(corner_vals, 'sub', axis=1, tiled=True)  43.6 us
    ppermute x20, starting transfers between devices, partner(): return lax.ppermute(block, axis, route)  23.1 us
    ppermute x20, waiting for transfers between devices, partner(): return lax.ppermute(block, axis, route)  11 us
  transfers between devices with their start and end apart: 20, of which 10 were waited for; matrix products, arithmetic and copies ran while one was open for 0% of the time, Pallas kernels for 0%

commit v1 on v0

v1 whole, which is shorter than its diff:
```python
import jax
import jax.numpy as jnp
from jax import lax
from jax.sharding import PartitionSpec as P

HI = lax.Precision.HIGHEST
NT = (((1,), (1,)), ((), ()))
TN = (((0,), (0,)), ((), ()))
NN = (((1,), (0,)), ((), ()))
Q4 = 4


def dot32(a, b, dims):
    return lax.dot_general(a, b, dims, precision=HI, preferred_element_type=jnp.float32)


def dot16(a, b):
    return lax.dot_general(a, b, NN, preferred_element_type=jnp.float32)


def swap(block, axis, distance):
    count = lax.axis_size(axis)
    return lax.ppermute(block, axis, [(i, i ^ distance) for i in range(count) if i ^ distance < count])


def exchange(field):
    width = field.shape[1] // 4
    face = [field[:, f * width : (f + 1) * width] for f in range(4)]
    return [swap(face[0], "sub", 1), swap(face[1], "sub", 2), swap(face[2], "sub", 4), swap(face[3], "grp", 1)]


def send_all(blocks):
    return lax.all_to_all(blocks, ("grp", "sub"), 0, 0, tiled=True)


def pack(columns):
    rows = columns.shape[0] // 4
    return jnp.concatenate([columns[r * rows : (r + 1) * rows] for r in range(4)], axis=1)


def unpack(lanes):
    loads = lanes.shape[1] // 4
    return jnp.concatenate([lanes[:, r * loads : (r + 1) * loads] for r in range(4)], axis=0)


def column(row):
    n = row.shape[1]
    eye = (lax.broadcasted_iota(jnp.int32, (n, n), 0) == lax.broadcasted_iota(jnp.int32, (n, n), 1))
    return jnp.sum(jnp.where(eye, row, 0.0), axis=1, keepdims=True)


def row_sum(product):
    return dot32(jnp.ones((1, product.shape[1]), jnp.float32), product, NT)


def jump(field, across, sign_mask):
    return (field - jnp.concatenate(across, axis=1)) * sign_mask


def contributions(image, corner_map, own_inverse, cross_inverse, sign_vec, scalars, groups, grp_pos):
    half = corner_map.shape[0] // 2
    corner = dot32(corner_map, 0.5 * sign_vec * image, NT)
    own = pack(dot32(own_inverse, corner[:half], NN))
    cross = pack(dot32(cross_inverse, corner[half:], NN))
    n_row = own.shape[0]
    is_last = lax.broadcasted_iota(jnp.int32, (n_row, 1), 0) % 4 == 3
    totals = jnp.where(is_last, jnp.concatenate(scalars, axis=1), 0.0)
    blocks = []
    for g in range(groups):
        blocks.append(totals + jnp.where(g == grp_pos, own, jnp.where(g == grp_pos ^ 1, cross, 0.0)))
    return jnp.stack(blocks)


def body(loads, stiffness, flexibility, coarse_inverse, face_nodes, corner_index):
    rhs, stiff, flex = loads[0, 0], stiffness[0, 0], flexibility[0, 0]
    live_nodes, ids = face_nodes[0, 0], corner_index[0, 0]
    n_load, dofs = rhs.shape
    face_dofs = dofs // 4
    nodes = face_dofs // 3
    corners = ids.shape[0]
    n_q = corners // 4
    groups, subs = lax.axis_size("grp"), lax.axis_size("sub")
    n_dev = groups * subs
    sub_pos, grp_pos = lax.axis_index("sub"), lax.axis_index("grp")

    position = jnp.arange(dofs)[None, :]
    face_of = position // face_dofs
    bits = jnp.stack([sub_pos & 1, sub_pos >> 1 & 1, sub_pos >> 2 & 1, grp_pos & 1])
    sign_vec = jnp.zeros((1, dofs), jnp.float32)
    live = jnp.zeros((1, dofs), jnp.int32)
    for f in range(4):
        sign_vec = jnp.where(face_of == f, 1.0 - 2.0 * bits[f].astype(jnp.float32), sign_vec)
        live = jnp.where(face_of == f, live_nodes[f], live)
    mask_vec = (position % nodes < live).astype(jnp.float32)
    sign_mask = sign_vec * mask_vec

    id_rq = jnp.pad(ids.reshape(n_q, 4), ((0, Q4 - n_q), (0, 0)), constant_values=-1).T.reshape(-1, 1)
    onehot = (id_rq == position).astype(jnp.float32)
    place = jnp.arange(subs * 16)[:, None]
    source = place % (subs * 4) // 4 * corners + place % 4 * 4 + place // (subs * 4)
    valid = place % 4 < n_q
    select = ((jnp.arange(subs * corners)[None, :] == source) & valid).astype(jnp.float32)
    own_inverse = dot32(dot32(select, coarse_inverse[0], NN), select, NT)
    cross_inverse = swap(own_inverse, "grp", 1)

    resid = rhs * mask_vec
    scaled = 0.5 * sign_vec * resid
    packed = pack(dot32(onehot, scaled, NT))
    packed_ids = pack(jnp.broadcast_to(id_rq.astype(jnp.float32), (16, n_load)))
    first = jnp.concatenate([packed, packed_ids], axis=0)
    first = send_all(jnp.broadcast_to(first[None], (n_dev,) + first.shape))
    local = dot16(scaled.astype(jnp.bfloat16), stiff)
    across = exchange(local)

    first = first.reshape(groups, subs, 2, 4, 4 * n_load)
    corner_map, field, own_field = [], [], []
    coarse = []
    sub_row = jnp.tile(jnp.repeat(jnp.arange(subs), 4), 4)[:, None]
    is_own = (sub_row == sub_pos).astype(jnp.float32)
    for which, matrix in ((grp_pos, own_inverse), (grp_pos ^ 1, cross_inverse)):
        pair = lax.dynamic_index_in_dim(first, which, 0, keepdims=False)
        values = unpack(pair[:, 0].reshape(subs * 4, -1))
        id_rows = unpack(pair[:, 1].reshape(subs * 4, -1))[:, :1]
        here = (id_rows == position.astype(jnp.float32)).astype(jnp.float32)
        coarse.append(dot32(matrix, values, NN))
        if len(coarse) == 1:
            weight = is_own
            for f in range(3):
                weight = weight - jnp.where(face_of == f, (sub_row == sub_pos ^ 1 << f).astype(jnp.float32), 0.0)
            own_field = dot32(coarse[0], here * is_own, TN)
        else:
            weight = -jnp.where(face_of == 3, is_own, 0.0)
        corner_map.append(here * weight * sign_mask)
    corner_map = jnp.concatenate(corner_map, axis=0)
    coarse = jnp.concatenate(coarse, axis=0)
    zvec = jump(local, across, sign_mask) + dot32(coarse, corner_map, TN)
    zero = jnp.zeros((1, n_load), jnp.float32)

    def spread(image, scalars):
        blocks = contributions(
            image, corner_map, own_inverse, cross_inverse, sign_vec, scalars, groups, grp_pos
        )
        return send_all(blocks.reshape(n_dev, 4, 4 * n_load))

    def collect(received):
        total = unpack(jnp.sum(received, axis=0))
        return dot32(total, onehot, TN), [total[4 * i + 3 : 4 * i + 4] for i in range(4)]

    signed = sign_vec * zvec
    image = dot16(signed.astype(jnp.bfloat16), flex)
    rz_part = row_sum(resid * zvec)
    curve_part = 2.0 * row_sum(signed * image)
    received = spread(image, [rz_part, curve_part, zero, zero])
    across = exchange(image)

    image_field, (rz0, curve0, _, _) = collect(received)
    flexed = jump(image, across, sign_mask)
    alpha = column(rz0 / curve0)
    mult = alpha * zvec
    resid = resid - alpha * flexed
    local_coarse = own_field - alpha * image_field
    local = dot16((0.5 * sign_vec * resid).astype(jnp.bfloat16), stiff) + local_coarse
    across = exchange(local)

    znew = jump(local, across, sign_mask)
    signed = sign_vec * znew
    high = signed.astype(jnp.bfloat16)
    low = (signed - high.astype(jnp.float32)).astype(jnp.bfloat16)
    both = dot16(jnp.concatenate([high, low], axis=0), flex)
    image = both[:n_load] + both[n_load:]
    parts = [row_sum(resid * znew), 2.0 * row_sum(signed * image), row_sum(znew * flexed), zero]
    received = spread(image, parts)
    across = exchange(image)

    new_field, (rz1, curve_zz, curve_zd, _) = collect(received)
    beta_row = rz1 / rz0
    beta = column(beta_row)
    flexed = jump(image, across, sign_mask) + beta * flexed
    direction = znew + beta * zvec
    alpha = column(rz1 / (curve_zz + 2.0 * beta_row * curve_zd + beta_row * beta_row * curve0))
    mult = mult + alpha * direction
    resid = resid - alpha * flexed
    local_coarse = local_coarse - alpha * (new_field + beta * image_field)
    local = dot16((0.5 * sign_vec * resid).astype(jnp.bfloat16), stiff) + local_coarse
    last = jnp.concatenate([2.0 * row_sum(sign_vec * resid * local), zero, zero, zero], axis=1)
    received = send_all(jnp.broadcast_to(last[None], (n_dev, 1, 4 * n_load)))
    across = exchange(local)
    rz2 = jnp.sum(received, axis=0)[:, :n_load]
    direction = jump(local, across, sign_mask) + column(rz2 / rz1) * direction
    return (mult[None, None], direction[None, None])


def solution(mesh):
    in_specs = (
        P("grp", "sub", None, None),
        P("grp", "sub", None, None),
        P("grp", "sub", None, None),
        P("grp", None, None),
        P("grp", "sub", None),
        P("grp", "sub", None),
    )
    out_specs = (P("grp", "sub", None, None), P("grp", "sub", None, None))
    return jax.shard_map(body, mesh=mesh, in_specs=in_specs, out_specs=out_specs, check_vma=False)
```

time: 249 us -> 106 us (0.43)
  blocking collectives: 202 us -> 0 us
  starting transfers between devices: 23.1 us -> 41.5 us
  local copies, waits for them, and re-layouts: 2.63 us -> 17.1 us
  matrix products: 3.47 us -> 14.7 us
  other arithmetic: 5.73 us -> 16.3 us
  waiting for transfers between devices: 11 us -> 14.2 us
    psum x4 -> x0, blocking collectives: 158 us -> none  [global_total(): return lax.psum(local_terms, ('grp', 'sub'))]
    all_gather x3 -> x0, blocking collectives: 43.6 us -> none  [coarse_solve(): piece = lax.all_gather(corner_vals, 'sub', axis=1, tiled=True)]
    all_to_all x0 -> x4, starting transfers between devices: none -> 18.8 us  [send_all(): return lax.all_to_all(blocks, ('grp', 'sub'), 0, 0, tiled=True)]
    dot_general x11 -> x26, matrix products: 3.47 us -> 14.7 us  [the longest x21 11.8 us: dot32(): lax.dot_general(a, b, dims, precision=HI, preferred_element_type=jnp.floa...]
    all_to_all x0 -> x4, waiting for transfers between devices: none -> 8.36 us  [send_all(): return lax.all_to_all(blocks, ('grp', 'sub'), 0, 0, tiled=True)]
    concatenate x0 -> x21, local copies, waits for them, and re-layouts: none -> 7.44 us  [the longest x20 7.43 us: pack(): jnp.concatenate([columns[r * rows:(r + 1) * rows] for r in range(4)], axi...]
    ppermute x20 -> x21, waiting for transfers between devices: 11 us -> 5.83 us  [swap(): lax.ppermute(block, axis, [(i, i ^ distance) for i in range(count) if i ^...]
    slice x5 -> x35, local copies, waits for them, and re-layouts: 0.41 us -> 4.99 us  [the longest x5 1.66 us: exchange(): face = [field[:, f * width:(f + 1) * width] for f in range(4)]]
  transfers between devices with their start and end apart: 20 -> 25, of which waited for: 10 -> 7; matrix products, arithmetic and copies ran while one was open for 0% -> 21% of each run, Pallas kernels for 0% -> 0%
where the time goes in v1:
time: 106 us; the launch traced here: 105 us
  starting transfers between devices  41.5 us (39%)
  local copies, waits for them, and re-layouts  17.1 us (16%)
  other arithmetic  16.3 us (15%)
  matrix products  14.7 us (14%)
  waiting for transfers between devices  14.2 us (13%)
  between operations  1.5 us (1%)
    ppermute x21, starting transfers between devices, swap(): lax.ppermute(block, axis, [(i, i ^ distance) for i in range(count) if i ^...  22.7 us
    all_to_all x4, starting transfers between devices, send_all(): return lax.all_to_all(blocks, ('grp', 'sub'), 0, 0, tiled=True)  18.8 us
    dot_general x21, matrix products, dot32(): lax.dot_general(a, b, dims, precision=HI, preferred_element_type=jnp.floa...  11.8 us
    all_to_all x4, waiting for transfers between devices, send_all(): return lax.all_to_all(blocks, ('grp', 'sub'), 0, 0, tiled=True)  8.36 us
    concatenate x20, local copies, waits for them, and re-layouts, pack(): jnp.concatenate([columns[r * rows:(r + 1) * rows] for r in range(4)], axi...  7.43 us
    ppermute x21, waiting for transfers between devices, swap(): lax.ppermute(block, axis, [(i, i ^ distance) for i in range(count) if i ^...  5.83 us
    dot_general x5, matrix products, dot16(): return lax.dot_general(a, b, NN, preferred_element_type=jnp.float32)  2.97 us
    select_n x1, other arithmetic, body(): jnp.where(face_of == f, 1.0 - 2.0 * bits[f].astype(jnp.float32), sign_vec)  2.63 us
  transfers between devices with their start and end apart: 25, of which 7 were waited for; matrix products, arithmetic and copies ran while one was open for 21% of the time, Pallas kernels for 0%

profile of v1, /device:TPU:0, one launch (start us, length us, event | category | flops | bytes accessed | tf_op | source)
XLA Modules:
  0.0 105.3 jit_solution(1828377294338122211)
XLA Ops:
  0.7 1.5 %fusion.189 = (s32[1,1,1]{2,1,0:T(1,128)}, s32[1,1,1]{2,1,0:T(1,128)}, s32[1,1,1]{2,1,0:T(1,128)}, s32[1,1,1]{2,1,0:T(1,128)}) fusion(s32[1,1,4]{2,1,0:T(1,128)} %param.10), kind=kLoop, calls=%fused_computation.295 | loop fusion | bytes 32 | tf_op jit(solution)/shard_map/slice | solution.py:93
  2.1 0.5 broadcast.1172
  2.6 1.2 %reduce.12 = s32[12]{0:T(128)S(1)} reduce(s32[1,1,12]{2,1,0:T(1,128)} %param.11, s32[]{:T(128)} %broadcast.1172), dimensions={0,1}, to_apply=%param.11.reduce_sub_computation.3 | reduce | bytes 100 | tf_op args[5]
  4.2 2.6 %fusion.149 = f32[768]{0:T(1024)S(1)} fusion(s32[]{:T(128)} %bitcast.4, s32[]{:T(128)} %bitcast.3, s32[]{:T(128)} %bitcast.2, s32[]{:T(128)} %bitcast.1), kind=kLoop, calls=%fused_computation.242 | loop fusion | flops 18432 | bytes 3088 | tf_op jit(solution)/shard_map/convert_element_type | solution.py:94
  6.8 1.1 %fusion.56 = f32[16,32]{1,0:T(8,128)S(1)} fusion(f32[1,1,32,768]{3,2,1,0:T(8,128)} %param.6, f32[768]{0:T(1024)S(1)} %broadcast_multiply_fusion, f32[768]{0:T(1024)S(1)} %fusion.149, s32[16]{0:T(128)S(1)} %eq.297), kind=kOutput, calls=%fused_computation.76 | convolution fusion | flops 4780032 | bytes 106560 | tf_op jit(solution)/shard_map/dot_general | solution.py:14
  8.5 0.7 broadcast_in_dim.226
  9.2 7.3 %all-to-all-start = ((f32[32,8,128]{2,1,0:T(8,128)}), f32[32,8,128]{2,1,0:T(8,128)S(1)}, u32[]{:S(2)}, u32[]{:S(2)}) async-start(f32[32,8,128]{2,1,0:T(8,128)} %broadcast_in_dim.226), calls=%async_computation | async-start | bytes 262144 | tf_op jit(solution)/shard_map/all_to_all | solution.py:33
  16.5 1.1 %fusion.63 = f32[128,96]{0,1:T(8,128)S(1)} fusion(f32[1,96,96]{2,1,0:T(8,128)} %param.9, s32[128]{0:T(128)S(1)} %fusion.150, pred[128]{0:T(512)(128)(4,1)S(1)} %broadcast_compare_fusion.4), kind=kOutput, calls=%fused_computation.88 | convolution fusion | flops 14180352 | bytes 86656 | tf_op jit(solution)/shard_map/dot_general | solution.py:14
  17.9 1.8 %collective-permute-start.4 = (f32[128,128]{1,0:T(8,128)S(1)}, f32[128,128]{1,0:T(8,128)S(1)}, u32[]{:S(2)}, u32[]{:S(2)}) collective-permute-start(f32[128,128]{1,0:T(8,128)S(1)} %fusion.61), channel_id=1, source_target_pairs={{0,8},{8,0},{16,24},{24,16},{1,9},{9,1},{17,25},{25,17},{2,10},{10... | collective-permute-start | bytes 196616 | tf_op jit(solution)/shard_map/ppermute | solution.py:23
  19.7 1.6 %fusion.8 = f32[32,768]{1,0:T(8,128)S(1)} fusion(bf16[1,1,768,768]{3,2,1,0:T(8,128)(2,1)} %param.7, f32[1,1,32,768]{3,2,1,0:T(8,128)} %param.6, f32[768]{0:T(1024)S(1)} %fusion.149, f32[768]{0:T(1024)S(1)} %broadcast_multiply_fusion), kind=kOutput, calls=%fused_computation.8 | convolution fusion | flops 37822464 | bytes 1382400 | tf_op jit(solution)/shard_map/dot_general | solution.py:18
  21.5 1.5 %collective-permute-start.1 = (f32[32,192]{1,0:T(8,128)S(1)}, f32[32,192]{1,0:T(8,128)S(1)}, u32[]{:S(2)}, u32[]{:S(2)}) collective-permute-start(f32[32,192]{1,0:T(8,128)S(1)} %get-tuple-element.39), channel_id=1, source_target_pairs={{0,2},{1,3},{2,0},{3,1},{4,6},{5,7},{6,4},{7,5},{8,10},{9,11},{10,... | collective-permute-start | bytes 73736 | tf_op jit(solution)/shard_map/ppermute | solution.py:23
  23.0 2.4 %collective-permute-start.2 = (f32[32,192]{1,0:T(8,128)S(1)}, f32[32,192]{1,0:T(8,128)S(1)}, u32[]{:S(2)}, u32[]{:S(2)}) collective-permute-start(f32[32,192]{1,0:T(8,128)S(1)} %get-tuple-element.38), channel_id=1, source_target_pairs={{0,4},{1,5},{2,6},{3,7},{4,0},{5,1},{6,2},{7,3},{8,12},{9,13},{10,... | collective-permute-start | bytes 73736 | tf_op jit(solution)/shard_map/ppermute | solution.py:23
  25.5 0.5 collective-permute-start.3
  26.1 0.5 fusion.151
  27.3 2.6 %select_select_fusion = (f32[768]{0:T(1024)S(1)}, f32[768]{0:T(1024)S(1)}) fusion(f32[]{:T(128)S(6)} %sub.102, f32[]{:T(128)S(6)} %sub.101, f32[]{:T(128)S(6)} %sub.100, f32[]{:T(128)S(6)} %sub.99, s32[]{:T(128)} %bitcast.4, s32[]{:T(128)} %bitcast.3, s32[]{:T(128)} %bitcast.2, s32[]{:T(128)} %bitcast.1), kind=kLoop, calls=%fused_computation.203 | loop fusion | flops 21504 | bytes 6176 | tf_op jit(solution)/shard_map/jit(_where)/select_n | solution.py:92
  33.2 0.6 fusion.31
  34.1 0.7 fusion.178
  34.8 0.8 fusion.23
  35.6 0.8 fusion.21
  36.4 0.8 fusion.54
  37.1 0.5 collective-permute-start.6
  37.9 1.8 %collective-permute-start.8 = (f32[32,192]{1,0:T(8,128)}, f32[32,192]{1,0:T(8,128)}, u32[]{:S(2)}, u32[]{:S(2)}) collective-permute-start(f32[32,192]{1,0:T(8,128)} %get-tuple-element.33), channel_id=1, source_target_pairs={{0,8},{8,0},{16,24},{24,16},{1,9},{9,1},{17,25},{25,17},{2,10},{10... | collective-permute-start | bytes 73736 | tf_op jit(solution)/shard_map/ppermute | solution.py:23
  39.9 0.7 slice_bitcast_fusion.15
  40.6 1.4 %copy.117 = f32[1,32,32]{2,1,0:T(8,128)} copy(f32[1,32,32]{1,2,0:T(8,128)} %get-tuple-element.58) | data formatting | bytes 8192 | tf_op jit(solution)/shard_map/concatenate | solution.py:38
  42.0 1.4 %copy.118 = f32[1,32,32]{2,1,0:T(8,128)} copy(f32[1,32,32]{1,2,0:T(8,128)} %get-tuple-element.61) | data formatting | bytes 8192 | tf_op jit(solution)/shard_map/concatenate | solution.py:38
  43.4 1.4 %copy.119 = f32[1,32,32]{2,1,0:T(8,128)} copy(f32[1,32,32]{1,2,0:T(8,128)} %get-tuple-element.60) | data formatting | bytes 8192 | tf_op jit(solution)/shard_map/concatenate | solution.py:38
  44.8 1.4 %copy.120 = f32[1,32,32]{2,1,0:T(8,128)} copy(f32[1,32,32]{1,2,0:T(8,128)} %get-tuple-element.59) | data formatting | bytes 8192 | tf_op jit(solution)/shard_map/concatenate | solution.py:38
  46.8 0.8 fusion.155
  47.5 0.9 select_add_fusion.7
  48.4 0.7 select_add_fusion.6
  49.1 0.6 pad_maximum_fusion.4
  49.7 4.8 %all-to-all-start.1 = ((f32[32,4,128]{2,1,0:T(4,128)}), f32[32,4,128]{2,1,0:T(4,128)}, u32[]{:S(2)}, u32[]{:S(2)}) async-start(f32[32,4,128]{2,1,0:T(4,128)} %bitcast.31), calls=%async_computation.1 | async-start | bytes 131072 | tf_op jit(solution)/shard_map/all_to_all | solution.py:33
  54.6 0.9 fusion.32
  55.5 6.4 %all-to-all-done.1 = f32[32,4,128]{2,1,0:T(4,128)} async-done(((f32[32,4,128]{2,1,0:T(4,128)}), f32[32,4,128]{2,1,0:T(4,128)}, u32[]{:S(2)}, u32[]{:S(2)}) %all-to-all-start.1) | async-done | bytes 65568 | tf_op jit(solution)/shard_map/all_to_all | solution.py:33
  61.9 0.9 reduce_sum.65
  63.3 0.9 fusion.77
  64.2 0.6 copy-done.13
  64.8 1.1 %convolution_subtract_fusion = f32[32,768]{1,0:T(8,128)S(1)} fusion(f32[128,32]{0,1:T(8,128)} %copy-done.16, f32[128]{0:T(128)} %copy-done.26, f32[768]{0:T(1024)} %copy-done.19, f32[128]{0:T(128)} %copy-done.25, f32[32,768]{1,0:T(8,128)S(1)} %fusion.77, f32[32]{0:T(128)S(1)} %select_reduce_fusion.3), kind=kOutput, calls=%fused_computation.15 | convolution fusion | flops 37994496 | bytes 217216 | tf_op jit(solution)/shard_map/dot_general | solution.py:14
  66.5 0.5 collective-permute-start.10
  67.0 0.9 collective-permute-start.11
  67.9 0.7 collective-permute-start.12
  68.5 2.2 %collective-permute-done.10 = f32[32,192]{1,0:T(8,128)S(1)} collective-permute-done((f32[32,192]{1,0:T(8,128)S(1)}, f32[32,192]{1,0:T(8,128)S(1)}, u32[]{:S(2)}, u32[]{:S(2)}) %collective-permute-start.10) | collective-permute-done | bytes 24608 | tf_op jit(solution)/shard_map/ppermute | solution.py:23
  70.8 1.2 %collective-permute-done.11 = f32[32,192]{1,0:T(8,128)S(1)} collective-permute-done((f32[32,192]{1,0:T(8,128)S(1)}, f32[32,192]{1,0:T(8,128)S(1)}, u32[]{:S(2)}, u32[]{:S(2)}) %collective-permute-start.11) | collective-permute-done | bytes 24608 | tf_op jit(solution)/shard_map/ppermute | solution.py:23
  72.1 0.8 fusion.50
  73.3 0.8 fusion.22
  75.1 1.1 %fusion.94 = f32[128,32]{0,1:T(8,128)S(1)} fusion(f32[128,128]{1,0:T(8,128)} %copy-done.7, f32[256,32]{0,1:T(8,128)} %copy-done.15), kind=kOutput, calls=%fused_computation.130 | convolution fusion | flops 6291456 | bytes 98304 | tf_op jit(solution)/shard_map/dot_general | solution.py:14
  76.6 0.7 fusion.154
  77.3 0.7 select_add_fusion.3
  78.1 0.6 pad_maximum_fusion.5
  78.8 3.4 %all-to-all-start.2 = ((f32[32,4,128]{2,1,0:T(4,128)}), f32[32,4,128]{2,1,0:T(4,128)S(1)}, u32[]{:S(2)}, u32[]{:S(2)}) async-start(f32[32,4,128]{2,1,0:T(4,128)} %bitcast.46), calls=%async_computation.2 | async-start | bytes 131072 | tf_op jit(solution)/shard_map/all_to_all | solution.py:33
  82.2 0.7 fusion.176
  83.1 1.7 %collective-permute-start.14 = (f32[32,192]{1,0:T(8,128)}, f32[32,192]{1,0:T(8,128)S(1)}, u32[]{:S(2)}, u32[]{:S(2)}) collective-permute-start(f32[32,192]{1,0:T(8,128)} %get-tuple-element.27), channel_id=1, source_target_pairs={{0,2},{1,3},{2,0},{3,1},{4,6},{5,7},{6,4},{7,5},{8,10},{9,11},{10,... | collective-permute-start | bytes 73736 | tf_op jit(solution)/shard_map/ppermute | solution.py:23
  84.8 2.4 %collective-permute-start.15 = (f32[32,192]{1,0:T(8,128)S(1)}, f32[32,192]{1,0:T(8,128)S(1)}, u32[]{:S(2)}, u32[]{:S(2)}) collective-permute-start(f32[32,192]{1,0:T(8,128)S(1)} %get-tuple-element.26), channel_id=1, source_target_pairs={{0,4},{1,5},{2,6},{3,7},{4,0},{5,1},{6,2},{7,3},{8,12},{9,13},{10,... | collective-permute-start | bytes 73736 | tf_op jit(solution)/shard_map/ppermute | solution.py:23
  87.2 1.5 %collective-permute-start.16 = (f32[32,192]{1,0:T(8,128)S(1)}, f32[32,192]{1,0:T(8,128)S(1)}, u32[]{:S(2)}, u32[]{:S(2)}) collective-permute-start(f32[32,192]{1,0:T(8,128)S(1)} %get-tuple-element.25), channel_id=1, source_target_pairs={{0,8},{8,0},{16,24},{24,16},{1,9},{9,1},{17,25},{25,17},{2,10},{10... | collective-permute-start | bytes 73736 | tf_op jit(solution)/shard_map/ppermute | solution.py:23
  88.7 0.8 all-to-all-done.2
  90.0 1.2 %collective-permute-done.16 = f32[32,192]{1,0:T(8,128)S(1)} collective-permute-done((f32[32,192]{1,0:T(8,128)S(1)}, f32[32,192]{1,0:T(8,128)S(1)}, u32[]{:S(2)}, u32[]{:S(2)}) %collective-permute-start.16) | collective-permute-done | bytes 24608 | tf_op jit(solution)/shard_map/ppermute | solution.py:23
  92.0 0.6 broadcast_in_dim.254
  92.7 3.4 %all-to-all-start.3 = ((f32[32,1,128]{2,1,0:T(1,128)}), f32[32,1,128]{2,1,0:T(1,128)S(1)}, u32[]{:S(2)}, u32[]{:S(2)}) async-start(f32[32,1,128]{2,1,0:T(1,128)} %broadcast_in_dim.254), calls=%async_computation.3 | async-start | bytes 32768 | tf_op jit(solution)/shard_map/all_to_all | solution.py:33
  96.5 1.7 %collective-permute-start.18 = (f32[32,192]{1,0:T(8,128)S(1)}, f32[32,192]{1,0:T(8,128)S(1)}, u32[]{:S(2)}, u32[]{:S(2)}) collective-permute-start(f32[32,192]{1,0:T(8,128)S(1)} %get-tuple-element.23), channel_id=1, source_target_pairs={{0,2},{1,3},{2,0},{3,1},{4,6},{5,7},{6,4},{7,5},{8,10},{9,11},{10,... | collective-permute-start | bytes 73736 | tf_op jit(solution)/shard_map/ppermute | solution.py:23
  98.2 2.4 %collective-permute-start.19 = (f32[32,192]{1,0:T(8,128)S(1)}, f32[32,192]{1,0:T(8,128)S(1)}, u32[]{:S(2)}, u32[]{:S(2)}) collective-permute-start(f32[32,192]{1,0:T(8,128)S(1)} %get-tuple-element.22), channel_id=1, source_target_pairs={{0,4},{1,5},{2,6},{3,7},{4,0},{5,1},{6,2},{7,3},{8,12},{9,13},{10,... | collective-permute-start | bytes 73736 | tf_op jit(solution)/shard_map/ppermute | solution.py:23
  100.6 1.5 %collective-permute-start.20 = (f32[32,192]{1,0:T(8,128)S(1)}, f32[32,192]{1,0:T(8,128)S(1)}, u32[]{:S(2)}, u32[]{:S(2)}) collective-permute-start(f32[32,192]{1,0:T(8,128)S(1)} %get-tuple-element.21), channel_id=1, source_target_pairs={{0,8},{8,0},{16,24},{24,16},{1,9},{9,1},{17,25},{25,17},{2,10},{10... | collective-permute-start | bytes 73736 | tf_op jit(solution)/shard_map/ppermute | solution.py:23
  102.0 1.1 %all-to-all-done.3 = f32[32,1,128]{2,1,0:T(1,128)S(1)} async-done(((f32[32,1,128]{2,1,0:T(1,128)}), f32[32,1,128]{2,1,0:T(1,128)S(1)}, u32[]{:S(2)}, u32[]{:S(2)}) %all-to-all-start.3) | async-done | bytes 16416 | tf_op jit(solution)/shard_map/all_to_all | solution.py:33
  103.3 1.1 %collective-permute-done.20 = f32[32,192]{1,0:T(8,128)S(1)} collective-permute-done((f32[32,192]{1,0:T(8,128)S(1)}, f32[32,192]{1,0:T(8,128)S(1)}, u32[]{:S(2)}, u32[]{:S(2)}) %collective-permute-start.20) | collective-permute-done | bytes 24608 | tf_op jit(solution)/shard_map/ppermute | solution.py:23
  104.5 0.8 fusion.43
  (191 shorter events, 11.5 us)
Async XLA Ops:
  0.6 33.1 %copy-start = (bf16[1,1,768,768]{3,2,1,0:T(8,128)(2,1)S(1)}, bf16[1,1,768,768]{3,2,1,0:T(8,128)(2,1)}, u32[]{:S(2)}) copy-start(bf16[1,1,768,768]{3,2,1,0:T(8,128)(2,1)} %param.8) | copy-start | bytes 3538948
  4.1 12.3 %copy-start.21 = (s32[16]{0:T(128)}, s32[16]{0:T(128)S(1)}, u32[]{:S(2)}) copy-start(s32[16]{0:T(128)S(1)} %eq.297) | copy-start | bytes 196
  9.2 20.8 %all-to-all-start = ((f32[32,8,128]{2,1,0:T(8,128)}), f32[32,8,128]{2,1,0:T(8,128)S(1)}, u32[]{:S(2)}, u32[]{:S(2)}) async-start(f32[32,8,128]{2,1,0:T(8,128)} %broadcast_in_dim.226), calls=%async_computation | async-start | bytes 262144 | tf_op jit(solution)/shard_map/all_to_all | solution.py:33
  17.9 14.4 %copy-start.8 = (f32[128,128]{1,0:T(8,128)}, f32[128,128]{1,0:T(8,128)S(1)}, u32[]{:S(2)}) copy-start(f32[128,128]{1,0:T(8,128)S(1)} %fusion.61) | copy-start | bytes 196612
  17.9 14.9 %collective-permute-start.4 = (f32[128,128]{1,0:T(8,128)S(1)}, f32[128,128]{1,0:T(8,128)S(1)}, u32[]{:S(2)}, u32[]{:S(2)}) collective-permute-start(f32[128,128]{1,0:T(8,128)S(1)} %fusion.61), channel_id=1, source_target_pairs={{0,8},{8,0},{16,24},{24,16},{1,9},{9,1},{17,25},{25,17},{2,10},{10... | collective-permute-start | bytes 196616 | tf_op jit(solution)/shard_map/ppermute | solution.py:23
  21.4 11.7 %collective-permute-start = (f32[32,192]{1,0:T(8,128)S(1)}, f32[32,192]{1,0:T(8,128)S(1)}, u32[]{:S(2)}, u32[]{:S(2)}) collective-permute-start(f32[32,192]{1,0:T(8,128)S(1)} %get-tuple-element.36), channel_id=1, source_target_pairs={{0,1},{1,0},{2,3},{3,2},{4,5},{5,4},{6,7},{7,6},{8,9},{9,8},{10,11... | collective-permute-start | bytes 73736 | tf_op jit(solution)/shard_map/ppermute | solution.py:23
  21.5 11.6 %collective-permute-start.1 = (f32[32,192]{1,0:T(8,128)S(1)}, f32[32,192]{1,0:T(8,128)S(1)}, u32[]{:S(2)}, u32[]{:S(2)}) collective-permute-start(f32[32,192]{1,0:T(8,128)S(1)} %get-tuple-element.39), channel_id=1, source_target_pairs={{0,2},{1,3},{2,0},{3,1},{4,6},{5,7},{6,4},{7,5},{8,10},{9,11},{10,... | collective-permute-start | bytes 73736 | tf_op jit(solution)/shard_map/ppermute | solution.py:23
  23.0 10.1 %collective-permute-start.2 = (f32[32,192]{1,0:T(8,128)S(1)}, f32[32,192]{1,0:T(8,128)S(1)}, u32[]{:S(2)}, u32[]{:S(2)}) collective-permute-start(f32[32,192]{1,0:T(8,128)S(1)} %get-tuple-element.38), channel_id=1, source_target_pairs={{0,4},{1,5},{2,6},{3,7},{4,0},{5,1},{6,2},{7,3},{8,12},{9,13},{10,... | collective-permute-start | bytes 73736 | tf_op jit(solution)/shard_map/ppermute | solution.py:23
  25.5 7.7 %collective-permute-start.3 = (f32[32,192]{1,0:T(8,128)S(1)}, f32[32,192]{1,0:T(8,128)S(1)}, u32[]{:S(2)}, u32[]{:S(2)}) collective-permute-start(f32[32,192]{1,0:T(8,128)S(1)} %get-tuple-element.37), channel_id=1, source_target_pairs={{0,8},{8,0},{16,24},{24,16},{1,9},{9,1},{17,25},{25,17},{2,10},{10... | collective-permute-start | bytes 73736 | tf_op jit(solution)/shard_map/ppermute | solution.py:23
  26.8 5.5 %copy-start.26 = (f32[128]{0:T(128)}, f32[128]{0:T(128)S(1)}, u32[]{:S(2)}) copy-start(f32[128]{0:T(128)S(1)} %convert_element_type.142) | copy-start | bytes 1540
  27.3 4.9 %copy-start.19 = (f32[768]{0:T(1024)}, f32[768]{0:T(1024)S(1)}, u32[]{:S(2)}) copy-start(f32[768]{0:T(1024)S(1)} %iota_convert_fusion) | copy-start | bytes 9220
  31.5 0.5 copy-start.25
  32.5 1.6 %copy-start.16 = (f32[128,32]{0,1:T(8,128)}, f32[128,32]{0,1:T(8,128)S(1)}, u32[]{:S(2)}) copy-start(f32[128,32]{0,1:T(8,128)S(1)} %fusion.102) | copy-start | bytes 49156
  32.8 13.3 %copy-start.7 = (f32[128,128]{1,0:T(8,128)}, f32[128,128]{1,0:T(8,128)S(1)}, u32[]{:S(2)}) copy-start(f32[128,128]{1,0:T(8,128)S(1)} %collective-permute-done.4) | copy-start | bytes 196612
  33.7 2.6 %copy-start.2 = (f32[1,1,32,768]{3,2,1,0:T(8,128)S(1)}, f32[1,1,32,768]{3,2,1,0:T(8,128)}, u32[]{:S(2)}) copy-start(f32[1,1,32,768]{3,2,1,0:T(8,128)} %param.6) | copy-start | bytes 294916
  33.7 5.9 %copy-start.9 = (f32[128,128]{1,0:T(8,128)S(1)}, f32[128,128]{1,0:T(8,128)}, u32[]{:S(2)}) copy-start(f32[128,128]{1,0:T(8,128)} %copy-done.8) | copy-start | bytes 196612
  36.4 29.6 %copy-start.1 = (bf16[1,1,768,768]{3,2,1,0:T(8,128)(2,1)S(1)}, bf16[1,1,768,768]{3,2,1,0:T(8,128)(2,1)}, u32[]{:S(2)}) copy-start(bf16[1,1,768,768]{3,2,1,0:T(8,128)(2,1)} %param.7) | copy-start | bytes 3538948
  37.1 17.4 %collective-permute-start.5 = (f32[32,192]{1,0:T(8,128)}, f32[32,192]{1,0:T(8,128)}, u32[]{:S(2)}, u32[]{:S(2)}) collective-permute-start(f32[32,192]{1,0:T(8,128)} %get-tuple-element.32), channel_id=1, source_target_pairs={{0,1},{1,0},{2,3},{3,2},{4,5},{5,4},{6,7},{7,6},{8,9},{9,8},{10,11... | collective-permute-start | bytes 73736 | tf_op jit(solution)/shard_map/ppermute | solution.py:23
  37.1 17.4 %collective-permute-start.6 = (f32[32,192]{1,0:T(8,128)}, f32[32,192]{1,0:T(8,128)}, u32[]{:S(2)}, u32[]{:S(2)}) collective-permute-start(f32[32,192]{1,0:T(8,128)} %get-tuple-element.35), channel_id=1, source_target_pairs={{0,2},{1,3},{2,0},{3,1},{4,6},{5,7},{6,4},{7,5},{8,10},{9,11},{10,... | collective-permute-start | bytes 73736 | tf_op jit(solution)/shard_map/ppermute | solution.py:23
  37.7 16.9 %collective-permute-start.7 = (f32[32,192]{1,0:T(8,128)}, f32[32,192]{1,0:T(8,128)}, u32[]{:S(2)}, u32[]{:S(2)}) collective-permute-start(f32[32,192]{1,0:T(8,128)} %get-tuple-element.34), channel_id=1, source_target_pairs={{0,4},{1,5},{2,6},{3,7},{4,0},{5,1},{6,2},{7,3},{8,12},{9,13},{10,... | collective-permute-start | bytes 73736 | tf_op jit(solution)/shard_map/ppermute | solution.py:23
  37.9 16.6 %collective-permute-start.8 = (f32[32,192]{1,0:T(8,128)}, f32[32,192]{1,0:T(8,128)}, u32[]{:S(2)}, u32[]{:S(2)}) collective-permute-start(f32[32,192]{1,0:T(8,128)} %get-tuple-element.33), channel_id=1, source_target_pairs={{0,8},{8,0},{16,24},{24,16},{1,9},{9,1},{17,25},{25,17},{2,10},{10... | collective-permute-start | bytes 73736 | tf_op jit(solution)/shard_map/ppermute | solution.py:23
  49.7 12.1 %all-to-all-start.1 = ((f32[32,4,128]{2,1,0:T(4,128)}), f32[32,4,128]{2,1,0:T(4,128)}, u32[]{:S(2)}, u32[]{:S(2)}) async-start(f32[32,4,128]{2,1,0:T(4,128)} %bitcast.31), calls=%async_computation.1 | async-start | bytes 131072 | tf_op jit(solution)/shard_map/all_to_all | solution.py:33
  62.8 0.6 copy-start.17
  63.0 9.1 %copy-start.23 = (f32[32]{0:T(128)}, f32[32]{0:T(128)S(1)}, u32[]{:S(2)}) copy-start(f32[32]{0:T(128)S(1)} %select_reduce_fusion.3) | copy-start | bytes 388
  64.2 0.6 copy-start.13
  66.0 6.0 %copy-start.11 = (f32[32,768]{1,0:T(8,128)}, f32[32,768]{1,0:T(8,128)S(1)}, u32[]{:S(2)}) copy-start(f32[32,768]{1,0:T(8,128)S(1)} %convolution_subtract_fusion) | copy-start | bytes 294916
  66.5 4.3 %collective-permute-start.10 = (f32[32,192]{1,0:T(8,128)S(1)}, f32[32,192]{1,0:T(8,128)S(1)}, u32[]{:S(2)}, u32[]{:S(2)}) collective-permute-start(f32[32,192]{1,0:T(8,128)S(1)} %get-tuple-element.31), channel_id=1, source_target_pairs={{0,2},{1,3},{2,0},{3,1},{4,6},{5,7},{6,4},{7,5},{8,10},{9,11},{10,... | collective-permute-start | bytes 73736 | tf_op jit(solution)/shard_map/ppermute | solution.py:23
  67.0 5.0 %collective-permute-start.11 = (f32[32,192]{1,0:T(8,128)S(1)}, f32[32,192]{1,0:T(8,128)S(1)}, u32[]{:S(2)}, u32[]{:S(2)}) collective-permute-start(f32[32,192]{1,0:T(8,128)S(1)} %get-tuple-element.30), channel_id=1, source_target_pairs={{0,4},{1,5},{2,6},{3,7},{4,0},{5,1},{6,2},{7,3},{8,12},{9,13},{10,... | collective-permute-start | bytes 73736 | tf_op jit(solution)/shard_map/ppermute | solution.py:23
  67.9 4.1 %collective-permute-start.12 = (f32[32,192]{1,0:T(8,128)S(1)}, f32[32,192]{1,0:T(8,128)S(1)}, u32[]{:S(2)}, u32[]{:S(2)}) collective-permute-start(f32[32,192]{1,0:T(8,128)S(1)} %get-tuple-element.29), channel_id=1, source_target_pairs={{0,8},{8,0},{16,24},{24,16},{1,9},{9,1},{17,25},{25,17},{2,10},{10... | collective-permute-start | bytes 73736 | tf_op jit(solution)/shard_map/ppermute | solution.py:23
  68.5 3.5 %collective-permute-start.9 = (f32[32,192]{1,0:T(8,128)S(1)}, f32[32,192]{1,0:T(8,128)S(1)}, u32[]{:S(2)}, u32[]{:S(2)}) collective-permute-start(f32[32,192]{1,0:T(8,128)S(1)} %get-tuple-element.28), channel_id=1, source_target_pairs={{0,1},{1,0},{2,3},{3,2},{4,5},{5,4},{6,7},{7,6},{8,9},{9,8},{10,11... | collective-permute-start | bytes 73736 | tf_op jit(solution)/shard_map/ppermute | solution.py:23
  72.9 1.6 %copy-start.10 = (f32[128,128]{1,0:T(8,128)S(1)}, f32[128,128]{1,0:T(8,128)}, u32[]{:S(2)}) copy-start(f32[128,128]{1,0:T(8,128)} %copy-done.8) | copy-start | bytes 196612
  73.3 1.0 copy-start.5
  73.3 0.8 copy-start.3
  74.1 0.8 copy-start.15
  74.1 3.9 %copy-start.20 = (pred[32]{0:T(512)(128)(4,1)S(1)}, pred[32]{0:T(512)(128)(4,1)}, u32[]{:S(2)}) copy-start(pred[32]{0:T(512)(128)(4,1)} %fusion.151) | copy-start | bytes 100
  74.1 15.4 %copy-start.18 = (f32[4,128]{1,0:T(4,128)S(1)}, f32[4,128]{1,0:T(4,128)}, u32[]{:S(2)}) copy-start(f32[4,128]{1,0:T(4,128)} %copy-done.17) | copy-start | bytes 6148
  74.1 17.0 %copy-start.24 = (f32[32]{0:T(128)S(1)}, f32[32]{0:T(128)}, u32[]{:S(2)}) copy-start(f32[32]{0:T(128)} %copy-done.23) | copy-start | bytes 388
  74.3 7.8 %copy-start.4 = (f32[32,768]{1,0:T(8,128)S(1)}, f32[32,768]{1,0:T(8,128)}, u32[]{:S(2)}) copy-start(f32[32,768]{1,0:T(8,128)} %copy-done.3) | copy-start | bytes 294916
  74.5 16.6 %copy-start.6 = (f32[64,768]{1,0:T(8,128)S(1)}, f32[64,768]{1,0:T(8,128)}, u32[]{:S(2)}) copy-start(f32[64,768]{1,0:T(8,128)} %copy-done.5) | copy-start | bytes 589828
  78.8 10.8 %all-to-all-start.2 = ((f32[32,4,128]{2,1,0:T(4,128)}), f32[32,4,128]{2,1,0:T(4,128)S(1)}, u32[]{:S(2)}, u32[]{:S(2)}) async-start(f32[32,4,128]{2,1,0:T(4,128)} %bitcast.46), calls=%async_computation.2 | async-start | bytes 131072 | tf_op jit(solution)/shard_map/all_to_all | solution.py:33
  82.1 9.4 %copy-start.12 = (f32[32,768]{1,0:T(8,128)S(1)}, f32[32,768]{1,0:T(8,128)}, u32[]{:S(2)}) copy-start(f32[32,768]{1,0:T(8,128)} %copy-done.11) | copy-start | bytes 294916
  82.2 9.4 %copy-start.14 = (f32[32,768]{1,0:T(8,128)S(1)}, f32[32,768]{1,0:T(8,128)}, u32[]{:S(2)}) copy-start(f32[32,768]{1,0:T(8,128)} %copy-done.13) | copy-start | bytes 294916
  82.2 9.4 %copy-start.22 = (s32[16]{0:T(128)S(1)}, s32[16]{0:T(128)}, u32[]{:S(2)}) copy-start(s32[16]{0:T(128)} %copy-done.21) | copy-start | bytes 196
  82.9 7.1 %collective-permute-start.13 = (f32[32,192]{1,0:T(8,128)}, f32[32,192]{1,0:T(8,128)S(1)}, u32[]{:S(2)}, u32[]{:S(2)}) collective-permute-start(f32[32,192]{1,0:T(8,128)} %get-tuple-element.24), channel_id=1, source_target_pairs={{0,1},{1,0},{2,3},{3,2},{4,5},{5,4},{6,7},{7,6},{8,9},{9,8},{10,11... | collective-permute-start | bytes 73736 | tf_op jit(solution)/shard_map/ppermute | solution.py:23
  83.1 6.8 %collective-permute-start.14 = (f32[32,192]{1,0:T(8,128)}, f32[32,192]{1,0:T(8,128)S(1)}, u32[]{:S(2)}, u32[]{:S(2)}) collective-permute-start(f32[32,192]{1,0:T(8,128)} %get-tuple-element.27), channel_id=1, source_target_pairs={{0,2},{1,3},{2,0},{3,1},{4,6},{5,7},{6,4},{7,5},{8,10},{9,11},{10,... | collective-permute-start | bytes 73736 | tf_op jit(solution)/shard_map/ppermute | solution.py:23
  84.8 5.2 %collective-permute-start.15 = (f32[32,192]{1,0:T(8,128)S(1)}, f32[32,192]{1,0:T(8,128)S(1)}, u32[]{:S(2)}, u32[]{:S(2)}) collective-permute-start(f32[32,192]{1,0:T(8,128)S(1)} %get-tuple-element.26), channel_id=1, source_target_pairs={{0,4},{1,5},{2,6},{3,7},{4,0},{5,1},{6,2},{7,3},{8,12},{9,13},{10,... | collective-permute-start | bytes 73736 | tf_op jit(solution)/shard_map/ppermute | solution.py:23
  87.2 3.9 %collective-permute-start.16 = (f32[32,192]{1,0:T(8,128)S(1)}, f32[32,192]{1,0:T(8,128)S(1)}, u32[]{:S(2)}, u32[]{:S(2)}) collective-permute-start(f32[32,192]{1,0:T(8,128)S(1)} %get-tuple-element.25), channel_id=1, source_target_pairs={{0,8},{8,0},{16,24},{24,16},{1,9},{9,1},{17,25},{25,17},{2,10},{10... | collective-permute-start | bytes 73736 | tf_op jit(solution)/shard_map/ppermute | solution.py:23
  92.7 10.5 %all-to-all-start.3 = ((f32[32,1,128]{2,1,0:T(1,128)}), f32[32,1,128]{2,1,0:T(1,128)S(1)}, u32[]{:S(2)}, u32[]{:S(2)}) async-start(f32[32,1,128]{2,1,0:T(1,128)} %broadcast_in_dim.254), calls=%async_computation.3 | async-start | bytes 32768 | tf_op jit(solution)/shard_map/all_to_all | solution.py:33
  96.2 7.1 %collective-permute-start.17 = (f32[32,192]{1,0:T(8,128)S(1)}, f32[32,192]{1,0:T(8,128)S(1)}, u32[]{:S(2)}, u32[]{:S(2)}) collective-permute-start(f32[32,192]{1,0:T(8,128)S(1)} %get-tuple-element.20), channel_id=1, source_target_pairs={{0,1},{1,0},{2,3},{3,2},{4,5},{5,4},{6,7},{7,6},{8,9},{9,8},{10,11... | collective-permute-start | bytes 73736 | tf_op jit(solution)/shard_map/ppermute | solution.py:23
  96.5 6.9 %collective-permute-start.18 = (f32[32,192]{1,0:T(8,128)S(1)}, f32[32,192]{1,0:T(8,128)S(1)}, u32[]{:S(2)}, u32[]{:S(2)}) collective-permute-start(f32[32,192]{1,0:T(8,128)S(1)} %get-tuple-element.23), channel_id=1, source_target_pairs={{0,2},{1,3},{2,0},{3,1},{4,6},{5,7},{6,4},{7,5},{8,10},{9,11},{10,... | collective-permute-start | bytes 73736 | tf_op jit(solution)/shard_map/ppermute | solution.py:23
  98.2 5.2 %collective-permute-start.19 = (f32[32,192]{1,0:T(8,128)S(1)}, f32[32,192]{1,0:T(8,128)S(1)}, u32[]{:S(2)}, u32[]{:S(2)}) collective-permute-start(f32[32,192]{1,0:T(8,128)S(1)} %get-tuple-element.22), channel_id=1, source_target_pairs={{0,4},{1,5},{2,6},{3,7},{4,0},{5,1},{6,2},{7,3},{8,12},{9,13},{10,... | collective-permute-start | bytes 73736 | tf_op jit(solution)/shard_map/ppermute | solution.py:23
  100.6 3.9 %collective-permute-start.20 = (f32[32,192]{1,0:T(8,128)S(1)}, f32[32,192]{1,0:T(8,128)S(1)}, u32[]{:S(2)}, u32[]{:S(2)}) collective-permute-start(f32[32,192]{1,0:T(8,128)S(1)} %get-tuple-element.21), channel_id=1, source_target_pairs={{0,8},{8,0},{16,24},{24,16},{1,9},{9,1},{17,25},{25,17},{2,10},{10... | collective-permute-start | bytes 73736 | tf_op jit(solution)/shard_map/ppermute | solution.py:23

commit v2 on v0

v2 whole, which is shorter than its diff:
```python
import functools

import jax
import jax.numpy as jnp
from jax import lax
from jax.experimental import pallas as pl
from jax.experimental.pallas import tpu as pltpu
from jax.sharding import PartitionSpec as P

F32, BF16 = jnp.float32, jnp.bfloat16
NT = (((1,), (1,)), ((), ()))
NN = (((1,), (0,)), ((), ()))
LANES = 128


def exact(a, b, dims=NN):
    return lax.dot_general(a, b, dims, precision=lax.Precision.HIGHEST, preferred_element_type=F32)


def rounded(a, b):
    return lax.dot_general(a, b, NN, preferred_element_type=F32)


def thirds(x):
    high = x.astype(BF16)
    rest = x - high.astype(F32)
    mid = rest.astype(BF16)
    return jnp.concatenate([high, mid, (rest - mid.astype(F32)).astype(BF16)], axis=0)


def by_map(x, corner_map, dims):
    n = x.shape[0]
    out = lax.dot_general(thirds(x), corner_map, dims, preferred_element_type=F32)
    return out[:n] + out[n : 2 * n] + out[2 * n :]


def iota(shape, axis):
    return lax.broadcasted_iota(jnp.int32, shape, axis)


def windows(dofs):
    width = dofs // 4
    return [(f * width // LANES * LANES, -(-(f + 1) * width // LANES) * LANES) for f in range(4)]


def face_vectors(info, nodes_ref, dofs):
    width = dofs // 4
    pos = iota((1, dofs), 1)
    sub_pos, grp_pos = info[0], info[1]
    bits = [sub_pos & 1, (sub_pos >> 1) & 1, (sub_pos >> 2) & 1, grp_pos & 1]
    sign = jnp.zeros((1, dofs), F32)
    live = jnp.zeros((1, dofs), jnp.int32)
    node = pos
    for f in range(4):
        inside = (pos >= f * width) & (pos < (f + 1) * width)
        sign = jnp.where(inside, (1 - 2 * bits[f]).astype(F32), sign)
        live = jnp.where(inside, nodes_ref[f], live)
    for step in range(1, 12):
        node = jnp.where(pos >= step * (width // 3), pos - step * (width // 3), node)
    mask = jnp.where(node < live, 1.0, 0.0)
    return sign, mask


def corner_rows(ids_ref, dofs):
    row = iota((16, 1), 0)
    ids = jnp.full((16, 1), -1, jnp.int32)
    for k in range(ids_ref.shape[0]):
        ids = jnp.where(row == 4 * (k % 4) + k // 4, ids_ref[k], ids)
    return jnp.where(ids == iota((16, dofs), 1), 1.0, 0.0)


def across(wins, dofs):
    spans, width = windows(dofs), dofs // 4
    n = wins[0].shape[0]
    tiles = []
    for low in range(0, dofs, LANES):
        tile = None
        for f, (start, stop) in enumerate(spans):
            if start <= low < stop:
                part = wins[f][:, low - start : low - start + LANES]
                tile = part if tile is None else jnp.where(iota((n, LANES), 1) + low < f * width, tile, part)
        tiles.append(tile)
    return jnp.concatenate(tiles, axis=1)


def put_windows(refs, field):
    for ref, (start, stop) in zip(refs, windows(field.shape[1])):
        ref[: field.shape[0], :] = field[:, start:stop]


def same_block(n_row, n_col, row_block, col_block):
    return iota((n_row, n_col), 0) // row_block == iota((n_row, n_col), 1) // col_block


def to_column(row):
    n = row.shape[1]
    return jnp.sum(jnp.where(same_block(n, n, 1, 1), row, 0.0), axis=1, keepdims=True)


def to_row(column):
    n = column.shape[0]
    return jnp.sum(jnp.where(same_block(n, n, 1, 1), column, 0.0), axis=0, keepdims=True)


def total_of(received):
    total = received[0:8]
    for low in range(8, received.shape[0], 8):
        total = total + received[low : low + 8]
    return total + pltpu.roll(total, 4, 0)


def sums_of(total, n_load):
    column = to_column(total[3:4])
    return [column[i * n_load : (i + 1) * n_load] for i in range(4)]


def corner_field(total, ids_ref, n_load, dofs):
    flipped = total.T
    pos = iota((1, dofs), 1)
    field = jnp.zeros((n_load, dofs), F32)
    for k in range(ids_ref.shape[0]):
        q, r = k // 4, k % 4
        field = jnp.where(pos == ids_ref[k], flipped[r * n_load : (r + 1) * n_load, q : q + 1], field)
    return field


def put_contributions(ref, image, corner_map, spread, sign, sums, info, groups):
    n_load = image.shape[0]
    at_corners = by_map(0.5 * sign * image, corner_map, NT)
    tiled = jnp.concatenate([at_corners] * 4, axis=0)
    n, n_corner = tiled.shape
    inner = iota((n, n_corner), 1) < 64
    pair = jnp.concatenate([jnp.where(inner, tiled, 0.0), jnp.where(inner, 0.0, tiled)], axis=0)
    full = exact(spread, pair, NT)
    rows = full.shape[0] // 4
    keep = iota((4 * rows, 2 * n), 0) // rows == iota((4 * rows, 2 * n), 1) % n // n_load
    full = jnp.where(keep, full, 0.0)
    packed = full[:rows] + full[rows : 2 * rows] + full[2 * rows : 3 * rows] + full[3 * rows :]
    zero = jnp.zeros((n_load, 1), F32)
    sums = to_row(jnp.concatenate(sums + [zero] * (4 - len(sums)), axis=0))
    is_last = iota((rows, 1), 0) % 4 == 3
    totals = jnp.where(is_last, sums, 0.0)
    for g in range(groups):
        same, near = g == info[1], g == (info[1] ^ 1)
        ref[g * rows : (g + 1) * rows, :] = totals + jnp.where(same, packed[:, :n], jnp.where(near, packed[:, n:], 0.0))


def first_corners(info, nodes, ids, loads, out):
    dofs, n_load = loads.shape[1], loads.shape[0]
    sign, mask = face_vectors(info, nodes, dofs)
    scaled = 0.5 * sign * (loads[...] * mask)
    values = by_map(scaled, corner_rows(ids, dofs).astype(BF16), NT)
    flipped = jnp.concatenate([values] * 4, axis=0).T
    flipped = jnp.where(same_block(16, 4 * n_load, 4, n_load), flipped, 0.0)
    block = flipped[:8] + flipped[8:]
    block = block + pltpu.roll(block, 4, 0)
    for low in range(0, out.shape[0], 8):
        out[low : low + 8, :] = block


def first_local(info, nodes, ids, loads, stiff, inverse, local_out, spread_out, *wins):
    dofs = loads.shape[1]
    sign, mask = face_vectors(info, nodes, dofs)
    scaled = 0.5 * sign * (loads[...] * mask)
    local = rounded(scaled.astype(BF16), stiff[...])
    local_out[...] = local
    put_windows(wins, local)
    corner = corner_rows(ids, dofs)
    for ref, (start, stop) in zip(wins, windows(dofs)):
        ref[32:48, :] = corner[:, start:stop]
    n = inverse.shape[0]
    corners = ids.shape[0]
    subs = n // corners
    sub_pos = info[0]
    row = iota((64, 1), 0)
    owner = jnp.where(row < 16, sub_pos, jnp.where(row < 32, sub_pos ^ 1, jnp.where(row < 48, sub_pos ^ 2, sub_pos ^ 4)))
    source = owner * corners + row % 4 * 4 + row // 4 % 4
    pick = jnp.where((source == iota((64, n), 1)) & (row % 4 * 4 < corners), 1.0, 0.0)
    place = iota((16 * subs, 1), 0)
    source = place // 4 % subs * corners + place % 4 * 4 + place // (4 * subs)
    order = jnp.where((source == iota((16 * subs, n), 1)) & (place % 4 * 4 < corners), 1.0, 0.0)
    spread = exact(exact(pick, inverse[...]), order, NT)
    spread_out[...] = spread
    last = wins[3]
    wide = last.shape[1]
    n_piece = (last.shape[0] - 48) // 16
    own = jnp.concatenate([spread[:16], jnp.zeros((16, max(n_piece * wide - 16 * subs, LANES)), F32)], axis=1)
    for i in range(n_piece):
        last[48 + 16 * i : 64 + 16 * i, :] = own[:, i * wide : (i + 1) * wide]


def maps(info, nodes, ids, local, spread, w0, w1, w2, w3, jumped_out, map_out, spread_out):
    n_load, dofs = local.shape
    sign, mask = face_vectors(info, nodes, dofs)
    sign_mask = sign * mask
    wins = [w0, w1, w2, w3]
    jumped_out[...] = (local[...] - across([w[:n_load, :] for w in wins], dofs)) * sign_mask
    map_out[0:16, :] = (corner_rows(ids, dofs) * sign_mask).astype(BF16)
    other = across([w[32:48, :] for w in wins], dofs) * sign_mask
    width = dofs // 4
    for f in range(4):
        pos = iota((1, dofs), 1)
        inside = (pos >= f * width) & (pos < (f + 1) * width)
        map_out[16 + 16 * f : 32 + 16 * f, :] = jnp.where(inside, -other, 0.0).astype(BF16)
    pieces = [w3[low : low + 16, :] for low in range(48, w3.shape[0], 16)]
    cross = pieces[0] if len(pieces) == 1 else jnp.concatenate(pieces, axis=1)
    rows = jnp.concatenate([spread[...], cross[:, : spread.shape[1]], jnp.zeros((48, spread.shape[1]), F32)], axis=0)
    spread_out[...] = rows.T[:, :80]


def first_image(
    groups, info, nodes, received, loads, jumped, corner_map, spread, flex, z_out, image_out, own_out, out, *wins
):
    n_load, dofs = loads.shape
    sign, mask = face_vectors(info, nodes, dofs)
    rows = spread.shape[0] // 4
    coarse = None
    for which, inner in ((info[1], True), (info[1] ^ 1, False)):
        block = received[pl.ds(pl.multiple_of(which * rows, 8), rows), :]
        flipped = block.T
        part = jnp.zeros((n_load, 80), F32)
        for r in range(4):
            part = part + exact(flipped[r * n_load : (r + 1) * n_load], spread[r * rows : (r + 1) * rows, :])
        coarse = part if coarse is None else jnp.where(iota((n_load, 80), 1) < 64, coarse, part)
    own = jnp.where(iota((n_load, 80), 1) < 16, coarse, 0.0)
    fields = by_map(jnp.concatenate([coarse, own], axis=0), corner_map[...], NN)
    zvec = jumped[...] + fields[:n_load]
    own_out[...] = sign * fields[n_load:]
    z_out[...] = zvec
    signed = sign * zvec
    image = rounded(signed.astype(BF16), flex[...])
    image_out[...] = image
    put_windows(wins, image)
    rz = jnp.sum(loads[...] * mask * zvec, axis=1, keepdims=True)
    curve = 2.0 * jnp.sum(signed * image, axis=1, keepdims=True)
    put_contributions(out, image, corner_map[...], spread[...], sign, [rz, curve], info, groups)


def second_local(
    info, nodes, ids, received, image, a0, a1, a2, a3, zvec, loads, own, stiff,
    resid_out, flexed_out, mult_out, own_out, added_out, total_out, local_out, *wins,
):
    n_load, dofs = loads.shape
    sign, mask = face_vectors(info, nodes, dofs)
    total = total_of(received)
    total_out[...] = total
    rz, curve, _, _ = sums_of(total, n_load)
    alpha = rz / curve
    flexed = (image[...] - across([a0, a1, a2, a3], dofs)) * (sign * mask)
    flexed_out[...] = flexed
    mult_out[...] = alpha * zvec[...]
    resid = loads[...] * mask - alpha * flexed
    resid_out[...] = resid
    added = corner_field(total, ids, n_load, dofs)
    added_out[...] = added
    own_new = own[...] - alpha * added
    own_out[...] = own_new
    local = rounded((0.5 * sign * resid).astype(BF16), stiff[...]) + own_new
    local_out[...] = local
    put_windows(wins, local)


def second_image(
    groups, info, nodes, local, a0, a1, a2, a3, resid, flexed, corner_map, spread, flex, z_out, image_out, out, *wins
):
    n_load, dofs = local.shape
    sign, mask = face_vectors(info, nodes, dofs)
    zvec = (local[...] - across([a0, a1, a2, a3], dofs)) * (sign * mask)
    z_out[...] = zvec
    signed = sign * zvec
    high = signed.astype(BF16)
    low = (signed - high.astype(F32)).astype(BF16)
    both = rounded(jnp.concatenate([high, low], axis=0), flex[...])
    image = both[:n_load] + both[n_load:]
    image_out[...] = image
    put_windows(wins, image)
    rz = jnp.sum(resid[...] * zvec, axis=1, keepdims=True)
    curve = 2.0 * jnp.sum(signed * image, axis=1, keepdims=True)
    mixed = jnp.sum(zvec * flexed[...], axis=1, keepdims=True)
    put_contributions(out, image, corner_map[...], spread[...], sign, [rz, curve, mixed], info, groups)


def third_local(
    info, nodes, ids, received, before, image, a0, a1, a2, a3, zold, znew, flexed, resid, mult, own, added, stiff,
    mult_out, direction_out, local_out, total_out, out, *wins,
):
    n_load, dofs = image.shape
    sign, mask = face_vectors(info, nodes, dofs)
    total = total_of(received)
    total_out[...] = total
    rz0, curve0, _, _ = sums_of(before[...], n_load)
    rz1, curve_new, curve_mixed, _ = sums_of(total, n_load)
    beta = rz1 / rz0
    alpha = rz1 / (curve_new + 2.0 * beta * curve_mixed + beta * beta * curve0)
    flexed_new = (image[...] - across([a0, a1, a2, a3], dofs)) * (sign * mask) + beta * flexed[...]
    direction = znew[...] + beta * zold[...]
    direction_out[...] = direction
    mult_out[...] = mult[...] + alpha * direction
    resid_new = resid[...] - alpha * flexed_new
    own_new = own[...] - alpha * (corner_field(total, ids, n_load, dofs) + beta * added[...])
    local = rounded((0.5 * sign * resid_new).astype(BF16), stiff[...]) + own_new
    local_out[...] = local
    put_windows(wins, local)
    rz2 = 2.0 * jnp.sum(sign * resid_new * local, axis=1, keepdims=True)
    zero = jnp.zeros((n_load, 1), F32)
    block = jnp.where(iota((8, 1), 0) % 4 == 3, to_row(jnp.concatenate([rz2, zero, zero, zero], axis=0)), 0.0)
    for low in range(0, out.shape[0], 8):
        out[low : low + 8, :] = block


def last_direction(info, nodes, received, before, local, a0, a1, a2, a3, direction, out):
    n_load, dofs = local.shape
    sign, mask = face_vectors(info, nodes, dofs)
    rz2 = sums_of(total_of(received), n_load)[0]
    rz1 = sums_of(before[...], n_load)[0]
    zvec = (local[...] - across([a0, a1, a2, a3], dofs)) * (sign * mask)
    out[...] = zvec + (rz2 / rz1) * direction[...]


def call(name, kernel, n_scalar, args, outs):
    shapes = [jax.ShapeDtypeStruct(s, d) for s, d in outs]
    n_bytes = sum(a.size * a.dtype.itemsize for a in args) + sum(s.size * s.dtype.itemsize for s in shapes)
    smem, vmem = pl.BlockSpec(memory_space=pltpu.SMEM), pl.BlockSpec(memory_space=pltpu.VMEM)
    return pl.pallas_call(
        kernel,
        out_shape=shapes,
        in_specs=[smem] * n_scalar + [vmem] * (len(args) - n_scalar),
        out_specs=[vmem] * len(shapes),
        cost_estimate=pl.CostEstimate(flops=40_000_000, bytes_accessed=n_bytes, transcendentals=0),
        compiler_params=pltpu.CompilerParams(vmem_limit_bytes=32 * 2**20),
        name=name,
    )(*args)


def swap(block, axis, distance):
    count = lax.axis_size(axis)
    return lax.ppermute(block, axis, [(i, i ^ distance) for i in range(count) if i ^ distance < count])


def exchange(wins):
    return [swap(wins[0], "sub", 1), swap(wins[1], "sub", 2), swap(wins[2], "sub", 4), swap(wins[3], "grp", 1)]


def send_all(rows):
    devices = lax.axis_size("grp") * lax.axis_size("sub")
    blocks = rows.reshape(devices, 4, rows.shape[1])
    return lax.all_to_all(blocks, ("grp", "sub"), 0, 0, tiled=True).reshape(rows.shape)


def body(loads, stiffness, flexibility, coarse_inverse, face_nodes, corner_index):
    rhs, stiff, flex, inverse = loads[0, 0], stiffness[0, 0], flexibility[0, 0], coarse_inverse[0]
    nodes, ids = face_nodes[0, 0], corner_index[0, 0]
    n_load, dofs = rhs.shape
    groups, subs = lax.axis_size("grp"), lax.axis_size("sub")
    info = jnp.stack([lax.axis_index("sub"), lax.axis_index("grp")])
    field = ((n_load, dofs), F32)
    sent = ((groups * subs * 4, 4 * n_load), F32)
    total = ((8, 4 * n_load), F32)
    spans = [stop - start for start, stop in windows(dofs)]
    wins = [((n_load, w), F32) for w in spans]
    extra = -(-16 * subs // spans[3]) * 16
    wide = [((48, w), F32) for w in spans[:3]] + [((48 + extra, spans[3]), F32)]

    (corners,) = call("corners1", first_corners, 3, [info, nodes, ids, rhs], [sent])
    corners = send_all(corners)
    local, spread, *faces = call(
        "local1", first_local, 3, [info, nodes, ids, rhs, stiff, inverse], [field, ((64, 16 * subs), F32)] + wide
    )
    faces = exchange(faces)
    jumped, corner_map, spread = call(
        "maps", maps, 3, [info, nodes, ids, local, spread] + faces, [field, ((80, dofs), BF16), ((16 * subs, 80), F32)]
    )
    zold, image, own, sums, *faces = call(
        "image1", functools.partial(first_image, groups), 2,
        [info, nodes, corners, rhs, jumped, corner_map, spread, flex], [field, field, field, sent] + wins,
    )
    sums = send_all(sums)
    faces = exchange(faces)
    resid, flexed, mult, own, added, before, local, *faces = call(
        "local2", second_local, 3, [info, nodes, ids, sums, image] + faces + [zold, rhs, own, stiff],
        [field] * 5 + [total, field] + wins,
    )
    faces = exchange(faces)
    znew, image, sums, *faces = call(
        "image2", functools.partial(second_image, groups), 2,
        [info, nodes, local] + faces + [resid, flexed, corner_map, spread, flex], [field, field, sent] + wins,
    )
    sums = send_all(sums)
    faces = exchange(faces)
    mult, direction, local, before, sums, *faces = call(
        "local3", third_local, 3,
        [info, nodes, ids, sums, before, image] + faces + [zold, znew, flexed, resid, mult, own, added, stiff],
        [field, field, field, total, sent] + wins,
    )
    sums = send_all(sums)
    faces = exchange(faces)
    (direction,) = call(
        "direction", last_direction, 2, [info, nodes, sums, before, local] + faces + [direction], [field]
    )
    return (mult[None, None], direction[None, None])


def solution(mesh):
    in_specs = (
        P("grp", "sub", None, None),
        P("grp", "sub", None, None),
        P("grp", "sub", None, None),
        P("grp", None, None),
        P("grp", "sub", None),
        P("grp", "sub", None),
    )
    out_specs = (P("grp", "sub", None, None), P("grp", "sub", None, None))
    return jax.shard_map(body, mesh=mesh, in_specs=in_specs, out_specs=out_specs, check_vma=False)
```

time: 249 us -> 82.2 us (0.33)
  blocking collectives: 202 us -> 0 us
  starting transfers between devices: 23.1 us -> 46.1 us
  Pallas kernels: 0 us -> 12 us
  local copies, waits for them, and re-layouts: 2.63 us -> 10.6 us
  other arithmetic: 5.73 us -> 0.08 us
  matrix products: 3.47 us -> 0 us
    psum x4 -> x0, blocking collectives: 158 us -> none  [global_total(): return lax.psum(local_terms, ('grp', 'sub'))]
    all_gather x3 -> x0, blocking collectives: 43.6 us -> none  [coarse_solve(): piece = lax.all_gather(corner_vals, 'sub', axis=1, tiled=True)]
    all_to_all x0 -> x4, starting transfers between devices: none -> 18.7 us  [send_all(): lax.all_to_all(blocks, ('grp', 'sub'), 0, 0, tiled=True).reshape(rows.shape)]
    pallas_call x0 -> x8, Pallas kernels: none -> 12 us  [call(): pl.pallas_call(kernel, out_shape=shapes, in_specs=[smem] * n_scalar + [vm...]
    unnamed x13 -> x38, local copies, waits for them, and re-layouts: 0.05 us -> 10.6 us
    ppermute x20, starting transfers between devices: 23.1 us -> 27.4 us  [swap(): lax.ppermute(block, axis, [(i, i ^ distance) for i in range(count) if i ^...]
    dot_general x11 -> x0, matrix products: 3.47 us -> none  [the longest x3 1.11 us: precondition(): jnp.dot(scaled.astype(jnp.bfloat16), stiff_matrix, preferred_element_type...]
  transfers between devices with their start and end apart: 20 -> 24, of which waited for: 10 -> 11; matrix products, arithmetic and copies ran while one was open for 0% -> 0% of each run, Pallas kernels for 0% -> 2%
where the time goes in v2:
time: 82.2 us; the launch traced here: 81.5 us
  starting transfers between devices  46.1 us (56%)
  Pallas kernels  12 us (15%)
  waiting for transfers between devices  12 us (15%)
  local copies, waits for them, and re-layouts  10.6 us (13%)
    ppermute x20, starting transfers between devices, swap(): lax.ppermute(block, axis, [(i, i ^ distance) for i in range(count) if i ^...  27.4 us
    all_to_all x4, starting transfers between devices, send_all(): lax.all_to_all(blocks, ('grp', 'sub'), 0, 0, tiled=True).reshape(rows.shape)  18.7 us
    pallas_call x8, Pallas kernels, call(): pl.pallas_call(kernel, out_shape=shapes, in_specs=[smem] * n_scalar + [vm...  12 us
    ppermute x20, waiting for transfers between devices, swap(): lax.ppermute(block, axis, [(i, i ^ distance) for i in range(count) if i ^...  12 us
    unnamed x38, local copies, waits for them, and re-layouts  10.6 us
  transfers between devices with their start and end apart: 24, of which 11 were waited for; matrix products, arithmetic and copies ran while one was open for 0% of the time, Pallas kernels for 2%

profile of v2, /device:TPU:0, one launch (start us, length us, event | category | flops | bytes accessed | tf_op | source)
XLA Modules:
  0.0 81.5 jit_solution(4020427413819619343)
XLA Ops:
  0.6 0.0 copy-start.15
  0.6 0.1 pad_add_fusion.info
  0.7 0.9 %copy-done.3 = f32[1,1,32,768]{3,2,1,0:T(8,128)S(1)} copy-done((f32[1,1,32,768]{3,2,1,0:T(8,128)S(1)}, f32[1,1,32,768]{3,2,1,0:T(8,128)}, u32[]{:S(2)}) %copy-start.3) | copy-done | bytes 98328
  1.6 0.7 copy-done.13
  2.3 0.7 copy-done.16
  2.9 1.4 %corners1.1 = f32[128,128]{1,0:T(8,128)} custom-call(s32[2]{0:T(128)S(1)} %pad_add_fusion.info, s32[4]{0:T(128)S(1)} %bitcast.32, s32[12]{0:T(128)S(1)} %bitcast.40, f32[32,768]{1,0:T(8,128)S(1)} %bitcast.23), custom_call_target="tpu_custom_call" | custom-call | flops 40000000 | bytes 163912 | tf_op jit(solution)/shard_map/corners1/pallas_call | solution.py:324
  4.4 7.3 %all-to-all-start = ((f32[32,4,128]{2,1,0:T(4,128)}), f32[32,4,128]{2,1,0:T(4,128)S(1)}, u32[]{:S(2)}, u32[]{:S(2)}) async-start(f32[32,4,128]{2,1,0:T(4,128)} %bitcast.5), calls=%async_computation | async-start | bytes 131072 | tf_op jit(solution)/shard_map/all_to_all | solution.py:347
  11.7 0.0 copy-start
  11.7 1.3 %copy-done = bf16[1,1,768,768]{3,2,1,0:T(8,128)(2,1)S(1)} copy-done((bf16[1,1,768,768]{3,2,1,0:T(8,128)(2,1)S(1)}, bf16[1,1,768,768]{3,2,1,0:T(8,128)(2,1)}, u32[]{:S(2)}) %copy-start) | copy-done | bytes 1179672
  12.9 0.9 %copy-done.4 = f32[1,1,32,768]{3,2,1,0:T(8,128)S(1)} copy-done((f32[1,1,32,768]{3,2,1,0:T(8,128)S(1)}, f32[1,1,32,768]{3,2,1,0:T(8,128)}, u32[]{:S(2)}) %copy-start.4) | copy-done | bytes 98328
  13.8 0.8 copy-done.6
  14.6 0.7 copy-done.14
  15.3 0.7 copy-done.17
  16.0 1.2 %local1.1 = (f32[32,768]{1,0:T(8,128)S(1)}, f32[64,128]{1,0:T(8,128)S(1)}, f32[48,256]{1,0:T(8,128)S(1)}, f32[48,256]{1,0:T(8,128)S(1)}, f32[48,256]{1,0:T(8,128)S(1)}, /*index=5*/f32[64,256]{1,0:T(8,128)S(1)}) custom-call(s32[2]{0:T(128)S(1)} %pad_add_fusion.info, s32[4]{0:T(128)S(1)} %bitcast.33, s32[12]{0:T(128)S(1)} %bitcast.41, f32[32,768]{1,0:T(8,128)S(1)} %bitcast.24, ...), custom_call_target="tpu_custom_call" | custom-call | flops 40000000 | bytes 1658952 | tf_op jit(solution)/shard_map/local1/pallas_call | solution.py:324
  17.2 0.0 copy-start.18
  17.2 1.8 %collective-permute-start.3 = (f32[64,256]{1,0:T(8,128)S(1)}, f32[64,256]{1,0:T(8,128)S(1)}, u32[]{:S(2)}, u32[]{:S(2)}) collective-permute-start(f32[64,256]{1,0:T(8,128)S(1)} %get-tuple-element.51), channel_id=1, source_target_pairs={{0,8},{8,0},{16,24},{24,16},{1,9},{9,1},{17,25},{25,17},{2,10},{10... | collective-permute-start | bytes 196616 | tf_op jit(solution)/shard_map/ppermute | solution.py:337
  19.1 1.5 %collective-permute-start.1 = (f32[48,256]{1,0:T(8,128)S(1)}, f32[48,256]{1,0:T(8,128)S(1)}, u32[]{:S(2)}, u32[]{:S(2)}) collective-permute-start(f32[48,256]{1,0:T(8,128)S(1)} %get-tuple-element.49), channel_id=1, source_target_pairs={{0,2},{1,3},{2,0},{3,1},{4,6},{5,7},{6,4},{7,5},{8,10},{9,11},{10,... | collective-permute-start | bytes 147464 | tf_op jit(solution)/shard_map/ppermute | solution.py:337
  20.5 2.4 %collective-permute-start.2 = (f32[48,256]{1,0:T(8,128)S(1)}, f32[48,256]{1,0:T(8,128)S(1)}, u32[]{:S(2)}, u32[]{:S(2)}) collective-permute-start(f32[48,256]{1,0:T(8,128)S(1)} %get-tuple-element.50), channel_id=1, source_target_pairs={{0,4},{1,5},{2,6},{3,7},{4,0},{5,1},{6,2},{7,3},{8,12},{9,13},{10,... | collective-permute-start | bytes 147464 | tf_op jit(solution)/shard_map/ppermute | solution.py:337
  23.0 0.3 collective-permute-done.1.w1
  23.2 3.2 %collective-permute-done.2.w2 = f32[48,256]{1,0:T(8,128)S(1)} collective-permute-done((f32[48,256]{1,0:T(8,128)S(1)}, f32[48,256]{1,0:T(8,128)S(1)}, u32[]{:S(2)}, u32[]{:S(2)}) %collective-permute-start.2) | collective-permute-done | bytes 49184 | tf_op jit(solution)/shard_map/ppermute | solution.py:337
  26.4 0.7 maps.1
  27.0 0.0 all-to-all-done
  27.1 2.5 %image1.1 = (f32[32,768]{1,0:T(8,128)S(1)}, f32[32,768]{1,0:T(8,128)S(1)}, f32[32,768]{1,0:T(8,128)S(1)}, f32[128,128]{1,0:T(8,128)}, f32[32,256]{1,0:T(8,128)S(...) custom-call(s32[2]{0:T(128)S(1)} %pad_add_fusion.info, s32[4]{0:T(128)S(1)} %bitcast.35, ...), custom_call_target="tpu_custom_call" | custom-call | flops 40000000 | bytes 2097176 | tf_op jit(solution)/shard_map/image1/pallas_call | solution.py:324
  29.6 3.8 %all-to-all-start.1 = ((f32[32,4,128]{2,1,0:T(4,128)}), f32[32,4,128]{2,1,0:T(4,128)S(1)}, u32[]{:S(2)}, u32[]{:S(2)}) async-start(f32[32,4,128]{2,1,0:T(4,128)} %bitcast.10), calls=%async_computation.1 | async-start | bytes 131072 | tf_op jit(solution)/shard_map/all_to_all | solution.py:347
  33.4 0.3 collective-permute-start.4
  33.7 1.7 %collective-permute-start.5 = (f32[32,256]{1,0:T(8,128)S(1)}, f32[32,256]{1,0:T(8,128)S(1)}, u32[]{:S(2)}, u32[]{:S(2)}) collective-permute-start(f32[32,256]{1,0:T(8,128)S(1)} %get-tuple-element.58), channel_id=1, source_target_pairs={{0,2},{1,3},{2,0},{3,1},{4,6},{5,7},{6,4},{7,5},{8,10},{9,11},{10,... | collective-permute-start | bytes 98312 | tf_op jit(solution)/shard_map/ppermute | solution.py:337
  35.4 2.4 %collective-permute-start.6 = (f32[32,256]{1,0:T(8,128)S(1)}, f32[32,256]{1,0:T(8,128)S(1)}, u32[]{:S(2)}, u32[]{:S(2)}) collective-permute-start(f32[32,256]{1,0:T(8,128)S(1)} %get-tuple-element.59), channel_id=1, source_target_pairs={{0,4},{1,5},{2,6},{3,7},{4,0},{5,1},{6,2},{7,3},{8,12},{9,13},{10,... | collective-permute-start | bytes 98312 | tf_op jit(solution)/shard_map/ppermute | solution.py:337
  37.8 1.5 %collective-permute-start.7 = (f32[32,256]{1,0:T(8,128)S(1)}, f32[32,256]{1,0:T(8,128)S(1)}, u32[]{:S(2)}, u32[]{:S(2)}) collective-permute-start(f32[32,256]{1,0:T(8,128)S(1)} %get-tuple-element.60), channel_id=1, source_target_pairs={{0,8},{8,0},{16,24},{24,16},{1,9},{9,1},{17,25},{25,17},{2,10},{10... | collective-permute-start | bytes 98312 | tf_op jit(solution)/shard_map/ppermute | solution.py:337
  39.3 0.6 copy-done.7
  39.9 0.8 collective-permute-done.6.a2
  40.7 0.6 copy-done.9
  41.3 0.4 collective-permute-done.7.a3
  41.7 0.6 copy-done.11
  42.4 0.7 copy-done.8
  43.1 0.8 copy-done.10
  43.9 0.8 copy-done.12
  44.6 1.0 %local2.1 = (f32[32,768]{1,0:T(8,128)S(1)}, f32[32,768]{1,0:T(8,128)S(1)}, f32[32,768]{1,0:T(8,128)S(1)}, f32[32,768]{1,0:T(8,128)S(1)}, f32[32,768]{1,0:T(8,128...) custom-call(s32[2]{0:T(128)S(1)} %pad_add_fusion.info, ...), custom_call_target="tpu_custom_call" | custom-call | flops 40000000 | bytes 2494536 | tf_op jit(solution)/shard_map/local2/pallas_call | solution.py:324
  45.6 0.1 collective-permute-start.8
  45.7 0.6 collective-permute-start.9
  46.2 1.9 %collective-permute-start.10 = (f32[32,256]{1,0:T(8,128)S(1)}, f32[32,256]{1,0:T(8,128)S(1)}, u32[]{:S(2)}, u32[]{:S(2)}) collective-permute-start(f32[32,256]{1,0:T(8,128)S(1)} %get-tuple-element.66), channel_id=1, source_target_pairs={{0,4},{1,5},{2,6},{3,7},{4,0},{5,1},{6,2},{7,3},{8,12},{9,13},{10,... | collective-permute-start | bytes 98312 | tf_op jit(solution)/shard_map/ppermute | solution.py:337
  48.1 1.5 %collective-permute-start.11 = (f32[32,256]{1,0:T(8,128)S(1)}, f32[32,256]{1,0:T(8,128)S(1)}, u32[]{:S(2)}, u32[]{:S(2)}) collective-permute-start(f32[32,256]{1,0:T(8,128)S(1)} %get-tuple-element.67), channel_id=1, source_target_pairs={{0,8},{8,0},{16,24},{24,16},{1,9},{9,1},{17,25},{25,17},{2,10},{10... | collective-permute-start | bytes 98312 | tf_op jit(solution)/shard_map/ppermute | solution.py:337
  49.6 0.0 collective-permute-done.8.a0
  49.6 0.1 collective-permute-done.9.a1
  49.6 1.8 %collective-permute-done.10.a2 = f32[32,256]{1,0:T(8,128)S(1)} collective-permute-done((f32[32,256]{1,0:T(8,128)S(1)}, f32[32,256]{1,0:T(8,128)S(1)}, u32[]{:S(2)}, u32[]{:S(2)}) %collective-permute-start.10) | collective-permute-done | bytes 32800 | tf_op jit(solution)/shard_map/ppermute | solution.py:337
  51.4 0.6 collective-permute-done.11.a3
  52.0 2.1 %image2.1 = (f32[32,768]{1,0:T(8,128)S(1)}, f32[32,768]{1,0:T(8,128)S(1)}, f32[128,128]{1,0:T(8,128)}, f32[32,256]{1,0:T(8,128)S(1)}, f32[32,256]{1,0:T(8,128)S(...) custom-call(s32[2]{0:T(128)S(1)} %pad_add_fusion.info, s32[4]{0:T(128)S(1)} %bitcast.37, ...), custom_call_target="tpu_custom_call" | custom-call | flops 40000000 | bytes 2162712 | tf_op jit(solution)/shard_map/image2/pallas_call | solution.py:324
  54.1 4.2 %all-to-all-start.2 = ((f32[32,4,128]{2,1,0:T(4,128)}), f32[32,4,128]{2,1,0:T(4,128)S(1)}, u32[]{:S(2)}, u32[]{:S(2)}) async-start(f32[32,4,128]{2,1,0:T(4,128)} %bitcast.12), calls=%async_computation.2 | async-start | bytes 131072 | tf_op jit(solution)/shard_map/all_to_all | solution.py:347
  58.4 0.3 collective-permute-start.12
  58.7 1.7 %collective-permute-start.13 = (f32[32,256]{1,0:T(8,128)S(1)}, f32[32,256]{1,0:T(8,128)S(1)}, u32[]{:S(2)}, u32[]{:S(2)}) collective-permute-start(f32[32,256]{1,0:T(8,128)S(1)} %get-tuple-element.74), channel_id=1, source_target_pairs={{0,2},{1,3},{2,0},{3,1},{4,6},{5,7},{6,4},{7,5},{8,10},{9,11},{10,... | collective-permute-start | bytes 98312 | tf_op jit(solution)/shard_map/ppermute | solution.py:337
  60.4 2.4 %collective-permute-start.14 = (f32[32,256]{1,0:T(8,128)S(1)}, f32[32,256]{1,0:T(8,128)S(1)}, u32[]{:S(2)}, u32[]{:S(2)}) collective-permute-start(f32[32,256]{1,0:T(8,128)S(1)} %get-tuple-element.75), channel_id=1, source_target_pairs={{0,4},{1,5},{2,6},{3,7},{4,0},{5,1},{6,2},{7,3},{8,12},{9,13},{10,... | collective-permute-start | bytes 98312 | tf_op jit(solution)/shard_map/ppermute | solution.py:337
  62.8 1.5 %collective-permute-start.15 = (f32[32,256]{1,0:T(8,128)S(1)}, f32[32,256]{1,0:T(8,128)S(1)}, u32[]{:S(2)}, u32[]{:S(2)}) collective-permute-start(f32[32,256]{1,0:T(8,128)S(1)} %get-tuple-element.76), channel_id=1, source_target_pairs={{0,8},{8,0},{16,24},{24,16},{1,9},{9,1},{17,25},{25,17},{2,10},{10... | collective-permute-start | bytes 98312 | tf_op jit(solution)/shard_map/ppermute | solution.py:337
  64.2 0.0 collective-permute-done.12.a0
  64.2 0.0 collective-permute-done.13.a1
  64.3 1.4 %collective-permute-done.14.a2 = f32[32,256]{1,0:T(8,128)S(1)} collective-permute-done((f32[32,256]{1,0:T(8,128)S(1)}, f32[32,256]{1,0:T(8,128)S(1)}, u32[]{:S(2)}, u32[]{:S(2)}) %collective-permute-start.14) | collective-permute-done | bytes 32800 | tf_op jit(solution)/shard_map/ppermute | solution.py:337
  65.6 1.1 %collective-permute-done.15.a3 = f32[32,256]{1,0:T(8,128)S(1)} collective-permute-done((f32[32,256]{1,0:T(8,128)S(1)}, f32[32,256]{1,0:T(8,128)S(1)}, u32[]{:S(2)}, u32[]{:S(2)}) %collective-permute-start.15) | collective-permute-done | bytes 32800 | tf_op jit(solution)/shard_map/ppermute | solution.py:337
  66.7 1.8 %local3.1 = (f32[32,768]{1,0:T(8,128)}, f32[32,768]{1,0:T(8,128)S(1)}, f32[32,768]{1,0:T(8,128)S(1)}, f32[8,128]{1,0:T(8,128)S(1)}, f32[128,128]{1,0:T(8,128)}, ...) custom-call(s32[2]{0:T(128)S(1)} %pad_add_fusion.info, ...), custom_call_target="tpu_custom_call" | custom-call | flops 40000000 | bytes 2662472 | tf_op jit(solution)/shard_map/local3/pallas_call | solution.py:324
  68.5 3.4 %all-to-all-start.3 = ((f32[32,4,128]{2,1,0:T(4,128)}), f32[32,4,128]{2,1,0:T(4,128)S(1)}, u32[]{:S(2)}, u32[]{:S(2)}) async-start(f32[32,4,128]{2,1,0:T(4,128)} %bitcast.15), calls=%async_computation.3 | async-start | bytes 131072 | tf_op jit(solution)/shard_map/all_to_all | solution.py:347
  71.9 0.3 collective-permute-start.16
  72.2 1.7 %collective-permute-start.17 = (f32[32,256]{1,0:T(8,128)S(1)}, f32[32,256]{1,0:T(8,128)S(1)}, u32[]{:S(2)}, u32[]{:S(2)}) collective-permute-start(f32[32,256]{1,0:T(8,128)S(1)} %get-tuple-element.86), channel_id=1, source_target_pairs={{0,2},{1,3},{2,0},{3,1},{4,6},{5,7},{6,4},{7,5},{8,10},{9,11},{10,... | collective-permute-start | bytes 98312 | tf_op jit(solution)/shard_map/ppermute | solution.py:337
  73.9 2.4 %collective-permute-start.18 = (f32[32,256]{1,0:T(8,128)S(1)}, f32[32,256]{1,0:T(8,128)S(1)}, u32[]{:S(2)}, u32[]{:S(2)}) collective-permute-start(f32[32,256]{1,0:T(8,128)S(1)} %get-tuple-element.87), channel_id=1, source_target_pairs={{0,4},{1,5},{2,6},{3,7},{4,0},{5,1},{6,2},{7,3},{8,12},{9,13},{10,... | collective-permute-start | bytes 98312 | tf_op jit(solution)/shard_map/ppermute | solution.py:337
  76.3 1.5 %collective-permute-start.19 = (f32[32,256]{1,0:T(8,128)S(1)}, f32[32,256]{1,0:T(8,128)S(1)}, u32[]{:S(2)}, u32[]{:S(2)}) collective-permute-start(f32[32,256]{1,0:T(8,128)S(1)} %get-tuple-element.88), channel_id=1, source_target_pairs={{0,8},{8,0},{16,24},{24,16},{1,9},{9,1},{17,25},{25,17},{2,10},{10... | collective-permute-start | bytes 98312 | tf_op jit(solution)/shard_map/ppermute | solution.py:337
  77.8 1.4 %collective-permute-done.18.a2 = f32[32,256]{1,0:T(8,128)S(1)} collective-permute-done((f32[32,256]{1,0:T(8,128)S(1)}, f32[32,256]{1,0:T(8,128)S(1)}, u32[]{:S(2)}, u32[]{:S(2)}) %collective-permute-start.18) | collective-permute-done | bytes 32800 | tf_op jit(solution)/shard_map/ppermute | solution.py:337
  79.2 1.1 %collective-permute-done.19.a3 = f32[32,256]{1,0:T(8,128)S(1)} collective-permute-done((f32[32,256]{1,0:T(8,128)S(1)}, f32[32,256]{1,0:T(8,128)S(1)}, u32[]{:S(2)}, u32[]{:S(2)}) %collective-permute-start.19) | collective-permute-done | bytes 32800 | tf_op jit(solution)/shard_map/ppermute | solution.py:337
  80.2 1.3 %direction.1 = f32[32,768]{1,0:T(8,128)} custom-call(s32[2]{0:T(128)S(1)} %pad_add_fusion.info, s32[4]{0:T(128)S(1)} %bitcast.39, f32[128,128]{1,0:T(8,128)S(1)} %bitcast.30, f32[8,128]{1,0:T(8,128)S(1)} %get-tuple-element.83.before, f32[32,768]{1,0:T(8,128)S(1)} %get-tuple-element.84.local, f32[32,256]{1,0:T(8,128)S(1)} %collective-permute-done.16.a0, ...), custom_call_target="tpu_custom_call" | custom-call | flops 40000000 | bytes 495640 | tf_op jit(solution)/shard_map/direction/pallas_call | solution.py:324
  (31 shorter events, 0.1 us)
Async XLA Ops:
  0.6 26.4 %copy-start.15 = (s32[1,1,4]{2,1,0:T(1,128)S(1)}, s32[1,1,4]{2,1,0:T(1,128)}, u32[]{:S(2)}) copy-start(s32[1,1,4]{2,1,0:T(1,128)} %param.10) | copy-start | bytes 52
  0.7 0.9 %copy-start.3 = (f32[1,1,32,768]{3,2,1,0:T(8,128)S(1)}, f32[1,1,32,768]{3,2,1,0:T(8,128)}, u32[]{:S(2)}) copy-start(f32[1,1,32,768]{3,2,1,0:T(8,128)} %param.6) | copy-start | bytes 294916
  1.6 0.7 copy-start.13
  2.3 0.7 copy-start.16
  2.9 24.1 %copy-start.5 = (f32[1,1,32,768]{3,2,1,0:T(8,128)S(1)}, f32[1,1,32,768]{3,2,1,0:T(8,128)}, u32[]{:S(2)}) copy-start(f32[1,1,32,768]{3,2,1,0:T(8,128)} %param.6) | copy-start | bytes 294916
  4.4 22.7 %all-to-all-start = ((f32[32,4,128]{2,1,0:T(4,128)}), f32[32,4,128]{2,1,0:T(4,128)S(1)}, u32[]{:S(2)}, u32[]{:S(2)}) async-start(f32[32,4,128]{2,1,0:T(4,128)} %bitcast.5), calls=%async_computation | async-start | bytes 131072 | tf_op jit(solution)/shard_map/all_to_all | solution.py:347
  11.7 1.3 %copy-start = (bf16[1,1,768,768]{3,2,1,0:T(8,128)(2,1)S(1)}, bf16[1,1,768,768]{3,2,1,0:T(8,128)(2,1)}, u32[]{:S(2)}) copy-start(bf16[1,1,768,768]{3,2,1,0:T(8,128)(2,1)} %param.7) | copy-start | bytes 3538948
  12.9 0.9 %copy-start.4 = (f32[1,1,32,768]{3,2,1,0:T(8,128)S(1)}, f32[1,1,32,768]{3,2,1,0:T(8,128)}, u32[]{:S(2)}) copy-start(f32[1,1,32,768]{3,2,1,0:T(8,128)} %param.6) | copy-start | bytes 294916
  13.8 0.8 copy-start.6
  14.6 0.7 copy-start.14
  15.3 0.7 copy-start.17
  15.9 11.1 %copy-start.2 = (bf16[1,1,768,768]{3,2,1,0:T(8,128)(2,1)S(1)}, bf16[1,1,768,768]{3,2,1,0:T(8,128)(2,1)}, u32[]{:S(2)}) copy-start(bf16[1,1,768,768]{3,2,1,0:T(8,128)(2,1)} %param.8) | copy-start | bytes 3538948
  17.2 25.2 %copy-start.1 = (bf16[1,1,768,768]{3,2,1,0:T(8,128)(2,1)S(1)}, bf16[1,1,768,768]{3,2,1,0:T(8,128)(2,1)}, u32[]{:S(2)}) copy-start(bf16[1,1,768,768]{3,2,1,0:T(8,128)(2,1)} %param.7) | copy-start | bytes 3538948
  17.2 25.1 %copy-start.18 = (s32[1,1,12]{2,1,0:T(1,128)S(1)}, s32[1,1,12]{2,1,0:T(1,128)}, u32[]{:S(2)}) copy-start(s32[1,1,12]{2,1,0:T(1,128)} %param.11) | copy-start | bytes 148
  17.2 9.2 %collective-permute-start.3 = (f32[64,256]{1,0:T(8,128)S(1)}, f32[64,256]{1,0:T(8,128)S(1)}, u32[]{:S(2)}, u32[]{:S(2)}) collective-permute-start(f32[64,256]{1,0:T(8,128)S(1)} %get-tuple-element.51), channel_id=1, source_target_pairs={{0,8},{8,0},{16,24},{24,16},{1,9},{9,1},{17,25},{25,17},{2,10},{10... | collective-permute-start | bytes 196616 | tf_op jit(solution)/shard_map/ppermute | solution.py:337
  19.1 3.9 %collective-permute-start = (f32[48,256]{1,0:T(8,128)S(1)}, f32[48,256]{1,0:T(8,128)S(1)}, u32[]{:S(2)}, u32[]{:S(2)}) collective-permute-start(f32[48,256]{1,0:T(8,128)S(1)} %get-tuple-element.48), channel_id=1, source_target_pairs={{0,1},{1,0},{2,3},{3,2},{4,5},{5,4},{6,7},{7,6},{8,9},{9,8},{10,11... | collective-permute-start | bytes 147464 | tf_op jit(solution)/shard_map/ppermute | solution.py:337
  19.1 4.2 %collective-permute-start.1 = (f32[48,256]{1,0:T(8,128)S(1)}, f32[48,256]{1,0:T(8,128)S(1)}, u32[]{:S(2)}, u32[]{:S(2)}) collective-permute-start(f32[48,256]{1,0:T(8,128)S(1)} %get-tuple-element.49), channel_id=1, source_target_pairs={{0,2},{1,3},{2,0},{3,1},{4,6},{5,7},{6,4},{7,5},{8,10},{9,11},{10,... | collective-permute-start | bytes 147464 | tf_op jit(solution)/shard_map/ppermute | solution.py:337
  20.5 5.9 %collective-permute-start.2 = (f32[48,256]{1,0:T(8,128)S(1)}, f32[48,256]{1,0:T(8,128)S(1)}, u32[]{:S(2)}, u32[]{:S(2)}) collective-permute-start(f32[48,256]{1,0:T(8,128)S(1)} %get-tuple-element.50), channel_id=1, source_target_pairs={{0,4},{1,5},{2,6},{3,7},{4,0},{5,1},{6,2},{7,3},{8,12},{9,13},{10,... | collective-permute-start | bytes 147464 | tf_op jit(solution)/shard_map/ppermute | solution.py:337
  29.6 12.8 %all-to-all-start.1 = ((f32[32,4,128]{2,1,0:T(4,128)}), f32[32,4,128]{2,1,0:T(4,128)S(1)}, u32[]{:S(2)}, u32[]{:S(2)}) async-start(f32[32,4,128]{2,1,0:T(4,128)} %bitcast.10), calls=%async_computation.1 | async-start | bytes 131072 | tf_op jit(solution)/shard_map/all_to_all | solution.py:347
  33.4 5.9 %collective-permute-start.4 = (f32[32,256]{1,0:T(8,128)S(1)}, f32[32,256]{1,0:T(8,128)S(1)}, u32[]{:S(2)}, u32[]{:S(2)}) collective-permute-start(f32[32,256]{1,0:T(8,128)S(1)} %get-tuple-element.57), channel_id=1, source_target_pairs={{0,1},{1,0},{2,3},{3,2},{4,5},{5,4},{6,7},{7,6},{8,9},{9,8},{10,11... | collective-permute-start | bytes 98312 | tf_op jit(solution)/shard_map/ppermute | solution.py:337
  33.7 5.6 %collective-permute-start.5 = (f32[32,256]{1,0:T(8,128)S(1)}, f32[32,256]{1,0:T(8,128)S(1)}, u32[]{:S(2)}, u32[]{:S(2)}) collective-permute-start(f32[32,256]{1,0:T(8,128)S(1)} %get-tuple-element.58), channel_id=1, source_target_pairs={{0,2},{1,3},{2,0},{3,1},{4,6},{5,7},{6,4},{7,5},{8,10},{9,11},{10,... | collective-permute-start | bytes 98312 | tf_op jit(solution)/shard_map/ppermute | solution.py:337
  35.4 5.3 %collective-permute-start.6 = (f32[32,256]{1,0:T(8,128)S(1)}, f32[32,256]{1,0:T(8,128)S(1)}, u32[]{:S(2)}, u32[]{:S(2)}) collective-permute-start(f32[32,256]{1,0:T(8,128)S(1)} %get-tuple-element.59), channel_id=1, source_target_pairs={{0,4},{1,5},{2,6},{3,7},{4,0},{5,1},{6,2},{7,3},{8,12},{9,13},{10,... | collective-permute-start | bytes 98312 | tf_op jit(solution)/shard_map/ppermute | solution.py:337
  37.8 3.9 %collective-permute-start.7 = (f32[32,256]{1,0:T(8,128)S(1)}, f32[32,256]{1,0:T(8,128)S(1)}, u32[]{:S(2)}, u32[]{:S(2)}) collective-permute-start(f32[32,256]{1,0:T(8,128)S(1)} %get-tuple-element.60), channel_id=1, source_target_pairs={{0,8},{8,0},{16,24},{24,16},{1,9},{9,1},{17,25},{25,17},{2,10},{10... | collective-permute-start | bytes 98312 | tf_op jit(solution)/shard_map/ppermute | solution.py:337
  39.3 0.6 copy-start.7
  40.7 0.6 copy-start.9
  41.7 0.6 copy-start.11
  42.3 0.8 copy-start.8
  43.1 0.8 copy-start.10
  43.9 0.8 copy-start.12
  45.6 4.0 %collective-permute-start.8 = (f32[32,256]{1,0:T(8,128)S(1)}, f32[32,256]{1,0:T(8,128)S(1)}, u32[]{:S(2)}, u32[]{:S(2)}) collective-permute-start(f32[32,256]{1,0:T(8,128)S(1)} %get-tuple-element.64), channel_id=1, source_target_pairs={{0,1},{1,0},{2,3},{3,2},{4,5},{5,4},{6,7},{7,6},{8,9},{9,8},{10,11... | collective-permute-start | bytes 98312 | tf_op jit(solution)/shard_map/ppermute | solution.py:337
  45.7 4.0 %collective-permute-start.9 = (f32[32,256]{1,0:T(8,128)S(1)}, f32[32,256]{1,0:T(8,128)S(1)}, u32[]{:S(2)}, u32[]{:S(2)}) collective-permute-start(f32[32,256]{1,0:T(8,128)S(1)} %get-tuple-element.65), channel_id=1, source_target_pairs={{0,2},{1,3},{2,0},{3,1},{4,6},{5,7},{6,4},{7,5},{8,10},{9,11},{10,... | collective-permute-start | bytes 98312 | tf_op jit(solution)/shard_map/ppermute | solution.py:337
  46.2 5.2 %collective-permute-start.10 = (f32[32,256]{1,0:T(8,128)S(1)}, f32[32,256]{1,0:T(8,128)S(1)}, u32[]{:S(2)}, u32[]{:S(2)}) collective-permute-start(f32[32,256]{1,0:T(8,128)S(1)} %get-tuple-element.66), channel_id=1, source_target_pairs={{0,4},{1,5},{2,6},{3,7},{4,0},{5,1},{6,2},{7,3},{8,12},{9,13},{10,... | collective-permute-start | bytes 98312 | tf_op jit(solution)/shard_map/ppermute | solution.py:337
  48.1 3.9 %collective-permute-start.11 = (f32[32,256]{1,0:T(8,128)S(1)}, f32[32,256]{1,0:T(8,128)S(1)}, u32[]{:S(2)}, u32[]{:S(2)}) collective-permute-start(f32[32,256]{1,0:T(8,128)S(1)} %get-tuple-element.67), channel_id=1, source_target_pairs={{0,8},{8,0},{16,24},{24,16},{1,9},{9,1},{17,25},{25,17},{2,10},{10... | collective-permute-start | bytes 98312 | tf_op jit(solution)/shard_map/ppermute | solution.py:337
  54.1 12.6 %all-to-all-start.2 = ((f32[32,4,128]{2,1,0:T(4,128)}), f32[32,4,128]{2,1,0:T(4,128)S(1)}, u32[]{:S(2)}, u32[]{:S(2)}) async-start(f32[32,4,128]{2,1,0:T(4,128)} %bitcast.12), calls=%async_computation.2 | async-start | bytes 131072 | tf_op jit(solution)/shard_map/all_to_all | solution.py:347
  58.4 5.9 %collective-permute-start.12 = (f32[32,256]{1,0:T(8,128)S(1)}, f32[32,256]{1,0:T(8,128)S(1)}, u32[]{:S(2)}, u32[]{:S(2)}) collective-permute-start(f32[32,256]{1,0:T(8,128)S(1)} %get-tuple-element.73), channel_id=1, source_target_pairs={{0,1},{1,0},{2,3},{3,2},{4,5},{5,4},{6,7},{7,6},{8,9},{9,8},{10,11... | collective-permute-start | bytes 98312 | tf_op jit(solution)/shard_map/ppermute | solution.py:337
  58.7 5.6 %collective-permute-start.13 = (f32[32,256]{1,0:T(8,128)S(1)}, f32[32,256]{1,0:T(8,128)S(1)}, u32[]{:S(2)}, u32[]{:S(2)}) collective-permute-start(f32[32,256]{1,0:T(8,128)S(1)} %get-tuple-element.74), channel_id=1, source_target_pairs={{0,2},{1,3},{2,0},{3,1},{4,6},{5,7},{6,4},{7,5},{8,10},{9,11},{10,... | collective-permute-start | bytes 98312 | tf_op jit(solution)/shard_map/ppermute | solution.py:337
  60.4 5.3 %collective-permute-start.14 = (f32[32,256]{1,0:T(8,128)S(1)}, f32[32,256]{1,0:T(8,128)S(1)}, u32[]{:S(2)}, u32[]{:S(2)}) collective-permute-start(f32[32,256]{1,0:T(8,128)S(1)} %get-tuple-element.75), channel_id=1, source_target_pairs={{0,4},{1,5},{2,6},{3,7},{4,0},{5,1},{6,2},{7,3},{8,12},{9,13},{10,... | collective-permute-start | bytes 98312 | tf_op jit(solution)/shard_map/ppermute | solution.py:337
  62.8 3.9 %collective-permute-start.15 = (f32[32,256]{1,0:T(8,128)S(1)}, f32[32,256]{1,0:T(8,128)S(1)}, u32[]{:S(2)}, u32[]{:S(2)}) collective-permute-start(f32[32,256]{1,0:T(8,128)S(1)} %get-tuple-element.76), channel_id=1, source_target_pairs={{0,8},{8,0},{16,24},{24,16},{1,9},{9,1},{17,25},{25,17},{2,10},{10... | collective-permute-start | bytes 98312 | tf_op jit(solution)/shard_map/ppermute | solution.py:337
  68.5 11.7 %all-to-all-start.3 = ((f32[32,4,128]{2,1,0:T(4,128)}), f32[32,4,128]{2,1,0:T(4,128)S(1)}, u32[]{:S(2)}, u32[]{:S(2)}) async-start(f32[32,4,128]{2,1,0:T(4,128)} %bitcast.15), calls=%async_computation.3 | async-start | bytes 131072 | tf_op jit(solution)/shard_map/all_to_all | solution.py:347
  71.9 5.9 %collective-permute-start.16 = (f32[32,256]{1,0:T(8,128)S(1)}, f32[32,256]{1,0:T(8,128)S(1)}, u32[]{:S(2)}, u32[]{:S(2)}) collective-permute-start(f32[32,256]{1,0:T(8,128)S(1)} %get-tuple-element.85), channel_id=1, source_target_pairs={{0,1},{1,0},{2,3},{3,2},{4,5},{5,4},{6,7},{7,6},{8,9},{9,8},{10,11... | collective-permute-start | bytes 98312 | tf_op jit(solution)/shard_map/ppermute | solution.py:337
  72.2 5.6 %collective-permute-start.17 = (f32[32,256]{1,0:T(8,128)S(1)}, f32[32,256]{1,0:T(8,128)S(1)}, u32[]{:S(2)}, u32[]{:S(2)}) collective-permute-start(f32[32,256]{1,0:T(8,128)S(1)} %get-tuple-element.86), channel_id=1, source_target_pairs={{0,2},{1,3},{2,0},{3,1},{4,6},{5,7},{6,4},{7,5},{8,10},{9,11},{10,... | collective-permute-start | bytes 98312 | tf_op jit(solution)/shard_map/ppermute | solution.py:337
  73.9 5.3 %collective-permute-start.18 = (f32[32,256]{1,0:T(8,128)S(1)}, f32[32,256]{1,0:T(8,128)S(1)}, u32[]{:S(2)}, u32[]{:S(2)}) collective-permute-start(f32[32,256]{1,0:T(8,128)S(1)} %get-tuple-element.87), channel_id=1, source_target_pairs={{0,4},{1,5},{2,6},{3,7},{4,0},{5,1},{6,2},{7,3},{8,12},{9,13},{10,... | collective-permute-start | bytes 98312 | tf_op jit(solution)/shard_map/ppermute | solution.py:337
  76.3 3.9 %collective-permute-start.19 = (f32[32,256]{1,0:T(8,128)S(1)}, f32[32,256]{1,0:T(8,128)S(1)}, u32[]{:S(2)}, u32[]{:S(2)}) collective-permute-start(f32[32,256]{1,0:T(8,128)S(1)} %get-tuple-element.88), channel_id=1, source_target_pairs={{0,8},{8,0},{16,24},{24,16},{1,9},{9,1},{17,25},{25,17},{2,10},{10... | collective-permute-start | bytes 98312 | tf_op jit(solution)/shard_map/ppermute | solution.py:337

commit v3 on v2

v3 whole, which is shorter than its diff:
```python
import functools

import jax
import jax.numpy as jnp
from jax import lax
from jax.experimental import pallas as pl
from jax.experimental.pallas import tpu as pltpu
from jax.sharding import PartitionSpec as P

F32, BF16 = jnp.float32, jnp.bfloat16
NT = (((1,), (1,)), ((), ()))
NN = (((1,), (0,)), ((), ()))
LANES = 128


def exact(a, b, dims=NN):
    return lax.dot_general(a, b, dims, precision=lax.Precision.HIGHEST, preferred_element_type=F32)


def rounded(a, b):
    return lax.dot_general(a, b, NN, preferred_element_type=F32)


def thirds(x):
    high = x.astype(BF16)
    rest = x - high.astype(F32)
    mid = rest.astype(BF16)
    return jnp.concatenate([high, mid, (rest - mid.astype(F32)).astype(BF16)], axis=0)


def by_map(x, corner_map, dims):
    n = x.shape[0]
    out = lax.dot_general(thirds(x), corner_map, dims, preferred_element_type=F32)
    return out[:n] + out[n : 2 * n] + out[2 * n :]


def iota(shape, axis):
    return lax.broadcasted_iota(jnp.int32, shape, axis)


def windows(dofs):
    width = dofs // 4
    return [(f * width // LANES * LANES, -(-(f + 1) * width // LANES) * LANES) for f in range(4)]


def face_vectors(nodes_ref, dofs):
    width = dofs // 4
    pos = iota((1, dofs), 1)
    sub_pos, grp_pos = lax.axis_index("sub"), lax.axis_index("grp")
    bits = [sub_pos & 1, (sub_pos >> 1) & 1, (sub_pos >> 2) & 1, grp_pos & 1]
    sign = jnp.zeros((1, dofs), F32)
    live = jnp.zeros((1, dofs), jnp.int32)
    node = pos
    for f in range(4):
        inside = (pos >= f * width) & (pos < (f + 1) * width)
        sign = jnp.where(inside, (1 - 2 * bits[f]).astype(F32), sign)
        live = jnp.where(inside, nodes_ref[f], live)
    for step in range(1, 12):
        node = jnp.where(pos >= step * (width // 3), pos - step * (width // 3), node)
    mask = jnp.where(node < live, 1.0, 0.0)
    return sign, mask


def corner_rows(ids_ref, dofs):
    row = iota((16, 1), 0)
    ids = jnp.full((16, 1), -1, jnp.int32)
    for k in range(ids_ref.shape[0]):
        ids = jnp.where(row == 4 * (k % 4) + k // 4, ids_ref[k], ids)
    return jnp.where(ids == iota((16, dofs), 1), 1.0, 0.0)


def across(wins, dofs):
    spans, width = windows(dofs), dofs // 4
    n = wins[0].shape[0]
    tiles = []
    for low in range(0, dofs, LANES):
        tile = None
        for f, (start, stop) in enumerate(spans):
            if start <= low < stop:
                part = wins[f][:, low - start : low - start + LANES]
                tile = part if tile is None else jnp.where(iota((n, LANES), 1) + low < f * width, tile, part)
        tiles.append(tile)
    return jnp.concatenate(tiles, axis=1)


def put_windows(refs, field):
    for ref, (start, stop) in zip(refs, windows(field.shape[1])):
        ref[: field.shape[0], :] = field[:, start:stop]


def same_block(n_row, n_col, row_block, col_block):
    return iota((n_row, n_col), 0) // row_block == iota((n_row, n_col), 1) // col_block


def to_column(row):
    n = row.shape[1]
    return jnp.sum(jnp.where(same_block(n, n, 1, 1), row, 0.0), axis=1, keepdims=True)


def to_row(column):
    n = column.shape[0]
    return jnp.sum(jnp.where(same_block(n, n, 1, 1), column, 0.0), axis=0, keepdims=True)


def total_of(received):
    total = received[0:8]
    for low in range(8, received.shape[0], 8):
        total = total + received[low : low + 8]
    return total + pltpu.roll(total, 4, 0)


def sums_of(total, n_load):
    column = to_column(total[3:4])
    return [column[i * n_load : (i + 1) * n_load] for i in range(4)]


def halves(x):
    high = x.astype(BF16)
    return jnp.concatenate([high, (x - high.astype(F32)).astype(BF16)], axis=0)


def fine(x, matrix):
    n = x.shape[0]
    both = rounded(halves(x), matrix)
    return both[:n] + both[n:]


def finer(x, matrix):
    n = x.shape[0]
    high = matrix.astype(BF16)
    parts = halves(x)
    both = rounded(parts, high)
    return both[:n] + both[n:] + rounded(parts[:n], (matrix - high.astype(F32)).astype(BF16))


def packed_corners(scaled, corner):
    n_load = scaled.shape[0]
    values = by_map(scaled, corner.astype(BF16), NT)
    flipped = jnp.concatenate([values] * 4, axis=0).T
    flipped = jnp.where(same_block(16, 4 * n_load, 4, n_load), flipped, 0.0)
    block = flipped[:8] + flipped[8:]
    return block + pltpu.roll(block, 4, 0)


def with_sums(block, sums):
    zero = jnp.zeros_like(sums[0])
    row = to_row(jnp.concatenate(sums + [zero] * (4 - len(sums)), axis=0))
    return jnp.where(iota(block.shape, 0) % 4 == 3, row, block)


def put_all(out, block):
    for low in range(0, out.shape[0], 8):
        out[low : low + 8, :] = block


def group_corners(received, which, rows, n_load):
    block = received[pl.ds(pl.multiple_of(which * rows, 8), rows), :]
    block = jnp.where(iota(block.shape, 0) % 4 == 3, 0.0, block)
    tall = jnp.concatenate([block] * 4, axis=0)
    flipped = jnp.where(same_block(4 * rows, 4 * n_load, rows, n_load), tall, 0.0).T
    return sum(flipped[r * n_load : (r + 1) * n_load] for r in range(1, 4)) + flipped[:n_load]


def coarse_of(received, spread, n_load):
    rows = spread.shape[0] // 4
    grp_pos = lax.axis_index("grp")
    inner = finer(group_corners(received, grp_pos, rows, n_load), spread)
    outer = finer(group_corners(received, grp_pos ^ 1, rows, n_load), spread)
    return jnp.where(iota(inner.shape, 1) < 64, inner, outer)


def to_wide(matrix, wide):
    n = matrix.shape[0]
    if n < wide:
        return jnp.concatenate([matrix[: n // 2], matrix[n // 2 :]], axis=1)
    return jnp.concatenate([matrix[:, low : low + wide] for low in range(0, n, wide)], axis=0)


def from_wide(rows, n):
    wide = rows.shape[1]
    if n < wide:
        return jnp.concatenate([rows[:, :n], rows[:, n:]], axis=0)
    return jnp.concatenate([rows[low : low + n] for low in range(0, rows.shape[0], n)], axis=1)


def rows_sum(x):
    return jnp.sum(x, axis=1, keepdims=True)


def start(
    rhs_hbm, stiff_hbm, inverse_hbm, nodes_hbm, ids_hbm,
    sent, local_out, vectors, corner_out, resid_out, spread_out, coarse_out, w0, w1, w2, w3,
    rhs, stiff, inverse, nodes, ids, sems,
):
    pairs = [(nodes_hbm, nodes), (ids_hbm, ids), (rhs_hbm, rhs), (inverse_hbm, inverse), (stiff_hbm, stiff)]
    copies = [pltpu.make_async_copy(a, b, sems.at[i]) for i, (a, b) in enumerate(pairs)]
    for copy in copies:
        copy.start()
    n_load, dofs = rhs.shape
    wins = [w0, w1, w2, w3]
    copies[0].wait()
    sign, mask = face_vectors(nodes, dofs)
    vectors[0:1, :] = sign
    vectors[1:2, :] = mask
    vectors[2:3, :] = sign * mask
    vectors[3:8, :] = jnp.zeros((5, dofs), F32)
    copies[1].wait()
    corner = corner_rows(ids, dofs)
    corner_out[...] = corner
    for ref, (low, high) in zip(wins, windows(dofs)):
        ref[2 * n_load : 2 * n_load + 16, :] = corner[:, low:high]
    copies[2].wait()
    resid = rhs[...] * mask
    resid_out[...] = resid
    scaled = 0.5 * sign * resid
    put_all(sent, packed_corners(scaled, corner))
    copies[3].wait()
    n = inverse.shape[0]
    corners = ids.shape[0]
    subs = n // corners
    sub_pos = lax.axis_index("sub")
    row = iota((64, 1), 0)
    owner = jnp.where(row < 16, sub_pos, jnp.where(row < 32, sub_pos ^ 1, jnp.where(row < 48, sub_pos ^ 2, sub_pos ^ 4)))
    source = owner * corners + row % 4 * 4 + row // 4 % 4
    pick = jnp.where((source == iota((64, n), 1)) & (row % 4 * 4 < corners), 1.0, 0.0)
    place = iota((16 * subs, 1), 0)
    source = place // 4 % subs * corners + place % 4 * 4 + place // (4 * subs)
    order = jnp.where((source == iota((16 * subs, n), 1)) & (place % 4 * 4 < corners), 1.0, 0.0)
    both = exact(exact(jnp.concatenate([pick, order], axis=0), inverse[...]), order, NT)
    spread = both[:64]
    spread_out[...] = spread
    coarse_out[...] = to_wide(both[64:], w3.shape[1])
    wide = w3.shape[1]
    low = 2 * n_load + 16
    own = spread[:16]
    if 16 * subs < wide:
        own = jnp.concatenate([own, jnp.zeros((16, wide - 16 * subs), F32)], axis=1)
    for i in range(own.shape[1] // wide):
        w3[low + 16 * i : low + 16 * i + 16, :] = own[:, i * wide : (i + 1) * wide]
    copies[4].wait()
    local = rounded(halves(scaled), stiff[...])
    local_out[...] = local
    put_windows(wins, local)


def first_image(
    received, a0, a1, a2, a3, local, vectors, corner, resid, spread, inverse, flex,
    z_out, exact_out, image_out, sums_out, map_out, spread_out, *wins,
):
    n_load, dofs = resid.shape
    both = 2 * n_load
    came = [a0, a1, a2, a3]
    sign, sign_mask = vectors[0:1, :], vectors[2:3, :]
    jumped = (local[...] - across([a[:both, :] for a in came], dofs)) * sign_mask
    own = corner[...] * sign_mask
    other = across([a[both : both + 16, :] for a in came], dofs) * sign_mask
    width = dofs // 4
    pos = iota((1, dofs), 1)
    pieces = [own]
    for f in range(4):
        pieces.append(jnp.where((pos >= f * width) & (pos < (f + 1) * width), -other, 0.0))
    corner_map = jnp.concatenate(pieces, axis=0).astype(BF16)
    map_out[...] = corner_map
    n = spread.shape[1]
    pieces = [a3[low : low + 16, :] for low in range(both + 16, a3.shape[0], 16)]
    cross = pieces[0] if len(pieces) == 1 else jnp.concatenate(pieces, axis=1)
    rows = jnp.concatenate([spread[...], cross[:, :n], jnp.zeros((48, n), F32)], axis=0)
    spread_columns = rows.T[:, :80]
    spread_out[...] = spread_columns
    coarse = coarse_of(received, spread_columns, n_load)
    zvec = jumped[:n_load] + by_map(coarse, corner_map, NN)
    z_out[...] = zvec
    exact_out[...] = zvec + jumped[n_load:]
    signed = sign * zvec
    image = rounded(signed.astype(BF16), flex[...])
    image_out[...] = image
    put_windows(wins, image)
    wins[3][n_load:, :] = inverse[...]
    sums_out[...] = with_sums(
        jnp.zeros((8, 4 * n_load), F32), [rows_sum(resid[...] * zvec), 2.0 * rows_sum(signed * image)]
    )


def second_local(
    a0, a1, a2, a3, image, sums, exact_z, vectors, corner, inverse, stiff,
    flexed_out, local_out, inverse_out, sent, *wins,
):
    n_load, dofs = image.shape
    sign, sign_mask = vectors[0:1, :], vectors[2:3, :]
    n_row = inverse.shape[0]
    inverse_out[:n_row, :] = inverse[...]
    inverse_out[n_row:, :] = a3[n_load:, :]
    flexed = (image[...] - across([a[:n_load, :] for a in [a0, a1, a2, a3]], dofs)) * sign_mask
    flexed_out[...] = flexed
    scaled = 0.5 * sign * flexed
    third = jnp.where(iota((1, 4 * n_load), 1) // n_load == 2, 1.0, 0.0)
    mixed = with_sums(jnp.zeros((8, 4 * n_load), F32), [rows_sum(exact_z[...] * flexed)] * 4) * third
    is_sum = iota((8, 1), 0) % 4 == 3
    put_all(sent, jnp.where(is_sum, sums[...] + mixed, packed_corners(scaled, corner[...])))
    local = fine(scaled, stiff[...])
    local_out[...] = local
    put_windows(wins, local)


def second_image(
    received, a0, a1, a2, a3, local, flexed, exact_z, resid, vectors, corner_map, spread, flex,
    z_out, step_out, image_out, sums_out, total_out, *wins,
):
    n_load, dofs = local.shape
    sign, sign_mask = vectors[0:1, :], vectors[2:3, :]
    total = total_of(received)
    total_out[...] = total
    rz, curve, _, _ = sums_of(total, n_load)
    alpha = rz / curve
    coarse = coarse_of(received, spread[...], n_load)
    step = (local[...] - across([a0, a1, a2, a3], dofs)) * sign_mask + by_map(coarse, corner_map[...], NN)
    step = alpha * step
    step_out[...] = step
    zvec = exact_z[...] - step
    z_out[...] = zvec
    signed = sign * zvec
    image = alpha * fine(signed, flex[...])
    image_out[...] = image
    put_windows(wins, image)
    scaled_flexed = alpha * flexed[...]
    sums = [
        rows_sum((resid[...] - scaled_flexed) * zvec),
        2.0 * rows_sum(signed * image),
        rows_sum(zvec * scaled_flexed),
    ]
    sums_out[...] = with_sums(jnp.zeros((8, 4 * n_load), F32), sums)


def third_local(a0, a1, a2, a3, image, sums, vectors, corner, stiff, local_out, sent, *wins):
    n_load, dofs = image.shape
    sign, sign_mask = vectors[0:1, :], vectors[2:3, :]
    flexed = (image[...] - across([a0, a1, a2, a3], dofs)) * sign_mask
    scaled = 0.5 * sign * flexed
    local = fine(scaled, stiff[...])
    local_out[...] = local
    put_windows(wins, local)
    fourth = jnp.where(iota((1, 4 * n_load), 1) // n_load == 3, 1.0, 0.0)
    square = with_sums(jnp.zeros((8, 4 * n_load), F32), [4.0 * rows_sum(scaled * local)] * 4) * fourth
    is_sum = iota((8, 1), 0) % 4 == 3
    put_all(sent, jnp.where(is_sum, sums[...] + square, packed_corners(scaled, corner[...])))


def finish(
    received, a0, a1, a2, a3, local, before, zold, znew, step, vectors, corner_map, spread, *rest
):
    inverses, (mult_out, direction_out) = rest[:-2], rest[-2:]
    n_load, dofs = local.shape
    sign_mask = vectors[2:3, :]
    rz0, curve0, mixed0, _ = sums_of(before[...], n_load)
    rz1, curve, mixed, square = sums_of(total_of(received), n_load)
    n = spread.shape[0]
    index = 0
    for ref in inverses:
        height = n * n // ref.shape[1]
        for low in range(0, ref.shape[0], height):
            values = group_corners(received, lax.axis_index("grp") ^ index, n // 4, n_load)
            matrix = from_wide(ref[low : low + height, :], n)
            square = square + 4.0 * rows_sum(values * finer(values, matrix))
            index += 1
    alpha = rz0 / curve0
    beta = rz1 / rz0
    gamma = rz1 / (curve + 2.0 * beta * mixed + beta * beta * rz0)
    rz2 = square + 2.0 * beta * (mixed - curve) + beta * beta * (alpha * mixed0 - mixed)
    rz2 = rz1 - 2.0 * gamma * (curve + beta * mixed) + gamma * gamma * rz2
    coarse = coarse_of(received, spread[...], n_load)
    image = (local[...] - across([a0, a1, a2, a3], dofs)) * sign_mask + by_map(coarse, corner_map[...], NN)
    direction = znew[...] + beta * zold[...]
    mult_out[...] = alpha * (zold[...] + gamma * direction)
    direction_out[...] = znew[...] - gamma * (image + beta * step[...]) + (rz2 / rz1) * direction


def call(name, kernel, args, outs, scratch=(), space=pltpu.VMEM):
    shapes = [jax.ShapeDtypeStruct(s, d) for s, d in outs]
    n_bytes = sum(a.size * a.dtype.itemsize for a in args) + sum(s.size * s.dtype.itemsize for s in shapes)
    return pl.pallas_call(
        kernel,
        out_shape=shapes,
        in_specs=[pl.BlockSpec(memory_space=space)] * len(args),
        out_specs=[pl.BlockSpec(memory_space=pltpu.VMEM)] * len(shapes),
        scratch_shapes=scratch,
        cost_estimate=pl.CostEstimate(flops=40_000_000, bytes_accessed=n_bytes, transcendentals=0),
        compiler_params=pltpu.CompilerParams(vmem_limit_bytes=(12 << 20) + 2 * n_bytes),
        name=name,
    )(*args)


def swap(block, axis, distance):
    count = lax.axis_size(axis)
    return lax.ppermute(block, axis, [(i, i ^ distance) for i in range(count) if i ^ distance < count])


def exchange(wins):
    a2 = swap(wins[2], "sub", 4)
    a1 = swap(wins[1], "sub", 2)
    a3 = swap(wins[3], "grp", 1)
    return [swap(wins[0], "sub", 1), a1, a2, a3]


def send_all(rows):
    devices = lax.axis_size("grp") * lax.axis_size("sub")
    blocks = rows.reshape(devices, 4, rows.shape[1])
    return lax.all_to_all(blocks, ("grp", "sub"), 0, 0, tiled=True).reshape(rows.shape)


def body(loads, stiffness, flexibility, coarse_inverse, face_nodes, corner_index):
    rhs, stiff, flex, inverse = loads[0, 0], stiffness[0, 0], flexibility[0, 0], coarse_inverse[0]
    nodes, ids = face_nodes[0, 0], corner_index[0, 0]
    n_load, dofs = rhs.shape
    groups, subs = lax.axis_size("grp"), lax.axis_size("sub")
    n = 16 * subs
    field = ((n_load, dofs), F32)
    sent = ((groups * subs * 4, 4 * n_load), F32)
    total = ((8, 4 * n_load), F32)
    spans = [high - low for low, high in windows(dofs)]
    wins = [((n_load, w), F32) for w in spans]
    height = 2 * n_load + 16
    wide = [((height, w), F32) for w in spans[:3]] + [((height - (-n // spans[3]) * 16, spans[3]), F32)]

    corners, local, vectors, corner, resid, spread, coarse, *faces = call(
        "start", start, [rhs, stiff, inverse, nodes, ids],
        [sent, ((2 * n_load, dofs), F32), ((8, dofs), F32), ((16, dofs), F32), field, ((64, n), F32),
         ((n * n // spans[3], spans[3]), F32)] + wide,
        [pltpu.VMEM(rhs.shape, F32), pltpu.VMEM(stiff.shape, BF16), pltpu.VMEM(inverse.shape, F32),
         pltpu.SMEM(nodes.shape, jnp.int32), pltpu.SMEM(ids.shape, jnp.int32), pltpu.SemaphoreType.DMA((5,))],
        pl.ANY,
    )
    received = send_all(corners)
    faces = exchange(faces)
    more = wins[:3] + [((n_load + coarse.shape[0], spans[3]), F32)]
    zold, exact_z, image, sums, corner_map, spread, *faces = call(
        "image1", first_image, [received] + faces + [local, vectors, corner, resid, spread, coarse, flex],
        [field, field, field, total, ((80, dofs), BF16), ((n, 80), F32)] + more,
    )
    faces = exchange(faces)
    flexed, local, coarse, sent_rows, *faces = call(
        "local2", second_local, faces + [image, sums, exact_z, vectors, corner, coarse, stiff],
        [field, field, ((2 * coarse.shape[0], spans[3]), F32), sent] + wins,
    )
    received = send_all(sent_rows)
    faces = exchange(faces)
    znew, step, image, sums, before, *faces = call(
        "image2", second_image,
        [received] + faces + [local, flexed, exact_z, resid, vectors, corner_map, spread, flex],
        [field, field, field, total, total] + wins,
    )
    faces = exchange(faces)
    distance, coarse = 2, [coarse]
    while distance < groups:
        coarse.append(swap(jnp.concatenate(coarse, axis=0), "grp", distance))
        distance *= 2
    local, sent_rows, *faces = call(
        "local3", third_local, faces + [image, sums, vectors, corner, stiff], [field, sent] + wins
    )
    received = send_all(sent_rows)
    faces = exchange(faces)
    mult, direction = call(
        "finish", finish,
        [received] + faces + [local, before, zold, znew, step, vectors, corner_map, spread] + coarse, [field, field],
    )
    return (mult[None, None], direction[None, None])


def solution(mesh):
    in_specs = (
        P("grp", "sub", None, None),
        P("grp", "sub", None, None),
        P("grp", "sub", None, None),
        P("grp", None, None),
        P("grp", "sub", None),
        P("grp", "sub", None),
    )
    out_specs = (P("grp", "sub", None, None), P("grp", "sub", None, None))
    return jax.shard_map(body, mesh=mesh, in_specs=in_specs, out_specs=out_specs, check_vma=False)
```

time: 82.2 us -> 71.9 us (0.87)
  Pallas kernels: 12 us -> 7.47 us
  starting transfers between devices: 46.1 us -> 42.8 us
  local copies, waits for them, and re-layouts: 10.6 us -> 7.3 us
  waiting for transfers between devices: 12 us -> 13.1 us
    pallas_call x8 -> x6, Pallas kernels: 12 us -> 7.47 us  [call(): pl.pallas_call(kernel, out_shape=shapes, in_specs=[pl.BlockSpec(memory_sp...]
    unnamed x38 -> x24, local copies, waits for them, and re-layouts: 10.6 us -> 7.3 us
    all_to_all x4 -> x3, starting transfers between devices: 18.7 us -> 16.9 us  [send_all(): lax.all_to_all(blocks, ('grp', 'sub'), 0, 0, tiled=True).reshape(rows.shape)]
    ppermute x20 -> x21, starting transfers between devices: 27.4 us -> 25.9 us  [swap(): lax.ppermute(block, axis, [(i, i ^ distance) for i in range(count) if i ^...]
    ppermute x20 -> x21, waiting for transfers between devices: 12 us -> 13.1 us  [swap(): lax.ppermute(block, axis, [(i, i ^ distance) for i in range(count) if i ^...]
  transfers between devices with their start and end apart: 24 -> 24, of which waited for: 11 -> 9; matrix products, arithmetic and copies ran while one was open for 0% -> 0% of each run, Pallas kernels for 2% -> 2%
where the time goes in v3:
time: 71.9 us; the launch traced here: 71.4 us
  starting transfers between devices  42.8 us (60%)
  waiting for transfers between devices  13.1 us (18%)
  Pallas kernels  7.47 us (10%)
  local copies, waits for them, and re-layouts  7.3 us (10%)
  between operations  0.75 us (1%)
    ppermute x21, starting transfers between devices, swap(): lax.ppermute(block, axis, [(i, i ^ distance) for i in range(count) if i ^...  25.9 us
    all_to_all x3, starting transfers between devices, send_all(): lax.all_to_all(blocks, ('grp', 'sub'), 0, 0, tiled=True).reshape(rows.shape)  16.9 us
    ppermute x21, waiting for transfers between devices, swap(): lax.ppermute(block, axis, [(i, i ^ distance) for i in range(count) if i ^...  13.1 us
    pallas_call x6, Pallas kernels, call(): pl.pallas_call(kernel, out_shape=shapes, in_specs=[pl.BlockSpec(memory_sp...  7.47 us
    unnamed x24, local copies, waits for them, and re-layouts  7.3 us
  transfers between devices with their start and end apart: 24, of which 9 were waited for; matrix products, arithmetic and copies ran while one was open for 0% of the time, Pallas kernels for 2%

profile of v3, /device:TPU:0, one launch (start us, length us, event | category | flops | bytes accessed | tf_op | source)
XLA Modules:
  0.0 71.4 jit_solution(3494270887373220300)
XLA Ops:
  0.6 0.0 copy-start
  0.6 1.3 %copy-done = bf16[1,1,768,768]{3,2,1,0:T(8,128)(2,1)S(1)} copy-done((bf16[1,1,768,768]{3,2,1,0:T(8,128)(2,1)S(1)}, bf16[1,1,768,768]{3,2,1,0:T(8,128)(2,1)}, u32[]{:S(2)}) %copy-start) | copy-done | bytes 1179672
  1.9 0.9 %copy-done.3 = f32[1,1,32,768]{3,2,1,0:T(8,128)S(1)} copy-done((f32[1,1,32,768]{3,2,1,0:T(8,128)S(1)}, f32[1,1,32,768]{3,2,1,0:T(8,128)}, u32[]{:S(2)}) %copy-start.3) | copy-done | bytes 98328
  2.8 0.8 %copy-done.8 = f32[1,96,96]{2,1,0:T(8,128)S(1)} copy-done((f32[1,96,96]{2,1,0:T(8,128)S(1)}, f32[1,96,96]{2,1,0:T(8,128)}, u32[]{:S(2)}) %copy-start.8) | copy-done | bytes 36888
  3.6 0.7 copy-done.9
  4.3 0.7 copy-done.10
  4.9 2.4 %start.1 = (f32[128,128]{1,0:T(8,128)}, f32[64,768]{1,0:T(8,128)S(1)}, f32[8,768]{1,0:T(8,128)S(1)}, f32[16,768]{1,0:T(8,128)S(1)}, f32[32,768]{1,0:T(8,128)S(1)...) custom-call(f32[32,768]{1,0:T(8,128)S(1)} %bitcast.22, ...), custom_call_target="tpu_custom_call" | custom-call | flops 40000000 | bytes 2191424 | tf_op jit(solution)/shard_map/start/pallas_call | solution.py:380
  7.3 0.0 copy-start.1
  7.3 7.3 %all-to-all-start = ((f32[32,4,128]{2,1,0:T(4,128)}), f32[32,4,128]{2,1,0:T(4,128)S(1)}, u32[]{:S(2)}, u32[]{:S(2)}) async-start(f32[32,4,128]{2,1,0:T(4,128)} %bitcast.5), calls=%async_computation | async-start | bytes 131072 | tf_op jit(solution)/shard_map/all_to_all | solution.py:407
  14.6 1.8 %collective-permute-start.3 = (f32[96,256]{1,0:T(8,128)S(1)}, f32[96,256]{1,0:T(8,128)S(1)}, u32[]{:S(2)}, u32[]{:S(2)}) collective-permute-start(f32[96,256]{1,0:T(8,128)S(1)} %get-tuple-element.52), channel_id=1, source_target_pairs={{0,8},{8,0},{16,24},{24,16},{1,9},{9,1},{17,25},{25,17},{2,10},{10... | collective-permute-start | bytes 294920 | tf_op jit(solution)/shard_map/ppermute | solution.py:394
  16.5 0.0 collective-permute-start
  16.5 1.5 %collective-permute-start.1 = (f32[80,256]{1,0:T(8,128)S(1)}, f32[80,256]{1,0:T(8,128)S(1)}, u32[]{:S(2)}, u32[]{:S(2)}) collective-permute-start(f32[80,256]{1,0:T(8,128)S(1)} %get-tuple-element.50), channel_id=1, source_target_pairs={{0,2},{1,3},{2,0},{3,1},{4,6},{5,7},{6,4},{7,5},{8,10},{9,11},{10,... | collective-permute-start | bytes 245768 | tf_op jit(solution)/shard_map/ppermute | solution.py:394
  18.0 2.4 %collective-permute-start.2 = (f32[80,256]{1,0:T(8,128)S(1)}, f32[80,256]{1,0:T(8,128)S(1)}, u32[]{:S(2)}, u32[]{:S(2)}) collective-permute-start(f32[80,256]{1,0:T(8,128)S(1)} %get-tuple-element.51), channel_id=1, source_target_pairs={{0,4},{1,5},{2,6},{3,7},{4,0},{5,1},{6,2},{7,3},{8,12},{9,13},{10,... | collective-permute-start | bytes 245768 | tf_op jit(solution)/shard_map/ppermute | solution.py:394
  20.4 0.0 collective-permute-done.a0
  20.4 1.3 %collective-permute-done.1.a1 = f32[80,256]{1,0:T(8,128)S(1)} collective-permute-done((f32[80,256]{1,0:T(8,128)S(1)}, f32[80,256]{1,0:T(8,128)S(1)}, u32[]{:S(2)}, u32[]{:S(2)}) %collective-permute-start.1) | collective-permute-done | bytes 81952 | tf_op jit(solution)/shard_map/ppermute | solution.py:394
  21.6 3.5 %collective-permute-done.2.a2 = f32[80,256]{1,0:T(8,128)S(1)} collective-permute-done((f32[80,256]{1,0:T(8,128)S(1)}, f32[80,256]{1,0:T(8,128)S(1)}, u32[]{:S(2)}, u32[]{:S(2)}) %collective-permute-start.2) | collective-permute-done | bytes 81952 | tf_op jit(solution)/shard_map/ppermute | solution.py:394
  25.2 0.6 copy-done.6
  25.8 0.0 collective-permute-done.3.a3
  25.8 0.0 all-to-all-done
  25.8 0.0 copy-start.7
  25.8 0.9 %copy-done.7 = f32[80,256]{1,0:T(8,128)S(1)} copy-done((f32[80,256]{1,0:T(8,128)S(1)}, f32[80,256]{1,0:T(8,128)}, u32[]{:S(2)}) %copy-start.7) | copy-done | bytes 81944
  26.7 0.9 %image1.1 = (f32[32,768]{1,0:T(8,128)S(1)}, f32[32,768]{1,0:T(8,128)S(1)}, f32[32,768]{1,0:T(8,128)S(1)}, f32[8,128]{1,0:T(8,128)S(1)}, bf16[80,768]{1,0:T(8,128...) custom-call(f32[128,128]{1,0:T(8,128)S(1)} %bitcast.20, ...), custom_call_target="tpu_custom_call" | custom-call | flops 40000000 | bytes 2715648 | tf_op jit(solution)/shard_map/image1/pallas_call | solution.py:380
  27.6 0.6 collective-permute-start.7
  28.2 0.0 collective-permute-start.4
  28.2 0.4 collective-permute-start.5
  28.6 2.5 %collective-permute-start.6 = (f32[32,256]{1,0:T(8,128)S(1)}, f32[32,256]{1,0:T(8,128)S(1)}, u32[]{:S(2)}, u32[]{:S(2)}) collective-permute-start(f32[32,256]{1,0:T(8,128)S(1)} %get-tuple-element.61), channel_id=1, source_target_pairs={{0,4},{1,5},{2,6},{3,7},{4,0},{5,1},{6,2},{7,3},{8,12},{9,13},{10,... | collective-permute-start | bytes 98312 | tf_op jit(solution)/shard_map/ppermute | solution.py:394
  31.2 0.0 collective-permute-done.4.a0
  31.2 1.0 %collective-permute-done.5.a1 = f32[32,256]{1,0:T(8,128)S(1)} collective-permute-done((f32[32,256]{1,0:T(8,128)S(1)}, f32[32,256]{1,0:T(8,128)S(1)}, u32[]{:S(2)}, u32[]{:S(2)}) %collective-permute-start.5) | collective-permute-done | bytes 32800 | tf_op jit(solution)/shard_map/ppermute | solution.py:394
  32.1 1.3 %collective-permute-done.6.a2 = f32[32,256]{1,0:T(8,128)S(1)} collective-permute-done((f32[32,256]{1,0:T(8,128)S(1)}, f32[32,256]{1,0:T(8,128)S(1)}, u32[]{:S(2)}, u32[]{:S(2)}) %collective-permute-start.6) | collective-permute-done | bytes 32800 | tf_op jit(solution)/shard_map/ppermute | solution.py:394
  33.4 0.0 collective-permute-done.7.a3
  33.4 1.0 %local2.1 = (f32[32,768]{1,0:T(8,128)S(1)}, f32[32,768]{1,0:T(8,128)S(1)}, f32[128,256]{1,0:T(8,128)S(1)}, f32[128,128]{1,0:T(8,128)}, f32[32,256]{1,0:T(8,128)}...) custom-call(f32[32,256]{1,0:T(8,128)S(1)} %collective-permute-done.4.a0, ...), custom_call_target="tpu_custom_call" | custom-call | flops 40000000 | bytes 2240512 | tf_op jit(solution)/shard_map/local2/pallas_call | solution.py:380
  34.4 0.6 copy-done.11
  35.0 4.7 %all-to-all-start.1 = ((f32[32,4,128]{2,1,0:T(4,128)}), f32[32,4,128]{2,1,0:T(4,128)S(1)}, u32[]{:S(2)}, u32[]{:S(2)}) async-start(f32[32,4,128]{2,1,0:T(4,128)} %bitcast.8), calls=%async_computation.1 | async-start | bytes 131072 | tf_op jit(solution)/shard_map/all_to_all | solution.py:407
  39.8 0.3 collective-permute-start.8
  40.1 1.7 %collective-permute-start.9 = (f32[32,256]{1,0:T(8,128)}, f32[32,256]{1,0:T(8,128)S(1)}, u32[]{:S(2)}, u32[]{:S(2)}) collective-permute-start(f32[32,256]{1,0:T(8,128)} %get-tuple-element.68), channel_id=1, source_target_pairs={{0,2},{1,3},{2,0},{3,1},{4,6},{5,7},{6,4},{7,5},{8,10},{9,11},{10,... | collective-permute-start | bytes 98312 | tf_op jit(solution)/shard_map/ppermute | solution.py:394
  41.8 2.4 %collective-permute-start.10 = (f32[32,256]{1,0:T(8,128)}, f32[32,256]{1,0:T(8,128)S(1)}, u32[]{:S(2)}, u32[]{:S(2)}) collective-permute-start(f32[32,256]{1,0:T(8,128)} %get-tuple-element.69), channel_id=1, source_target_pairs={{0,4},{1,5},{2,6},{3,7},{4,0},{5,1},{6,2},{7,3},{8,12},{9,13},{10,... | collective-permute-start | bytes 98312 | tf_op jit(solution)/shard_map/ppermute | solution.py:394
  44.2 1.5 %collective-permute-start.11 = (f32[32,256]{1,0:T(8,128)}, f32[32,256]{1,0:T(8,128)S(1)}, u32[]{:S(2)}, u32[]{:S(2)}) collective-permute-start(f32[32,256]{1,0:T(8,128)} %copy-done.11), channel_id=1, source_target_pairs={{0,8},{8,0},{16,24},{24,16},{1,9},{9,1},{17,25},{25,17},{2,10},{10... | collective-permute-start | bytes 98312 | tf_op jit(solution)/shard_map/ppermute | solution.py:394
  45.7 0.0 collective-permute-done.8.a0
  45.7 0.0 collective-permute-done.9.a1
  45.7 1.6 %collective-permute-done.10.a2 = f32[32,256]{1,0:T(8,128)S(1)} collective-permute-done((f32[32,256]{1,0:T(8,128)}, f32[32,256]{1,0:T(8,128)S(1)}, u32[]{:S(2)}, u32[]{:S(2)}) %collective-permute-start.10) | collective-permute-done | bytes 32800 | tf_op jit(solution)/shard_map/ppermute | solution.py:394
  47.2 1.1 %collective-permute-done.11.a3 = f32[32,256]{1,0:T(8,128)S(1)} collective-permute-done((f32[32,256]{1,0:T(8,128)}, f32[32,256]{1,0:T(8,128)S(1)}, u32[]{:S(2)}, u32[]{:S(2)}) %collective-permute-start.11) | collective-permute-done | bytes 32800 | tf_op jit(solution)/shard_map/ppermute | solution.py:394
  48.3 0.0 all-to-all-done.1
  48.3 0.9 %copy-done.5 = f32[32,768]{1,0:T(8,128)S(1)} copy-done((f32[32,768]{1,0:T(8,128)S(1)}, f32[32,768]{1,0:T(8,128)}, u32[]{:S(2)}) %copy-start.5) | copy-done | bytes 98328
  49.2 0.9 %image2.1 = (f32[32,768]{1,0:T(8,128)S(1)}, f32[32,768]{1,0:T(8,128)S(1)}, f32[32,768]{1,0:T(8,128)S(1)}, f32[8,128]{1,0:T(8,128)S(1)}, f32[8,128]{1,0:T(8,128)S...) custom-call(f32[128,128]{1,0:T(8,128)S(1)} %bitcast.21, ...), custom_call_target="tpu_custom_call" | custom-call | flops 40000000 | bytes 2392064 | tf_op jit(solution)/shard_map/image2/pallas_call | solution.py:380
  50.1 0.1 collective-permute-start.12
  50.2 0.6 collective-permute-start.13
  50.8 1.3 %collective-permute-start.14 = (f32[32,256]{1,0:T(8,128)S(1)}, f32[32,256]{1,0:T(8,128)S(1)}, u32[]{:S(2)}, u32[]{:S(2)}) collective-permute-start(f32[32,256]{1,0:T(8,128)S(1)} %get-tuple-element.77), channel_id=1, source_target_pairs={{0,4},{1,5},{2,6},{3,7},{4,0},{5,1},{6,2},{7,3},{8,12},{9,13},{10,... | collective-permute-start | bytes 98312 | tf_op jit(solution)/shard_map/ppermute | solution.py:394
  52.0 1.5 %collective-permute-start.15 = (f32[32,256]{1,0:T(8,128)S(1)}, f32[32,256]{1,0:T(8,128)S(1)}, u32[]{:S(2)}, u32[]{:S(2)}) collective-permute-start(f32[32,256]{1,0:T(8,128)S(1)} %get-tuple-element.78), channel_id=1, source_target_pairs={{0,8},{8,0},{16,24},{24,16},{1,9},{9,1},{17,25},{25,17},{2,10},{10... | collective-permute-start | bytes 98312 | tf_op jit(solution)/shard_map/ppermute | solution.py:394
  53.5 1.5 %collective-permute-start.20 = (f32[128,256]{1,0:T(8,128)S(1)}, f32[128,256]{1,0:T(8,128)S(1)}, u32[]{:S(2)}, u32[]{:S(2)}) collective-permute-start(f32[128,256]{1,0:T(8,128)S(1)} %get-tuple-element.91.rest_0_), channel_id=1, source_target_pairs={{0,16},{8,24},{16,0},{24,8},{1,17},{9,25},{17,1},{25,9},{2,18},{10... | collective-permute-start | bytes 393224 | tf_op jit(solution)/shard_map/ppermute | solution.py:394
  55.0 0.0 collective-permute-done.12.a0
  55.0 0.0 collective-permute-done.13.a1
  55.0 0.9 %collective-permute-done.14.a2 = f32[32,256]{1,0:T(8,128)S(1)} collective-permute-done((f32[32,256]{1,0:T(8,128)S(1)}, f32[32,256]{1,0:T(8,128)S(1)}, u32[]{:S(2)}, u32[]{:S(2)}) %collective-permute-start.14) | collective-permute-done | bytes 32800 | tf_op jit(solution)/shard_map/ppermute | solution.py:394
  55.9 0.0 collective-permute-done.15.a3
  55.9 1.2 %local3.1 = (f32[32,768]{1,0:T(8,128)S(1)}, f32[128,128]{1,0:T(8,128)}, f32[32,256]{1,0:T(8,128)S(1)}, f32[32,256]{1,0:T(8,128)S(1)}, f32[32,256]{1,0:T(8,128)S(1)}, /*index=5*/f32[32,256]{1,0:T(8,128)S(1)}) custom-call(f32[32,256]{1,0:T(8,128)S(1)} %collective-permute-done.12.a0, f32[32,256]{1,0:T(8,128)S(1)} %collective-permute-done.13.a1, ...), custom_call_target="tpu_custom_call" | custom-call | flops 40000000 | bytes 1781760 | tf_op jit(solution)/shard_map/local3/pallas_call | solution.py:380
  57.1 4.8 %all-to-all-start.2 = ((f32[32,4,128]{2,1,0:T(4,128)}), f32[32,4,128]{2,1,0:T(4,128)S(1)}, u32[]{:S(2)}, u32[]{:S(2)}) async-start(f32[32,4,128]{2,1,0:T(4,128)} %bitcast.10), calls=%async_computation.2 | async-start | bytes 131072 | tf_op jit(solution)/shard_map/all_to_all | solution.py:407
  62.0 0.3 collective-permute-start.16
  62.3 1.7 %collective-permute-start.17 = (f32[32,256]{1,0:T(8,128)S(1)}, f32[32,256]{1,0:T(8,128)S(1)}, u32[]{:S(2)}, u32[]{:S(2)}) collective-permute-start(f32[32,256]{1,0:T(8,128)S(1)} %get-tuple-element.83), channel_id=1, source_target_pairs={{0,2},{1,3},{2,0},{3,1},{4,6},{5,7},{6,4},{7,5},{8,10},{9,11},{10,... | collective-permute-start | bytes 98312 | tf_op jit(solution)/shard_map/ppermute | solution.py:394
  64.0 2.4 %collective-permute-start.18 = (f32[32,256]{1,0:T(8,128)S(1)}, f32[32,256]{1,0:T(8,128)S(1)}, u32[]{:S(2)}, u32[]{:S(2)}) collective-permute-start(f32[32,256]{1,0:T(8,128)S(1)} %get-tuple-element.84), channel_id=1, source_target_pairs={{0,4},{1,5},{2,6},{3,7},{4,0},{5,1},{6,2},{7,3},{8,12},{9,13},{10,... | collective-permute-start | bytes 98312 | tf_op jit(solution)/shard_map/ppermute | solution.py:394
  66.4 1.5 %collective-permute-start.19 = (f32[32,256]{1,0:T(8,128)S(1)}, f32[32,256]{1,0:T(8,128)S(1)}, u32[]{:S(2)}, u32[]{:S(2)}) collective-permute-start(f32[32,256]{1,0:T(8,128)S(1)} %get-tuple-element.85), channel_id=1, source_target_pairs={{0,8},{8,0},{16,24},{24,16},{1,9},{9,1},{17,25},{25,17},{2,10},{10... | collective-permute-start | bytes 98312 | tf_op jit(solution)/shard_map/ppermute | solution.py:394
  67.8 0.0 collective-permute-done.20.rest_1_
  67.9 1.4 %collective-permute-done.18.a2 = f32[32,256]{1,0:T(8,128)S(1)} collective-permute-done((f32[32,256]{1,0:T(8,128)S(1)}, f32[32,256]{1,0:T(8,128)S(1)}, u32[]{:S(2)}, u32[]{:S(2)}) %collective-permute-start.18) | collective-permute-done | bytes 32800 | tf_op jit(solution)/shard_map/ppermute | solution.py:394
  69.2 1.1 %collective-permute-done.19.a3 = f32[32,256]{1,0:T(8,128)S(1)} collective-permute-done((f32[32,256]{1,0:T(8,128)S(1)}, f32[32,256]{1,0:T(8,128)S(1)}, u32[]{:S(2)}, u32[]{:S(2)}) %collective-permute-start.19) | collective-permute-done | bytes 32800 | tf_op jit(solution)/shard_map/ppermute | solution.py:394
  70.3 0.0 all-to-all-done.2
  70.3 1.1 %finish.1 = (f32[32,768]{1,0:T(8,128)}, f32[32,768]{1,0:T(8,128)}) custom-call(f32[128,128]{1,0:T(8,128)S(1)} %bitcast.19, f32[32,256]{1,0:T(8,128)S(1)} %collective-permute-done.16.a0, f32[32,256]{1,0:T(8,128)S(1)} %collective-permute-done.17.a1, f32[32,256]{1,0:T(8,128)S(1)} %collective-permute-done.18.a2, f32[32,256]{1,0:T(8,128)S(1)} %collective-permute-done.19.a3, ...), custom_call_target="tpu_custom_call" | custom-call | flops 40000000 | bytes 1241088 | tf_op jit(solution)/shard_map/finish/pallas_call | solution.py:380
  (14 shorter events, 0.0 us)
Async XLA Ops:
  0.6 1.3 %copy-start = (bf16[1,1,768,768]{3,2,1,0:T(8,128)(2,1)S(1)}, bf16[1,1,768,768]{3,2,1,0:T(8,128)(2,1)}, u32[]{:S(2)}) copy-start(bf16[1,1,768,768]{3,2,1,0:T(8,128)(2,1)} %param.7) | copy-start | bytes 3538948
  1.9 0.9 %copy-start.3 = (f32[1,1,32,768]{3,2,1,0:T(8,128)S(1)}, f32[1,1,32,768]{3,2,1,0:T(8,128)}, u32[]{:S(2)}) copy-start(f32[1,1,32,768]{3,2,1,0:T(8,128)} %param.6) | copy-start | bytes 294916
  2.8 0.8 %copy-start.8 = (f32[1,96,96]{2,1,0:T(8,128)S(1)}, f32[1,96,96]{2,1,0:T(8,128)}, u32[]{:S(2)}) copy-start(f32[1,96,96]{2,1,0:T(8,128)} %param.9) | copy-start | bytes 110596
  3.6 0.7 copy-start.9
  4.3 0.7 copy-start.10
  4.9 20.9 %copy-start.2 = (bf16[1,1,768,768]{3,2,1,0:T(8,128)(2,1)S(1)}, bf16[1,1,768,768]{3,2,1,0:T(8,128)(2,1)}, u32[]{:S(2)}) copy-start(bf16[1,1,768,768]{3,2,1,0:T(8,128)(2,1)} %param.8) | copy-start | bytes 3538948
  7.3 26.1 %copy-start.1 = (bf16[1,1,768,768]{3,2,1,0:T(8,128)(2,1)S(1)}, bf16[1,1,768,768]{3,2,1,0:T(8,128)(2,1)}, u32[]{:S(2)}) copy-start(bf16[1,1,768,768]{3,2,1,0:T(8,128)(2,1)} %param.7) | copy-start | bytes 3538948
  7.3 18.5 %all-to-all-start = ((f32[32,4,128]{2,1,0:T(4,128)}), f32[32,4,128]{2,1,0:T(4,128)S(1)}, u32[]{:S(2)}, u32[]{:S(2)}) async-start(f32[32,4,128]{2,1,0:T(4,128)} %bitcast.5), calls=%async_computation | async-start | bytes 131072 | tf_op jit(solution)/shard_map/all_to_all | solution.py:407
  14.6 11.2 %collective-permute-start.3 = (f32[96,256]{1,0:T(8,128)S(1)}, f32[96,256]{1,0:T(8,128)S(1)}, u32[]{:S(2)}, u32[]{:S(2)}) collective-permute-start(f32[96,256]{1,0:T(8,128)S(1)} %get-tuple-element.52), channel_id=1, source_target_pairs={{0,8},{8,0},{16,24},{24,16},{1,9},{9,1},{17,25},{25,17},{2,10},{10... | collective-permute-start | bytes 294920 | tf_op jit(solution)/shard_map/ppermute | solution.py:394
  16.5 3.9 %collective-permute-start = (f32[80,256]{1,0:T(8,128)}, f32[80,256]{1,0:T(8,128)S(1)}, u32[]{:S(2)}, u32[]{:S(2)}) collective-permute-start(f32[80,256]{1,0:T(8,128)} %get-tuple-element.49), channel_id=1, source_target_pairs={{0,1},{1,0},{2,3},{3,2},{4,5},{5,4},{6,7},{7,6},{8,9},{9,8},{10,11... | collective-permute-start | bytes 245768 | tf_op jit(solution)/shard_map/ppermute | solution.py:394
  16.5 5.2 %collective-permute-start.1 = (f32[80,256]{1,0:T(8,128)S(1)}, f32[80,256]{1,0:T(8,128)S(1)}, u32[]{:S(2)}, u32[]{:S(2)}) collective-permute-start(f32[80,256]{1,0:T(8,128)S(1)} %get-tuple-element.50), channel_id=1, source_target_pairs={{0,2},{1,3},{2,0},{3,1},{4,6},{5,7},{6,4},{7,5},{8,10},{9,11},{10,... | collective-permute-start | bytes 245768 | tf_op jit(solution)/shard_map/ppermute | solution.py:394
  18.0 7.2 %collective-permute-start.2 = (f32[80,256]{1,0:T(8,128)S(1)}, f32[80,256]{1,0:T(8,128)S(1)}, u32[]{:S(2)}, u32[]{:S(2)}) collective-permute-start(f32[80,256]{1,0:T(8,128)S(1)} %get-tuple-element.51), channel_id=1, source_target_pairs={{0,4},{1,5},{2,6},{3,7},{4,0},{5,1},{6,2},{7,3},{8,12},{9,13},{10,... | collective-permute-start | bytes 245768 | tf_op jit(solution)/shard_map/ppermute | solution.py:394
  25.2 0.6 copy-start.6
  25.8 0.9 %copy-start.7 = (f32[80,256]{1,0:T(8,128)S(1)}, f32[80,256]{1,0:T(8,128)}, u32[]{:S(2)}) copy-start(f32[80,256]{1,0:T(8,128)} %copy-done.6) | copy-start | bytes 245764
  27.6 5.8 %collective-permute-start.7 = (f32[96,256]{1,0:T(8,128)S(1)}, f32[96,256]{1,0:T(8,128)S(1)}, u32[]{:S(2)}, u32[]{:S(2)}) collective-permute-start(f32[96,256]{1,0:T(8,128)S(1)} %get-tuple-element.62), channel_id=1, source_target_pairs={{0,8},{8,0},{16,24},{24,16},{1,9},{9,1},{17,25},{25,17},{2,10},{10... | collective-permute-start | bytes 294920 | tf_op jit(solution)/shard_map/ppermute | solution.py:394
  28.2 2.9 %collective-permute-start.4 = (f32[32,256]{1,0:T(8,128)S(1)}, f32[32,256]{1,0:T(8,128)S(1)}, u32[]{:S(2)}, u32[]{:S(2)}) collective-permute-start(f32[32,256]{1,0:T(8,128)S(1)} %get-tuple-element.59), channel_id=1, source_target_pairs={{0,1},{1,0},{2,3},{3,2},{4,5},{5,4},{6,7},{7,6},{8,9},{9,8},{10,11... | collective-permute-start | bytes 98312 | tf_op jit(solution)/shard_map/ppermute | solution.py:394
  28.2 3.9 %collective-permute-start.5 = (f32[32,256]{1,0:T(8,128)S(1)}, f32[32,256]{1,0:T(8,128)S(1)}, u32[]{:S(2)}, u32[]{:S(2)}) collective-permute-start(f32[32,256]{1,0:T(8,128)S(1)} %get-tuple-element.60), channel_id=1, source_target_pairs={{0,2},{1,3},{2,0},{3,1},{4,6},{5,7},{6,4},{7,5},{8,10},{9,11},{10,... | collective-permute-start | bytes 98312 | tf_op jit(solution)/shard_map/ppermute | solution.py:394
  28.6 4.8 %collective-permute-start.6 = (f32[32,256]{1,0:T(8,128)S(1)}, f32[32,256]{1,0:T(8,128)S(1)}, u32[]{:S(2)}, u32[]{:S(2)}) collective-permute-start(f32[32,256]{1,0:T(8,128)S(1)} %get-tuple-element.61), channel_id=1, source_target_pairs={{0,4},{1,5},{2,6},{3,7},{4,0},{5,1},{6,2},{7,3},{8,12},{9,13},{10,... | collective-permute-start | bytes 98312 | tf_op jit(solution)/shard_map/ppermute | solution.py:394
  34.4 0.6 copy-start.11
  35.0 13.3 %copy-start.4 = (f32[32,768]{1,0:T(8,128)}, f32[32,768]{1,0:T(8,128)S(1)}, u32[]{:S(2)}) copy-start(f32[32,768]{1,0:T(8,128)S(1)} %get-tuple-element.71.local) | copy-start | bytes 294916
  35.0 13.3 %all-to-all-start.1 = ((f32[32,4,128]{2,1,0:T(4,128)}), f32[32,4,128]{2,1,0:T(4,128)S(1)}, u32[]{:S(2)}, u32[]{:S(2)}) async-start(f32[32,4,128]{2,1,0:T(4,128)} %bitcast.8), calls=%async_computation.1 | async-start | bytes 131072 | tf_op jit(solution)/shard_map/all_to_all | solution.py:407
  39.8 5.9 %collective-permute-start.8 = (f32[32,256]{1,0:T(8,128)}, f32[32,256]{1,0:T(8,128)S(1)}, u32[]{:S(2)}, u32[]{:S(2)}) collective-permute-start(f32[32,256]{1,0:T(8,128)} %get-tuple-element.67), channel_id=1, source_target_pairs={{0,1},{1,0},{2,3},{3,2},{4,5},{5,4},{6,7},{7,6},{8,9},{9,8},{10,11... | collective-permute-start | bytes 98312 | tf_op jit(solution)/shard_map/ppermute | solution.py:394
  40.1 5.6 %collective-permute-start.9 = (f32[32,256]{1,0:T(8,128)}, f32[32,256]{1,0:T(8,128)S(1)}, u32[]{:S(2)}, u32[]{:S(2)}) collective-permute-start(f32[32,256]{1,0:T(8,128)} %get-tuple-element.68), channel_id=1, source_target_pairs={{0,2},{1,3},{2,0},{3,1},{4,6},{5,7},{6,4},{7,5},{8,10},{9,11},{10,... | collective-permute-start | bytes 98312 | tf_op jit(solution)/shard_map/ppermute | solution.py:394
  41.8 5.5 %collective-permute-start.10 = (f32[32,256]{1,0:T(8,128)}, f32[32,256]{1,0:T(8,128)S(1)}, u32[]{:S(2)}, u32[]{:S(2)}) collective-permute-start(f32[32,256]{1,0:T(8,128)} %get-tuple-element.69), channel_id=1, source_target_pairs={{0,4},{1,5},{2,6},{3,7},{4,0},{5,1},{6,2},{7,3},{8,12},{9,13},{10,... | collective-permute-start | bytes 98312 | tf_op jit(solution)/shard_map/ppermute | solution.py:394
  44.2 4.1 %collective-permute-start.11 = (f32[32,256]{1,0:T(8,128)}, f32[32,256]{1,0:T(8,128)S(1)}, u32[]{:S(2)}, u32[]{:S(2)}) collective-permute-start(f32[32,256]{1,0:T(8,128)} %copy-done.11), channel_id=1, source_target_pairs={{0,8},{8,0},{16,24},{24,16},{1,9},{9,1},{17,25},{25,17},{2,10},{10... | collective-permute-start | bytes 98312 | tf_op jit(solution)/shard_map/ppermute | solution.py:394
  48.3 0.9 %copy-start.5 = (f32[32,768]{1,0:T(8,128)S(1)}, f32[32,768]{1,0:T(8,128)}, u32[]{:S(2)}) copy-start(f32[32,768]{1,0:T(8,128)} %copy-done.4) | copy-start | bytes 294916
  50.1 4.9 %collective-permute-start.12 = (f32[32,256]{1,0:T(8,128)S(1)}, f32[32,256]{1,0:T(8,128)S(1)}, u32[]{:S(2)}, u32[]{:S(2)}) collective-permute-start(f32[32,256]{1,0:T(8,128)S(1)} %get-tuple-element.75), channel_id=1, source_target_pairs={{0,1},{1,0},{2,3},{3,2},{4,5},{5,4},{6,7},{7,6},{8,9},{9,8},{10,11... | collective-permute-start | bytes 98312 | tf_op jit(solution)/shard_map/ppermute | solution.py:394
  50.2 4.8 %collective-permute-start.13 = (f32[32,256]{1,0:T(8,128)S(1)}, f32[32,256]{1,0:T(8,128)S(1)}, u32[]{:S(2)}, u32[]{:S(2)}) collective-permute-start(f32[32,256]{1,0:T(8,128)S(1)} %get-tuple-element.76), channel_id=1, source_target_pairs={{0,2},{1,3},{2,0},{3,1},{4,6},{5,7},{6,4},{7,5},{8,10},{9,11},{10,... | collective-permute-start | bytes 98312 | tf_op jit(solution)/shard_map/ppermute | solution.py:394
  50.8 5.2 %collective-permute-start.14 = (f32[32,256]{1,0:T(8,128)S(1)}, f32[32,256]{1,0:T(8,128)S(1)}, u32[]{:S(2)}, u32[]{:S(2)}) collective-permute-start(f32[32,256]{1,0:T(8,128)S(1)} %get-tuple-element.77), channel_id=1, source_target_pairs={{0,4},{1,5},{2,6},{3,7},{4,0},{5,1},{6,2},{7,3},{8,12},{9,13},{10,... | collective-permute-start | bytes 98312 | tf_op jit(solution)/shard_map/ppermute | solution.py:394
  52.0 3.9 %collective-permute-start.15 = (f32[32,256]{1,0:T(8,128)S(1)}, f32[32,256]{1,0:T(8,128)S(1)}, u32[]{:S(2)}, u32[]{:S(2)}) collective-permute-start(f32[32,256]{1,0:T(8,128)S(1)} %get-tuple-element.78), channel_id=1, source_target_pairs={{0,8},{8,0},{16,24},{24,16},{1,9},{9,1},{17,25},{25,17},{2,10},{10... | collective-permute-start | bytes 98312 | tf_op jit(solution)/shard_map/ppermute | solution.py:394
  53.5 14.4 %collective-permute-start.20 = (f32[128,256]{1,0:T(8,128)S(1)}, f32[128,256]{1,0:T(8,128)S(1)}, u32[]{:S(2)}, u32[]{:S(2)}) collective-permute-start(f32[128,256]{1,0:T(8,128)S(1)} %get-tuple-element.91.rest_0_), channel_id=1, source_target_pairs={{0,16},{8,24},{16,0},{24,8},{1,17},{9,25},{17,1},{25,9},{2,18},{10... | collective-permute-start | bytes 393224 | tf_op jit(solution)/shard_map/ppermute | solution.py:394
  57.1 13.2 %all-to-all-start.2 = ((f32[32,4,128]{2,1,0:T(4,128)}), f32[32,4,128]{2,1,0:T(4,128)S(1)}, u32[]{:S(2)}, u32[]{:S(2)}) async-start(f32[32,4,128]{2,1,0:T(4,128)} %bitcast.10), calls=%async_computation.2 | async-start | bytes 131072 | tf_op jit(solution)/shard_map/all_to_all | solution.py:407
  62.0 5.9 %collective-permute-start.16 = (f32[32,256]{1,0:T(8,128)S(1)}, f32[32,256]{1,0:T(8,128)S(1)}, u32[]{:S(2)}, u32[]{:S(2)}) collective-permute-start(f32[32,256]{1,0:T(8,128)S(1)} %get-tuple-element.82), channel_id=1, source_target_pairs={{0,1},{1,0},{2,3},{3,2},{4,5},{5,4},{6,7},{7,6},{8,9},{9,8},{10,11... | collective-permute-start | bytes 98312 | tf_op jit(solution)/shard_map/ppermute | solution.py:394
  62.3 5.6 %collective-permute-start.17 = (f32[32,256]{1,0:T(8,128)S(1)}, f32[32,256]{1,0:T(8,128)S(1)}, u32[]{:S(2)}, u32[]{:S(2)}) collective-permute-start(f32[32,256]{1,0:T(8,128)S(1)} %get-tuple-element.83), channel_id=1, source_target_pairs={{0,2},{1,3},{2,0},{3,1},{4,6},{5,7},{6,4},{7,5},{8,10},{9,11},{10,... | collective-permute-start | bytes 98312 | tf_op jit(solution)/shard_map/ppermute | solution.py:394
  64.0 5.3 %collective-permute-start.18 = (f32[32,256]{1,0:T(8,128)S(1)}, f32[32,256]{1,0:T(8,128)S(1)}, u32[]{:S(2)}, u32[]{:S(2)}) collective-permute-start(f32[32,256]{1,0:T(8,128)S(1)} %get-tuple-element.84), channel_id=1, source_target_pairs={{0,4},{1,5},{2,6},{3,7},{4,0},{5,1},{6,2},{7,3},{8,12},{9,13},{10,... | collective-permute-start | bytes 98312 | tf_op jit(solution)/shard_map/ppermute | solution.py:394
  66.4 3.9 %collective-permute-start.19 = (f32[32,256]{1,0:T(8,128)S(1)}, f32[32,256]{1,0:T(8,128)S(1)}, u32[]{:S(2)}, u32[]{:S(2)}) collective-permute-start(f32[32,256]{1,0:T(8,128)S(1)} %get-tuple-element.85), channel_id=1, source_target_pairs={{0,8},{8,0},{16,24},{24,16},{1,9},{9,1},{17,25},{25,17},{2,10},{10... | collective-permute-start | bytes 98312 | tf_op jit(solution)/shard_map/ppermute | solution.py:394

commit v4 on v3

v4 whole, which is shorter than its diff:
```python
import functools

import jax
import jax.numpy as jnp
from jax import lax
from jax.experimental import pallas as pl
from jax.experimental.pallas import tpu as pltpu
from jax.sharding import PartitionSpec as P

F32, BF16 = jnp.float32, jnp.bfloat16
NT = (((1,), (1,)), ((), ()))
NN = (((1,), (0,)), ((), ()))
LANES = 128


def exact(a, b, dims=NN):
    return lax.dot_general(a, b, dims, precision=lax.Precision.HIGHEST, preferred_element_type=F32)


def rounded(a, b):
    return lax.dot_general(a, b, NN, preferred_element_type=F32)


def thirds(x):
    high = x.astype(BF16)
    rest = x - high.astype(F32)
    mid = rest.astype(BF16)
    return jnp.concatenate([high, mid, (rest - mid.astype(F32)).astype(BF16)], axis=0)


def by_map(x, corner_map, dims):
    n = x.shape[0]
    out = lax.dot_general(thirds(x), corner_map, dims, preferred_element_type=F32)
    return out[:n] + out[n : 2 * n] + out[2 * n :]


def iota(shape, axis):
    return lax.broadcasted_iota(jnp.int32, shape, axis)


FACES = (2, 1, 3, 0)
LAST = FACES.index(3)


def windows(dofs):
    width = dofs // 4
    return [(f * width // LANES * LANES, -(-(f + 1) * width // LANES) * LANES) for f in FACES]


def face_vectors(nodes_ref, dofs):
    width = dofs // 4
    pos = iota((1, dofs), 1)
    sub_pos, grp_pos = lax.axis_index("sub"), lax.axis_index("grp")
    bits = [sub_pos & 1, (sub_pos >> 1) & 1, (sub_pos >> 2) & 1, grp_pos & 1]
    sign = jnp.zeros((1, dofs), F32)
    live = jnp.zeros((1, dofs), jnp.int32)
    node = pos
    for f in range(4):
        inside = (pos >= f * width) & (pos < (f + 1) * width)
        sign = jnp.where(inside, (1 - 2 * bits[f]).astype(F32), sign)
        live = jnp.where(inside, nodes_ref[f], live)
    for step in range(1, 12):
        node = jnp.where(pos >= step * (width // 3), pos - step * (width // 3), node)
    mask = jnp.where(node < live, 1.0, 0.0)
    return sign, mask


def corner_ids(ids_ref, shape, axis):
    place = iota(shape, axis)
    ids = jnp.full(shape, -1, jnp.int32)
    for k in range(ids_ref.shape[0]):
        ids = jnp.where(place == 4 * (k % 4) + k // 4, ids_ref[k], ids)
    return ids


def corner_rows(ids, dofs):
    return jnp.where(ids == iota((16, dofs), 1), 1.0, 0.0)


def across(wins, dofs):
    by_face = sorted(zip(FACES, windows(dofs), wins), key=lambda item: item[0])
    width = dofs // 4
    n = wins[0].shape[0]
    tiles = []
    for low in range(0, dofs, LANES):
        tile = None
        for f, (start, stop), win in by_face:
            if start <= low < stop:
                part = win[:, low - start : low - start + LANES]
                tile = part if tile is None else jnp.where(iota((n, LANES), 1) + low < f * width, tile, part)
        tiles.append(tile)
    return jnp.concatenate(tiles, axis=1)


def jump(own, came, rows, sign_mask):
    return across([a[:rows, :] - b[:rows, :] for a, b in zip(own, came)], sign_mask.shape[1]) * sign_mask


def put_windows(refs, field):
    for ref, (start, stop) in zip(refs, windows(field.shape[1])):
        ref[: field.shape[0], :] = field[:, start:stop]


def same_block(n_row, n_col, row_block, col_block):
    return iota((n_row, n_col), 0) // row_block == iota((n_row, n_col), 1) // col_block


def to_column(row):
    n = row.shape[1]
    return jnp.sum(jnp.where(same_block(n, n, 1, 1), row, 0.0), axis=1, keepdims=True)


def to_row(column):
    n = column.shape[0]
    return jnp.sum(jnp.where(same_block(n, n, 1, 1), column, 0.0), axis=0, keepdims=True)


def total_of(received):
    total = received[0:8]
    for low in range(8, received.shape[0], 8):
        total = total + received[low : low + 8]
    return total + pltpu.roll(total, 4, 0)


def sums_of(total, n_load):
    column = to_column(total[3:4])
    return [column[i * n_load : (i + 1) * n_load] for i in range(4)]


def halves(x):
    high = x.astype(BF16)
    return jnp.concatenate([high, (x - high.astype(F32)).astype(BF16)], axis=0)


def fine(x, matrix):
    n = x.shape[0]
    both = rounded(halves(x), matrix)
    return both[:n] + both[n:]


def finer(x, matrix):
    n = x.shape[0]
    high = matrix.astype(BF16)
    low = (matrix - high.astype(F32)).astype(BF16)
    parts = halves(x)
    both = lax.dot_general(parts, high, NT, preferred_element_type=F32)
    return both[:n] + both[n:] + lax.dot_general(parts[:n], low, NT, preferred_element_type=F32)


def packed_corners(scaled, corner):
    n_load = scaled.shape[0]
    values = by_map(scaled, corner, NT)
    flipped = jnp.concatenate([values] * 4, axis=0).T
    flipped = jnp.where(same_block(16, 4 * n_load, 4, n_load), flipped, 0.0)
    block = flipped[:8] + flipped[8:]
    return block + pltpu.roll(block, 4, 0)


def with_sums(block, sums):
    zero = jnp.zeros_like(sums[0])
    row = to_row(jnp.concatenate(sums + [zero] * (4 - len(sums)), axis=0))
    return jnp.where(iota(block.shape, 0) % 4 == 3, row, block)


def put_all(out, block):
    for low in range(0, out.shape[0], 8):
        out[low : low + 8, :] = block


def group_corners(received, which, rows, n_load):
    block = received[pl.ds(pl.multiple_of(which * rows, 8), rows), :]
    block = jnp.where(iota(block.shape, 0) % 4 == 3, 0.0, block)
    tall = jnp.concatenate([block] * 4, axis=0)
    flipped = jnp.where(same_block(4 * rows, 4 * n_load, rows, n_load), tall, 0.0).T
    return sum(flipped[r * n_load : (r + 1) * n_load] for r in range(1, 4)) + flipped[:n_load]


def coarse_of(received, spread, n_load):
    rows = spread.shape[1] // 4
    grp_pos = lax.axis_index("grp")
    inner = finer(group_corners(received, grp_pos, rows, n_load), spread)
    outer = finer(group_corners(received, grp_pos ^ 1, rows, n_load), spread)
    return jnp.where(iota(inner.shape, 1) < 64, inner, outer)


def to_wide(matrix, wide):
    n_row, n = matrix.shape
    if n < wide:
        return jnp.concatenate([matrix[: n_row // 2], matrix[n_row // 2 :]], axis=1)
    return jnp.concatenate([matrix[:, low : low + wide] for low in range(0, n, wide)], axis=0)


def from_wide(rows, n):
    wide = rows.shape[1]
    if n < wide:
        return jnp.concatenate([rows[:, :n], rows[:, n:]], axis=0)
    n_row = rows.shape[0] * wide // n
    return jnp.concatenate([rows[low : low + n_row] for low in range(0, rows.shape[0], n_row)], axis=1)


def rows_sum(x):
    return jnp.sum(x, axis=1, keepdims=True)


def start(
    rhs_hbm, stiff_hbm, inverse_hbm, nodes_hbm, ids_hbm,
    sent, vectors, corner_out, resid_out, spread_out, coarse_out, low_out, w0, w1, w2, w3,
    rhs, stiff, inverse, nodes, ids, sems,
):
    pairs = [(nodes_hbm, nodes), (ids_hbm, ids), (rhs_hbm, rhs), (inverse_hbm, inverse), (stiff_hbm, stiff)]
    copies = [pltpu.make_async_copy(a, b, sems.at[i]) for i, (a, b) in enumerate(pairs)]
    for copy in copies:
        copy.start()
    n_load, dofs = rhs.shape
    wins = [w0, w1, w2, w3]
    copies[0].wait()
    sign, mask = face_vectors(nodes, dofs)
    vectors[0:1, :] = sign
    vectors[1:2, :] = mask
    vectors[2:3, :] = sign * mask
    vectors[3:8, :] = jnp.zeros((5, dofs), F32)
    copies[1].wait()
    corner = corner_rows(corner_ids(ids, (16, 1), 0), dofs).astype(BF16)
    corner_out[...] = corner
    for ref in wins:
        ref[n_load : n_load + 8, :] = corner_ids(ids, (8, ref.shape[1]), 1).astype(F32)
    copies[2].wait()
    resid = rhs[...] * mask
    resid_out[...] = resid
    scaled = 0.5 * sign * resid
    put_all(sent, packed_corners(scaled, corner))
    copies[3].wait()
    n = inverse.shape[0]
    corners = ids.shape[0]
    subs = n // corners
    sub_pos = lax.axis_index("sub")
    row = iota((64, 1), 0)
    owner = jnp.where(row < 16, sub_pos, jnp.where(row < 32, sub_pos ^ 1, jnp.where(row < 48, sub_pos ^ 2, sub_pos ^ 4)))
    source = owner * corners + row % 4 * 4 + row // 4 % 4
    pick = jnp.where((source == iota((64, n), 1)) & (row % 4 * 4 < corners), 1.0, 0.0)
    place = iota((16 * subs, 1), 0)
    source = place // 4 % subs * corners + place % 4 * 4 + place // (4 * subs)
    order = jnp.where((source == iota((16 * subs, n), 1)) & (place % 4 * 4 < corners), 1.0, 0.0)
    both = exact(exact(jnp.concatenate([pick, order], axis=0), inverse[...]), order, NT)
    spread_out[...] = both[:64]
    last = wins[LAST]
    coarse_out[...] = to_wide(both[64:], last.shape[1])
    last[n_load + 8 :, :] = to_wide(both[:16], last.shape[1])
    copies[4].wait()
    local = rounded(halves(scaled), stiff[...])
    put_windows(wins, local[:n_load])
    low_out[...] = local[n_load:]


def first_image(
    received, o0, o1, o2, o3, a0, a1, a2, a3, vectors, corner, resid, spread, low, flex,
    z_out, sums_out, map_out, spread_out, *wins,
):
    n_load, dofs = resid.shape
    came = [a0, a1, a2, a3]
    sign, sign_mask = vectors[0:1, :], vectors[2:3, :]
    width = dofs // 4
    pos = iota((1, dofs), 1)
    pieces = [corner[...].astype(F32) * sign_mask]
    for f in range(4):
        ids = to_column(came[FACES.index(f)][n_load : n_load + 1, :LANES])[:16].astype(jnp.int32)
        inside = (pos >= f * width) & (pos < (f + 1) * width)
        pieces.append(corner_rows(ids, dofs) * jnp.where(inside, -sign_mask, 0.0))
    corner_map = jnp.concatenate(pieces, axis=0).astype(BF16)
    map_out[...] = corner_map
    n = spread.shape[1]
    cross = from_wide(came[LAST][n_load + 8 :, :], n)
    spread_rows = jnp.concatenate([spread[...], cross], axis=0)
    spread_out[...] = spread_rows
    coarse = coarse_of(received, spread_rows, n_load)
    zvec = jump([o0, o1, o2, o3], came, n_load, sign_mask) + by_map(coarse, corner_map, NN)
    z_out[...] = zvec
    signed = sign * zvec
    image = rounded(signed.astype(BF16), flex[...])
    put_windows(wins, jnp.concatenate([image, low[...]], axis=0))
    sums_out[...] = with_sums(
        jnp.zeros((8, 4 * n_load), F32), [rows_sum(resid[...] * zvec), 2.0 * rows_sum(signed * image)]
    )


def second_local(
    o0, o1, o2, o3, a0, a1, a2, a3, sums, vectors, corner_map, stiff, flexed_out, low_out, sent, *wins
):
    n_load, dofs = flexed_out.shape
    sign, sign_mask = vectors[0:1, :], vectors[2:3, :]
    jumped = jump([o0, o1, o2, o3], [a0, a1, a2, a3], 2 * n_load, sign_mask)
    flexed = jumped[:n_load]
    flexed_out[...] = flexed
    low_out[...] = jumped[n_load:].astype(BF16)
    scaled = 0.5 * sign * flexed
    is_sum = iota((8, 1), 0) % 4 == 3
    corners = packed_corners(scaled, abs(corner_map[:16, :]))
    put_all(sent, jnp.where(is_sum, sums[...], corners))
    put_windows(wins, fine(scaled, stiff[...]))


def second_image(
    received, o0, o1, o2, o3, a0, a1, a2, a3, flexed, zold, low, resid, inverse, vectors, corner_map, spread, flex,
    z_out, step_out, sums_out, total_out, inverse_out, *wins,
):
    n_load, dofs = resid.shape
    sign, sign_mask = vectors[0:1, :], vectors[2:3, :]
    inverse_out[...] = inverse[...]
    total = total_of(received)
    total_out[...] = total
    rz, curve, _, _ = sums_of(total, n_load)
    alpha = rz / curve
    coarse = coarse_of(received, spread[...], n_load)
    step = jump([o0, o1, o2, o3], [a0, a1, a2, a3], n_load, sign_mask) + by_map(coarse, corner_map[...], NN)
    step = alpha * step
    step_out[...] = step
    zvec = zold[...] + low[...].astype(F32) - step
    z_out[...] = zvec
    signed = sign * zvec
    image = alpha * fine(signed, flex[...])
    put_windows(wins, image)
    scaled_flexed = alpha * flexed[...]
    sums = [
        rows_sum((resid[...] - scaled_flexed) * zvec),
        2.0 * rows_sum(signed * image),
        rows_sum(zvec * scaled_flexed),
    ]
    sums_out[...] = with_sums(jnp.zeros((8, 4 * n_load), F32), sums)


def third_local(o0, o1, o2, o3, a0, a1, a2, a3, sums, vectors, corner_map, stiff, *rest):
    inverses, (sent, *wins) = rest[:-5], rest[-5:]
    n_load, dofs = o0.shape[0], vectors.shape[1]
    sign, sign_mask = vectors[0:1, :], vectors[2:3, :]
    flexed = jump([o0, o1, o2, o3], [a0, a1, a2, a3], n_load, sign_mask)
    scaled = 0.5 * sign * flexed
    local = fine(scaled, stiff[...])
    put_windows(wins, local)
    low = n_load
    for ref in inverses:
        wins[LAST][low : low + ref.shape[0], :] = ref[...]
        low += ref.shape[0]
    fourth = jnp.where(iota((1, 4 * n_load), 1) // n_load == 3, 1.0, 0.0)
    square = with_sums(jnp.zeros((8, 4 * n_load), F32), [4.0 * rows_sum(scaled * local)] * 4) * fourth
    is_sum = iota((8, 1), 0) % 4 == 3
    put_all(sent, jnp.where(is_sum, sums[...] + square, packed_corners(scaled, abs(corner_map[:16, :]))))


def finish(
    received, o0, o1, o2, o3, a0, a1, a2, a3, before, zold, znew, step, vectors, corner_map, spread, *rest
):
    inverses, (mult_out, direction_out) = rest[:-2], rest[-2:]
    n_load, dofs = zold.shape
    sign_mask = vectors[2:3, :]
    rz0, curve0, _, _ = sums_of(before[...], n_load)
    rz1, curve, mixed, square = sums_of(total_of(received), n_load)
    n = spread.shape[1]
    height = n * n // a0.shape[1]
    held = jnp.concatenate([ref[...] for ref in inverses], axis=0)
    for side, rows in enumerate([held, [a0, a1, a2, a3][LAST][n_load:, :]]):
        for i in range(rows.shape[0] // height):
            values = group_corners(received, lax.axis_index("grp") ^ (2 * i + side), n // 4, n_load)
            matrix = from_wide(rows[i * height : (i + 1) * height], n)
            square = square + 4.0 * rows_sum(values * finer(values, matrix))
    alpha = rz0 / curve0
    beta = rz1 / rz0
    gamma = rz1 / (curve + 2.0 * beta * mixed + beta * beta * rz0)
    rz2 = square + 2.0 * beta * (mixed - curve) + beta * beta * (rz0 - mixed)
    rz2 = rz1 - 2.0 * gamma * (curve + beta * mixed) + gamma * gamma * rz2
    coarse = coarse_of(received, spread[...], n_load)
    image = jump([o0, o1, o2, o3], [a0, a1, a2, a3], n_load, sign_mask) + by_map(coarse, corner_map[...], NN)
    direction = znew[...] + beta * zold[...]
    mult_out[...] = alpha * (zold[...] + gamma * direction)
    direction_out[...] = znew[...] - gamma * (image + beta * step[...]) + (rz2 / rz1) * direction


def call(name, kernel, args, outs, scratch=(), space=pltpu.VMEM):
    shapes = [jax.ShapeDtypeStruct(s, d) for s, d in outs]
    n_bytes = sum(a.size * a.dtype.itemsize for a in args) + sum(s.size * s.dtype.itemsize for s in shapes)
    return pl.pallas_call(
        kernel,
        out_shape=shapes,
        in_specs=[pl.BlockSpec(memory_space=space)] * len(args),
        out_specs=[pl.BlockSpec(memory_space=pltpu.VMEM)] * len(shapes),
        scratch_shapes=scratch,
        cost_estimate=pl.CostEstimate(flops=40_000_000, bytes_accessed=n_bytes, transcendentals=0),
        compiler_params=pltpu.CompilerParams(vmem_limit_bytes=(12 << 20) + 2 * n_bytes if space == pltpu.VMEM else 54600 << 10),
        name=name,
    )(*args)


def swap(block, axis, distance):
    count = lax.axis_size(axis)
    return lax.ppermute(block, axis, [(i, i ^ distance) for i in range(count) if i ^ distance < count])


def exchange(wins):
    return [swap(win, "grp", 1) if f == 3 else swap(win, "sub", 1 << f) for f, win in zip(FACES, wins)]


def send_all(rows):
    devices = lax.axis_size("grp") * lax.axis_size("sub")
    blocks = rows.reshape(devices, 4, rows.shape[1])
    return lax.all_to_all(blocks, ("grp", "sub"), 0, 0, tiled=True).reshape(rows.shape)


def body(loads, stiffness, flexibility, coarse_inverse, face_nodes, corner_index):
    rhs, stiff, flex, inverse = loads[0, 0], stiffness[0, 0], flexibility[0, 0], coarse_inverse[0]
    nodes, ids = face_nodes[0, 0], corner_index[0, 0]
    n_load, dofs = rhs.shape
    groups, subs = lax.axis_size("grp"), lax.axis_size("sub")
    n = 16 * subs
    field = ((n_load, dofs), F32)
    sent = ((groups * subs * 4, 4 * n_load), F32)
    total = ((8, 4 * n_load), F32)
    spans = [high - low for low, high in windows(dofs)]
    coarse = ((n * n // spans[LAST], spans[LAST]), F32)

    def wins(rows, more=0):
        return [((rows + more * (i == LAST), w), F32) for i, w in enumerate(spans)]

    corners, vectors, corner, resid, spread, inverse, low, *own = call(
        "start", start, [rhs, stiff, inverse, nodes, ids],
        [sent, ((8, dofs), F32), ((16, dofs), BF16), field, ((64, n), F32), coarse, field]
        + wins(n_load + 8, 16 * n // spans[LAST]),
        [pltpu.VMEM(rhs.shape, F32), pltpu.VMEM(stiff.shape, BF16), pltpu.VMEM(inverse.shape, F32),
         pltpu.SMEM(nodes.shape, jnp.int32), pltpu.SMEM(ids.shape, jnp.int32), pltpu.SemaphoreType.DMA((5,))],
        pl.ANY,
    )
    received = send_all(corners)
    came = exchange(own)
    zold, sums, corner_map, spread, *own = call(
        "image1", first_image, [received] + own + came + [vectors, corner, resid, spread, low, flex],
        [field, total, ((80, dofs), BF16), ((80, n), F32)] + wins(2 * n_load),
    )
    came = exchange(own)
    flexed, low, sent_rows, *own = call(
        "local2", second_local, own + came + [sums, vectors, corner_map, stiff],
        [field, ((n_load, dofs), BF16), sent] + wins(n_load),
    )
    received = send_all(sent_rows)
    came = exchange(own)
    znew, step, sums, before, inverse, *own = call(
        "image2", second_image,
        [received] + own + came + [flexed, zold, low, resid, inverse, vectors, corner_map, spread, flex],
        [field, field, total, total, coarse] + wins(n_load),
    )
    came = exchange(own)
    distance, inverses = 2, [inverse]
    while distance < groups:
        inverses.append(swap(jnp.concatenate(inverses, axis=0), "grp", distance))
        distance *= 2
    sent_rows, *own = call(
        "local3", third_local, own + came + [sums, vectors, corner_map, stiff] + inverses,
        [sent] + wins(n_load, sum(a.shape[0] for a in inverses)),
    )
    received = send_all(sent_rows)
    came = exchange(own)
    mult, direction = call(
        "finish", finish,
        [received] + own + came + [before, zold, znew, step, vectors, corner_map, spread] + inverses, [field, field],
    )
    return (mult[None, None], direction[None, None])


def solution(mesh):
    in_specs = (
        P("grp", "sub", None, None),
        P("grp", "sub", None, None),
        P("grp", "sub", None, None),
        P("grp", None, None),
        P("grp", "sub", None),
        P("grp", "sub", None),
    )
    out_specs = (P("grp", "sub", None, None), P("grp", "sub", None, None))
    return jax.shard_map(body, mesh=mesh, in_specs=in_specs, out_specs=out_specs, check_vma=False)
```

time: 71.9 us -> 63.8 us (0.89)
  local copies, waits for them, and re-layouts: 7.3 us -> 2.21 us
  starting transfers between devices: 42.8 us -> 38.7 us
  waiting for transfers between devices: 13.1 us -> 14.4 us
    unnamed x24 -> x10, local copies, waits for them, and re-layouts: 7.3 us -> 2.21 us
    all_to_all x3, starting transfers between devices: 16.9 us -> 13.8 us  [send_all(): lax.all_to_all(blocks, ('grp', 'sub'), 0, 0, tiled=True).reshape(rows.shape)]
    ppermute x21, starting transfers between devices: 25.9 us -> 24.9 us  [swap(): lax.ppermute(block, axis, [(i, i ^ distance) for i in range(count) if i ^...]
    all_to_all x3, waiting for transfers between devices: 0.01 us -> 0.95 us  [send_all(): lax.all_to_all(blocks, ('grp', 'sub'), 0, 0, tiled=True).reshape(rows.shape)]
  transfers between devices with their start and end apart: 24 -> 24, of which waited for: 9 -> 12; matrix products, arithmetic and copies ran while one was open for 0% -> 0% of each run, Pallas kernels for 2% -> 0%
where the time goes in v4:
time: 63.8 us; the launch traced here: 63.5 us
  starting transfers between devices  38.7 us (61%)
  waiting for transfers between devices  14.4 us (23%)
  Pallas kernels  7.53 us (12%)
  local copies, waits for them, and re-layouts  2.21 us (3%)
  between operations  0.74 us (1%)
    ppermute x21, starting transfers between devices, swap(): lax.ppermute(block, axis, [(i, i ^ distance) for i in range(count) if i ^...  24.9 us
    all_to_all x3, starting transfers between devices, send_all(): lax.all_to_all(blocks, ('grp', 'sub'), 0, 0, tiled=True).reshape(rows.shape)  13.8 us
    ppermute x21, waiting for transfers between devices, swap(): lax.ppermute(block, axis, [(i, i ^ distance) for i in range(count) if i ^...  13.5 us
    pallas_call x6, Pallas kernels, call(): pl.pallas_call(kernel, out_shape=shapes, in_specs=[pl.BlockSpec(memory_sp...  7.53 us
    unnamed x10, local copies, waits for them, and re-layouts  2.21 us
  transfers between devices with their start and end apart: 24, of which 12 were waited for; matrix products, arithmetic and copies ran while one was open for 0% of the time, Pallas kernels for 0%

profile of v4, /device:TPU:0, one launch (start us, length us, event | category | flops | bytes accessed | tf_op | source)
XLA Modules:
  0.0 63.5 jit_solution(14752158357578708411)
XLA Ops:
  0.6 0.0 copy-start.1
  0.6 0.0 copy-start.2
  0.7 0.9 %copy-done.2 = f32[1,96,96]{2,1,0:T(8,128)S(1)} copy-done((f32[1,96,96]{2,1,0:T(8,128)S(1)}, f32[1,96,96]{2,1,0:T(8,128)}, u32[]{:S(2)}) %copy-start.2) | copy-done | bytes 36888
  1.5 0.0 copy-start.3
  1.5 0.7 %copy-done.3 = s32[1,1,4]{2,1,0:T(1,128)S(1)} copy-done((s32[1,1,4]{2,1,0:T(1,128)S(1)}, s32[1,1,4]{2,1,0:T(1,128)}, u32[]{:S(2)}) %copy-start.3) | copy-done | bytes 40
  2.2 0.0 copy-start.4
  2.2 0.7 %copy-done.4 = s32[1,1,12]{2,1,0:T(1,128)S(1)} copy-done((s32[1,1,12]{2,1,0:T(1,128)S(1)}, s32[1,1,12]{2,1,0:T(1,128)}, u32[]{:S(2)}) %copy-start.4) | copy-done | bytes 72
  2.8 2.4 %start.1 = (f32[128,128]{1,0:T(8,128)}, f32[8,768]{1,0:T(8,128)S(1)}, bf16[16,768]{1,0:T(8,128)(2,1)S(1)}, f32[32,768]{1,0:T(8,128)S(1)}, f32[64,128]{1,0:T(8,12...) custom-call(f32[32,768]{1,0:T(8,128)} %bitcast.25, ...), custom_call_target="tpu_custom_call" | custom-call | flops 40000000 | bytes 1896512 | tf_op jit(solution)/shard_map/start/pallas_call | solution.py:380
  5.3 0.0 copy-start
  5.3 7.3 %all-to-all-start = ((f32[32,4,128]{2,1,0:T(4,128)}), f32[32,4,128]{2,1,0:T(4,128)S(1)}, u32[]{:S(2)}, u32[]{:S(2)}) async-start(f32[32,4,128]{2,1,0:T(4,128)} %bitcast.5), calls=%async_computation | async-start | bytes 131072 | tf_op jit(solution)/shard_map/all_to_all | solution.py:404
  12.6 1.8 %collective-permute-start.2 = (f32[48,256]{1,0:T(8,128)S(1)}, f32[48,256]{1,0:T(8,128)S(1)}, u32[]{:S(2)}, u32[]{:S(2)}) collective-permute-start(f32[48,256]{1,0:T(8,128)S(1)} %get-tuple-element.47.o2), channel_id=1, source_target_pairs={{0,8},{8,0},{16,24},{24,16},{1,9},{9,1},{17,25},{25,17},{2,10},{10... | collective-permute-start | bytes 147464 | tf_op jit(solution)/shard_map/ppermute | solution.py:394
  14.5 2.4 %collective-permute-start = (f32[40,256]{1,0:T(8,128)S(1)}, f32[40,256]{1,0:T(8,128)S(1)}, u32[]{:S(2)}, u32[]{:S(2)}) collective-permute-start(f32[40,256]{1,0:T(8,128)S(1)} %get-tuple-element.45.o0), channel_id=1, source_target_pairs={{0,4},{1,5},{2,6},{3,7},{4,0},{5,1},{6,2},{7,3},{8,12},{9,13},{10,... | collective-permute-start | bytes 122888 | tf_op jit(solution)/shard_map/ppermute | solution.py:394
  16.8 1.5 %collective-permute-start.1 = (f32[40,256]{1,0:T(8,128)S(1)}, f32[40,256]{1,0:T(8,128)S(1)}, u32[]{:S(2)}, u32[]{:S(2)}) collective-permute-start(f32[40,256]{1,0:T(8,128)S(1)} %get-tuple-element.46.o1), channel_id=1, source_target_pairs={{0,2},{1,3},{2,0},{3,1},{4,6},{5,7},{6,4},{7,5},{8,10},{9,11},{10,... | collective-permute-start | bytes 122888 | tf_op jit(solution)/shard_map/ppermute | solution.py:394
  18.4 0.0 collective-permute-start.3
  18.4 1.4 %collective-permute-done.a0 = f32[40,256]{1,0:T(8,128)S(1)} collective-permute-done((f32[40,256]{1,0:T(8,128)S(1)}, f32[40,256]{1,0:T(8,128)S(1)}, u32[]{:S(2)}, u32[]{:S(2)}) %collective-permute-start) | collective-permute-done | bytes 40992 | tf_op jit(solution)/shard_map/ppermute | solution.py:394
  19.7 1.1 %collective-permute-done.1.a1 = f32[40,256]{1,0:T(8,128)S(1)} collective-permute-done((f32[40,256]{1,0:T(8,128)S(1)}, f32[40,256]{1,0:T(8,128)S(1)}, u32[]{:S(2)}, u32[]{:S(2)}) %collective-permute-start.1) | collective-permute-done | bytes 40992 | tf_op jit(solution)/shard_map/ppermute | solution.py:394
  20.8 0.0 collective-permute-done.3.a3
  20.8 0.0 collective-permute-done.2.a2
  20.8 0.0 all-to-all-done
  20.8 0.0 copy-done.1
  20.9 0.9 %image1.1 = (f32[32,768]{1,0:T(8,128)S(1)}, f32[8,128]{1,0:T(8,128)S(1)}, bf16[80,768]{1,0:T(8,128)(2,1)S(1)}, f32[80,128]{1,0:T(8,128)S(1)}, f32[64,256]{1,0:T(...) custom-call(f32[128,128]{1,0:T(8,128)S(1)} %bitcast.20, ...), custom_call_target="tpu_custom_call" | custom-call | flops 40000000 | bytes 2396160 | tf_op jit(solution)/shard_map/image1/pallas_call | solution.py:380
  21.7 1.3 %collective-permute-start.4 = (f32[64,256]{1,0:T(8,128)S(1)}, f32[64,256]{1,0:T(8,128)S(1)}, u32[]{:S(2)}, u32[]{:S(2)}) collective-permute-start(f32[64,256]{1,0:T(8,128)S(1)} %get-tuple-element.54.o0), channel_id=1, source_target_pairs={{0,4},{1,5},{2,6},{3,7},{4,0},{5,1},{6,2},{7,3},{8,12},{9,13},{10,... | collective-permute-start | bytes 196616 | tf_op jit(solution)/shard_map/ppermute | solution.py:394
  23.0 1.6 %collective-permute-start.5 = (f32[64,256]{1,0:T(8,128)S(1)}, f32[64,256]{1,0:T(8,128)S(1)}, u32[]{:S(2)}, u32[]{:S(2)}) collective-permute-start(f32[64,256]{1,0:T(8,128)S(1)} %get-tuple-element.55.o1), channel_id=1, source_target_pairs={{0,2},{1,3},{2,0},{3,1},{4,6},{5,7},{6,4},{7,5},{8,10},{9,11},{10,... | collective-permute-start | bytes 196616 | tf_op jit(solution)/shard_map/ppermute | solution.py:394
  24.6 0.6 collective-permute-start.6
  25.2 0.0 collective-permute-start.7
  25.2 2.0 %collective-permute-done.4.a0 = f32[64,256]{1,0:T(8,128)S(1)} collective-permute-done((f32[64,256]{1,0:T(8,128)S(1)}, f32[64,256]{1,0:T(8,128)S(1)}, u32[]{:S(2)}, u32[]{:S(2)}) %collective-permute-start.4) | collective-permute-done | bytes 65568 | tf_op jit(solution)/shard_map/ppermute | solution.py:394
  27.1 0.6 %collective-permute-done.5.a1 = f32[64,256]{1,0:T(8,128)S(1)} collective-permute-done((f32[64,256]{1,0:T(8,128)S(1)}, f32[64,256]{1,0:T(8,128)S(1)}, u32[]{:S(2)}, u32[]{:S(2)}) %collective-permute-start.5) | collective-permute-done | bytes 65568 | tf_op jit(solution)/shard_map/ppermute | solution.py:394
  27.8 1.1 %collective-permute-done.6.a2 = f32[64,256]{1,0:T(8,128)S(1)} collective-permute-done((f32[64,256]{1,0:T(8,128)S(1)}, f32[64,256]{1,0:T(8,128)S(1)}, u32[]{:S(2)}, u32[]{:S(2)}) %collective-permute-start.6) | collective-permute-done | bytes 65568 | tf_op jit(solution)/shard_map/ppermute | solution.py:394
  28.9 0.0 collective-permute-done.7.a3
  28.9 0.0 copy-done
  28.9 0.9 %local2.1 = (f32[32,768]{1,0:T(8,128)S(1)}, bf16[32,768]{1,0:T(8,128)(2,1)S(1)}, f32[128,128]{1,0:T(8,128)}, f32[32,256]{1,0:T(8,128)S(1)}, f32[32,256]{1,0:T(8,...) custom-call(f32[64,256]{1,0:T(8,128)S(1)} %get-tuple-element.54.o0, f32[64,256]{1,0:T(8,128)S(1)} %get-tuple-element.55.o1, ...), custom_call_target="tpu_custom_call" | custom-call | flops 40000000 | bytes 2199552 | tf_op jit(solution)/shard_map/local2/pallas_call | solution.py:380
  29.8 2.9 %all-to-all-start.1 = ((f32[32,4,128]{2,1,0:T(4,128)}), f32[32,4,128]{2,1,0:T(4,128)S(1)}, u32[]{:S(2)}, u32[]{:S(2)}) async-start(f32[32,4,128]{2,1,0:T(4,128)} %bitcast.8), calls=%async_computation.1 | async-start | bytes 131072 | tf_op jit(solution)/shard_map/all_to_all | solution.py:404
  32.7 2.7 %collective-permute-start.8 = (f32[32,256]{1,0:T(8,128)S(1)}, f32[32,256]{1,0:T(8,128)S(1)}, u32[]{:S(2)}, u32[]{:S(2)}) collective-permute-start(f32[32,256]{1,0:T(8,128)S(1)} %get-tuple-element.61.o0), channel_id=1, source_target_pairs={{0,4},{1,5},{2,6},{3,7},{4,0},{5,1},{6,2},{7,3},{8,12},{9,13},{10,... | collective-permute-start | bytes 98312 | tf_op jit(solution)/shard_map/ppermute | solution.py:394
  35.5 1.5 %collective-permute-start.9 = (f32[32,256]{1,0:T(8,128)S(1)}, f32[32,256]{1,0:T(8,128)S(1)}, u32[]{:S(2)}, u32[]{:S(2)}) collective-permute-start(f32[32,256]{1,0:T(8,128)S(1)} %get-tuple-element.62.o1), channel_id=1, source_target_pairs={{0,2},{1,3},{2,0},{3,1},{4,6},{5,7},{6,4},{7,5},{8,10},{9,11},{10,... | collective-permute-start | bytes 98312 | tf_op jit(solution)/shard_map/ppermute | solution.py:394
  37.0 1.5 %collective-permute-start.10 = (f32[32,256]{1,0:T(8,128)S(1)}, f32[32,256]{1,0:T(8,128)S(1)}, u32[]{:S(2)}, u32[]{:S(2)}) collective-permute-start(f32[32,256]{1,0:T(8,128)S(1)} %get-tuple-element.63.o2), channel_id=1, source_target_pairs={{0,8},{8,0},{16,24},{24,16},{1,9},{9,1},{17,25},{25,17},{2,10},{10... | collective-permute-start | bytes 98312 | tf_op jit(solution)/shard_map/ppermute | solution.py:394
  38.5 0.0 collective-permute-start.11
  38.5 0.5 collective-permute-done.8.a0
  38.9 0.5 collective-permute-done.9.a1
  39.4 1.5 %collective-permute-done.10.a2 = f32[32,256]{1,0:T(8,128)S(1)} collective-permute-done((f32[32,256]{1,0:T(8,128)S(1)}, f32[32,256]{1,0:T(8,128)S(1)}, u32[]{:S(2)}, u32[]{:S(2)}) %collective-permute-start.10) | collective-permute-done | bytes 32800 | tf_op jit(solution)/shard_map/ppermute | solution.py:394
  40.9 0.0 collective-permute-done.11.a3
  40.9 0.0 all-to-all-done.1
  40.9 0.9 %image2.1 = (f32[32,768]{1,0:T(8,128)S(1)}, f32[32,768]{1,0:T(8,128)S(1)}, f32[8,128]{1,0:T(8,128)S(1)}, f32[8,128]{1,0:T(8,128)S(1)}, f32[64,256]{1,0:T(8,128)S...) custom-call(f32[128,128]{1,0:T(8,128)S(1)} %bitcast.19, ...), custom_call_target="tpu_custom_call" | custom-call | flops 40000000 | bytes 2506752 | tf_op jit(solution)/shard_map/image2/pallas_call | solution.py:380
  41.8 1.6 %collective-permute-start.16 = (f32[64,256]{1,0:T(8,128)S(1)}, f32[64,256]{1,0:T(8,128)S(1)}, u32[]{:S(2)}, u32[]{:S(2)}) collective-permute-start(f32[64,256]{1,0:T(8,128)S(1)} %get-tuple-element.75.rest_0_), channel_id=1, source_target_pairs={{0,16},{8,24},{16,0},{24,8},{1,17},{9,25},{17,1},{25,9},{2,18},{10... | collective-permute-start | bytes 196616 | tf_op jit(solution)/shard_map/ppermute | solution.py:394
  43.4 0.5 collective-permute-start.12
  43.8 0.7 %collective-permute-start.13 = (f32[32,256]{1,0:T(8,128)S(1)}, f32[32,256]{1,0:T(8,128)S(1)}, u32[]{:S(2)}, u32[]{:S(2)}) collective-permute-start(f32[32,256]{1,0:T(8,128)S(1)} %get-tuple-element.71.o1), channel_id=1, source_target_pairs={{0,2},{1,3},{2,0},{3,1},{4,6},{5,7},{6,4},{7,5},{8,10},{9,11},{10,... | collective-permute-start | bytes 98312 | tf_op jit(solution)/shard_map/ppermute | solution.py:394
  44.6 1.5 %collective-permute-start.14 = (f32[32,256]{1,0:T(8,128)S(1)}, f32[32,256]{1,0:T(8,128)S(1)}, u32[]{:S(2)}, u32[]{:S(2)}) collective-permute-start(f32[32,256]{1,0:T(8,128)S(1)} %get-tuple-element.72.o2), channel_id=1, source_target_pairs={{0,8},{8,0},{16,24},{24,16},{1,9},{9,1},{17,25},{25,17},{2,10},{10... | collective-permute-start | bytes 98312 | tf_op jit(solution)/shard_map/ppermute | solution.py:394
  46.0 0.0 collective-permute-start.15
  46.1 2.4 %collective-permute-done.12.a0 = f32[32,256]{1,0:T(8,128)S(1)} collective-permute-done((f32[32,256]{1,0:T(8,128)S(1)}, f32[32,256]{1,0:T(8,128)S(1)}, u32[]{:S(2)}, u32[]{:S(2)}) %collective-permute-start.12) | collective-permute-done | bytes 32800 | tf_op jit(solution)/shard_map/ppermute | solution.py:394
  48.5 0.0 collective-permute-done.13.a1
  48.5 0.0 collective-permute-done.14.a2
  48.5 0.0 collective-permute-done.15.a3
  48.5 0.0 collective-permute-done.16.rest_1_
  48.5 1.2 %local3.1 = (f32[128,128]{1,0:T(8,128)}, f32[32,256]{1,0:T(8,128)S(1)}, f32[32,256]{1,0:T(8,128)S(1)}, f32[160,256]{1,0:T(8,128)S(1)}, f32[32,256]{1,0:T(8,128)S(1)}) custom-call(f32[32,256]{1,0:T(8,128)S(1)} %get-tuple-element.70.o0, f32[32,256]{1,0:T(8,128)S(1)} %get-tuple-element.71.o1, f32[32,256]{1,0:T(8,128)S(1)} %get-tuple-element.72.o2, ...), custom_call_target="tpu_custom_call" | custom-call | flops 40000000 | bytes 2052096 | tf_op jit(solution)/shard_map/local3/pallas_call | solution.py:380
  49.7 1.5 %collective-permute-start.19 = (f32[160,256]{1,0:T(8,128)S(1)}, f32[160,256]{1,0:T(8,128)S(1)}, u32[]{:S(2)}, u32[]{:S(2)}) collective-permute-start(f32[160,256]{1,0:T(8,128)S(1)} %get-tuple-element.79.o2), channel_id=1, source_target_pairs={{0,8},{8,0},{16,24},{24,16},{1,9},{9,1},{17,25},{25,17},{2,10},{10... | collective-permute-start | bytes 491528 | tf_op jit(solution)/shard_map/ppermute | solution.py:394
  51.2 3.5 %all-to-all-start.2 = ((f32[32,4,128]{2,1,0:T(4,128)}), f32[32,4,128]{2,1,0:T(4,128)S(1)}, u32[]{:S(2)}, u32[]{:S(2)}) async-start(f32[32,4,128]{2,1,0:T(4,128)} %bitcast.10), calls=%async_computation.2 | async-start | bytes 131072 | tf_op jit(solution)/shard_map/all_to_all | solution.py:404
  54.7 2.7 %collective-permute-start.17 = (f32[32,256]{1,0:T(8,128)S(1)}, f32[32,256]{1,0:T(8,128)S(1)}, u32[]{:S(2)}, u32[]{:S(2)}) collective-permute-start(f32[32,256]{1,0:T(8,128)S(1)} %get-tuple-element.77.o0), channel_id=1, source_target_pairs={{0,4},{1,5},{2,6},{3,7},{4,0},{5,1},{6,2},{7,3},{8,12},{9,13},{10,... | collective-permute-start | bytes 98312 | tf_op jit(solution)/shard_map/ppermute | solution.py:394
  57.5 1.5 %collective-permute-start.18 = (f32[32,256]{1,0:T(8,128)S(1)}, f32[32,256]{1,0:T(8,128)S(1)}, u32[]{:S(2)}, u32[]{:S(2)}) collective-permute-start(f32[32,256]{1,0:T(8,128)S(1)} %get-tuple-element.78.o1), channel_id=1, source_target_pairs={{0,2},{1,3},{2,0},{3,1},{4,6},{5,7},{6,4},{7,5},{8,10},{9,11},{10,... | collective-permute-start | bytes 98312 | tf_op jit(solution)/shard_map/ppermute | solution.py:394
  59.0 0.0 collective-permute-start.20
  59.0 1.9 %collective-permute-done.17.a0 = f32[32,256]{1,0:T(8,128)S(1)} collective-permute-done((f32[32,256]{1,0:T(8,128)S(1)}, f32[32,256]{1,0:T(8,128)S(1)}, u32[]{:S(2)}, u32[]{:S(2)}) %collective-permute-start.17) | collective-permute-done | bytes 32800 | tf_op jit(solution)/shard_map/ppermute | solution.py:394
  60.9 0.5 collective-permute-done.18.a1
  61.4 0.0 collective-permute-done.20.a3
  61.4 0.9 %all-to-all-done.2 = f32[32,4,128]{2,1,0:T(4,128)S(1)} async-done(((f32[32,4,128]{2,1,0:T(4,128)}), f32[32,4,128]{2,1,0:T(4,128)S(1)}, u32[]{:S(2)}, u32[]{:S(2)}) %all-to-all-start.2) | async-done | bytes 65568 | tf_op jit(solution)/shard_map/all_to_all | solution.py:404
  62.3 0.0 collective-permute-done.19.a2
  62.3 1.2 %finish.1 = (f32[32,768]{1,0:T(8,128)}, f32[32,768]{1,0:T(8,128)}) custom-call(f32[128,128]{1,0:T(8,128)S(1)} %bitcast.21, f32[32,256]{1,0:T(8,128)S(1)} %get-tuple-element.77.o0, f32[32,256]{1,0:T(8,128)S(1)} %get-tuple-element.78.o1, f32[160,256]{1,0:T(8,128)S(1)} %get-tuple-element.79.o2, f32[32,256]{1,0:T(8,128)S(1)} %get-tuple-element.80.o3, ...), custom_call_target="tpu_custom_call" | custom-call | flops 40000000 | bytes 1404928 | tf_op jit(solution)/shard_map/finish/pallas_call | solution.py:380
Async XLA Ops:
  0.6 20.2 %copy-start.1 = (bf16[1,1,768,768]{3,2,1,0:T(8,128)(2,1)S(1)}, bf16[1,1,768,768]{3,2,1,0:T(8,128)(2,1)}, u32[]{:S(2)}) copy-start(bf16[1,1,768,768]{3,2,1,0:T(8,128)(2,1)} %param.8) | copy-start | bytes 3538948
  0.6 0.9 %copy-start.2 = (f32[1,96,96]{2,1,0:T(8,128)S(1)}, f32[1,96,96]{2,1,0:T(8,128)}, u32[]{:S(2)}) copy-start(f32[1,96,96]{2,1,0:T(8,128)} %param.9) | copy-start | bytes 110596
  1.5 0.7 %copy-start.3 = (s32[1,1,4]{2,1,0:T(1,128)S(1)}, s32[1,1,4]{2,1,0:T(1,128)}, u32[]{:S(2)}) copy-start(s32[1,1,4]{2,1,0:T(1,128)} %param.10) | copy-start | bytes 52
  2.2 0.7 %copy-start.4 = (s32[1,1,12]{2,1,0:T(1,128)S(1)}, s32[1,1,12]{2,1,0:T(1,128)}, u32[]{:S(2)}) copy-start(s32[1,1,12]{2,1,0:T(1,128)} %param.11) | copy-start | bytes 148
  5.3 23.6 %copy-start = (bf16[1,1,768,768]{3,2,1,0:T(8,128)(2,1)S(1)}, bf16[1,1,768,768]{3,2,1,0:T(8,128)(2,1)}, u32[]{:S(2)}) copy-start(bf16[1,1,768,768]{3,2,1,0:T(8,128)(2,1)} %param.7) | copy-start | bytes 3538948
  5.3 15.5 %all-to-all-start = ((f32[32,4,128]{2,1,0:T(4,128)}), f32[32,4,128]{2,1,0:T(4,128)S(1)}, u32[]{:S(2)}, u32[]{:S(2)}) async-start(f32[32,4,128]{2,1,0:T(4,128)} %bitcast.5), calls=%async_computation | async-start | bytes 131072 | tf_op jit(solution)/shard_map/all_to_all | solution.py:404
  12.6 8.2 %collective-permute-start.2 = (f32[48,256]{1,0:T(8,128)S(1)}, f32[48,256]{1,0:T(8,128)S(1)}, u32[]{:S(2)}, u32[]{:S(2)}) collective-permute-start(f32[48,256]{1,0:T(8,128)S(1)} %get-tuple-element.47.o2), channel_id=1, source_target_pairs={{0,8},{8,0},{16,24},{24,16},{1,9},{9,1},{17,25},{25,17},{2,10},{10... | collective-permute-start | bytes 147464 | tf_op jit(solution)/shard_map/ppermute | solution.py:394
  14.5 5.2 %collective-permute-start = (f32[40,256]{1,0:T(8,128)S(1)}, f32[40,256]{1,0:T(8,128)S(1)}, u32[]{:S(2)}, u32[]{:S(2)}) collective-permute-start(f32[40,256]{1,0:T(8,128)S(1)} %get-tuple-element.45.o0), channel_id=1, source_target_pairs={{0,4},{1,5},{2,6},{3,7},{4,0},{5,1},{6,2},{7,3},{8,12},{9,13},{10,... | collective-permute-start | bytes 122888 | tf_op jit(solution)/shard_map/ppermute | solution.py:394
  16.8 4.0 %collective-permute-start.1 = (f32[40,256]{1,0:T(8,128)S(1)}, f32[40,256]{1,0:T(8,128)S(1)}, u32[]{:S(2)}, u32[]{:S(2)}) collective-permute-start(f32[40,256]{1,0:T(8,128)S(1)} %get-tuple-element.46.o1), channel_id=1, source_target_pairs={{0,2},{1,3},{2,0},{3,1},{4,6},{5,7},{6,4},{7,5},{8,10},{9,11},{10,... | collective-permute-start | bytes 122888 | tf_op jit(solution)/shard_map/ppermute | solution.py:394
  18.4 2.5 %collective-permute-start.3 = (f32[40,256]{1,0:T(8,128)S(1)}, f32[40,256]{1,0:T(8,128)S(1)}, u32[]{:S(2)}, u32[]{:S(2)}) collective-permute-start(f32[40,256]{1,0:T(8,128)S(1)} %get-tuple-element.48.o3), channel_id=1, source_target_pairs={{0,1},{1,0},{2,3},{3,2},{4,5},{5,4},{6,7},{7,6},{8,9},{9,8},{10,11... | collective-permute-start | bytes 122888 | tf_op jit(solution)/shard_map/ppermute | solution.py:394
  21.7 5.4 %collective-permute-start.4 = (f32[64,256]{1,0:T(8,128)S(1)}, f32[64,256]{1,0:T(8,128)S(1)}, u32[]{:S(2)}, u32[]{:S(2)}) collective-permute-start(f32[64,256]{1,0:T(8,128)S(1)} %get-tuple-element.54.o0), channel_id=1, source_target_pairs={{0,4},{1,5},{2,6},{3,7},{4,0},{5,1},{6,2},{7,3},{8,12},{9,13},{10,... | collective-permute-start | bytes 196616 | tf_op jit(solution)/shard_map/ppermute | solution.py:394
  23.0 4.8 %collective-permute-start.5 = (f32[64,256]{1,0:T(8,128)S(1)}, f32[64,256]{1,0:T(8,128)S(1)}, u32[]{:S(2)}, u32[]{:S(2)}) collective-permute-start(f32[64,256]{1,0:T(8,128)S(1)} %get-tuple-element.55.o1), channel_id=1, source_target_pairs={{0,2},{1,3},{2,0},{3,1},{4,6},{5,7},{6,4},{7,5},{8,10},{9,11},{10,... | collective-permute-start | bytes 196616 | tf_op jit(solution)/shard_map/ppermute | solution.py:394
  24.6 4.3 %collective-permute-start.6 = (f32[64,256]{1,0:T(8,128)S(1)}, f32[64,256]{1,0:T(8,128)S(1)}, u32[]{:S(2)}, u32[]{:S(2)}) collective-permute-start(f32[64,256]{1,0:T(8,128)S(1)} %get-tuple-element.56.o2), channel_id=1, source_target_pairs={{0,8},{8,0},{16,24},{24,16},{1,9},{9,1},{17,25},{25,17},{2,10},{10... | collective-permute-start | bytes 196616 | tf_op jit(solution)/shard_map/ppermute | solution.py:394
  25.2 3.7 %collective-permute-start.7 = (f32[64,256]{1,0:T(8,128)S(1)}, f32[64,256]{1,0:T(8,128)S(1)}, u32[]{:S(2)}, u32[]{:S(2)}) collective-permute-start(f32[64,256]{1,0:T(8,128)S(1)} %get-tuple-element.57.o3), channel_id=1, source_target_pairs={{0,1},{1,0},{2,3},{3,2},{4,5},{5,4},{6,7},{7,6},{8,9},{9,8},{10,11... | collective-permute-start | bytes 196616 | tf_op jit(solution)/shard_map/ppermute | solution.py:394
  29.8 11.1 %all-to-all-start.1 = ((f32[32,4,128]{2,1,0:T(4,128)}), f32[32,4,128]{2,1,0:T(4,128)S(1)}, u32[]{:S(2)}, u32[]{:S(2)}) async-start(f32[32,4,128]{2,1,0:T(4,128)} %bitcast.8), calls=%async_computation.1 | async-start | bytes 131072 | tf_op jit(solution)/shard_map/all_to_all | solution.py:404
  32.7 6.2 %collective-permute-start.8 = (f32[32,256]{1,0:T(8,128)S(1)}, f32[32,256]{1,0:T(8,128)S(1)}, u32[]{:S(2)}, u32[]{:S(2)}) collective-permute-start(f32[32,256]{1,0:T(8,128)S(1)} %get-tuple-element.61.o0), channel_id=1, source_target_pairs={{0,4},{1,5},{2,6},{3,7},{4,0},{5,1},{6,2},{7,3},{8,12},{9,13},{10,... | collective-permute-start | bytes 98312 | tf_op jit(solution)/shard_map/ppermute | solution.py:394
  35.5 3.9 %collective-permute-start.9 = (f32[32,256]{1,0:T(8,128)S(1)}, f32[32,256]{1,0:T(8,128)S(1)}, u32[]{:S(2)}, u32[]{:S(2)}) collective-permute-start(f32[32,256]{1,0:T(8,128)S(1)} %get-tuple-element.62.o1), channel_id=1, source_target_pairs={{0,2},{1,3},{2,0},{3,1},{4,6},{5,7},{6,4},{7,5},{8,10},{9,11},{10,... | collective-permute-start | bytes 98312 | tf_op jit(solution)/shard_map/ppermute | solution.py:394
  37.0 3.9 %collective-permute-start.10 = (f32[32,256]{1,0:T(8,128)S(1)}, f32[32,256]{1,0:T(8,128)S(1)}, u32[]{:S(2)}, u32[]{:S(2)}) collective-permute-start(f32[32,256]{1,0:T(8,128)S(1)} %get-tuple-element.63.o2), channel_id=1, source_target_pairs={{0,8},{8,0},{16,24},{24,16},{1,9},{9,1},{17,25},{25,17},{2,10},{10... | collective-permute-start | bytes 98312 | tf_op jit(solution)/shard_map/ppermute | solution.py:394
  38.5 2.4 %collective-permute-start.11 = (f32[32,256]{1,0:T(8,128)S(1)}, f32[32,256]{1,0:T(8,128)S(1)}, u32[]{:S(2)}, u32[]{:S(2)}) collective-permute-start(f32[32,256]{1,0:T(8,128)S(1)} %get-tuple-element.64.o3), channel_id=1, source_target_pairs={{0,1},{1,0},{2,3},{3,2},{4,5},{5,4},{6,7},{7,6},{8,9},{9,8},{10,11... | collective-permute-start | bytes 98312 | tf_op jit(solution)/shard_map/ppermute | solution.py:394
  41.8 6.7 %collective-permute-start.16 = (f32[64,256]{1,0:T(8,128)S(1)}, f32[64,256]{1,0:T(8,128)S(1)}, u32[]{:S(2)}, u32[]{:S(2)}) collective-permute-start(f32[64,256]{1,0:T(8,128)S(1)} %get-tuple-element.75.rest_0_), channel_id=1, source_target_pairs={{0,16},{8,24},{16,0},{24,8},{1,17},{9,25},{17,1},{25,9},{2,18},{10... | collective-permute-start | bytes 196616 | tf_op jit(solution)/shard_map/ppermute | solution.py:394
  43.4 5.1 %collective-permute-start.12 = (f32[32,256]{1,0:T(8,128)S(1)}, f32[32,256]{1,0:T(8,128)S(1)}, u32[]{:S(2)}, u32[]{:S(2)}) collective-permute-start(f32[32,256]{1,0:T(8,128)S(1)} %get-tuple-element.70.o0), channel_id=1, source_target_pairs={{0,4},{1,5},{2,6},{3,7},{4,0},{5,1},{6,2},{7,3},{8,12},{9,13},{10,... | collective-permute-start | bytes 98312 | tf_op jit(solution)/shard_map/ppermute | solution.py:394
  43.8 4.6 %collective-permute-start.13 = (f32[32,256]{1,0:T(8,128)S(1)}, f32[32,256]{1,0:T(8,128)S(1)}, u32[]{:S(2)}, u32[]{:S(2)}) collective-permute-start(f32[32,256]{1,0:T(8,128)S(1)} %get-tuple-element.71.o1), channel_id=1, source_target_pairs={{0,2},{1,3},{2,0},{3,1},{4,6},{5,7},{6,4},{7,5},{8,10},{9,11},{10,... | collective-permute-start | bytes 98312 | tf_op jit(solution)/shard_map/ppermute | solution.py:394
  44.6 3.9 %collective-permute-start.14 = (f32[32,256]{1,0:T(8,128)S(1)}, f32[32,256]{1,0:T(8,128)S(1)}, u32[]{:S(2)}, u32[]{:S(2)}) collective-permute-start(f32[32,256]{1,0:T(8,128)S(1)} %get-tuple-element.72.o2), channel_id=1, source_target_pairs={{0,8},{8,0},{16,24},{24,16},{1,9},{9,1},{17,25},{25,17},{2,10},{10... | collective-permute-start | bytes 98312 | tf_op jit(solution)/shard_map/ppermute | solution.py:394
  46.0 2.4 %collective-permute-start.15 = (f32[32,256]{1,0:T(8,128)S(1)}, f32[32,256]{1,0:T(8,128)S(1)}, u32[]{:S(2)}, u32[]{:S(2)}) collective-permute-start(f32[32,256]{1,0:T(8,128)S(1)} %get-tuple-element.73.o3), channel_id=1, source_target_pairs={{0,1},{1,0},{2,3},{3,2},{4,5},{5,4},{6,7},{7,6},{8,9},{9,8},{10,11... | collective-permute-start | bytes 98312 | tf_op jit(solution)/shard_map/ppermute | solution.py:394
  49.7 12.6 %collective-permute-start.19 = (f32[160,256]{1,0:T(8,128)S(1)}, f32[160,256]{1,0:T(8,128)S(1)}, u32[]{:S(2)}, u32[]{:S(2)}) collective-permute-start(f32[160,256]{1,0:T(8,128)S(1)} %get-tuple-element.79.o2), channel_id=1, source_target_pairs={{0,8},{8,0},{16,24},{24,16},{1,9},{9,1},{17,25},{25,17},{2,10},{10... | collective-permute-start | bytes 491528 | tf_op jit(solution)/shard_map/ppermute | solution.py:394
  51.2 11.2 %all-to-all-start.2 = ((f32[32,4,128]{2,1,0:T(4,128)}), f32[32,4,128]{2,1,0:T(4,128)S(1)}, u32[]{:S(2)}, u32[]{:S(2)}) async-start(f32[32,4,128]{2,1,0:T(4,128)} %bitcast.10), calls=%async_computation.2 | async-start | bytes 131072 | tf_op jit(solution)/shard_map/all_to_all | solution.py:404
  54.7 6.2 %collective-permute-start.17 = (f32[32,256]{1,0:T(8,128)S(1)}, f32[32,256]{1,0:T(8,128)S(1)}, u32[]{:S(2)}, u32[]{:S(2)}) collective-permute-start(f32[32,256]{1,0:T(8,128)S(1)} %get-tuple-element.77.o0), channel_id=1, source_target_pairs={{0,4},{1,5},{2,6},{3,7},{4,0},{5,1},{6,2},{7,3},{8,12},{9,13},{10,... | collective-permute-start | bytes 98312 | tf_op jit(solution)/shard_map/ppermute | solution.py:394
  57.5 3.9 %collective-permute-start.18 = (f32[32,256]{1,0:T(8,128)S(1)}, f32[32,256]{1,0:T(8,128)S(1)}, u32[]{:S(2)}, u32[]{:S(2)}) collective-permute-start(f32[32,256]{1,0:T(8,128)S(1)} %get-tuple-element.78.o1), channel_id=1, source_target_pairs={{0,2},{1,3},{2,0},{3,1},{4,6},{5,7},{6,4},{7,5},{8,10},{9,11},{10,... | collective-permute-start | bytes 98312 | tf_op jit(solution)/shard_map/ppermute | solution.py:394
  59.0 2.4 %collective-permute-start.20 = (f32[32,256]{1,0:T(8,128)S(1)}, f32[32,256]{1,0:T(8,128)S(1)}, u32[]{:S(2)}, u32[]{:S(2)}) collective-permute-start(f32[32,256]{1,0:T(8,128)S(1)} %get-tuple-element.80.o3), channel_id=1, source_target_pairs={{0,1},{1,0},{2,3},{3,2},{4,5},{5,4},{6,7},{7,6},{8,9},{9,8},{10,11... | collective-permute-start | bytes 98312 | tf_op jit(solution)/shard_map/ppermute | solution.py:394

commit v5 on v4

v5 whole, which is shorter than its diff:
```python
import functools

import jax
import jax.numpy as jnp
from jax import lax
from jax.experimental import pallas as pl
from jax.experimental.pallas import tpu as pltpu
from jax.sharding import PartitionSpec as P

F32, BF16 = jnp.float32, jnp.bfloat16
NT = (((1,), (1,)), ((), ()))
NN = (((1,), (0,)), ((), ()))
LANES = 128
START_LIMIT = 54600


def exact(a, b, dims=NN):
    return lax.dot_general(a, b, dims, precision=lax.Precision.HIGHEST, preferred_element_type=F32)


def rounded(a, b):
    return lax.dot_general(a, b, NN, preferred_element_type=F32)


def thirds(x):
    high = x.astype(BF16)
    rest = x - high.astype(F32)
    mid = rest.astype(BF16)
    return jnp.concatenate([high, mid, (rest - mid.astype(F32)).astype(BF16)], axis=0)


def by_map(x, corner_map, dims):
    n = x.shape[0]
    out = lax.dot_general(thirds(x), corner_map, dims, preferred_element_type=F32)
    return out[:n] + out[n : 2 * n] + out[2 * n :]


def iota(shape, axis):
    return lax.broadcasted_iota(jnp.int32, shape, axis)


FACES = (2, 1, 3, 0)
LAST = FACES.index(3)


def pick_lane(row, lane):
    return jnp.sum(jnp.where(iota(row.shape, 1) == lane, row, 0.0), axis=1, keepdims=True)


def face_vectors(info, dofs):
    width = dofs // 4
    pos = iota((1, dofs), 1)
    sub_pos, grp_pos = lax.axis_index("sub"), lax.axis_index("grp")
    bits = [sub_pos & 1, (sub_pos >> 1) & 1, (sub_pos >> 2) & 1, grp_pos & 1]
    sign = jnp.zeros((1, dofs), F32)
    live = jnp.zeros((1, dofs), jnp.int32)
    node = pos
    for f in range(4):
        inside = (pos >= f * width) & (pos < (f + 1) * width)
        sign = jnp.where(inside, (1 - 2 * bits[f]).astype(F32), sign)
        live = jnp.where(inside, pick_lane(info, f).astype(jnp.int32), live)
    for step in range(1, 12):
        node = jnp.where(pos >= step * (width // 3), pos - step * (width // 3), node)
    mask = jnp.where(node < live, 1.0, 0.0)
    return sign, mask


def corner_ids(info, corners):
    row = iota((16, 1), 0)
    ids = jnp.sum(jnp.where(iota((16, info.shape[1]), 1) == 4 + row % 4 * 4 + row // 4, info, 0.0), axis=1, keepdims=True)
    return jnp.where(row % 4 * 4 < corners, ids, -1.0)


def corner_rows(ids, dofs):
    return jnp.where(ids == iota((16, dofs), 1), 1.0, 0.0)


def size(n_row):
    return n_row + n_row // 2


def put_faces(refs, field):
    n, dofs = field.shape
    width = dofs // 4
    for f, ref in zip(FACES, refs):
        low = f * width
        start = low if low % LANES == 0 else low + LANES // 2
        half = field[:, low + LANES : low + 2 * LANES] if low % LANES == 0 else field[:, start - LANES : start]
        top, bottom = half[: n // 2], half[n // 2 :]
        if low % LANES == 0:
            bottom = pltpu.roll(bottom, LANES // 2, 1)
        else:
            top = pltpu.roll(top, LANES // 2, 1)
        ref[:n, :] = field[:, start : start + LANES]
        ref[n : size(n), :] = jnp.where(iota(top.shape, 1) < LANES // 2, top, bottom)


def from_faces(faces, n):
    by_face = [face for _, face in sorted(zip(FACES, faces), key=lambda item: item[0])]
    tiles = []
    for even, odd in (by_face[:2], by_face[2:]):
        first, second = even[n:], odd[n:]
        left = iota(first.shape, 1) < LANES // 2
        top = jnp.where(left, first, pltpu.roll(second, LANES // 2, 1))
        bottom = jnp.where(left, pltpu.roll(first, LANES // 2, 1), second)
        tiles += [even[:n], jnp.concatenate([top, bottom], axis=0), odd[:n]]
    return jnp.concatenate(tiles, axis=1)


def jump(own, came, n, sign_mask):
    return from_faces([a[: size(n), :] - b[: size(n), :] for a, b in zip(own, came)], n) * sign_mask


def same_block(n_row, n_col, row_block, col_block):
    return iota((n_row, n_col), 0) // row_block == iota((n_row, n_col), 1) // col_block


def to_column(row):
    n = row.shape[1]
    return jnp.sum(jnp.where(same_block(n, n, 1, 1), row, 0.0), axis=1, keepdims=True)


def to_row(column):
    n = column.shape[0]
    return jnp.sum(jnp.where(same_block(n, n, 1, 1), column, 0.0), axis=0, keepdims=True)


def total_of(received):
    total = received[0:8]
    for low in range(8, received.shape[0], 8):
        total = total + received[low : low + 8]
    return total + pltpu.roll(total, 4, 0)


def sums_of(total, n_load):
    column = to_column(total[3:4])
    return [column[i * n_load : (i + 1) * n_load] for i in range(4)]


def halves(x):
    high = x.astype(BF16)
    return jnp.concatenate([high, (x - high.astype(F32)).astype(BF16)], axis=0)


def fine(x, matrix):
    n = x.shape[0]
    both = rounded(halves(x), matrix)
    return both[:n] + both[n:]


def finer(x, matrix):
    n = x.shape[0]
    high = matrix.astype(BF16)
    low = (matrix - high.astype(F32)).astype(BF16)
    parts = halves(x)
    both = lax.dot_general(parts, high, NT, preferred_element_type=F32)
    return both[:n] + both[n:] + lax.dot_general(parts[:n], low, NT, preferred_element_type=F32)


def packed_corners(scaled, corner):
    n_load = scaled.shape[0]
    values = by_map(scaled, corner, NT)
    flipped = jnp.concatenate([values] * 4, axis=0).T
    flipped = jnp.where(same_block(16, 4 * n_load, 4, n_load), flipped, 0.0)
    block = flipped[:8] + flipped[8:]
    return block + pltpu.roll(block, 4, 0)


def with_sums(block, sums):
    zero = jnp.zeros_like(sums[0])
    row = to_row(jnp.concatenate(sums + [zero] * (4 - len(sums)), axis=0))
    return jnp.where(iota(block.shape, 0) % 4 == 3, row, block)


def put_all(out, block):
    for low in range(0, out.shape[0], 8):
        out[low : low + 8, :] = block


def group_corners(received, which, rows, n_load):
    block = received[pl.ds(pl.multiple_of(which * rows, 8), rows), :]
    block = jnp.where(iota(block.shape, 0) % 4 == 3, 0.0, block)
    tall = jnp.concatenate([block] * 4, axis=0)
    flipped = jnp.where(same_block(4 * rows, 4 * n_load, rows, n_load), tall, 0.0).T
    return sum(flipped[r * n_load : (r + 1) * n_load] for r in range(1, 4)) + flipped[:n_load]


def coarse_of(received, spread, n_load):
    rows = spread.shape[1] // 4
    grp_pos = lax.axis_index("grp")
    inner = finer(group_corners(received, grp_pos, rows, n_load), spread)
    outer = finer(group_corners(received, grp_pos ^ 1, rows, n_load), spread)
    return jnp.where(iota(inner.shape, 1) < 64, inner, outer)


def to_tiles(matrix):
    return jnp.concatenate([matrix[:, low : low + LANES] for low in range(0, matrix.shape[1], LANES)], axis=0)


def from_tiles(rows, n):
    n_row = rows.shape[0] * LANES // n
    return jnp.concatenate([rows[low : low + n_row] for low in range(0, rows.shape[0], n_row)], axis=1)


def rows_sum(x):
    return jnp.sum(x, axis=1, keepdims=True)


def start(
    corners, rhs_hbm, stiff_hbm, small,
    sent, vectors, corner_out, resid_out, spread_out, coarse_out, low_out, w0, w1, w2, w3,
    rhs, stiff, block, sems,
):
    pairs = [(rhs_hbm, rhs), (stiff_hbm, stiff), (block, sent)]
    copies = [pltpu.make_async_copy(a, b, sems.at[i]) for i, (a, b) in enumerate(pairs)]
    for copy in copies[:2]:
        copy.start()
    n_load, dofs = rhs.shape
    wins = [w0, w1, w2, w3]
    n = small.shape[0] - 8
    info = small[n : n + 1, :LANES]
    sign, mask = face_vectors(info, dofs)
    vectors[0:1, :] = sign
    vectors[1:2, :] = mask
    vectors[2:3, :] = sign * mask
    vectors[3:8, :] = jnp.zeros((5, dofs), F32)
    ids = corner_ids(info, corners)
    corner = corner_rows(ids.astype(jnp.int32), dofs).astype(BF16)
    corner_out[...] = corner
    ids = jnp.sum(jnp.where(same_block(16, LANES, 1, 1), ids, 0.0), axis=0, keepdims=True)
    for ref in wins:
        ref[size(n_load) : size(n_load) + 8, :] = jnp.broadcast_to(ids, (8, LANES))
    copies[0].wait()
    resid = rhs[...] * mask
    resid_out[...] = resid
    scaled = 0.5 * sign * resid
    put_all(block, packed_corners(scaled, corner))
    copies[2].start()
    wide = small.shape[1]
    subs = n // corners
    sub_pos = lax.axis_index("sub")
    row = iota((64, 1), 0)
    owner = jnp.where(row < 16, sub_pos, jnp.where(row < 32, sub_pos ^ 1, jnp.where(row < 48, sub_pos ^ 2, sub_pos ^ 4)))
    source = owner * corners + row % 4 * 4 + row // 4 % 4
    pick = jnp.where((source == iota((64, n), 1)) & (row % 4 * 4 < corners), 1.0, 0.0)
    place = iota((16 * subs, 1), 0)
    source = place // 4 % subs * corners + place % 4 * 4 + place // (4 * subs)
    order = jnp.where((source == iota((16 * subs, wide), 1)) & (place % 4 * 4 < corners), 1.0, 0.0).astype(BF16)
    pick = jnp.concatenate([pick, order[:, :n].astype(F32)], axis=0).astype(BF16)
    parts = thirds(small[:n, :])
    picked = rounded(pick, parts[:n]) + rounded(pick, parts[n : 2 * n]) + rounded(pick, parts[2 * n :])
    both = by_map(picked, order, NT)
    spread_out[...] = both[:64]
    coarse_out[...] = to_tiles(both[64:])
    wins[LAST][size(n_load) + 8 :, :] = to_tiles(both[:16])
    copies[1].wait()
    local = rounded(halves(scaled), stiff[...])
    put_faces(wins, local[:n_load])
    low_out[...] = local[n_load:]
    copies[2].wait()


def first_image(
    received, o0, o1, o2, o3, a0, a1, a2, a3, vectors, corner, resid, spread, low, inverse, flex,
    z_out, sums_out, map_out, spread_out, *wins,
):
    n_load, dofs = resid.shape
    came = [a0, a1, a2, a3]
    sign, sign_mask = vectors[0:1, :], vectors[2:3, :]
    width = dofs // 4
    pos = iota((1, dofs), 1)
    pieces = [corner[...].astype(F32) * sign_mask]
    for f in range(4):
        ids = to_column(came[FACES.index(f)][size(n_load) : size(n_load) + 1, :])[:16].astype(jnp.int32)
        inside = (pos >= f * width) & (pos < (f + 1) * width)
        pieces.append(corner_rows(ids, dofs) * jnp.where(inside, -sign_mask, 0.0))
    corner_map = jnp.concatenate(pieces, axis=0).astype(BF16)
    map_out[...] = corner_map
    n = spread.shape[1]
    cross = from_tiles(came[LAST][size(n_load) + 8 :, :], n)
    spread_rows = jnp.concatenate([spread[...], cross], axis=0)
    spread_out[...] = spread_rows
    coarse = coarse_of(received, spread_rows, n_load)
    zvec = jump([o0, o1, o2, o3], came, n_load, sign_mask) + by_map(coarse, corner_map, NN)
    z_out[...] = zvec
    signed = sign * zvec
    image = rounded(signed.astype(BF16), flex[...])
    put_faces(wins, jnp.concatenate([image, low[...]], axis=0))
    wins[LAST][size(2 * n_load) :, :] = inverse[...]
    sums_out[...] = with_sums(
        jnp.zeros((8, 4 * n_load), F32), [rows_sum(resid[...] * zvec), 2.0 * rows_sum(signed * image)]
    )


def second_local(
    o0, o1, o2, o3, a0, a1, a2, a3, sums, vectors, corner_map, stiff,
    flexed_out, low_out, inverse_out, sent, w0, w1, w2, w3, block, sem,
):
    n_load, dofs = flexed_out.shape
    sign, sign_mask = vectors[0:1, :], vectors[2:3, :]
    jumped = jump([o0, o1, o2, o3], [a0, a1, a2, a3], 2 * n_load, sign_mask)
    flexed = jumped[:n_load]
    flexed_out[...] = flexed
    for i, ref in enumerate([[o0, o1, o2, o3][LAST], [a0, a1, a2, a3][LAST]]):
        n_row = inverse_out.shape[0] // 2
        inverse_out[i * n_row : (i + 1) * n_row, :] = ref[size(2 * n_load) :, :]
    low_out[...] = jumped[n_load:].astype(BF16)
    scaled = 0.5 * sign * flexed
    is_sum = iota((8, 1), 0) % 4 == 3
    corners = packed_corners(scaled, abs(corner_map[:16, :]))
    put_all(block, jnp.where(is_sum, sums[...], corners))
    copy = pltpu.make_async_copy(block, sent, sem)
    copy.start()
    put_faces([w0, w1, w2, w3], fine(scaled, stiff[...]))
    copy.wait()


def second_image(
    received, o0, o1, o2, o3, a0, a1, a2, a3, flexed, zold, low, resid, vectors, corner_map, spread, flex,
    z_out, step_out, sums_out, total_out, *wins,
):
    n_load, dofs = resid.shape
    sign, sign_mask = vectors[0:1, :], vectors[2:3, :]
    total = total_of(received)
    total_out[...] = total
    rz, curve, _, _ = sums_of(total, n_load)
    alpha = rz / curve
    coarse = coarse_of(received, spread[...], n_load)
    step = jump([o0, o1, o2, o3], [a0, a1, a2, a3], n_load, sign_mask) + by_map(coarse, corner_map[...], NN)
    step = alpha * step
    step_out[...] = step
    zvec = zold[...] + low[...].astype(F32) - step
    z_out[...] = zvec
    signed = sign * zvec
    image = alpha * fine(signed, flex[...])
    put_faces(wins, image)
    scaled_flexed = alpha * flexed[...]
    sums = [
        rows_sum((resid[...] - scaled_flexed) * zvec),
        2.0 * rows_sum(signed * image),
        rows_sum(zvec * scaled_flexed),
    ]
    sums_out[...] = with_sums(jnp.zeros((8, 4 * n_load), F32), sums)


def third_local(o0, o1, o2, o3, a0, a1, a2, a3, sums, vectors, corner_map, stiff, sent, w0, w1, w2, w3, block, sem):
    n_load, dofs = o0.shape[0] * 2 // 3, vectors.shape[1]
    sign, sign_mask = vectors[0:1, :], vectors[2:3, :]
    flexed = jump([o0, o1, o2, o3], [a0, a1, a2, a3], n_load, sign_mask)
    scaled = 0.5 * sign * flexed
    local = fine(scaled, stiff[...])
    fourth = jnp.where(iota((1, 4 * n_load), 1) // n_load == 3, 1.0, 0.0)
    square = with_sums(jnp.zeros((8, 4 * n_load), F32), [4.0 * rows_sum(scaled * local)] * 4) * fourth
    is_sum = iota((8, 1), 0) % 4 == 3
    put_all(block, jnp.where(is_sum, sums[...] + square, packed_corners(scaled, abs(corner_map[:16, :]))))
    copy = pltpu.make_async_copy(block, sent, sem)
    copy.start()
    put_faces([w0, w1, w2, w3], local)
    copy.wait()


def finish(
    received, o0, o1, o2, o3, a0, a1, a2, a3, before, zold, znew, step, vectors, corner_map, spread, *rest
):
    inverses, (mult_hbm, direction_hbm, mult, direction_out, sems) = rest[:-5], rest[-5:]
    n_load, dofs = zold.shape
    sign_mask = vectors[2:3, :]
    rz0, curve0, _, _ = sums_of(before[...], n_load)
    rz1, curve, mixed, square = sums_of(total_of(received), n_load)
    alpha = rz0 / curve0
    beta = rz1 / rz0
    gamma = rz1 / (curve + 2.0 * beta * mixed + beta * beta * rz0)
    direction = znew[...] + beta * zold[...]
    mult[...] = alpha * (zold[...] + gamma * direction)
    copies = [pltpu.make_async_copy(a, b, sems.at[i]) for i, (a, b) in enumerate([(mult, mult_hbm), (direction_out, direction_hbm)])]
    copies[0].start()
    n = spread.shape[1]
    height = n * n // LANES
    index = 0
    for ref in inverses:
        for low in range(0, ref.shape[0], height):
            values = group_corners(received, lax.axis_index("grp") ^ index, n // 4, n_load)
            square = square + 4.0 * rows_sum(values * finer(values, from_tiles(ref[low : low + height, :], n)))
            index += 1
    rz2 = square + 2.0 * beta * (mixed - curve) + beta * beta * (rz0 - mixed)
    rz2 = rz1 - 2.0 * gamma * (curve + beta * mixed) + gamma * gamma * rz2
    coarse = coarse_of(received, spread[...], n_load)
    image = jump([o0, o1, o2, o3], [a0, a1, a2, a3], n_load, sign_mask) + by_map(coarse, corner_map[...], NN)
    direction_out[...] = znew[...] - gamma * (image + beta * step[...]) + (rz2 / rz1) * direction
    copies[1].start()
    copies[0].wait()
    copies[1].wait()


def call(name, kernel, args, outs, scratch=(), in_place=(), out_place=(), limit=None):
    shapes = [jax.ShapeDtypeStruct(s, d) for s, d in outs]
    n_bytes = sum(a.size * a.dtype.itemsize for a in args) + sum(s.size * s.dtype.itemsize for s in shapes)
    return pl.pallas_call(
        kernel,
        out_shape=shapes,
        in_specs=[pl.BlockSpec(memory_space=pl.ANY if i in in_place else pltpu.VMEM) for i in range(len(args))],
        out_specs=[pl.BlockSpec(memory_space=pl.ANY if i in out_place else pltpu.VMEM) for i in range(len(outs))],
        scratch_shapes=scratch,
        cost_estimate=pl.CostEstimate(flops=40_000_000, bytes_accessed=n_bytes, transcendentals=0),
        compiler_params=pltpu.CompilerParams(vmem_limit_bytes=limit or (12 << 20) + 2 * n_bytes),
        name=name,
    )(*args)


def behind(block, other):
    return pl.pallas_call(
        lambda block_ref, other_ref, out_ref: None,
        out_shape=jax.ShapeDtypeStruct(block.shape, block.dtype),
        in_specs=[pl.BlockSpec(memory_space=pl.ANY)] * 2,
        out_specs=pl.BlockSpec(memory_space=pl.ANY),
        input_output_aliases={0: 0},
        compiler_params=pltpu.CompilerParams(vmem_limit_bytes=1 << 20),
        name="behind",
    )(block, other)


def swap(block, axis, distance):
    count = lax.axis_size(axis)
    return lax.ppermute(block, axis, [(i, i ^ distance) for i in range(count) if i ^ distance < count])


def exchange(wins):
    return [swap(win, "grp", 1) if f == 3 else swap(win, "sub", 1 << f) for f, win in zip(FACES, wins)]


def send_all(rows):
    devices = lax.axis_size("grp") * lax.axis_size("sub")
    blocks = rows.reshape(devices, 4, rows.shape[1])
    return lax.all_to_all(blocks, ("grp", "sub"), 0, 0, tiled=True).reshape(rows.shape)


def body(loads, stiffness, flexibility, coarse_inverse, face_nodes, corner_index):
    rhs, stiff, flex, inverse = loads[0, 0], stiffness[0, 0], flexibility[0, 0], coarse_inverse[0]
    nodes, ids = face_nodes[0, 0], corner_index[0, 0]
    n_load, dofs = rhs.shape
    groups, subs = lax.axis_size("grp"), lax.axis_size("sub")
    n = 16 * subs
    field = ((n_load, dofs), F32)
    sent = ((groups * subs * 4, 4 * n_load), F32)
    total = ((8, 4 * n_load), F32)
    n_tile = n * n // LANES

    def faces(rows, more=0, last=0):
        return [((size(rows) + more + last * (i == LAST), LANES), F32) for i in range(4)]

    order = inverse.shape[0]
    wide = -(-order // LANES) * LANES
    few = ids.shape[0]
    small = jnp.pad(inverse, ((0, 8), (0, wide - order)))
    small = small + jnp.pad(nodes[None], ((order, 7), (0, wide - 4))).astype(F32)
    small = small + jnp.pad(ids[None], ((order, 7), (4, wide - 4 - few))).astype(F32)
    block = [pltpu.VMEM(sent[0], F32), pltpu.SemaphoreType.DMA]
    corners, vectors, corner, resid, spread, inverse, low, *own = call(
        "start", functools.partial(start, ids.shape[0]), [rhs, stiff, small],
        [sent, ((8, dofs), F32), ((16, dofs), BF16), field, ((64, n), F32), ((n_tile, LANES), F32), field]
        + faces(n_load, 8, 16 * n // LANES),
        [pltpu.VMEM(rhs.shape, F32), pltpu.VMEM(stiff.shape, BF16), block[0],
         pltpu.SemaphoreType.DMA((3,))],
        [0, 1], [0], START_LIMIT << 10,
    )
    received = send_all(corners)
    came = exchange(own)
    zold, sums, corner_map, spread, *own = call(
        "image1", first_image, [received] + own + came + [vectors, corner, resid, spread, low, inverse, flex],
        [field, total, ((80, dofs), BF16), ((80, n), F32)] + faces(2 * n_load, 0, n_tile),
    )
    came = exchange(own)
    flexed, low, inverse, sent_rows, *own = call(
        "local2", second_local, own + came + [sums, vectors, corner_map, stiff],
        [field, ((n_load, dofs), BF16), ((2 * n_tile, LANES), F32), sent] + faces(n_load),
        block, out_place=[3],
    )
    received = send_all(sent_rows)
    came = exchange(own)
    znew, step, sums, before, *own = call(
        "image2", second_image, [received] + own + came + [flexed, zold, low, resid, vectors, corner_map, spread, flex],
        [field, field, total, total] + faces(n_load),
    )
    came = exchange(own)
    inverses = [inverse]
    distance = 2
    while distance < groups:
        held = inverses[0] if distance == 2 else jnp.concatenate(inverses, axis=0)
        inverses.append(swap(behind(held, came[-1]), "grp", distance))
        distance *= 2
    sent_rows, *own = call(
        "local3", third_local, own + came + [sums, vectors, corner_map, stiff], [sent] + faces(n_load),
        block, out_place=[0],
    )
    received = send_all(sent_rows)
    came = exchange(own)
    mult, direction = call(
        "finish", finish,
        [received] + own + came + [before, zold, znew, step, vectors, corner_map, spread] + inverses, [field, field],
        [pltpu.VMEM(rhs.shape, F32)] * 2 + [pltpu.SemaphoreType.DMA((2,))], out_place=[0, 1],
    )
    return (mult[None, None], direction[None, None])


def solution(mesh):
    in_specs = (
        P("grp", "sub", None, None),
        P("grp", "sub", None, None),
        P("grp", "sub", None, None),
        P("grp", None, None),
        P("grp", "sub", None),
        P("grp", "sub", None),
    )
    out_specs = (P("grp", "sub", None, None), P("grp", "sub", None, None))
    return jax.shard_map(body, mesh=mesh, in_specs=in_specs, out_specs=out_specs, check_vma=False)
```

time: 63.8 us -> 62.1 us (0.973)
  waiting for transfers between devices: 14.4 us -> 10.7 us
  starting transfers between devices: 38.7 us -> 42.3 us
  local copies, waits for them, and re-layouts: 2.21 us -> 0.02 us
  other arithmetic: 0 us -> 1 us
    all_to_all x3, starting transfers between devices: 13.8 us -> 17.5 us  [send_all(): lax.all_to_all(blocks, ('grp', 'sub'), 0, 0, tiled=True).reshape(rows.shape)]
    ppermute x21, waiting for transfers between devices: 13.5 us -> 10.7 us  [swap(): lax.ppermute(block, axis, [(i, i ^ distance) for i in range(count) if i ^...]
    unnamed x10 -> x5, local copies, waits for them, and re-layouts: 2.21 us -> 0.02 us
    add x0 -> x1, other arithmetic: none -> 1 us  [body(): small + jnp.pad(ids[None], ((order, 7), (4, wide - 4 - few))).astype(F32)]
    all_to_all x3, waiting for transfers between devices: 0.95 us -> 0.01 us  [send_all(): lax.all_to_all(blocks, ('grp', 'sub'), 0, 0, tiled=True).reshape(rows.shape)]
  transfers between devices with their start and end apart: 24 -> 24, of which waited for: 12 -> 9; matrix products, arithmetic and copies ran while one was open for 0% -> 0% of each run, Pallas kernels for 0% -> 2%
where the time goes in v5:
time: 62.1 us; the launch traced here: 61.9 us
  starting transfers between devices  42.3 us (68%)
  waiting for transfers between devices  10.7 us (17%)
  Pallas kernels  7.15 us (12%)
  other arithmetic  1 us (2%)
  between operations  0.77 us (1%)
    ppermute x21, starting transfers between devices, swap(): lax.ppermute(block, axis, [(i, i ^ distance) for i in range(count) if i ^...  24.8 us
    all_to_all x3, starting transfers between devices, send_all(): lax.all_to_all(blocks, ('grp', 'sub'), 0, 0, tiled=True).reshape(rows.shape)  17.5 us
    ppermute x21, waiting for transfers between devices, swap(): lax.ppermute(block, axis, [(i, i ^ distance) for i in range(count) if i ^...  10.7 us
    pallas_call x6, Pallas kernels, call(): pl.pallas_call(kernel, out_shape=shapes, in_specs=[pl.BlockSpec(memory_sp...  7.14 us
  transfers between devices with their start and end apart: 24, of which 9 were waited for; matrix products, arithmetic and copies ran while one was open for 0% of the time, Pallas kernels for 2%

profile of v5, /device:TPU:0, one launch (start us, length us, event | category | flops | bytes accessed | tf_op | source)
XLA Modules:
  0.0 61.9 jit_solution(11704063685417027180)
XLA Ops:
  0.6 0.0 copy-start.1
  0.6 1.0 %convert_add_fusion.small = f32[104,128]{1,0:T(8,128)S(1)} fusion(s32[1,12]{1,0:T(1,128)} %bitcast.24, s32[1,4]{1,0:T(1,128)} %bitcast.25, f32[96,96]{1,0:T(8,128)} %bitcast.23), kind=kLoop, calls=%fused_computation | loop fusion | flops 53248 | bytes 90176 | tf_op jit(solution)/shard_map/add | solution.py:456
  1.6 1.9 %start.1 = (f32[128,128]{1,0:T(8,128)}, f32[8,768]{1,0:T(8,128)S(1)}, bf16[16,768]{1,0:T(8,128)(2,1)S(1)}, f32[32,768]{1,0:T(8,128)S(1)}, f32[64,128]{1,0:T(8,12...) custom-call(f32[32,768]{1,0:T(8,128)} %bitcast.22, ...), custom_call_target="tpu_custom_call" | custom-call | flops 40000000 | bytes 1863680 | tf_op jit(solution)/shard_map/start/pallas_call | solution.py:398
  3.5 0.0 copy-start
  3.5 7.3 %all-to-all-start = ((f32[32,4,128]{2,1,0:T(4,128)}), f32[32,4,128]{2,1,0:T(4,128)S(1)}, u32[]{:S(2)}, u32[]{:S(2)}) async-start(f32[32,4,128]{2,1,0:T(4,128)} %bitcast.5), calls=%async_computation | async-start | bytes 131072 | tf_op jit(solution)/shard_map/all_to_all | solution.py:434
  10.8 1.8 %collective-permute-start.2 = (f32[72,128]{1,0:T(8,128)S(1)}, f32[72,128]{1,0:T(8,128)S(1)}, u32[]{:S(2)}, u32[]{:S(2)}) collective-permute-start(f32[72,128]{1,0:T(8,128)S(1)} %get-tuple-element.47.o2), channel_id=1, source_target_pairs={{0,8},{8,0},{16,24},{24,16},{1,9},{9,1},{17,25},{25,17},{2,10},{10... | collective-permute-start | bytes 110600 | tf_op jit(solution)/shard_map/ppermute | solution.py:424
  12.7 2.4 %collective-permute-start = (f32[56,128]{1,0:T(8,128)S(1)}, f32[56,128]{1,0:T(8,128)S(1)}, u32[]{:S(2)}, u32[]{:S(2)}) collective-permute-start(f32[56,128]{1,0:T(8,128)S(1)} %get-tuple-element.45.o0), channel_id=1, source_target_pairs={{0,4},{1,5},{2,6},{3,7},{4,0},{5,1},{6,2},{7,3},{8,12},{9,13},{10,... | collective-permute-start | bytes 86024 | tf_op jit(solution)/shard_map/ppermute | solution.py:424
  15.0 1.5 %collective-permute-start.1 = (f32[56,128]{1,0:T(8,128)S(1)}, f32[56,128]{1,0:T(8,128)S(1)}, u32[]{:S(2)}, u32[]{:S(2)}) collective-permute-start(f32[56,128]{1,0:T(8,128)S(1)} %get-tuple-element.46.o1), channel_id=1, source_target_pairs={{0,2},{1,3},{2,0},{3,1},{4,6},{5,7},{6,4},{7,5},{8,10},{9,11},{10,... | collective-permute-start | bytes 86024 | tf_op jit(solution)/shard_map/ppermute | solution.py:424
  16.6 0.0 collective-permute-start.3
  16.6 1.1 %collective-permute-done.a0 = f32[56,128]{1,0:T(8,128)S(1)} collective-permute-done((f32[56,128]{1,0:T(8,128)S(1)}, f32[56,128]{1,0:T(8,128)S(1)}, u32[]{:S(2)}, u32[]{:S(2)}) %collective-permute-start) | collective-permute-done | bytes 28704 | tf_op jit(solution)/shard_map/ppermute | solution.py:424
  17.7 1.3 %collective-permute-done.1.a1 = f32[56,128]{1,0:T(8,128)S(1)} collective-permute-done((f32[56,128]{1,0:T(8,128)S(1)}, f32[56,128]{1,0:T(8,128)S(1)}, u32[]{:S(2)}, u32[]{:S(2)}) %collective-permute-start.1) | collective-permute-done | bytes 28704 | tf_op jit(solution)/shard_map/ppermute | solution.py:424
  18.9 0.0 collective-permute-done.3.a3
  18.9 0.0 collective-permute-done.2.a2
  18.9 0.0 all-to-all-done
  18.9 0.0 copy-done.1
  18.9 0.9 %image1.1 = (f32[32,768]{1,0:T(8,128)S(1)}, f32[8,128]{1,0:T(8,128)S(1)}, bf16[80,768]{1,0:T(8,128)(2,1)S(1)}, f32[80,128]{1,0:T(8,128)S(1)}, f32[96,128]{1,0:T(...) custom-call(f32[128,128]{1,0:T(8,128)S(1)} %bitcast.20, ...), custom_call_target="tpu_custom_call" | custom-call | flops 40000000 | bytes 2363392 | tf_op jit(solution)/shard_map/image1/pallas_call | solution.py:398
  19.8 0.6 %collective-permute-start.6 = (f32[224,128]{1,0:T(8,128)S(1)}, f32[224,128]{1,0:T(8,128)S(1)}, u32[]{:S(2)}, u32[]{:S(2)}) collective-permute-start(f32[224,128]{1,0:T(8,128)S(1)} %get-tuple-element.57.o2), channel_id=1, source_target_pairs={{0,8},{8,0},{16,24},{24,16},{1,9},{9,1},{17,25},{25,17},{2,10},{10... | collective-permute-start | bytes 344072 | tf_op jit(solution)/shard_map/ppermute | solution.py:424
  20.4 1.1 %collective-permute-start.4 = (f32[96,128]{1,0:T(8,128)S(1)}, f32[96,128]{1,0:T(8,128)S(1)}, u32[]{:S(2)}, u32[]{:S(2)}) collective-permute-start(f32[96,128]{1,0:T(8,128)S(1)} %get-tuple-element.55.o0), channel_id=1, source_target_pairs={{0,4},{1,5},{2,6},{3,7},{4,0},{5,1},{6,2},{7,3},{8,12},{9,13},{10,... | collective-permute-start | bytes 147464 | tf_op jit(solution)/shard_map/ppermute | solution.py:424
  21.5 1.6 %collective-permute-start.5 = (f32[96,128]{1,0:T(8,128)S(1)}, f32[96,128]{1,0:T(8,128)S(1)}, u32[]{:S(2)}, u32[]{:S(2)}) collective-permute-start(f32[96,128]{1,0:T(8,128)S(1)} %get-tuple-element.56.o1), channel_id=1, source_target_pairs={{0,2},{1,3},{2,0},{3,1},{4,6},{5,7},{6,4},{7,5},{8,10},{9,11},{10,... | collective-permute-start | bytes 147464 | tf_op jit(solution)/shard_map/ppermute | solution.py:424
  23.1 0.0 collective-permute-start.7
  23.1 2.3 %collective-permute-done.4.a0 = f32[96,128]{1,0:T(8,128)S(1)} collective-permute-done((f32[96,128]{1,0:T(8,128)S(1)}, f32[96,128]{1,0:T(8,128)S(1)}, u32[]{:S(2)}, u32[]{:S(2)}) %collective-permute-start.4) | collective-permute-done | bytes 49184 | tf_op jit(solution)/shard_map/ppermute | solution.py:424
  25.5 0.5 collective-permute-done.5.a1
  26.0 0.0 collective-permute-done.7.a3
  26.0 0.0 collective-permute-done.6.a2
  26.0 0.0 copy-done
  26.0 1.0 %local2.1 = (f32[32,768]{1,0:T(8,128)S(1)}, bf16[32,768]{1,0:T(8,128)(2,1)S(1)}, f32[256,128]{1,0:T(8,128)S(1)}, f32[128,128]{1,0:T(8,128)}, f32[48,128]{1,0:T(8...) custom-call(f32[96,128]{1,0:T(8,128)S(1)} %get-tuple-element.55.o0, ...), custom_call_target="tpu_custom_call" | custom-call | flops 40000000 | bytes 2297856 | tf_op jit(solution)/shard_map/local2/pallas_call | solution.py:398
  27.0 4.7 %all-to-all-start.1 = ((f32[32,4,128]{2,1,0:T(4,128)}), f32[32,4,128]{2,1,0:T(4,128)S(1)}, u32[]{:S(2)}, u32[]{:S(2)}) async-start(f32[32,4,128]{2,1,0:T(4,128)} %bitcast.8), calls=%async_computation.1 | async-start | bytes 131072 | tf_op jit(solution)/shard_map/all_to_all | solution.py:434
  31.7 2.7 %collective-permute-start.8 = (f32[48,128]{1,0:T(8,128)S(1)}, f32[48,128]{1,0:T(8,128)S(1)}, u32[]{:S(2)}, u32[]{:S(2)}) collective-permute-start(f32[48,128]{1,0:T(8,128)S(1)} %get-tuple-element.62.o0), channel_id=1, source_target_pairs={{0,4},{1,5},{2,6},{3,7},{4,0},{5,1},{6,2},{7,3},{8,12},{9,13},{10,... | collective-permute-start | bytes 73736 | tf_op jit(solution)/shard_map/ppermute | solution.py:424
  34.5 1.5 %collective-permute-start.9 = (f32[48,128]{1,0:T(8,128)S(1)}, f32[48,128]{1,0:T(8,128)S(1)}, u32[]{:S(2)}, u32[]{:S(2)}) collective-permute-start(f32[48,128]{1,0:T(8,128)S(1)} %get-tuple-element.63.o1), channel_id=1, source_target_pairs={{0,2},{1,3},{2,0},{3,1},{4,6},{5,7},{6,4},{7,5},{8,10},{9,11},{10,... | collective-permute-start | bytes 73736 | tf_op jit(solution)/shard_map/ppermute | solution.py:424
  36.0 1.5 %collective-permute-start.10 = (f32[48,128]{1,0:T(8,128)S(1)}, f32[48,128]{1,0:T(8,128)S(1)}, u32[]{:S(2)}, u32[]{:S(2)}) collective-permute-start(f32[48,128]{1,0:T(8,128)S(1)} %get-tuple-element.64.o2), channel_id=1, source_target_pairs={{0,8},{8,0},{16,24},{24,16},{1,9},{9,1},{17,25},{25,17},{2,10},{10... | collective-permute-start | bytes 73736 | tf_op jit(solution)/shard_map/ppermute | solution.py:424
  37.4 0.0 collective-permute-start.11
  37.4 0.0 collective-permute-done.8.a0
  37.4 0.8 %collective-permute-done.9.a1 = f32[48,128]{1,0:T(8,128)S(1)} collective-permute-done((f32[48,128]{1,0:T(8,128)S(1)}, f32[48,128]{1,0:T(8,128)S(1)}, u32[]{:S(2)}, u32[]{:S(2)}) %collective-permute-start.9) | collective-permute-done | bytes 24608 | tf_op jit(solution)/shard_map/ppermute | solution.py:424
  38.3 1.5 %collective-permute-done.10.a2 = f32[48,128]{1,0:T(8,128)S(1)} collective-permute-done((f32[48,128]{1,0:T(8,128)S(1)}, f32[48,128]{1,0:T(8,128)S(1)}, u32[]{:S(2)}, u32[]{:S(2)}) %collective-permute-start.10) | collective-permute-done | bytes 24608 | tf_op jit(solution)/shard_map/ppermute | solution.py:424
  39.8 0.0 collective-permute-done.11.a3
  39.8 0.0 all-to-all-done.1
  39.8 0.9 %image2.1 = (f32[32,768]{1,0:T(8,128)S(1)}, f32[32,768]{1,0:T(8,128)S(1)}, f32[8,128]{1,0:T(8,128)S(1)}, f32[8,128]{1,0:T(8,128)S(1)}, f32[48,128]{1,0:T(8,128)S...) custom-call(f32[128,128]{1,0:T(8,128)S(1)} %bitcast.21, ...), custom_call_target="tpu_custom_call" | custom-call | flops 40000000 | bytes 2277376 | tf_op jit(solution)/shard_map/image2/pallas_call | solution.py:398
  40.7 0.1 collective-permute-start.15
  40.8 0.6 collective-permute-start.12
  41.3 0.6 %collective-permute-start.13 = (f32[48,128]{1,0:T(8,128)S(1)}, f32[48,128]{1,0:T(8,128)S(1)}, u32[]{:S(2)}, u32[]{:S(2)}) collective-permute-start(f32[48,128]{1,0:T(8,128)S(1)} %get-tuple-element.71.o1), channel_id=1, source_target_pairs={{0,2},{1,3},{2,0},{3,1},{4,6},{5,7},{6,4},{7,5},{8,10},{9,11},{10,... | collective-permute-start | bytes 73736 | tf_op jit(solution)/shard_map/ppermute | solution.py:424
  42.0 1.5 %collective-permute-start.14 = (f32[48,128]{1,0:T(8,128)S(1)}, f32[48,128]{1,0:T(8,128)S(1)}, u32[]{:S(2)}, u32[]{:S(2)}) collective-permute-start(f32[48,128]{1,0:T(8,128)S(1)} %get-tuple-element.72.o2), channel_id=1, source_target_pairs={{0,8},{8,0},{16,24},{24,16},{1,9},{9,1},{17,25},{25,17},{2,10},{10... | collective-permute-start | bytes 73736 | tf_op jit(solution)/shard_map/ppermute | solution.py:424
  43.5 0.0 collective-permute-done.15.a3.other_ref
  43.5 1.6 %collective-permute-start.20 = (f32[256,128]{1,0:T(8,128)S(1)}, f32[256,128]{1,0:T(8,128)S(1)}, u32[]{:S(2)}, u32[]{:S(2)}) collective-permute-start(f32[256,128]{1,0:T(8,128)S(1)} %behind.1), channel_id=1, source_target_pairs={{0,16},{8,24},{16,0},{24,8},{1,17},{9,25},{17,1},{25,9},{2,18},{10... | collective-permute-start | bytes 393224 | tf_op jit(solution)/shard_map/ppermute | solution.py:424
  45.0 0.8 %collective-permute-done.12.a0 = f32[48,128]{1,0:T(8,128)S(1)} collective-permute-done((f32[48,128]{1,0:T(8,128)S(1)}, f32[48,128]{1,0:T(8,128)S(1)}, u32[]{:S(2)}, u32[]{:S(2)}) %collective-permute-start.12) | collective-permute-done | bytes 24608 | tf_op jit(solution)/shard_map/ppermute | solution.py:424
  45.8 0.0 collective-permute-done.13.a1
  45.8 0.0 collective-permute-done.14.a2
  45.8 1.2 %local3.1 = (f32[128,128]{1,0:T(8,128)}, f32[48,128]{1,0:T(8,128)S(1)}, f32[48,128]{1,0:T(8,128)S(1)}, f32[48,128]{1,0:T(8,128)S(1)}, f32[48,128]{1,0:T(8,128)S(1)}) custom-call(f32[48,128]{1,0:T(8,128)S(1)} %get-tuple-element.70.o0, f32[48,128]{1,0:T(8,128)S(1)} %get-tuple-element.71.o1, f32[48,128]{1,0:T(8,128)S(1)} %get-tuple-element.72.o2, ...), custom_call_target="tpu_custom_call" | custom-call | flops 40000000 | bytes 1691648 | tf_op jit(solution)/shard_map/local3/pallas_call | solution.py:398
  47.1 5.5 %all-to-all-start.2 = ((f32[32,4,128]{2,1,0:T(4,128)}), f32[32,4,128]{2,1,0:T(4,128)S(1)}, u32[]{:S(2)}, u32[]{:S(2)}) async-start(f32[32,4,128]{2,1,0:T(4,128)} %bitcast.10), calls=%async_computation.2 | async-start | bytes 131072 | tf_op jit(solution)/shard_map/all_to_all | solution.py:434
  52.5 2.7 %collective-permute-start.16 = (f32[48,128]{1,0:T(8,128)S(1)}, f32[48,128]{1,0:T(8,128)S(1)}, u32[]{:S(2)}, u32[]{:S(2)}) collective-permute-start(f32[48,128]{1,0:T(8,128)S(1)} %get-tuple-element.76.o0), channel_id=1, source_target_pairs={{0,4},{1,5},{2,6},{3,7},{4,0},{5,1},{6,2},{7,3},{8,12},{9,13},{10,... | collective-permute-start | bytes 73736 | tf_op jit(solution)/shard_map/ppermute | solution.py:424
  55.3 1.5 %collective-permute-start.17 = (f32[48,128]{1,0:T(8,128)S(1)}, f32[48,128]{1,0:T(8,128)S(1)}, u32[]{:S(2)}, u32[]{:S(2)}) collective-permute-start(f32[48,128]{1,0:T(8,128)S(1)} %get-tuple-element.77.o1), channel_id=1, source_target_pairs={{0,2},{1,3},{2,0},{3,1},{4,6},{5,7},{6,4},{7,5},{8,10},{9,11},{10,... | collective-permute-start | bytes 73736 | tf_op jit(solution)/shard_map/ppermute | solution.py:424
  56.8 1.5 %collective-permute-start.18 = (f32[48,128]{1,0:T(8,128)S(1)}, f32[48,128]{1,0:T(8,128)S(1)}, u32[]{:S(2)}, u32[]{:S(2)}) collective-permute-start(f32[48,128]{1,0:T(8,128)S(1)} %get-tuple-element.78.o2), channel_id=1, source_target_pairs={{0,8},{8,0},{16,24},{24,16},{1,9},{9,1},{17,25},{25,17},{2,10},{10... | collective-permute-start | bytes 73736 | tf_op jit(solution)/shard_map/ppermute | solution.py:424
  58.3 0.0 collective-permute-start.19
  58.3 0.0 collective-permute-done.16.a0
  58.3 0.8 %collective-permute-done.17.a1 = f32[48,128]{1,0:T(8,128)S(1)} collective-permute-done((f32[48,128]{1,0:T(8,128)S(1)}, f32[48,128]{1,0:T(8,128)S(1)}, u32[]{:S(2)}, u32[]{:S(2)}) %collective-permute-start.17) | collective-permute-done | bytes 24608 | tf_op jit(solution)/shard_map/ppermute | solution.py:424
  59.1 1.5 %collective-permute-done.18.a2 = f32[48,128]{1,0:T(8,128)S(1)} collective-permute-done((f32[48,128]{1,0:T(8,128)S(1)}, f32[48,128]{1,0:T(8,128)S(1)}, u32[]{:S(2)}, u32[]{:S(2)}) %collective-permute-start.18) | collective-permute-done | bytes 24608 | tf_op jit(solution)/shard_map/ppermute | solution.py:424
  60.6 0.0 collective-permute-done.19.a3
  60.6 0.0 all-to-all-done.2
  60.6 0.0 collective-permute-done.20.rest_1_
  60.6 1.2 %finish.1 = (f32[32,768]{1,0:T(8,128)}, f32[32,768]{1,0:T(8,128)}) custom-call(f32[128,128]{1,0:T(8,128)S(1)} %bitcast.19, f32[48,128]{1,0:T(8,128)S(1)} %get-tuple-element.76.o0, f32[48,128]{1,0:T(8,128)S(1)} %get-tuple-element.77.o1, f32[48,128]{1,0:T(8,128)S(1)} %get-tuple-element.78.o2, f32[48,128]{1,0:T(8,128)S(1)} %get-tuple-element.79.o3, ...), custom_call_target="tpu_custom_call" | custom-call | flops 40000000 | bytes 1208320 | tf_op jit(solution)/shard_map/finish/pallas_call | solution.py:398
  (2 shorter events, 0.0 us)
Async XLA Ops:
  0.6 18.3 %copy-start.1 = (bf16[1,1,768,768]{3,2,1,0:T(8,128)(2,1)S(1)}, bf16[1,1,768,768]{3,2,1,0:T(8,128)(2,1)}, u32[]{:S(2)}) copy-start(bf16[1,1,768,768]{3,2,1,0:T(8,128)(2,1)} %param.8) | copy-start | bytes 3538948
  3.5 22.4 %copy-start = (bf16[1,1,768,768]{3,2,1,0:T(8,128)(2,1)S(1)}, bf16[1,1,768,768]{3,2,1,0:T(8,128)(2,1)}, u32[]{:S(2)}) copy-start(bf16[1,1,768,768]{3,2,1,0:T(8,128)(2,1)} %param.7) | copy-start | bytes 3538948
  3.5 15.4 %all-to-all-start = ((f32[32,4,128]{2,1,0:T(4,128)}), f32[32,4,128]{2,1,0:T(4,128)S(1)}, u32[]{:S(2)}, u32[]{:S(2)}) async-start(f32[32,4,128]{2,1,0:T(4,128)} %bitcast.5), calls=%async_computation | async-start | bytes 131072 | tf_op jit(solution)/shard_map/all_to_all | solution.py:434
  10.8 8.1 %collective-permute-start.2 = (f32[72,128]{1,0:T(8,128)S(1)}, f32[72,128]{1,0:T(8,128)S(1)}, u32[]{:S(2)}, u32[]{:S(2)}) collective-permute-start(f32[72,128]{1,0:T(8,128)S(1)} %get-tuple-element.47.o2), channel_id=1, source_target_pairs={{0,8},{8,0},{16,24},{24,16},{1,9},{9,1},{17,25},{25,17},{2,10},{10... | collective-permute-start | bytes 110600 | tf_op jit(solution)/shard_map/ppermute | solution.py:424
  12.7 5.0 %collective-permute-start = (f32[56,128]{1,0:T(8,128)S(1)}, f32[56,128]{1,0:T(8,128)S(1)}, u32[]{:S(2)}, u32[]{:S(2)}) collective-permute-start(f32[56,128]{1,0:T(8,128)S(1)} %get-tuple-element.45.o0), channel_id=1, source_target_pairs={{0,4},{1,5},{2,6},{3,7},{4,0},{5,1},{6,2},{7,3},{8,12},{9,13},{10,... | collective-permute-start | bytes 86024 | tf_op jit(solution)/shard_map/ppermute | solution.py:424
  15.0 3.9 %collective-permute-start.1 = (f32[56,128]{1,0:T(8,128)S(1)}, f32[56,128]{1,0:T(8,128)S(1)}, u32[]{:S(2)}, u32[]{:S(2)}) collective-permute-start(f32[56,128]{1,0:T(8,128)S(1)} %get-tuple-element.46.o1), channel_id=1, source_target_pairs={{0,2},{1,3},{2,0},{3,1},{4,6},{5,7},{6,4},{7,5},{8,10},{9,11},{10,... | collective-permute-start | bytes 86024 | tf_op jit(solution)/shard_map/ppermute | solution.py:424
  16.6 2.3 %collective-permute-start.3 = (f32[56,128]{1,0:T(8,128)S(1)}, f32[56,128]{1,0:T(8,128)S(1)}, u32[]{:S(2)}, u32[]{:S(2)}) collective-permute-start(f32[56,128]{1,0:T(8,128)S(1)} %get-tuple-element.48.o3), channel_id=1, source_target_pairs={{0,1},{1,0},{2,3},{3,2},{4,5},{5,4},{6,7},{7,6},{8,9},{9,8},{10,11... | collective-permute-start | bytes 86024 | tf_op jit(solution)/shard_map/ppermute | solution.py:424
  19.8 6.1 %collective-permute-start.6 = (f32[224,128]{1,0:T(8,128)S(1)}, f32[224,128]{1,0:T(8,128)S(1)}, u32[]{:S(2)}, u32[]{:S(2)}) collective-permute-start(f32[224,128]{1,0:T(8,128)S(1)} %get-tuple-element.57.o2), channel_id=1, source_target_pairs={{0,8},{8,0},{16,24},{24,16},{1,9},{9,1},{17,25},{25,17},{2,10},{10... | collective-permute-start | bytes 344072 | tf_op jit(solution)/shard_map/ppermute | solution.py:424
  20.4 5.0 %collective-permute-start.4 = (f32[96,128]{1,0:T(8,128)S(1)}, f32[96,128]{1,0:T(8,128)S(1)}, u32[]{:S(2)}, u32[]{:S(2)}) collective-permute-start(f32[96,128]{1,0:T(8,128)S(1)} %get-tuple-element.55.o0), channel_id=1, source_target_pairs={{0,4},{1,5},{2,6},{3,7},{4,0},{5,1},{6,2},{7,3},{8,12},{9,13},{10,... | collective-permute-start | bytes 147464 | tf_op jit(solution)/shard_map/ppermute | solution.py:424
  21.5 4.4 %collective-permute-start.5 = (f32[96,128]{1,0:T(8,128)S(1)}, f32[96,128]{1,0:T(8,128)S(1)}, u32[]{:S(2)}, u32[]{:S(2)}) collective-permute-start(f32[96,128]{1,0:T(8,128)S(1)} %get-tuple-element.56.o1), channel_id=1, source_target_pairs={{0,2},{1,3},{2,0},{3,1},{4,6},{5,7},{6,4},{7,5},{8,10},{9,11},{10,... | collective-permute-start | bytes 147464 | tf_op jit(solution)/shard_map/ppermute | solution.py:424
  23.1 2.8 %collective-permute-start.7 = (f32[96,128]{1,0:T(8,128)S(1)}, f32[96,128]{1,0:T(8,128)S(1)}, u32[]{:S(2)}, u32[]{:S(2)}) collective-permute-start(f32[96,128]{1,0:T(8,128)S(1)} %get-tuple-element.58.o3), channel_id=1, source_target_pairs={{0,1},{1,0},{2,3},{3,2},{4,5},{5,4},{6,7},{7,6},{8,9},{9,8},{10,11... | collective-permute-start | bytes 147464 | tf_op jit(solution)/shard_map/ppermute | solution.py:424
  27.0 12.8 %all-to-all-start.1 = ((f32[32,4,128]{2,1,0:T(4,128)}), f32[32,4,128]{2,1,0:T(4,128)S(1)}, u32[]{:S(2)}, u32[]{:S(2)}) async-start(f32[32,4,128]{2,1,0:T(4,128)} %bitcast.8), calls=%async_computation.1 | async-start | bytes 131072 | tf_op jit(solution)/shard_map/all_to_all | solution.py:434
  31.7 5.7 %collective-permute-start.8 = (f32[48,128]{1,0:T(8,128)S(1)}, f32[48,128]{1,0:T(8,128)S(1)}, u32[]{:S(2)}, u32[]{:S(2)}) collective-permute-start(f32[48,128]{1,0:T(8,128)S(1)} %get-tuple-element.62.o0), channel_id=1, source_target_pairs={{0,4},{1,5},{2,6},{3,7},{4,0},{5,1},{6,2},{7,3},{8,12},{9,13},{10,... | collective-permute-start | bytes 73736 | tf_op jit(solution)/shard_map/ppermute | solution.py:424
  34.5 3.8 %collective-permute-start.9 = (f32[48,128]{1,0:T(8,128)S(1)}, f32[48,128]{1,0:T(8,128)S(1)}, u32[]{:S(2)}, u32[]{:S(2)}) collective-permute-start(f32[48,128]{1,0:T(8,128)S(1)} %get-tuple-element.63.o1), channel_id=1, source_target_pairs={{0,2},{1,3},{2,0},{3,1},{4,6},{5,7},{6,4},{7,5},{8,10},{9,11},{10,... | collective-permute-start | bytes 73736 | tf_op jit(solution)/shard_map/ppermute | solution.py:424
  36.0 3.8 %collective-permute-start.10 = (f32[48,128]{1,0:T(8,128)S(1)}, f32[48,128]{1,0:T(8,128)S(1)}, u32[]{:S(2)}, u32[]{:S(2)}) collective-permute-start(f32[48,128]{1,0:T(8,128)S(1)} %get-tuple-element.64.o2), channel_id=1, source_target_pairs={{0,8},{8,0},{16,24},{24,16},{1,9},{9,1},{17,25},{25,17},{2,10},{10... | collective-permute-start | bytes 73736 | tf_op jit(solution)/shard_map/ppermute | solution.py:424
  37.4 2.4 %collective-permute-start.11 = (f32[48,128]{1,0:T(8,128)S(1)}, f32[48,128]{1,0:T(8,128)S(1)}, u32[]{:S(2)}, u32[]{:S(2)}) collective-permute-start(f32[48,128]{1,0:T(8,128)S(1)} %get-tuple-element.65.o3), channel_id=1, source_target_pairs={{0,1},{1,0},{2,3},{3,2},{4,5},{5,4},{6,7},{7,6},{8,9},{9,8},{10,11... | collective-permute-start | bytes 73736 | tf_op jit(solution)/shard_map/ppermute | solution.py:424
  40.7 2.8 %collective-permute-start.15 = (f32[48,128]{1,0:T(8,128)S(1)}, f32[48,128]{1,0:T(8,128)S(1)}, u32[]{:S(2)}, u32[]{:S(2)}) collective-permute-start(f32[48,128]{1,0:T(8,128)S(1)} %get-tuple-element.73.o3), channel_id=1, source_target_pairs={{0,1},{1,0},{2,3},{3,2},{4,5},{5,4},{6,7},{7,6},{8,9},{9,8},{10,11... | collective-permute-start | bytes 73736 | tf_op jit(solution)/shard_map/ppermute | solution.py:424
  40.8 5.0 %collective-permute-start.12 = (f32[48,128]{1,0:T(8,128)S(1)}, f32[48,128]{1,0:T(8,128)S(1)}, u32[]{:S(2)}, u32[]{:S(2)}) collective-permute-start(f32[48,128]{1,0:T(8,128)S(1)} %get-tuple-element.70.o0), channel_id=1, source_target_pairs={{0,4},{1,5},{2,6},{3,7},{4,0},{5,1},{6,2},{7,3},{8,12},{9,13},{10,... | collective-permute-start | bytes 73736 | tf_op jit(solution)/shard_map/ppermute | solution.py:424
  41.3 4.4 %collective-permute-start.13 = (f32[48,128]{1,0:T(8,128)S(1)}, f32[48,128]{1,0:T(8,128)S(1)}, u32[]{:S(2)}, u32[]{:S(2)}) collective-permute-start(f32[48,128]{1,0:T(8,128)S(1)} %get-tuple-element.71.o1), channel_id=1, source_target_pairs={{0,2},{1,3},{2,0},{3,1},{4,6},{5,7},{6,4},{7,5},{8,10},{9,11},{10,... | collective-permute-start | bytes 73736 | tf_op jit(solution)/shard_map/ppermute | solution.py:424
  42.0 3.8 %collective-permute-start.14 = (f32[48,128]{1,0:T(8,128)S(1)}, f32[48,128]{1,0:T(8,128)S(1)}, u32[]{:S(2)}, u32[]{:S(2)}) collective-permute-start(f32[48,128]{1,0:T(8,128)S(1)} %get-tuple-element.72.o2), channel_id=1, source_target_pairs={{0,8},{8,0},{16,24},{24,16},{1,9},{9,1},{17,25},{25,17},{2,10},{10... | collective-permute-start | bytes 73736 | tf_op jit(solution)/shard_map/ppermute | solution.py:424
  43.5 17.1 %collective-permute-start.20 = (f32[256,128]{1,0:T(8,128)S(1)}, f32[256,128]{1,0:T(8,128)S(1)}, u32[]{:S(2)}, u32[]{:S(2)}) collective-permute-start(f32[256,128]{1,0:T(8,128)S(1)} %behind.1), channel_id=1, source_target_pairs={{0,16},{8,24},{16,0},{24,8},{1,17},{9,25},{17,1},{25,9},{2,18},{10... | collective-permute-start | bytes 393224 | tf_op jit(solution)/shard_map/ppermute | solution.py:424
  47.1 13.6 %all-to-all-start.2 = ((f32[32,4,128]{2,1,0:T(4,128)}), f32[32,4,128]{2,1,0:T(4,128)S(1)}, u32[]{:S(2)}, u32[]{:S(2)}) async-start(f32[32,4,128]{2,1,0:T(4,128)} %bitcast.10), calls=%async_computation.2 | async-start | bytes 131072 | tf_op jit(solution)/shard_map/all_to_all | solution.py:434
  52.5 5.7 %collective-permute-start.16 = (f32[48,128]{1,0:T(8,128)S(1)}, f32[48,128]{1,0:T(8,128)S(1)}, u32[]{:S(2)}, u32[]{:S(2)}) collective-permute-start(f32[48,128]{1,0:T(8,128)S(1)} %get-tuple-element.76.o0), channel_id=1, source_target_pairs={{0,4},{1,5},{2,6},{3,7},{4,0},{5,1},{6,2},{7,3},{8,12},{9,13},{10,... | collective-permute-start | bytes 73736 | tf_op jit(solution)/shard_map/ppermute | solution.py:424
  55.3 3.8 %collective-permute-start.17 = (f32[48,128]{1,0:T(8,128)S(1)}, f32[48,128]{1,0:T(8,128)S(1)}, u32[]{:S(2)}, u32[]{:S(2)}) collective-permute-start(f32[48,128]{1,0:T(8,128)S(1)} %get-tuple-element.77.o1), channel_id=1, source_target_pairs={{0,2},{1,3},{2,0},{3,1},{4,6},{5,7},{6,4},{7,5},{8,10},{9,11},{10,... | collective-permute-start | bytes 73736 | tf_op jit(solution)/shard_map/ppermute | solution.py:424
  56.8 3.8 %collective-permute-start.18 = (f32[48,128]{1,0:T(8,128)S(1)}, f32[48,128]{1,0:T(8,128)S(1)}, u32[]{:S(2)}, u32[]{:S(2)}) collective-permute-start(f32[48,128]{1,0:T(8,128)S(1)} %get-tuple-element.78.o2), channel_id=1, source_target_pairs={{0,8},{8,0},{16,24},{24,16},{1,9},{9,1},{17,25},{25,17},{2,10},{10... | collective-permute-start | bytes 73736 | tf_op jit(solution)/shard_map/ppermute | solution.py:424
  58.3 2.4 %collective-permute-start.19 = (f32[48,128]{1,0:T(8,128)S(1)}, f32[48,128]{1,0:T(8,128)S(1)}, u32[]{:S(2)}, u32[]{:S(2)}) collective-permute-start(f32[48,128]{1,0:T(8,128)S(1)} %get-tuple-element.79.o3), channel_id=1, source_target_pairs={{0,1},{1,0},{2,3},{3,2},{4,5},{5,4},{6,7},{7,6},{8,9},{9,8},{10,11... | collective-permute-start | bytes 73736 | tf_op jit(solution)/shard_map/ppermute | solution.py:424

commit v6 on v5

--- a/solution.py
+++ b/solution.py
@@ -11,6 +11,7 @@
 NT = (((1,), (1,)), ((), ()))
 NN = (((1,), (0,)), ((), ()))
 LANES = 128
+EXTRA = 72
 START_LIMIT = 54600
 
 
@@ -185,12 +186,17 @@
     return sum(flipped[r * n_load : (r + 1) * n_load] for r in range(1, 4)) + flipped[:n_load]
 
 
-def coarse_of(received, spread, n_load):
-    rows = spread.shape[1] // 4
+def coarse_of(inner, outer, spread):
+    n = inner.shape[0]
+    both = finer(jnp.concatenate([inner, outer], axis=0), spread)
+    return jnp.where(iota((n, both.shape[1]), 1) < 64, both[:n], both[n:])
+
+
+def two_groups(received, rows, n_load):
     grp_pos = lax.axis_index("grp")
-    inner = finer(group_corners(received, grp_pos, rows, n_load), spread)
-    outer = finer(group_corners(received, grp_pos ^ 1, rows, n_load), spread)
-    return jnp.where(iota(inner.shape, 1) < 64, inner, outer)
+    if received.shape[0] == 2 * rows:
+        grp_pos = grp_pos & 1
+    return [group_corners(received, which, rows, n_load) for which in (grp_pos, grp_pos ^ 1)]
 
 
 def to_tiles(matrix):
@@ -253,6 +259,7 @@
     spread_out[...] = both[:64]
     coarse_out[...] = to_tiles(both[64:])
     wins[LAST][size(n_load) + 8 :, :] = to_tiles(both[:16])
+    wins[0][size(n_load) + 8 :, :] = jnp.zeros((EXTRA, LANES), F32)
     copies[1].wait()
     local = rounded(halves(scaled), stiff[...])
     put_faces(wins, local[:n_load])
@@ -280,7 +287,7 @@
     cross = from_tiles(came[LAST][size(n_load) + 8 :, :], n)
     spread_rows = jnp.concatenate([spread[...], cross], axis=0)
     spread_out[...] = spread_rows
-    coarse = coarse_of(received, spread_rows, n_load)
+    coarse = coarse_of(*two_groups(received, n // 4, n_load), spread_rows)
     zvec = jump([o0, o1, o2, o3], came, n_load, sign_mask) + by_map(coarse, corner_map, NN)
     z_out[...] = zvec
     signed = sign * zvec
@@ -325,7 +332,7 @@
     total_out[...] = total
     rz, curve, _, _ = sums_of(total, n_load)
     alpha = rz / curve
-    coarse = coarse_of(received, spread[...], n_load)
+    coarse = coarse_of(*two_groups(received, spread.shape[1] // 4, n_load), spread[...])
     step = jump([o0, o1, o2, o3], [a0, a1, a2, a3], n_load, sign_mask) + by_map(coarse, corner_map[...], NN)
     step = alpha * step
     step_out[...] = step
@@ -376,15 +383,18 @@
     copies[0].start()
     n = spread.shape[1]
     height = n * n // LANES
+    corners = two_groups(received, n // 4, n_load)
     index = 0
     for ref in inverses:
         for low in range(0, ref.shape[0], height):
-            values = group_corners(received, lax.axis_index("grp") ^ index, n // 4, n_load)
+            if index == len(corners):
+                corners.append(group_corners(received, lax.axis_index("grp") ^ index, n // 4, n_load))
+            values = corners[index]
             square = square + 4.0 * rows_sum(values * finer(values, from_tiles(ref[low : low + height, :], n)))
             index += 1
     rz2 = square + 2.0 * beta * (mixed - curve) + beta * beta * (rz0 - mixed)
     rz2 = rz1 - 2.0 * gamma * (curve + beta * mixed) + gamma * gamma * rz2
-    coarse = coarse_of(received, spread[...], n_load)
+    coarse = coarse_of(*corners[:2], spread[...])
     image = jump([o0, o1, o2, o3], [a0, a1, a2, a3], n_load, sign_mask) + by_map(coarse, corner_map[...], NN)
     direction_out[...] = znew[...] - gamma * (image + beta * step[...]) + (rz2 / rz1) * direction
     copies[1].start()
@@ -428,6 +438,14 @@
     return [swap(win, "grp", 1) if f == 3 else swap(win, "sub", 1 << f) for f, win in zip(FACES, wins)]
 
 
+def send_pair(rows):
+    subs = lax.axis_size("sub")
+    devices = 2 * subs
+    blocks = rows.reshape(devices, 4, rows.shape[1])
+    teams = [list(range(low, low + devices)) for low in range(0, lax.axis_size("grp") * subs, devices)]
+    return lax.all_to_all(blocks, ("grp", "sub"), 0, 0, tiled=True, axis_index_groups=teams).reshape(rows.shape)
+
+
 def send_all(rows):
     devices = lax.axis_size("grp") * lax.axis_size("sub")
     blocks = rows.reshape(devices, 4, rows.shape[1])
@@ -445,8 +463,8 @@
     total = ((8, 4 * n_load), F32)
     n_tile = n * n // LANES
 
-    def faces(rows, more=0, last=0):
-        return [((size(rows) + more + last * (i == LAST), LANES), F32) for i in range(4)]
+    def faces(rows, more=0, last=0, first=0):
+        return [((size(rows) + more + last * (i == LAST) + first * (i == 0), LANES), F32) for i in range(4)]
 
     order = inverse.shape[0]
     wide = -(-order // LANES) * LANES
@@ -457,13 +475,13 @@
     block = [pltpu.VMEM(sent[0], F32), pltpu.SemaphoreType.DMA]
     corners, vectors, corner, resid, spread, inverse, low, *own = call(
         "start", functools.partial(start, ids.shape[0]), [rhs, stiff, small],
-        [sent, ((8, dofs), F32), ((16, dofs), BF16), field, ((64, n), F32), ((n_tile, LANES), F32), field]
-        + faces(n_load, 8, 16 * n // LANES),
-        [pltpu.VMEM(rhs.shape, F32), pltpu.VMEM(stiff.shape, BF16), block[0],
+        [((2 * subs * 4, 4 * n_load), F32), ((8, dofs), F32), ((16, dofs), BF16), field, ((64, n), F32), ((n_tile, LANES), F32), field]
+        + faces(n_load, 8, 16 * n // LANES, EXTRA),
+        [pltpu.VMEM(rhs.shape, F32), pltpu.VMEM(stiff.shape, BF16), pltpu.VMEM((2 * subs * 4, 4 * n_load), F32),
          pltpu.SemaphoreType.DMA((3,))],
         [0, 1], [0], START_LIMIT << 10,
     )
-    received = send_all(corners)
+    received = send_pair(corners)
     came = exchange(own)
     zold, sums, corner_map, spread, *own = call(
         "image1", first_image, [received] + own + came + [vectors, corner, resid, spread, low, inverse, flex],

time: 62.1 us -> 61.3 us (0.987)
  starting transfers between devices: 42.3 us -> 40.6 us
  waiting for transfers between devices: 10.7 us -> 11.6 us
    all_to_all x3 -> x2, starting transfers between devices: 17.5 us -> 9.89 us  [send_all(): lax.all_to_all(blocks, ('grp', 'sub'), 0, 0, tiled=True).reshape(rows.shape)]
    all_to_all x0 -> x1, starting transfers between devices: none -> 3.88 us  [send_pair(): lax.all_to_all(blocks, ('grp', 'sub'), 0, 0, tiled=True, axis_index_group...]
    ppermute x21, starting transfers between devices: 24.8 us -> 26.8 us  [swap(): lax.ppermute(block, axis, [(i, i ^ distance) for i in range(count) if i ^...]
    all_to_all x0 -> x1, waiting for transfers between devices: none -> 0.86 us  [send_pair(): lax.all_to_all(blocks, ('grp', 'sub'), 0, 0, tiled=True, axis_index_group...]
where the time goes in v6:
time: 61.3 us; the launch traced here: 61 us
  starting transfers between devices  40.6 us (66%)
  waiting for transfers between devices  11.6 us (19%)
  Pallas kernels  7.08 us (12%)
  other arithmetic  1 us (2%)
  between operations  0.76 us (1%)
    ppermute x21, starting transfers between devices, swap(): lax.ppermute(block, axis, [(i, i ^ distance) for i in range(count) if i ^...  26.8 us
    ppermute x21, waiting for transfers between devices, swap(): lax.ppermute(block, axis, [(i, i ^ distance) for i in range(count) if i ^...  10.7 us
    all_to_all x2, starting transfers between devices, send_all(): lax.all_to_all(blocks, ('grp', 'sub'), 0, 0, tiled=True).reshape(rows.shape)  9.89 us
    pallas_call x6, Pallas kernels, call(): pl.pallas_call(kernel, out_shape=shapes, in_specs=[pl.BlockSpec(memory_sp...  7.07 us
    all_to_all x1, starting transfers between devices, send_pair(): lax.all_to_all(blocks, ('grp', 'sub'), 0, 0, tiled=True, axis_index_group...  3.88 us
  transfers between devices with their start and end apart: 24, of which 9 were waited for; matrix products, arithmetic and copies ran while one was open for 0% of the time, Pallas kernels for 2%

profile of v6, /device:TPU:0, one launch (start us, length us, event | category | flops | bytes accessed | tf_op | source)
XLA Modules:
  0.0 61.0 jit_solution(2138929296478501617)
XLA Ops:
  0.6 0.0 copy-start.1
  0.6 1.0 %convert_add_fusion.small = f32[104,128]{1,0:T(8,128)S(1)} fusion(s32[1,12]{1,0:T(1,128)} %bitcast.24, s32[1,4]{1,0:T(1,128)} %bitcast.25, f32[96,96]{1,0:T(8,128)} %bitcast.23), kind=kLoop, calls=%fused_computation | loop fusion | flops 53248 | bytes 90176 | tf_op jit(solution)/shard_map/add | solution.py:474
  1.6 1.8 %start.1 = (f32[64,128]{1,0:T(8,128)}, f32[8,768]{1,0:T(8,128)S(1)}, bf16[16,768]{1,0:T(8,128)(2,1)S(1)}, f32[32,768]{1,0:T(8,128)S(1)}, f32[64,128]{1,0:T(8,128...) custom-call(f32[32,768]{1,0:T(8,128)} %bitcast.22, ...), custom_call_target="tpu_custom_call" | custom-call | flops 40000000 | bytes 1867776 | tf_op jit(solution)/shard_map/start/pallas_call | solution.py:408
  3.5 0.0 copy-start
  3.5 4.1 %collective-permute-start = (f32[128,128]{1,0:T(8,128)S(1)}, f32[128,128]{1,0:T(8,128)S(1)}, u32[]{:S(2)}, u32[]{:S(2)}) collective-permute-start(f32[128,128]{1,0:T(8,128)S(1)} %get-tuple-element.45.o0), channel_id=1, source_target_pairs={{0,4},{1,5},{2,6},{3,7},{4,0},{5,1},{6,2},{7,3},{8,12},{9,13},{10,... | collective-permute-start | bytes 196616 | tf_op jit(solution)/shard_map/ppermute | solution.py:434
  7.6 3.9 %all-to-all-start = ((f32[16,4,128]{2,1,0:T(4,128)}), f32[16,4,128]{2,1,0:T(4,128)S(1)}, u32[]{:S(2)}, u32[]{:S(2)}) async-start(f32[16,4,128]{2,1,0:T(4,128)} %bitcast.5), calls=%async_computation | async-start | bytes 65536 | tf_op jit(solution)/shard_map/all_to_all | solution.py:446
  11.5 1.9 %collective-permute-start.2 = (f32[72,128]{1,0:T(8,128)S(1)}, f32[72,128]{1,0:T(8,128)S(1)}, u32[]{:S(2)}, u32[]{:S(2)}) collective-permute-start(f32[72,128]{1,0:T(8,128)S(1)} %get-tuple-element.47.o2), channel_id=1, source_target_pairs={{0,8},{8,0},{16,24},{24,16},{1,9},{9,1},{17,25},{25,17},{2,10},{10... | collective-permute-start | bytes 110600 | tf_op jit(solution)/shard_map/ppermute | solution.py:434
  13.4 1.5 %collective-permute-start.1 = (f32[56,128]{1,0:T(8,128)S(1)}, f32[56,128]{1,0:T(8,128)S(1)}, u32[]{:S(2)}, u32[]{:S(2)}) collective-permute-start(f32[56,128]{1,0:T(8,128)S(1)} %get-tuple-element.46.o1), channel_id=1, source_target_pairs={{0,2},{1,3},{2,0},{3,1},{4,6},{5,7},{6,4},{7,5},{8,10},{9,11},{10,... | collective-permute-start | bytes 86024 | tf_op jit(solution)/shard_map/ppermute | solution.py:434
  14.9 0.0 collective-permute-start.3
  14.9 2.5 %collective-permute-done.1.a1 = f32[56,128]{1,0:T(8,128)S(1)} collective-permute-done((f32[56,128]{1,0:T(8,128)S(1)}, f32[56,128]{1,0:T(8,128)S(1)}, u32[]{:S(2)}, u32[]{:S(2)}) %collective-permute-start.1) | collective-permute-done | bytes 28704 | tf_op jit(solution)/shard_map/ppermute | solution.py:434
  17.4 0.0 collective-permute-done.3.a3
  17.4 0.0 collective-permute-done.2.a2
  17.4 0.9 %all-to-all-done = f32[16,4,128]{2,1,0:T(4,128)S(1)} async-done(((f32[16,4,128]{2,1,0:T(4,128)}), f32[16,4,128]{2,1,0:T(4,128)S(1)}, u32[]{:S(2)}, u32[]{:S(2)}) %all-to-all-start) | async-done | bytes 32800 | tf_op jit(solution)/shard_map/all_to_all | solution.py:446
  18.3 0.0 collective-permute-done.a0
  18.3 0.0 copy-done.1
  18.3 0.8 %image1.1 = (f32[32,768]{1,0:T(8,128)S(1)}, f32[8,128]{1,0:T(8,128)S(1)}, bf16[80,768]{1,0:T(8,128)(2,1)S(1)}, f32[80,128]{1,0:T(8,128)S(1)}, f32[96,128]{1,0:T(...) custom-call(f32[64,128]{1,0:T(8,128)S(1)} %bitcast.21, ...), custom_call_target="tpu_custom_call" | custom-call | flops 40000000 | bytes 2404352 | tf_op jit(solution)/shard_map/image1/pallas_call | solution.py:408
  19.1 0.5 collective-permute-start.6
  19.6 1.6 %collective-permute-start.4 = (f32[96,128]{1,0:T(8,128)S(1)}, f32[96,128]{1,0:T(8,128)S(1)}, u32[]{:S(2)}, u32[]{:S(2)}) collective-permute-start(f32[96,128]{1,0:T(8,128)S(1)} %get-tuple-element.55.o0), channel_id=1, source_target_pairs={{0,4},{1,5},{2,6},{3,7},{4,0},{5,1},{6,2},{7,3},{8,12},{9,13},{10,... | collective-permute-start | bytes 147464 | tf_op jit(solution)/shard_map/ppermute | solution.py:434
  21.2 1.5 %collective-permute-start.5 = (f32[96,128]{1,0:T(8,128)S(1)}, f32[96,128]{1,0:T(8,128)S(1)}, u32[]{:S(2)}, u32[]{:S(2)}) collective-permute-start(f32[96,128]{1,0:T(8,128)S(1)} %get-tuple-element.56.o1), channel_id=1, source_target_pairs={{0,2},{1,3},{2,0},{3,1},{4,6},{5,7},{6,4},{7,5},{8,10},{9,11},{10,... | collective-permute-start | bytes 147464 | tf_op jit(solution)/shard_map/ppermute | solution.py:434
  22.6 0.0 collective-permute-start.7
  22.6 2.4 %collective-permute-done.4.a0 = f32[96,128]{1,0:T(8,128)S(1)} collective-permute-done((f32[96,128]{1,0:T(8,128)S(1)}, f32[96,128]{1,0:T(8,128)S(1)}, u32[]{:S(2)}, u32[]{:S(2)}) %collective-permute-start.4) | collective-permute-done | bytes 49184 | tf_op jit(solution)/shard_map/ppermute | solution.py:434
  25.0 0.4 collective-permute-done.5.a1
  25.4 0.0 collective-permute-done.7.a3
  25.4 0.0 collective-permute-done.6.a2
  25.4 0.0 copy-done
  25.4 1.0 %local2.1 = (f32[32,768]{1,0:T(8,128)S(1)}, bf16[32,768]{1,0:T(8,128)(2,1)S(1)}, f32[256,128]{1,0:T(8,128)S(1)}, f32[128,128]{1,0:T(8,128)}, f32[48,128]{1,0:T(8...) custom-call(f32[96,128]{1,0:T(8,128)S(1)} %get-tuple-element.55.o0, ...), custom_call_target="tpu_custom_call" | custom-call | flops 40000000 | bytes 2297856 | tf_op jit(solution)/shard_map/local2/pallas_call | solution.py:408
  26.5 4.4 %all-to-all-start.1 = ((f32[32,4,128]{2,1,0:T(4,128)}), f32[32,4,128]{2,1,0:T(4,128)S(1)}, u32[]{:S(2)}, u32[]{:S(2)}) async-start(f32[32,4,128]{2,1,0:T(4,128)} %bitcast.8), calls=%async_computation.1 | async-start | bytes 131072 | tf_op jit(solution)/shard_map/all_to_all | solution.py:452
  30.9 2.7 %collective-permute-start.8 = (f32[48,128]{1,0:T(8,128)S(1)}, f32[48,128]{1,0:T(8,128)S(1)}, u32[]{:S(2)}, u32[]{:S(2)}) collective-permute-start(f32[48,128]{1,0:T(8,128)S(1)} %get-tuple-element.62.o0), channel_id=1, source_target_pairs={{0,4},{1,5},{2,6},{3,7},{4,0},{5,1},{6,2},{7,3},{8,12},{9,13},{10,... | collective-permute-start | bytes 73736 | tf_op jit(solution)/shard_map/ppermute | solution.py:434
  33.6 1.5 %collective-permute-start.9 = (f32[48,128]{1,0:T(8,128)S(1)}, f32[48,128]{1,0:T(8,128)S(1)}, u32[]{:S(2)}, u32[]{:S(2)}) collective-permute-start(f32[48,128]{1,0:T(8,128)S(1)} %get-tuple-element.63.o1), channel_id=1, source_target_pairs={{0,2},{1,3},{2,0},{3,1},{4,6},{5,7},{6,4},{7,5},{8,10},{9,11},{10,... | collective-permute-start | bytes 73736 | tf_op jit(solution)/shard_map/ppermute | solution.py:434
  35.2 1.5 %collective-permute-start.10 = (f32[48,128]{1,0:T(8,128)S(1)}, f32[48,128]{1,0:T(8,128)S(1)}, u32[]{:S(2)}, u32[]{:S(2)}) collective-permute-start(f32[48,128]{1,0:T(8,128)S(1)} %get-tuple-element.64.o2), channel_id=1, source_target_pairs={{0,8},{8,0},{16,24},{24,16},{1,9},{9,1},{17,25},{25,17},{2,10},{10... | collective-permute-start | bytes 73736 | tf_op jit(solution)/shard_map/ppermute | solution.py:434
  36.6 0.0 collective-permute-start.11
  36.6 0.0 collective-permute-done.8.a0
  36.6 0.8 %collective-permute-done.9.a1 = f32[48,128]{1,0:T(8,128)S(1)} collective-permute-done((f32[48,128]{1,0:T(8,128)S(1)}, f32[48,128]{1,0:T(8,128)S(1)}, u32[]{:S(2)}, u32[]{:S(2)}) %collective-permute-start.9) | collective-permute-done | bytes 24608 | tf_op jit(solution)/shard_map/ppermute | solution.py:434
  37.5 1.5 %collective-permute-done.10.a2 = f32[48,128]{1,0:T(8,128)S(1)} collective-permute-done((f32[48,128]{1,0:T(8,128)S(1)}, f32[48,128]{1,0:T(8,128)S(1)}, u32[]{:S(2)}, u32[]{:S(2)}) %collective-permute-start.10) | collective-permute-done | bytes 24608 | tf_op jit(solution)/shard_map/ppermute | solution.py:434
  39.0 0.0 collective-permute-done.11.a3
  39.0 0.0 all-to-all-done.1
  39.0 0.9 %image2.1 = (f32[32,768]{1,0:T(8,128)S(1)}, f32[32,768]{1,0:T(8,128)S(1)}, f32[8,128]{1,0:T(8,128)S(1)}, f32[8,128]{1,0:T(8,128)S(1)}, f32[48,128]{1,0:T(8,128)S...) custom-call(f32[128,128]{1,0:T(8,128)S(1)} %bitcast.20, ...), custom_call_target="tpu_custom_call" | custom-call | flops 40000000 | bytes 2277376 | tf_op jit(solution)/shard_map/image2/pallas_call | solution.py:408
  39.9 0.1 collective-permute-start.15
  39.9 0.6 collective-permute-start.12
  40.5 0.6 %collective-permute-start.13 = (f32[48,128]{1,0:T(8,128)S(1)}, f32[48,128]{1,0:T(8,128)S(1)}, u32[]{:S(2)}, u32[]{:S(2)}) collective-permute-start(f32[48,128]{1,0:T(8,128)S(1)} %get-tuple-element.71.o1), channel_id=1, source_target_pairs={{0,2},{1,3},{2,0},{3,1},{4,6},{5,7},{6,4},{7,5},{8,10},{9,11},{10,... | collective-permute-start | bytes 73736 | tf_op jit(solution)/shard_map/ppermute | solution.py:434
  41.1 1.5 %collective-permute-start.14 = (f32[48,128]{1,0:T(8,128)S(1)}, f32[48,128]{1,0:T(8,128)S(1)}, u32[]{:S(2)}, u32[]{:S(2)}) collective-permute-start(f32[48,128]{1,0:T(8,128)S(1)} %get-tuple-element.72.o2), channel_id=1, source_target_pairs={{0,8},{8,0},{16,24},{24,16},{1,9},{9,1},{17,25},{25,17},{2,10},{10... | collective-permute-start | bytes 73736 | tf_op jit(solution)/shard_map/ppermute | solution.py:434
  42.6 0.0 collective-permute-done.15.a3.other_ref
  42.6 1.6 %collective-permute-start.20 = (f32[256,128]{1,0:T(8,128)S(1)}, f32[256,128]{1,0:T(8,128)S(1)}, u32[]{:S(2)}, u32[]{:S(2)}) collective-permute-start(f32[256,128]{1,0:T(8,128)S(1)} %behind.1), channel_id=1, source_target_pairs={{0,16},{8,24},{16,0},{24,8},{1,17},{9,25},{17,1},{25,9},{2,18},{10... | collective-permute-start | bytes 393224 | tf_op jit(solution)/shard_map/ppermute | solution.py:434
  44.2 0.8 %collective-permute-done.12.a0 = f32[48,128]{1,0:T(8,128)S(1)} collective-permute-done((f32[48,128]{1,0:T(8,128)S(1)}, f32[48,128]{1,0:T(8,128)S(1)}, u32[]{:S(2)}, u32[]{:S(2)}) %collective-permute-start.12) | collective-permute-done | bytes 24608 | tf_op jit(solution)/shard_map/ppermute | solution.py:434
  45.0 0.0 collective-permute-done.13.a1
  45.0 0.0 collective-permute-done.14.a2
  45.0 1.2 %local3.1 = (f32[128,128]{1,0:T(8,128)}, f32[48,128]{1,0:T(8,128)S(1)}, f32[48,128]{1,0:T(8,128)S(1)}, f32[48,128]{1,0:T(8,128)S(1)}, f32[48,128]{1,0:T(8,128)S(1)}) custom-call(f32[48,128]{1,0:T(8,128)S(1)} %get-tuple-element.70.o0, f32[48,128]{1,0:T(8,128)S(1)} %get-tuple-element.71.o1, f32[48,128]{1,0:T(8,128)S(1)} %get-tuple-element.72.o2, ...), custom_call_target="tpu_custom_call" | custom-call | flops 40000000 | bytes 1691648 | tf_op jit(solution)/shard_map/local3/pallas_call | solution.py:408
  46.2 5.5 %all-to-all-start.2 = ((f32[32,4,128]{2,1,0:T(4,128)}), f32[32,4,128]{2,1,0:T(4,128)S(1)}, u32[]{:S(2)}, u32[]{:S(2)}) async-start(f32[32,4,128]{2,1,0:T(4,128)} %bitcast.10), calls=%async_computation.2 | async-start | bytes 131072 | tf_op jit(solution)/shard_map/all_to_all | solution.py:452
  51.7 2.7 %collective-permute-start.16 = (f32[48,128]{1,0:T(8,128)S(1)}, f32[48,128]{1,0:T(8,128)S(1)}, u32[]{:S(2)}, u32[]{:S(2)}) collective-permute-start(f32[48,128]{1,0:T(8,128)S(1)} %get-tuple-element.76.o0), channel_id=1, source_target_pairs={{0,4},{1,5},{2,6},{3,7},{4,0},{5,1},{6,2},{7,3},{8,12},{9,13},{10,... | collective-permute-start | bytes 73736 | tf_op jit(solution)/shard_map/ppermute | solution.py:434
  54.4 1.5 %collective-permute-start.17 = (f32[48,128]{1,0:T(8,128)S(1)}, f32[48,128]{1,0:T(8,128)S(1)}, u32[]{:S(2)}, u32[]{:S(2)}) collective-permute-start(f32[48,128]{1,0:T(8,128)S(1)} %get-tuple-element.77.o1), channel_id=1, source_target_pairs={{0,2},{1,3},{2,0},{3,1},{4,6},{5,7},{6,4},{7,5},{8,10},{9,11},{10,... | collective-permute-start | bytes 73736 | tf_op jit(solution)/shard_map/ppermute | solution.py:434
  55.9 1.5 %collective-permute-start.18 = (f32[48,128]{1,0:T(8,128)S(1)}, f32[48,128]{1,0:T(8,128)S(1)}, u32[]{:S(2)}, u32[]{:S(2)}) collective-permute-start(f32[48,128]{1,0:T(8,128)S(1)} %get-tuple-element.78.o2), channel_id=1, source_target_pairs={{0,8},{8,0},{16,24},{24,16},{1,9},{9,1},{17,25},{25,17},{2,10},{10... | collective-permute-start | bytes 73736 | tf_op jit(solution)/shard_map/ppermute | solution.py:434
  57.4 0.0 collective-permute-start.19
  57.4 0.0 collective-permute-done.16.a0
  57.4 0.8 %collective-permute-done.17.a1 = f32[48,128]{1,0:T(8,128)S(1)} collective-permute-done((f32[48,128]{1,0:T(8,128)S(1)}, f32[48,128]{1,0:T(8,128)S(1)}, u32[]{:S(2)}, u32[]{:S(2)}) %collective-permute-start.17) | collective-permute-done | bytes 24608 | tf_op jit(solution)/shard_map/ppermute | solution.py:434
  58.3 1.5 %collective-permute-done.18.a2 = f32[48,128]{1,0:T(8,128)S(1)} collective-permute-done((f32[48,128]{1,0:T(8,128)S(1)}, f32[48,128]{1,0:T(8,128)S(1)}, u32[]{:S(2)}, u32[]{:S(2)}) %collective-permute-start.18) | collective-permute-done | bytes 24608 | tf_op jit(solution)/shard_map/ppermute | solution.py:434
  59.8 0.0 collective-permute-done.19.a3
  59.8 0.0 all-to-all-done.2
  59.8 0.0 collective-permute-done.20.rest_1_
  59.8 1.2 %finish.1 = (f32[32,768]{1,0:T(8,128)}, f32[32,768]{1,0:T(8,128)}) custom-call(f32[128,128]{1,0:T(8,128)S(1)} %bitcast.19, f32[48,128]{1,0:T(8,128)S(1)} %get-tuple-element.76.o0, f32[48,128]{1,0:T(8,128)S(1)} %get-tuple-element.77.o1, f32[48,128]{1,0:T(8,128)S(1)} %get-tuple-element.78.o2, f32[48,128]{1,0:T(8,128)S(1)} %get-tuple-element.79.o3, ...), custom_call_target="tpu_custom_call" | custom-call | flops 40000000 | bytes 1208320 | tf_op jit(solution)/shard_map/finish/pallas_call | solution.py:408
  (2 shorter events, 0.0 us)
Async XLA Ops:
  0.6 17.6 %copy-start.1 = (bf16[1,1,768,768]{3,2,1,0:T(8,128)(2,1)S(1)}, bf16[1,1,768,768]{3,2,1,0:T(8,128)(2,1)}, u32[]{:S(2)}) copy-start(bf16[1,1,768,768]{3,2,1,0:T(8,128)(2,1)} %param.8) | copy-start | bytes 3538948
  3.5 21.9 %copy-start = (bf16[1,1,768,768]{3,2,1,0:T(8,128)(2,1)S(1)}, bf16[1,1,768,768]{3,2,1,0:T(8,128)(2,1)}, u32[]{:S(2)}) copy-start(bf16[1,1,768,768]{3,2,1,0:T(8,128)(2,1)} %param.7) | copy-start | bytes 3538948
  3.5 14.8 %collective-permute-start = (f32[128,128]{1,0:T(8,128)S(1)}, f32[128,128]{1,0:T(8,128)S(1)}, u32[]{:S(2)}, u32[]{:S(2)}) collective-permute-start(f32[128,128]{1,0:T(8,128)S(1)} %get-tuple-element.45.o0), channel_id=1, source_target_pairs={{0,4},{1,5},{2,6},{3,7},{4,0},{5,1},{6,2},{7,3},{8,12},{9,13},{10,... | collective-permute-start | bytes 196616 | tf_op jit(solution)/shard_map/ppermute | solution.py:434
  7.6 10.7 %all-to-all-start = ((f32[16,4,128]{2,1,0:T(4,128)}), f32[16,4,128]{2,1,0:T(4,128)S(1)}, u32[]{:S(2)}, u32[]{:S(2)}) async-start(f32[16,4,128]{2,1,0:T(4,128)} %bitcast.5), calls=%async_computation | async-start | bytes 65536 | tf_op jit(solution)/shard_map/all_to_all | solution.py:446
  11.5 5.9 %collective-permute-start.2 = (f32[72,128]{1,0:T(8,128)S(1)}, f32[72,128]{1,0:T(8,128)S(1)}, u32[]{:S(2)}, u32[]{:S(2)}) collective-permute-start(f32[72,128]{1,0:T(8,128)S(1)} %get-tuple-element.47.o2), channel_id=1, source_target_pairs={{0,8},{8,0},{16,24},{24,16},{1,9},{9,1},{17,25},{25,17},{2,10},{10... | collective-permute-start | bytes 110600 | tf_op jit(solution)/shard_map/ppermute | solution.py:434
  13.4 4.0 %collective-permute-start.1 = (f32[56,128]{1,0:T(8,128)S(1)}, f32[56,128]{1,0:T(8,128)S(1)}, u32[]{:S(2)}, u32[]{:S(2)}) collective-permute-start(f32[56,128]{1,0:T(8,128)S(1)} %get-tuple-element.46.o1), channel_id=1, source_target_pairs={{0,2},{1,3},{2,0},{3,1},{4,6},{5,7},{6,4},{7,5},{8,10},{9,11},{10,... | collective-permute-start | bytes 86024 | tf_op jit(solution)/shard_map/ppermute | solution.py:434
  14.9 2.5 %collective-permute-start.3 = (f32[56,128]{1,0:T(8,128)S(1)}, f32[56,128]{1,0:T(8,128)S(1)}, u32[]{:S(2)}, u32[]{:S(2)}) collective-permute-start(f32[56,128]{1,0:T(8,128)S(1)} %get-tuple-element.48.o3), channel_id=1, source_target_pairs={{0,1},{1,0},{2,3},{3,2},{4,5},{5,4},{6,7},{7,6},{8,9},{9,8},{10,11... | collective-permute-start | bytes 86024 | tf_op jit(solution)/shard_map/ppermute | solution.py:434
  19.1 6.3 %collective-permute-start.6 = (f32[224,128]{1,0:T(8,128)S(1)}, f32[224,128]{1,0:T(8,128)S(1)}, u32[]{:S(2)}, u32[]{:S(2)}) collective-permute-start(f32[224,128]{1,0:T(8,128)S(1)} %get-tuple-element.57.o2), channel_id=1, source_target_pairs={{0,8},{8,0},{16,24},{24,16},{1,9},{9,1},{17,25},{25,17},{2,10},{10... | collective-permute-start | bytes 344072 | tf_op jit(solution)/shard_map/ppermute | solution.py:434
  19.6 5.4 %collective-permute-start.4 = (f32[96,128]{1,0:T(8,128)S(1)}, f32[96,128]{1,0:T(8,128)S(1)}, u32[]{:S(2)}, u32[]{:S(2)}) collective-permute-start(f32[96,128]{1,0:T(8,128)S(1)} %get-tuple-element.55.o0), channel_id=1, source_target_pairs={{0,4},{1,5},{2,6},{3,7},{4,0},{5,1},{6,2},{7,3},{8,12},{9,13},{10,... | collective-permute-start | bytes 147464 | tf_op jit(solution)/shard_map/ppermute | solution.py:434
  21.2 4.2 %collective-permute-start.5 = (f32[96,128]{1,0:T(8,128)S(1)}, f32[96,128]{1,0:T(8,128)S(1)}, u32[]{:S(2)}, u32[]{:S(2)}) collective-permute-start(f32[96,128]{1,0:T(8,128)S(1)} %get-tuple-element.56.o1), channel_id=1, source_target_pairs={{0,2},{1,3},{2,0},{3,1},{4,6},{5,7},{6,4},{7,5},{8,10},{9,11},{10,... | collective-permute-start | bytes 147464 | tf_op jit(solution)/shard_map/ppermute | solution.py:434
  22.6 2.8 %collective-permute-start.7 = (f32[96,128]{1,0:T(8,128)S(1)}, f32[96,128]{1,0:T(8,128)S(1)}, u32[]{:S(2)}, u32[]{:S(2)}) collective-permute-start(f32[96,128]{1,0:T(8,128)S(1)} %get-tuple-element.58.o3), channel_id=1, source_target_pairs={{0,1},{1,0},{2,3},{3,2},{4,5},{5,4},{6,7},{7,6},{8,9},{9,8},{10,11... | collective-permute-start | bytes 147464 | tf_op jit(solution)/shard_map/ppermute | solution.py:434
  26.5 12.5 %all-to-all-start.1 = ((f32[32,4,128]{2,1,0:T(4,128)}), f32[32,4,128]{2,1,0:T(4,128)S(1)}, u32[]{:S(2)}, u32[]{:S(2)}) async-start(f32[32,4,128]{2,1,0:T(4,128)} %bitcast.8), calls=%async_computation.1 | async-start | bytes 131072 | tf_op jit(solution)/shard_map/all_to_all | solution.py:452
  30.9 5.7 %collective-permute-start.8 = (f32[48,128]{1,0:T(8,128)S(1)}, f32[48,128]{1,0:T(8,128)S(1)}, u32[]{:S(2)}, u32[]{:S(2)}) collective-permute-start(f32[48,128]{1,0:T(8,128)S(1)} %get-tuple-element.62.o0), channel_id=1, source_target_pairs={{0,4},{1,5},{2,6},{3,7},{4,0},{5,1},{6,2},{7,3},{8,12},{9,13},{10,... | collective-permute-start | bytes 73736 | tf_op jit(solution)/shard_map/ppermute | solution.py:434
  33.6 3.8 %collective-permute-start.9 = (f32[48,128]{1,0:T(8,128)S(1)}, f32[48,128]{1,0:T(8,128)S(1)}, u32[]{:S(2)}, u32[]{:S(2)}) collective-permute-start(f32[48,128]{1,0:T(8,128)S(1)} %get-tuple-element.63.o1), channel_id=1, source_target_pairs={{0,2},{1,3},{2,0},{3,1},{4,6},{5,7},{6,4},{7,5},{8,10},{9,11},{10,... | collective-permute-start | bytes 73736 | tf_op jit(solution)/shard_map/ppermute | solution.py:434
  35.2 3.8 %collective-permute-start.10 = (f32[48,128]{1,0:T(8,128)S(1)}, f32[48,128]{1,0:T(8,128)S(1)}, u32[]{:S(2)}, u32[]{:S(2)}) collective-permute-start(f32[48,128]{1,0:T(8,128)S(1)} %get-tuple-element.64.o2), channel_id=1, source_target_pairs={{0,8},{8,0},{16,24},{24,16},{1,9},{9,1},{17,25},{25,17},{2,10},{10... | collective-permute-start | bytes 73736 | tf_op jit(solution)/shard_map/ppermute | solution.py:434
  36.6 2.4 %collective-permute-start.11 = (f32[48,128]{1,0:T(8,128)S(1)}, f32[48,128]{1,0:T(8,128)S(1)}, u32[]{:S(2)}, u32[]{:S(2)}) collective-permute-start(f32[48,128]{1,0:T(8,128)S(1)} %get-tuple-element.65.o3), channel_id=1, source_target_pairs={{0,1},{1,0},{2,3},{3,2},{4,5},{5,4},{6,7},{7,6},{8,9},{9,8},{10,11... | collective-permute-start | bytes 73736 | tf_op jit(solution)/shard_map/ppermute | solution.py:434
  39.9 2.8 %collective-permute-start.15 = (f32[48,128]{1,0:T(8,128)S(1)}, f32[48,128]{1,0:T(8,128)S(1)}, u32[]{:S(2)}, u32[]{:S(2)}) collective-permute-start(f32[48,128]{1,0:T(8,128)S(1)} %get-tuple-element.73.o3), channel_id=1, source_target_pairs={{0,1},{1,0},{2,3},{3,2},{4,5},{5,4},{6,7},{7,6},{8,9},{9,8},{10,11... | collective-permute-start | bytes 73736 | tf_op jit(solution)/shard_map/ppermute | solution.py:434
  39.9 5.0 %collective-permute-start.12 = (f32[48,128]{1,0:T(8,128)S(1)}, f32[48,128]{1,0:T(8,128)S(1)}, u32[]{:S(2)}, u32[]{:S(2)}) collective-permute-start(f32[48,128]{1,0:T(8,128)S(1)} %get-tuple-element.70.o0), channel_id=1, source_target_pairs={{0,4},{1,5},{2,6},{3,7},{4,0},{5,1},{6,2},{7,3},{8,12},{9,13},{10,... | collective-permute-start | bytes 73736 | tf_op jit(solution)/shard_map/ppermute | solution.py:434
  40.5 4.4 %collective-permute-start.13 = (f32[48,128]{1,0:T(8,128)S(1)}, f32[48,128]{1,0:T(8,128)S(1)}, u32[]{:S(2)}, u32[]{:S(2)}) collective-permute-start(f32[48,128]{1,0:T(8,128)S(1)} %get-tuple-element.71.o1), channel_id=1, source_target_pairs={{0,2},{1,3},{2,0},{3,1},{4,6},{5,7},{6,4},{7,5},{8,10},{9,11},{10,... | collective-permute-start | bytes 73736 | tf_op jit(solution)/shard_map/ppermute | solution.py:434
  41.1 3.8 %collective-permute-start.14 = (f32[48,128]{1,0:T(8,128)S(1)}, f32[48,128]{1,0:T(8,128)S(1)}, u32[]{:S(2)}, u32[]{:S(2)}) collective-permute-start(f32[48,128]{1,0:T(8,128)S(1)} %get-tuple-element.72.o2), channel_id=1, source_target_pairs={{0,8},{8,0},{16,24},{24,16},{1,9},{9,1},{17,25},{25,17},{2,10},{10... | collective-permute-start | bytes 73736 | tf_op jit(solution)/shard_map/ppermute | solution.py:434
  42.6 17.1 %collective-permute-start.20 = (f32[256,128]{1,0:T(8,128)S(1)}, f32[256,128]{1,0:T(8,128)S(1)}, u32[]{:S(2)}, u32[]{:S(2)}) collective-permute-start(f32[256,128]{1,0:T(8,128)S(1)} %behind.1), channel_id=1, source_target_pairs={{0,16},{8,24},{16,0},{24,8},{1,17},{9,25},{17,1},{25,9},{2,18},{10... | collective-permute-start | bytes 393224 | tf_op jit(solution)/shard_map/ppermute | solution.py:434
  46.2 13.6 %all-to-all-start.2 = ((f32[32,4,128]{2,1,0:T(4,128)}), f32[32,4,128]{2,1,0:T(4,128)S(1)}, u32[]{:S(2)}, u32[]{:S(2)}) async-start(f32[32,4,128]{2,1,0:T(4,128)} %bitcast.10), calls=%async_computation.2 | async-start | bytes 131072 | tf_op jit(solution)/shard_map/all_to_all | solution.py:452
  51.7 5.7 %collective-permute-start.16 = (f32[48,128]{1,0:T(8,128)S(1)}, f32[48,128]{1,0:T(8,128)S(1)}, u32[]{:S(2)}, u32[]{:S(2)}) collective-permute-start(f32[48,128]{1,0:T(8,128)S(1)} %get-tuple-element.76.o0), channel_id=1, source_target_pairs={{0,4},{1,5},{2,6},{3,7},{4,0},{5,1},{6,2},{7,3},{8,12},{9,13},{10,... | collective-permute-start | bytes 73736 | tf_op jit(solution)/shard_map/ppermute | solution.py:434
  54.4 3.8 %collective-permute-start.17 = (f32[48,128]{1,0:T(8,128)S(1)}, f32[48,128]{1,0:T(8,128)S(1)}, u32[]{:S(2)}, u32[]{:S(2)}) collective-permute-start(f32[48,128]{1,0:T(8,128)S(1)} %get-tuple-element.77.o1), channel_id=1, source_target_pairs={{0,2},{1,3},{2,0},{3,1},{4,6},{5,7},{6,4},{7,5},{8,10},{9,11},{10,... | collective-permute-start | bytes 73736 | tf_op jit(solution)/shard_map/ppermute | solution.py:434
  55.9 3.8 %collective-permute-start.18 = (f32[48,128]{1,0:T(8,128)S(1)}, f32[48,128]{1,0:T(8,128)S(1)}, u32[]{:S(2)}, u32[]{:S(2)}) collective-permute-start(f32[48,128]{1,0:T(8,128)S(1)} %get-tuple-element.78.o2), channel_id=1, source_target_pairs={{0,8},{8,0},{16,24},{24,16},{1,9},{9,1},{17,25},{25,17},{2,10},{10... | collective-permute-start | bytes 73736 | tf_op jit(solution)/shard_map/ppermute | solution.py:434
  57.4 2.4 %collective-permute-start.19 = (f32[48,128]{1,0:T(8,128)S(1)}, f32[48,128]{1,0:T(8,128)S(1)}, u32[]{:S(2)}, u32[]{:S(2)}) collective-permute-start(f32[48,128]{1,0:T(8,128)S(1)} %get-tuple-element.79.o3), channel_id=1, source_target_pairs={{0,1},{1,0},{2,3},{3,2},{4,5},{5,4},{6,7},{7,6},{8,9},{9,8},{10,11... | collective-permute-start | bytes 73736 | tf_op jit(solution)/shard_map/ppermute | solution.py:434

commit v7 on v6

--- a/solution.py
+++ b/solution.py
@@ -268,7 +268,7 @@
 
 
 def first_image(
-    received, o0, o1, o2, o3, a0, a1, a2, a3, vectors, corner, resid, spread, low, inverse, flex,
+    received, o0, o1, o2, o3, a0, a1, a2, a3, vectors, corner, resid, spread, low, flex,
     z_out, sums_out, map_out, spread_out, *wins,
 ):
     n_load, dofs = resid.shape
@@ -293,14 +293,13 @@
     signed = sign * zvec
     image = rounded(signed.astype(BF16), flex[...])
     put_faces(wins, jnp.concatenate([image, low[...]], axis=0))
-    wins[LAST][size(2 * n_load) :, :] = inverse[...]
     sums_out[...] = with_sums(
         jnp.zeros((8, 4 * n_load), F32), [rows_sum(resid[...] * zvec), 2.0 * rows_sum(signed * image)]
     )
 
 
 def second_local(
-    o0, o1, o2, o3, a0, a1, a2, a3, sums, vectors, corner_map, stiff,
+    o0, o1, o2, o3, a0, a1, a2, a3, sums, vectors, corner_map, inverse, other, stiff,
     flexed_out, low_out, inverse_out, sent, w0, w1, w2, w3, block, sem,
 ):
     n_load, dofs = flexed_out.shape
@@ -308,9 +307,8 @@
     jumped = jump([o0, o1, o2, o3], [a0, a1, a2, a3], 2 * n_load, sign_mask)
     flexed = jumped[:n_load]
     flexed_out[...] = flexed
-    for i, ref in enumerate([[o0, o1, o2, o3][LAST], [a0, a1, a2, a3][LAST]]):
-        n_row = inverse_out.shape[0] // 2
-        inverse_out[i * n_row : (i + 1) * n_row, :] = ref[size(2 * n_load) :, :]
+    inverse_out[: inverse.shape[0], :] = inverse[...]
+    inverse_out[inverse.shape[0] :, :] = other[...]
     low_out[...] = jumped[n_load:].astype(BF16)
     scaled = 0.5 * sign * flexed
     is_sum = iota((8, 1), 0) % 4 == 3
@@ -483,13 +481,15 @@
     )
     received = send_pair(corners)
     came = exchange(own)
+    inverse = behind(inverse, came[-1])
+    other = swap(inverse, "grp", 1)
     zold, sums, corner_map, spread, *own = call(
-        "image1", first_image, [received] + own + came + [vectors, corner, resid, spread, low, inverse, flex],
-        [field, total, ((80, dofs), BF16), ((80, n), F32)] + faces(2 * n_load, 0, n_tile),
+        "image1", first_image, [received] + own + came + [vectors, corner, resid, spread, low, flex],
+        [field, total, ((80, dofs), BF16), ((80, n), F32)] + faces(2 * n_load),
     )
     came = exchange(own)
     flexed, low, inverse, sent_rows, *own = call(
-        "local2", second_local, own + came + [sums, vectors, corner_map, stiff],
+        "local2", second_local, own + came + [sums, vectors, corner_map, inverse, other, stiff],
         [field, ((n_load, dofs), BF16), ((2 * n_tile, LANES), F32), sent] + faces(n_load),
         block, out_place=[3],
     )

time: 61.3 us -> 60.4 us (0.985)
  starting transfers between devices: 40.6 us -> 39.7 us
    all_to_all x2, starting transfers between devices: 9.89 us -> 8.09 us  [send_all(): lax.all_to_all(blocks, ('grp', 'sub'), 0, 0, tiled=True).reshape(rows.shape)]
    ppermute x21 -> x22, starting transfers between devices: 26.8 us -> 27.7 us  [swap(): lax.ppermute(block, axis, [(i, i ^ distance) for i in range(count) if i ^...]
    ppermute x21 -> x22, waiting for transfers between devices: 10.7 us -> 10.9 us  [swap(): lax.ppermute(block, axis, [(i, i ^ distance) for i in range(count) if i ^...]
  transfers between devices with their start and end apart: 24 -> 25, of which waited for: 9 -> 10; matrix products, arithmetic and copies ran while one was open for 0% -> 0% of each run, Pallas kernels for 2% -> 3%
where the time goes in v7:
time: 60.4 us; the launch traced here: 60.1 us
  starting transfers between devices  39.7 us (66%)
  waiting for transfers between devices  11.6 us (19%)
  Pallas kernels  7.07 us (12%)
  other arithmetic  1 us (2%)
  between operations  0.76 us (1%)
    ppermute x22, starting transfers between devices, swap(): lax.ppermute(block, axis, [(i, i ^ distance) for i in range(count) if i ^...  27.7 us
    ppermute x22, waiting for transfers between devices, swap(): lax.ppermute(block, axis, [(i, i ^ distance) for i in range(count) if i ^...  10.9 us
    all_to_all x2, starting transfers between devices, send_all(): lax.all_to_all(blocks, ('grp', 'sub'), 0, 0, tiled=True).reshape(rows.shape)  8.09 us
    pallas_call x6, Pallas kernels, call(): pl.pallas_call(kernel, out_shape=shapes, in_specs=[pl.BlockSpec(memory_sp...  7.07 us
    all_to_all x1, starting transfers between devices, send_pair(): lax.all_to_all(blocks, ('grp', 'sub'), 0, 0, tiled=True, axis_index_group...  3.88 us
  transfers between devices with their start and end apart: 25, of which 10 were waited for; matrix products, arithmetic and copies ran while one was open for 0% of the time, Pallas kernels for 3%

profile of v7, /device:TPU:0, one launch (start us, length us, event | category | flops | bytes accessed | tf_op | source)
XLA Modules:
  0.0 60.1 jit_solution(14369700259006332831)
XLA Ops:
  0.6 0.0 copy-start.1
  0.6 1.0 %convert_add_fusion.small = f32[104,128]{1,0:T(8,128)S(1)} fusion(s32[1,12]{1,0:T(1,128)} %bitcast.24, s32[1,4]{1,0:T(1,128)} %bitcast.25, f32[96,96]{1,0:T(8,128)} %bitcast.23), kind=kLoop, calls=%fused_computation | loop fusion | flops 53248 | bytes 90176 | tf_op jit(solution)/shard_map/add | solution.py:472
  1.6 1.8 %start.1 = (f32[64,128]{1,0:T(8,128)}, f32[8,768]{1,0:T(8,128)S(1)}, bf16[16,768]{1,0:T(8,128)(2,1)S(1)}, f32[32,768]{1,0:T(8,128)S(1)}, f32[64,128]{1,0:T(8,128...) custom-call(f32[32,768]{1,0:T(8,128)} %bitcast.22, ...), custom_call_target="tpu_custom_call" | custom-call | flops 40000000 | bytes 1867776 | tf_op jit(solution)/shard_map/start/pallas_call | solution.py:406
  3.5 0.0 copy-start
  3.5 4.1 %collective-permute-start = (f32[128,128]{1,0:T(8,128)S(1)}, f32[128,128]{1,0:T(8,128)S(1)}, u32[]{:S(2)}, u32[]{:S(2)}) collective-permute-start(f32[128,128]{1,0:T(8,128)S(1)} %get-tuple-element.45.o0), channel_id=1, source_target_pairs={{0,4},{1,5},{2,6},{3,7},{4,0},{5,1},{6,2},{7,3},{8,12},{9,13},{10,... | collective-permute-start | bytes 196616 | tf_op jit(solution)/shard_map/ppermute | solution.py:432
  7.6 3.9 %all-to-all-start = ((f32[16,4,128]{2,1,0:T(4,128)}), f32[16,4,128]{2,1,0:T(4,128)S(1)}, u32[]{:S(2)}, u32[]{:S(2)}) async-start(f32[16,4,128]{2,1,0:T(4,128)} %bitcast.5), calls=%async_computation | async-start | bytes 65536 | tf_op jit(solution)/shard_map/all_to_all | solution.py:444
  11.5 0.4 collective-permute-start.3
  11.9 1.7 %collective-permute-start.2 = (f32[72,128]{1,0:T(8,128)S(1)}, f32[72,128]{1,0:T(8,128)S(1)}, u32[]{:S(2)}, u32[]{:S(2)}) collective-permute-start(f32[72,128]{1,0:T(8,128)S(1)} %get-tuple-element.47.o2), channel_id=1, source_target_pairs={{0,8},{8,0},{16,24},{24,16},{1,9},{9,1},{17,25},{25,17},{2,10},{10... | collective-permute-start | bytes 110600 | tf_op jit(solution)/shard_map/ppermute | solution.py:432
  13.6 1.5 %collective-permute-start.1 = (f32[56,128]{1,0:T(8,128)S(1)}, f32[56,128]{1,0:T(8,128)S(1)}, u32[]{:S(2)}, u32[]{:S(2)}) collective-permute-start(f32[56,128]{1,0:T(8,128)S(1)} %get-tuple-element.46.o1), channel_id=1, source_target_pairs={{0,2},{1,3},{2,0},{3,1},{4,6},{5,7},{6,4},{7,5},{8,10},{9,11},{10,... | collective-permute-start | bytes 86024 | tf_op jit(solution)/shard_map/ppermute | solution.py:432
  15.1 0.0 collective-permute-done.3.a3.other_ref
  15.1 0.6 collective-permute-start.8
  15.6 1.9 %collective-permute-done.1.a1 = f32[56,128]{1,0:T(8,128)S(1)} collective-permute-done((f32[56,128]{1,0:T(8,128)S(1)}, f32[56,128]{1,0:T(8,128)S(1)}, u32[]{:S(2)}, u32[]{:S(2)}) %collective-permute-start.1) | collective-permute-done | bytes 28704 | tf_op jit(solution)/shard_map/ppermute | solution.py:432
  17.5 0.0 collective-permute-done.2.a2
  17.5 0.7 %all-to-all-done = f32[16,4,128]{2,1,0:T(4,128)S(1)} async-done(((f32[16,4,128]{2,1,0:T(4,128)}), f32[16,4,128]{2,1,0:T(4,128)S(1)}, u32[]{:S(2)}, u32[]{:S(2)}) %all-to-all-start) | async-done | bytes 32800 | tf_op jit(solution)/shard_map/all_to_all | solution.py:444
  18.2 0.0 collective-permute-done.a0
  18.2 0.0 copy-done.1
  18.2 0.8 %image1.1 = (f32[32,768]{1,0:T(8,128)S(1)}, f32[8,128]{1,0:T(8,128)S(1)}, bf16[80,768]{1,0:T(8,128)(2,1)S(1)}, f32[80,128]{1,0:T(8,128)S(1)}, f32[96,128]{1,0:T(...) custom-call(f32[64,128]{1,0:T(8,128)S(1)} %bitcast.21, ...), custom_call_target="tpu_custom_call" | custom-call | flops 40000000 | bytes 2273280 | tf_op jit(solution)/shard_map/image1/pallas_call | solution.py:406
  19.1 1.7 %collective-permute-start.4 = (f32[96,128]{1,0:T(8,128)S(1)}, f32[96,128]{1,0:T(8,128)S(1)}, u32[]{:S(2)}, u32[]{:S(2)}) collective-permute-start(f32[96,128]{1,0:T(8,128)S(1)} %get-tuple-element.54.o0), channel_id=1, source_target_pairs={{0,4},{1,5},{2,6},{3,7},{4,0},{5,1},{6,2},{7,3},{8,12},{9,13},{10,... | collective-permute-start | bytes 147464 | tf_op jit(solution)/shard_map/ppermute | solution.py:432
  20.8 1.5 %collective-permute-start.5 = (f32[96,128]{1,0:T(8,128)S(1)}, f32[96,128]{1,0:T(8,128)S(1)}, u32[]{:S(2)}, u32[]{:S(2)}) collective-permute-start(f32[96,128]{1,0:T(8,128)S(1)} %get-tuple-element.55.o1), channel_id=1, source_target_pairs={{0,2},{1,3},{2,0},{3,1},{4,6},{5,7},{6,4},{7,5},{8,10},{9,11},{10,... | collective-permute-start | bytes 147464 | tf_op jit(solution)/shard_map/ppermute | solution.py:432
  22.2 0.6 collective-permute-start.6
  22.8 0.0 collective-permute-start.7
  22.8 0.0 collective-permute-done.8.other
  22.8 1.9 %collective-permute-done.4.a0 = f32[96,128]{1,0:T(8,128)S(1)} collective-permute-done((f32[96,128]{1,0:T(8,128)S(1)}, f32[96,128]{1,0:T(8,128)S(1)}, u32[]{:S(2)}, u32[]{:S(2)}) %collective-permute-start.4) | collective-permute-done | bytes 49184 | tf_op jit(solution)/shard_map/ppermute | solution.py:432
  24.7 0.4 collective-permute-done.5.a1
  25.0 1.3 %collective-permute-done.6.a2 = f32[96,128]{1,0:T(8,128)S(1)} collective-permute-done((f32[96,128]{1,0:T(8,128)S(1)}, f32[96,128]{1,0:T(8,128)S(1)}, u32[]{:S(2)}, u32[]{:S(2)}) %collective-permute-start.6) | collective-permute-done | bytes 49184 | tf_op jit(solution)/shard_map/ppermute | solution.py:432
  26.3 0.0 collective-permute-done.7.a3
  26.3 0.0 copy-done
  26.3 1.0 %local2.1 = (f32[32,768]{1,0:T(8,128)S(1)}, bf16[32,768]{1,0:T(8,128)(2,1)S(1)}, f32[256,128]{1,0:T(8,128)S(1)}, f32[128,128]{1,0:T(8,128)}, f32[48,128]{1,0:T(8...) custom-call(f32[96,128]{1,0:T(8,128)S(1)} %get-tuple-element.54.o0, ...), custom_call_target="tpu_custom_call" | custom-call | flops 40000000 | bytes 2297856 | tf_op jit(solution)/shard_map/local2/pallas_call | solution.py:406
  27.4 2.6 %all-to-all-start.1 = ((f32[32,4,128]{2,1,0:T(4,128)}), f32[32,4,128]{2,1,0:T(4,128)S(1)}, u32[]{:S(2)}, u32[]{:S(2)}) async-start(f32[32,4,128]{2,1,0:T(4,128)} %bitcast.8), calls=%async_computation.1 | async-start | bytes 131072 | tf_op jit(solution)/shard_map/all_to_all | solution.py:450
  30.0 2.7 %collective-permute-start.9 = (f32[48,128]{1,0:T(8,128)S(1)}, f32[48,128]{1,0:T(8,128)S(1)}, u32[]{:S(2)}, u32[]{:S(2)}) collective-permute-start(f32[48,128]{1,0:T(8,128)S(1)} %get-tuple-element.62.o0), channel_id=1, source_target_pairs={{0,4},{1,5},{2,6},{3,7},{4,0},{5,1},{6,2},{7,3},{8,12},{9,13},{10,... | collective-permute-start | bytes 73736 | tf_op jit(solution)/shard_map/ppermute | solution.py:432
  32.7 1.5 %collective-permute-start.10 = (f32[48,128]{1,0:T(8,128)S(1)}, f32[48,128]{1,0:T(8,128)S(1)}, u32[]{:S(2)}, u32[]{:S(2)}) collective-permute-start(f32[48,128]{1,0:T(8,128)S(1)} %get-tuple-element.63.o1), channel_id=1, source_target_pairs={{0,2},{1,3},{2,0},{3,1},{4,6},{5,7},{6,4},{7,5},{8,10},{9,11},{10,... | collective-permute-start | bytes 73736 | tf_op jit(solution)/shard_map/ppermute | solution.py:432
  34.3 1.5 %collective-permute-start.11 = (f32[48,128]{1,0:T(8,128)S(1)}, f32[48,128]{1,0:T(8,128)S(1)}, u32[]{:S(2)}, u32[]{:S(2)}) collective-permute-start(f32[48,128]{1,0:T(8,128)S(1)} %get-tuple-element.64.o2), channel_id=1, source_target_pairs={{0,8},{8,0},{16,24},{24,16},{1,9},{9,1},{17,25},{25,17},{2,10},{10... | collective-permute-start | bytes 73736 | tf_op jit(solution)/shard_map/ppermute | solution.py:432
  35.7 0.0 collective-permute-start.12
  35.7 0.0 collective-permute-done.9.a0
  35.7 0.8 %collective-permute-done.10.a1 = f32[48,128]{1,0:T(8,128)S(1)} collective-permute-done((f32[48,128]{1,0:T(8,128)S(1)}, f32[48,128]{1,0:T(8,128)S(1)}, u32[]{:S(2)}, u32[]{:S(2)}) %collective-permute-start.10) | collective-permute-done | bytes 24608 | tf_op jit(solution)/shard_map/ppermute | solution.py:432
  36.6 1.5 %collective-permute-done.11.a2 = f32[48,128]{1,0:T(8,128)S(1)} collective-permute-done((f32[48,128]{1,0:T(8,128)S(1)}, f32[48,128]{1,0:T(8,128)S(1)}, u32[]{:S(2)}, u32[]{:S(2)}) %collective-permute-start.11) | collective-permute-done | bytes 24608 | tf_op jit(solution)/shard_map/ppermute | solution.py:432
  38.1 0.0 collective-permute-done.12.a3
  38.1 0.0 all-to-all-done.1
  38.1 0.9 %image2.1 = (f32[32,768]{1,0:T(8,128)S(1)}, f32[32,768]{1,0:T(8,128)S(1)}, f32[8,128]{1,0:T(8,128)S(1)}, f32[8,128]{1,0:T(8,128)S(1)}, f32[48,128]{1,0:T(8,128)S...) custom-call(f32[128,128]{1,0:T(8,128)S(1)} %bitcast.20, ...), custom_call_target="tpu_custom_call" | custom-call | flops 40000000 | bytes 2277376 | tf_op jit(solution)/shard_map/image2/pallas_call | solution.py:406
  39.0 0.1 collective-permute-start.16
  39.0 0.6 collective-permute-start.13
  39.6 0.6 %collective-permute-start.14 = (f32[48,128]{1,0:T(8,128)S(1)}, f32[48,128]{1,0:T(8,128)S(1)}, u32[]{:S(2)}, u32[]{:S(2)}) collective-permute-start(f32[48,128]{1,0:T(8,128)S(1)} %get-tuple-element.71.o1), channel_id=1, source_target_pairs={{0,2},{1,3},{2,0},{3,1},{4,6},{5,7},{6,4},{7,5},{8,10},{9,11},{10,... | collective-permute-start | bytes 73736 | tf_op jit(solution)/shard_map/ppermute | solution.py:432
  40.2 1.5 %collective-permute-start.15 = (f32[48,128]{1,0:T(8,128)S(1)}, f32[48,128]{1,0:T(8,128)S(1)}, u32[]{:S(2)}, u32[]{:S(2)}) collective-permute-start(f32[48,128]{1,0:T(8,128)S(1)} %get-tuple-element.72.o2), channel_id=1, source_target_pairs={{0,8},{8,0},{16,24},{24,16},{1,9},{9,1},{17,25},{25,17},{2,10},{10... | collective-permute-start | bytes 73736 | tf_op jit(solution)/shard_map/ppermute | solution.py:432
  41.7 0.0 collective-permute-done.16.a3.other_ref
  41.7 1.6 %collective-permute-start.21 = (f32[256,128]{1,0:T(8,128)S(1)}, f32[256,128]{1,0:T(8,128)S(1)}, u32[]{:S(2)}, u32[]{:S(2)}) collective-permute-start(f32[256,128]{1,0:T(8,128)S(1)} %behind.3), channel_id=1, source_target_pairs={{0,16},{8,24},{16,0},{24,8},{1,17},{9,25},{17,1},{25,9},{2,18},{10... | collective-permute-start | bytes 393224 | tf_op jit(solution)/shard_map/ppermute | solution.py:432
  43.3 0.8 %collective-permute-done.13.a0 = f32[48,128]{1,0:T(8,128)S(1)} collective-permute-done((f32[48,128]{1,0:T(8,128)S(1)}, f32[48,128]{1,0:T(8,128)S(1)}, u32[]{:S(2)}, u32[]{:S(2)}) %collective-permute-start.13) | collective-permute-done | bytes 24608 | tf_op jit(solution)/shard_map/ppermute | solution.py:432
  44.1 0.0 collective-permute-done.14.a1
  44.1 0.0 collective-permute-done.15.a2
  44.1 1.2 %local3.1 = (f32[128,128]{1,0:T(8,128)}, f32[48,128]{1,0:T(8,128)S(1)}, f32[48,128]{1,0:T(8,128)S(1)}, f32[48,128]{1,0:T(8,128)S(1)}, f32[48,128]{1,0:T(8,128)S(1)}) custom-call(f32[48,128]{1,0:T(8,128)S(1)} %get-tuple-element.70.o0, f32[48,128]{1,0:T(8,128)S(1)} %get-tuple-element.71.o1, f32[48,128]{1,0:T(8,128)S(1)} %get-tuple-element.72.o2, ...), custom_call_target="tpu_custom_call" | custom-call | flops 40000000 | bytes 1691648 | tf_op jit(solution)/shard_map/local3/pallas_call | solution.py:406
  45.3 5.5 %all-to-all-start.2 = ((f32[32,4,128]{2,1,0:T(4,128)}), f32[32,4,128]{2,1,0:T(4,128)S(1)}, u32[]{:S(2)}, u32[]{:S(2)}) async-start(f32[32,4,128]{2,1,0:T(4,128)} %bitcast.10), calls=%async_computation.2 | async-start | bytes 131072 | tf_op jit(solution)/shard_map/all_to_all | solution.py:450
  50.8 2.7 %collective-permute-start.17 = (f32[48,128]{1,0:T(8,128)S(1)}, f32[48,128]{1,0:T(8,128)S(1)}, u32[]{:S(2)}, u32[]{:S(2)}) collective-permute-start(f32[48,128]{1,0:T(8,128)S(1)} %get-tuple-element.76.o0), channel_id=1, source_target_pairs={{0,4},{1,5},{2,6},{3,7},{4,0},{5,1},{6,2},{7,3},{8,12},{9,13},{10,... | collective-permute-start | bytes 73736 | tf_op jit(solution)/shard_map/ppermute | solution.py:432
  53.5 1.5 %collective-permute-start.18 = (f32[48,128]{1,0:T(8,128)S(1)}, f32[48,128]{1,0:T(8,128)S(1)}, u32[]{:S(2)}, u32[]{:S(2)}) collective-permute-start(f32[48,128]{1,0:T(8,128)S(1)} %get-tuple-element.77.o1), channel_id=1, source_target_pairs={{0,2},{1,3},{2,0},{3,1},{4,6},{5,7},{6,4},{7,5},{8,10},{9,11},{10,... | collective-permute-start | bytes 73736 | tf_op jit(solution)/shard_map/ppermute | solution.py:432
  55.0 1.5 %collective-permute-start.19 = (f32[48,128]{1,0:T(8,128)S(1)}, f32[48,128]{1,0:T(8,128)S(1)}, u32[]{:S(2)}, u32[]{:S(2)}) collective-permute-start(f32[48,128]{1,0:T(8,128)S(1)} %get-tuple-element.78.o2), channel_id=1, source_target_pairs={{0,8},{8,0},{16,24},{24,16},{1,9},{9,1},{17,25},{25,17},{2,10},{10... | collective-permute-start | bytes 73736 | tf_op jit(solution)/shard_map/ppermute | solution.py:432
  56.5 0.0 collective-permute-start.20
  56.5 0.0 collective-permute-done.17.a0
  56.5 0.8 %collective-permute-done.18.a1 = f32[48,128]{1,0:T(8,128)S(1)} collective-permute-done((f32[48,128]{1,0:T(8,128)S(1)}, f32[48,128]{1,0:T(8,128)S(1)}, u32[]{:S(2)}, u32[]{:S(2)}) %collective-permute-start.18) | collective-permute-done | bytes 24608 | tf_op jit(solution)/shard_map/ppermute | solution.py:432
  57.4 1.5 %collective-permute-done.19.a2 = f32[48,128]{1,0:T(8,128)S(1)} collective-permute-done((f32[48,128]{1,0:T(8,128)S(1)}, f32[48,128]{1,0:T(8,128)S(1)}, u32[]{:S(2)}, u32[]{:S(2)}) %collective-permute-start.19) | collective-permute-done | bytes 24608 | tf_op jit(solution)/shard_map/ppermute | solution.py:432
  58.9 0.0 collective-permute-done.20.a3
  58.9 0.0 all-to-all-done.2
  58.9 0.0 collective-permute-done.21.rest_1_
  58.9 1.2 %finish.1 = (f32[32,768]{1,0:T(8,128)}, f32[32,768]{1,0:T(8,128)}) custom-call(f32[128,128]{1,0:T(8,128)S(1)} %bitcast.19, f32[48,128]{1,0:T(8,128)S(1)} %get-tuple-element.76.o0, f32[48,128]{1,0:T(8,128)S(1)} %get-tuple-element.77.o1, f32[48,128]{1,0:T(8,128)S(1)} %get-tuple-element.78.o2, f32[48,128]{1,0:T(8,128)S(1)} %get-tuple-element.79.o3, ...), custom_call_target="tpu_custom_call" | custom-call | flops 40000000 | bytes 1208320 | tf_op jit(solution)/shard_map/finish/pallas_call | solution.py:406
  (3 shorter events, 0.0 us)
Async XLA Ops:
  0.6 17.6 %copy-start.1 = (bf16[1,1,768,768]{3,2,1,0:T(8,128)(2,1)S(1)}, bf16[1,1,768,768]{3,2,1,0:T(8,128)(2,1)}, u32[]{:S(2)}) copy-start(bf16[1,1,768,768]{3,2,1,0:T(8,128)(2,1)} %param.8) | copy-start | bytes 3538948
  3.5 22.8 %copy-start = (bf16[1,1,768,768]{3,2,1,0:T(8,128)(2,1)S(1)}, bf16[1,1,768,768]{3,2,1,0:T(8,128)(2,1)}, u32[]{:S(2)}) copy-start(bf16[1,1,768,768]{3,2,1,0:T(8,128)(2,1)} %param.7) | copy-start | bytes 3538948
  3.5 14.7 %collective-permute-start = (f32[128,128]{1,0:T(8,128)S(1)}, f32[128,128]{1,0:T(8,128)S(1)}, u32[]{:S(2)}, u32[]{:S(2)}) collective-permute-start(f32[128,128]{1,0:T(8,128)S(1)} %get-tuple-element.45.o0), channel_id=1, source_target_pairs={{0,4},{1,5},{2,6},{3,7},{4,0},{5,1},{6,2},{7,3},{8,12},{9,13},{10,... | collective-permute-start | bytes 196616 | tf_op jit(solution)/shard_map/ppermute | solution.py:432
  7.6 10.6 %all-to-all-start = ((f32[16,4,128]{2,1,0:T(4,128)}), f32[16,4,128]{2,1,0:T(4,128)S(1)}, u32[]{:S(2)}, u32[]{:S(2)}) async-start(f32[16,4,128]{2,1,0:T(4,128)} %bitcast.5), calls=%async_computation | async-start | bytes 65536 | tf_op jit(solution)/shard_map/all_to_all | solution.py:444
  11.5 3.6 %collective-permute-start.3 = (f32[56,128]{1,0:T(8,128)S(1)}, f32[56,128]{1,0:T(8,128)S(1)}, u32[]{:S(2)}, u32[]{:S(2)}) collective-permute-start(f32[56,128]{1,0:T(8,128)S(1)} %get-tuple-element.48.o3), channel_id=1, source_target_pairs={{0,1},{1,0},{2,3},{3,2},{4,5},{5,4},{6,7},{7,6},{8,9},{9,8},{10,11... | collective-permute-start | bytes 86024 | tf_op jit(solution)/shard_map/ppermute | solution.py:432
  11.9 5.6 %collective-permute-start.2 = (f32[72,128]{1,0:T(8,128)S(1)}, f32[72,128]{1,0:T(8,128)S(1)}, u32[]{:S(2)}, u32[]{:S(2)}) collective-permute-start(f32[72,128]{1,0:T(8,128)S(1)} %get-tuple-element.47.o2), channel_id=1, source_target_pairs={{0,8},{8,0},{16,24},{24,16},{1,9},{9,1},{17,25},{25,17},{2,10},{10... | collective-permute-start | bytes 110600 | tf_op jit(solution)/shard_map/ppermute | solution.py:432
  13.6 3.9 %collective-permute-start.1 = (f32[56,128]{1,0:T(8,128)S(1)}, f32[56,128]{1,0:T(8,128)S(1)}, u32[]{:S(2)}, u32[]{:S(2)}) collective-permute-start(f32[56,128]{1,0:T(8,128)S(1)} %get-tuple-element.46.o1), channel_id=1, source_target_pairs={{0,2},{1,3},{2,0},{3,1},{4,6},{5,7},{6,4},{7,5},{8,10},{9,11},{10,... | collective-permute-start | bytes 86024 | tf_op jit(solution)/shard_map/ppermute | solution.py:432
  15.1 7.7 %collective-permute-start.8 = (f32[128,128]{1,0:T(8,128)S(1)}, f32[128,128]{1,0:T(8,128)S(1)}, u32[]{:S(2)}, u32[]{:S(2)}) collective-permute-start(f32[128,128]{1,0:T(8,128)S(1)} %behind.2.inverse), channel_id=1, source_target_pairs={{0,8},{8,0},{16,24},{24,16},{1,9},{9,1},{17,25},{25,17},{2,10},{10... | collective-permute-start | bytes 196616 | tf_op jit(solution)/shard_map/ppermute | solution.py:432
  19.1 5.6 %collective-permute-start.4 = (f32[96,128]{1,0:T(8,128)S(1)}, f32[96,128]{1,0:T(8,128)S(1)}, u32[]{:S(2)}, u32[]{:S(2)}) collective-permute-start(f32[96,128]{1,0:T(8,128)S(1)} %get-tuple-element.54.o0), channel_id=1, source_target_pairs={{0,4},{1,5},{2,6},{3,7},{4,0},{5,1},{6,2},{7,3},{8,12},{9,13},{10,... | collective-permute-start | bytes 147464 | tf_op jit(solution)/shard_map/ppermute | solution.py:432
  20.8 4.3 %collective-permute-start.5 = (f32[96,128]{1,0:T(8,128)S(1)}, f32[96,128]{1,0:T(8,128)S(1)}, u32[]{:S(2)}, u32[]{:S(2)}) collective-permute-start(f32[96,128]{1,0:T(8,128)S(1)} %get-tuple-element.55.o1), channel_id=1, source_target_pairs={{0,2},{1,3},{2,0},{3,1},{4,6},{5,7},{6,4},{7,5},{8,10},{9,11},{10,... | collective-permute-start | bytes 147464 | tf_op jit(solution)/shard_map/ppermute | solution.py:432
  22.2 4.1 %collective-permute-start.6 = (f32[96,128]{1,0:T(8,128)S(1)}, f32[96,128]{1,0:T(8,128)S(1)}, u32[]{:S(2)}, u32[]{:S(2)}) collective-permute-start(f32[96,128]{1,0:T(8,128)S(1)} %get-tuple-element.56.o2), channel_id=1, source_target_pairs={{0,8},{8,0},{16,24},{24,16},{1,9},{9,1},{17,25},{25,17},{2,10},{10... | collective-permute-start | bytes 147464 | tf_op jit(solution)/shard_map/ppermute | solution.py:432
  22.8 3.5 %collective-permute-start.7 = (f32[96,128]{1,0:T(8,128)S(1)}, f32[96,128]{1,0:T(8,128)S(1)}, u32[]{:S(2)}, u32[]{:S(2)}) collective-permute-start(f32[96,128]{1,0:T(8,128)S(1)} %get-tuple-element.57.o3), channel_id=1, source_target_pairs={{0,1},{1,0},{2,3},{3,2},{4,5},{5,4},{6,7},{7,6},{8,9},{9,8},{10,11... | collective-permute-start | bytes 147464 | tf_op jit(solution)/shard_map/ppermute | solution.py:432
  27.4 10.7 %all-to-all-start.1 = ((f32[32,4,128]{2,1,0:T(4,128)}), f32[32,4,128]{2,1,0:T(4,128)S(1)}, u32[]{:S(2)}, u32[]{:S(2)}) async-start(f32[32,4,128]{2,1,0:T(4,128)} %bitcast.8), calls=%async_computation.1 | async-start | bytes 131072 | tf_op jit(solution)/shard_map/all_to_all | solution.py:450
  30.0 5.7 %collective-permute-start.9 = (f32[48,128]{1,0:T(8,128)S(1)}, f32[48,128]{1,0:T(8,128)S(1)}, u32[]{:S(2)}, u32[]{:S(2)}) collective-permute-start(f32[48,128]{1,0:T(8,128)S(1)} %get-tuple-element.62.o0), channel_id=1, source_target_pairs={{0,4},{1,5},{2,6},{3,7},{4,0},{5,1},{6,2},{7,3},{8,12},{9,13},{10,... | collective-permute-start | bytes 73736 | tf_op jit(solution)/shard_map/ppermute | solution.py:432
  32.7 3.8 %collective-permute-start.10 = (f32[48,128]{1,0:T(8,128)S(1)}, f32[48,128]{1,0:T(8,128)S(1)}, u32[]{:S(2)}, u32[]{:S(2)}) collective-permute-start(f32[48,128]{1,0:T(8,128)S(1)} %get-tuple-element.63.o1), channel_id=1, source_target_pairs={{0,2},{1,3},{2,0},{3,1},{4,6},{5,7},{6,4},{7,5},{8,10},{9,11},{10,... | collective-permute-start | bytes 73736 | tf_op jit(solution)/shard_map/ppermute | solution.py:432
  34.3 3.8 %collective-permute-start.11 = (f32[48,128]{1,0:T(8,128)S(1)}, f32[48,128]{1,0:T(8,128)S(1)}, u32[]{:S(2)}, u32[]{:S(2)}) collective-permute-start(f32[48,128]{1,0:T(8,128)S(1)} %get-tuple-element.64.o2), channel_id=1, source_target_pairs={{0,8},{8,0},{16,24},{24,16},{1,9},{9,1},{17,25},{25,17},{2,10},{10... | collective-permute-start | bytes 73736 | tf_op jit(solution)/shard_map/ppermute | solution.py:432
  35.7 2.4 %collective-permute-start.12 = (f32[48,128]{1,0:T(8,128)S(1)}, f32[48,128]{1,0:T(8,128)S(1)}, u32[]{:S(2)}, u32[]{:S(2)}) collective-permute-start(f32[48,128]{1,0:T(8,128)S(1)} %get-tuple-element.65.o3), channel_id=1, source_target_pairs={{0,1},{1,0},{2,3},{3,2},{4,5},{5,4},{6,7},{7,6},{8,9},{9,8},{10,11... | collective-permute-start | bytes 73736 | tf_op jit(solution)/shard_map/ppermute | solution.py:432
  39.0 2.8 %collective-permute-start.16 = (f32[48,128]{1,0:T(8,128)S(1)}, f32[48,128]{1,0:T(8,128)S(1)}, u32[]{:S(2)}, u32[]{:S(2)}) collective-permute-start(f32[48,128]{1,0:T(8,128)S(1)} %get-tuple-element.73.o3), channel_id=1, source_target_pairs={{0,1},{1,0},{2,3},{3,2},{4,5},{5,4},{6,7},{7,6},{8,9},{9,8},{10,11... | collective-permute-start | bytes 73736 | tf_op jit(solution)/shard_map/ppermute | solution.py:432
  39.0 5.0 %collective-permute-start.13 = (f32[48,128]{1,0:T(8,128)S(1)}, f32[48,128]{1,0:T(8,128)S(1)}, u32[]{:S(2)}, u32[]{:S(2)}) collective-permute-start(f32[48,128]{1,0:T(8,128)S(1)} %get-tuple-element.70.o0), channel_id=1, source_target_pairs={{0,4},{1,5},{2,6},{3,7},{4,0},{5,1},{6,2},{7,3},{8,12},{9,13},{10,... | collective-permute-start | bytes 73736 | tf_op jit(solution)/shard_map/ppermute | solution.py:432
  39.6 4.4 %collective-permute-start.14 = (f32[48,128]{1,0:T(8,128)S(1)}, f32[48,128]{1,0:T(8,128)S(1)}, u32[]{:S(2)}, u32[]{:S(2)}) collective-permute-start(f32[48,128]{1,0:T(8,128)S(1)} %get-tuple-element.71.o1), channel_id=1, source_target_pairs={{0,2},{1,3},{2,0},{3,1},{4,6},{5,7},{6,4},{7,5},{8,10},{9,11},{10,... | collective-permute-start | bytes 73736 | tf_op jit(solution)/shard_map/ppermute | solution.py:432
  40.2 3.8 %collective-permute-start.15 = (f32[48,128]{1,0:T(8,128)S(1)}, f32[48,128]{1,0:T(8,128)S(1)}, u32[]{:S(2)}, u32[]{:S(2)}) collective-permute-start(f32[48,128]{1,0:T(8,128)S(1)} %get-tuple-element.72.o2), channel_id=1, source_target_pairs={{0,8},{8,0},{16,24},{24,16},{1,9},{9,1},{17,25},{25,17},{2,10},{10... | collective-permute-start | bytes 73736 | tf_op jit(solution)/shard_map/ppermute | solution.py:432
  41.7 17.1 %collective-permute-start.21 = (f32[256,128]{1,0:T(8,128)S(1)}, f32[256,128]{1,0:T(8,128)S(1)}, u32[]{:S(2)}, u32[]{:S(2)}) collective-permute-start(f32[256,128]{1,0:T(8,128)S(1)} %behind.3), channel_id=1, source_target_pairs={{0,16},{8,24},{16,0},{24,8},{1,17},{9,25},{17,1},{25,9},{2,18},{10... | collective-permute-start | bytes 393224 | tf_op jit(solution)/shard_map/ppermute | solution.py:432
  45.3 13.6 %all-to-all-start.2 = ((f32[32,4,128]{2,1,0:T(4,128)}), f32[32,4,128]{2,1,0:T(4,128)S(1)}, u32[]{:S(2)}, u32[]{:S(2)}) async-start(f32[32,4,128]{2,1,0:T(4,128)} %bitcast.10), calls=%async_computation.2 | async-start | bytes 131072 | tf_op jit(solution)/shard_map/all_to_all | solution.py:450
  50.8 5.7 %collective-permute-start.17 = (f32[48,128]{1,0:T(8,128)S(1)}, f32[48,128]{1,0:T(8,128)S(1)}, u32[]{:S(2)}, u32[]{:S(2)}) collective-permute-start(f32[48,128]{1,0:T(8,128)S(1)} %get-tuple-element.76.o0), channel_id=1, source_target_pairs={{0,4},{1,5},{2,6},{3,7},{4,0},{5,1},{6,2},{7,3},{8,12},{9,13},{10,... | collective-permute-start | bytes 73736 | tf_op jit(solution)/shard_map/ppermute | solution.py:432
  53.5 3.8 %collective-permute-start.18 = (f32[48,128]{1,0:T(8,128)S(1)}, f32[48,128]{1,0:T(8,128)S(1)}, u32[]{:S(2)}, u32[]{:S(2)}) collective-permute-start(f32[48,128]{1,0:T(8,128)S(1)} %get-tuple-element.77.o1), channel_id=1, source_target_pairs={{0,2},{1,3},{2,0},{3,1},{4,6},{5,7},{6,4},{7,5},{8,10},{9,11},{10,... | collective-permute-start | bytes 73736 | tf_op jit(solution)/shard_map/ppermute | solution.py:432
  55.0 3.8 %collective-permute-start.19 = (f32[48,128]{1,0:T(8,128)S(1)}, f32[48,128]{1,0:T(8,128)S(1)}, u32[]{:S(2)}, u32[]{:S(2)}) collective-permute-start(f32[48,128]{1,0:T(8,128)S(1)} %get-tuple-element.78.o2), channel_id=1, source_target_pairs={{0,8},{8,0},{16,24},{24,16},{1,9},{9,1},{17,25},{25,17},{2,10},{10... | collective-permute-start | bytes 73736 | tf_op jit(solution)/shard_map/ppermute | solution.py:432
  56.5 2.4 %collective-permute-start.20 = (f32[48,128]{1,0:T(8,128)S(1)}, f32[48,128]{1,0:T(8,128)S(1)}, u32[]{:S(2)}, u32[]{:S(2)}) collective-permute-start(f32[48,128]{1,0:T(8,128)S(1)} %get-tuple-element.79.o3), channel_id=1, source_target_pairs={{0,1},{1,0},{2,3},{3,2},{4,5},{5,4},{6,7},{7,6},{8,9},{9,8},{10,11... | collective-permute-start | bytes 73736 | tf_op jit(solution)/shard_map/ppermute | solution.py:432

commit v8 on v7

--- a/solution.py
+++ b/solution.py
@@ -320,18 +320,22 @@
     copy.wait()
 
 
+def second_coarse(received, corner_map, spread, total_out, field_out):
+    n_load = field_out.shape[0]
+    total_out[...] = total_of(received)
+    coarse = coarse_of(*two_groups(received, spread.shape[1] // 4, n_load), spread[...])
+    field_out[...] = by_map(coarse, corner_map[...], NN)
+
+
 def second_image(
-    received, o0, o1, o2, o3, a0, a1, a2, a3, flexed, zold, low, resid, vectors, corner_map, spread, flex,
-    z_out, step_out, sums_out, total_out, *wins,
+    total, field, o0, o1, o2, o3, a0, a1, a2, a3, flexed, zold, low, resid, vectors, flex,
+    z_out, step_out, sums_out, *wins,
 ):
     n_load, dofs = resid.shape
     sign, sign_mask = vectors[0:1, :], vectors[2:3, :]
-    total = total_of(received)
-    total_out[...] = total
-    rz, curve, _, _ = sums_of(total, n_load)
+    rz, curve, _, _ = sums_of(total[...], n_load)
     alpha = rz / curve
-    coarse = coarse_of(*two_groups(received, spread.shape[1] // 4, n_load), spread[...])
-    step = jump([o0, o1, o2, o3], [a0, a1, a2, a3], n_load, sign_mask) + by_map(coarse, corner_map[...], NN)
+    step = jump([o0, o1, o2, o3], [a0, a1, a2, a3], n_load, sign_mask) + field[...]
     step = alpha * step
     step_out[...] = step
     zvec = zold[...] + low[...].astype(F32) - step
@@ -364,21 +368,16 @@
     copy.wait()
 
 
-def finish(
-    received, o0, o1, o2, o3, a0, a1, a2, a3, before, zold, znew, step, vectors, corner_map, spread, *rest
-):
-    inverses, (mult_hbm, direction_hbm, mult, direction_out, sems) = rest[:-5], rest[-5:]
-    n_load, dofs = zold.shape
-    sign_mask = vectors[2:3, :]
+def third_coarse(received, before, zold, znew, step, corner_map, spread, *rest):
+    inverses, (mult_out, base_out, gamma_out) = rest[:-3], rest[-3:]
+    n_load = zold.shape[0]
     rz0, curve0, _, _ = sums_of(before[...], n_load)
     rz1, curve, mixed, square = sums_of(total_of(received), n_load)
     alpha = rz0 / curve0
     beta = rz1 / rz0
     gamma = rz1 / (curve + 2.0 * beta * mixed + beta * beta * rz0)
     direction = znew[...] + beta * zold[...]
-    mult[...] = alpha * (zold[...] + gamma * direction)
-    copies = [pltpu.make_async_copy(a, b, sems.at[i]) for i, (a, b) in enumerate([(mult, mult_hbm), (direction_out, direction_hbm)])]
-    copies[0].start()
+    mult_out[...] = alpha * (zold[...] + gamma * direction)
     n = spread.shape[1]
     height = n * n // LANES
     corners = two_groups(received, n // 4, n_load)
@@ -392,12 +391,21 @@
             index += 1
     rz2 = square + 2.0 * beta * (mixed - curve) + beta * beta * (rz0 - mixed)
     rz2 = rz1 - 2.0 * gamma * (curve + beta * mixed) + gamma * gamma * rz2
-    coarse = coarse_of(*corners[:2], spread[...])
-    image = jump([o0, o1, o2, o3], [a0, a1, a2, a3], n_load, sign_mask) + by_map(coarse, corner_map[...], NN)
-    direction_out[...] = znew[...] - gamma * (image + beta * step[...]) + (rz2 / rz1) * direction
-    copies[1].start()
-    copies[0].wait()
-    copies[1].wait()
+    field = by_map(coarse_of(*corners[:2], spread[...]), corner_map[...], NN)
+    base_out[...] = znew[...] - gamma * (field + beta * step[...]) + (rz2 / rz1) * direction
+    gamma_out[...] = jnp.broadcast_to(gamma, gamma_out.shape)
+
+
+def finish(o0, o1, o2, o3, a0, a1, a2, a3, base, gamma, mult, vectors, mult_hbm, direction_hbm, out, sems):
+    n_load = base.shape[0]
+    first = pltpu.make_async_copy(mult, mult_hbm, sems.at[0])
+    first.start()
+    jumped = jump([o0, o1, o2, o3], [a0, a1, a2, a3], n_load, vectors[2:3, :])
+    out[...] = base[...] - gamma[:, :1] * jumped
+    second = pltpu.make_async_copy(out, direction_hbm, sems.at[1])
+    second.start()
+    first.wait()
+    second.wait()
 
 
 def call(name, kernel, args, outs, scratch=(), in_place=(), out_place=(), limit=None):
@@ -495,9 +503,10 @@
     )
     received = send_all(sent_rows)
     came = exchange(own)
-    znew, step, sums, before, *own = call(
-        "image2", second_image, [received] + own + came + [flexed, zold, low, resid, vectors, corner_map, spread, flex],
-        [field, field, total, total] + faces(n_load),
+    before, coarse = call("coarse2", second_coarse, [received, corner_map, spread], [total, field])
+    znew, step, sums, *own = call(
+        "image2", second_image, [before, coarse] + own + came + [flexed, zold, low, resid, vectors, flex],
+        [field, field, total] + faces(n_load),
     )
     came = exchange(own)
     inverses = [inverse]
@@ -512,10 +521,13 @@
     )
     received = send_all(sent_rows)
     came = exchange(own)
+    mult, base, gamma = call(
+        "coarse3", third_coarse, [received, before, zold, znew, step, corner_map, spread] + inverses,
+        [field, field, ((n_load, LANES), F32)],
+    )
     mult, direction = call(
-        "finish", finish,
-        [received] + own + came + [before, zold, znew, step, vectors, corner_map, spread] + inverses, [field, field],
-        [pltpu.VMEM(rhs.shape, F32)] * 2 + [pltpu.SemaphoreType.DMA((2,))], out_place=[0, 1],
+        "finish", finish, own + came + [base, gamma, mult, vectors], [field, field],
+        [pltpu.VMEM(rhs.shape, F32), pltpu.SemaphoreType.DMA((2,))], out_place=[0, 1],
     )
     return (mult[None, None], direction[None, None])
 

time: 60.4 us -> 59.8 us (0.990)
  waiting for transfers between devices: 11.6 us -> 10.7 us
    ppermute x22, waiting for transfers between devices: 10.9 us -> 6.26 us  [swap(): lax.ppermute(block, axis, [(i, i ^ distance) for i in range(count) if i ^...]
    all_to_all x2, waiting for transfers between devices: 0.01 us -> 3.75 us  [send_all(): lax.all_to_all(blocks, ('grp', 'sub'), 0, 0, tiled=True).reshape(rows.shape)]
    pallas_call x6 -> x8, Pallas kernels: 7.07 us -> 7.3 us  [call(): pl.pallas_call(kernel, out_shape=shapes, in_specs=[pl.BlockSpec(memory_sp...]
  transfers between devices with their start and end apart: 25 -> 25, of which waited for: 10 -> 8; matrix products, arithmetic and copies ran while one was open for 0% -> 0% of each run, Pallas kernels for 3% -> 5%
where the time goes in v8:
time: 59.8 us; the launch traced here: 59.5 us
  starting transfers between devices  39.6 us (66%)
  waiting for transfers between devices  10.7 us (18%)
  Pallas kernels  7.3 us (12%)
  other arithmetic  1 us (2%)
  between operations  0.83 us (1%)
    ppermute x22, starting transfers between devices, swap(): lax.ppermute(block, axis, [(i, i ^ distance) for i in range(count) if i ^...  27.7 us
    all_to_all x2, starting transfers between devices, send_all(): lax.all_to_all(blocks, ('grp', 'sub'), 0, 0, tiled=True).reshape(rows.shape)  8.05 us
    pallas_call x8, Pallas kernels, call(): pl.pallas_call(kernel, out_shape=shapes, in_specs=[pl.BlockSpec(memory_sp...  7.3 us
    ppermute x22, waiting for transfers between devices, swap(): lax.ppermute(block, axis, [(i, i ^ distance) for i in range(count) if i ^...  6.26 us
    all_to_all x1, starting transfers between devices, send_pair(): lax.all_to_all(blocks, ('grp', 'sub'), 0, 0, tiled=True, axis_index_group...  3.88 us
    all_to_all x2, waiting for transfers between devices, send_all(): lax.all_to_all(blocks, ('grp', 'sub'), 0, 0, tiled=True).reshape(rows.shape)  3.75 us
  transfers between devices with their start and end apart: 25, of which 8 were waited for; matrix products, arithmetic and copies ran while one was open for 0% of the time, Pallas kernels for 5%

profile of v8, /device:TPU:0, one launch (start us, length us, event | category | flops | bytes accessed | tf_op | source)
XLA Modules:
  0.0 59.5 jit_solution(2345420353864939376)
XLA Ops:
  0.6 0.0 copy-start.1
  0.6 1.0 %convert_add_fusion.small = f32[104,128]{1,0:T(8,128)S(1)} fusion(s32[1,12]{1,0:T(1,128)} %bitcast.24, s32[1,4]{1,0:T(1,128)} %bitcast.25, f32[96,96]{1,0:T(8,128)} %bitcast.23), kind=kLoop, calls=%fused_computation | loop fusion | flops 53248 | bytes 90176 | tf_op jit(solution)/shard_map/add | solution.py:480
  1.6 1.8 %start.1 = (f32[64,128]{1,0:T(8,128)}, f32[8,768]{1,0:T(8,128)S(1)}, bf16[16,768]{1,0:T(8,128)(2,1)S(1)}, f32[32,768]{1,0:T(8,128)S(1)}, f32[64,128]{1,0:T(8,128...) custom-call(f32[32,768]{1,0:T(8,128)} %bitcast.22, ...), custom_call_target="tpu_custom_call" | custom-call | flops 40000000 | bytes 1867776 | tf_op jit(solution)/shard_map/start/pallas_call | solution.py:414
  3.5 0.0 copy-start
  3.5 4.1 %collective-permute-start = (f32[128,128]{1,0:T(8,128)S(1)}, f32[128,128]{1,0:T(8,128)S(1)}, u32[]{:S(2)}, u32[]{:S(2)}) collective-permute-start(f32[128,128]{1,0:T(8,128)S(1)} %get-tuple-element.49.o0), channel_id=1, source_target_pairs={{0,4},{1,5},{2,6},{3,7},{4,0},{5,1},{6,2},{7,3},{8,12},{9,13},{10,... | collective-permute-start | bytes 196616 | tf_op jit(solution)/shard_map/ppermute | solution.py:440
  7.6 3.9 %all-to-all-start = ((f32[16,4,128]{2,1,0:T(4,128)}), f32[16,4,128]{2,1,0:T(4,128)S(1)}, u32[]{:S(2)}, u32[]{:S(2)}) async-start(f32[16,4,128]{2,1,0:T(4,128)} %bitcast.5), calls=%async_computation | async-start | bytes 65536 | tf_op jit(solution)/shard_map/all_to_all | solution.py:452
  11.5 0.4 collective-permute-start.3
  11.9 1.7 %collective-permute-start.2 = (f32[72,128]{1,0:T(8,128)S(1)}, f32[72,128]{1,0:T(8,128)S(1)}, u32[]{:S(2)}, u32[]{:S(2)}) collective-permute-start(f32[72,128]{1,0:T(8,128)S(1)} %get-tuple-element.51.o2), channel_id=1, source_target_pairs={{0,8},{8,0},{16,24},{24,16},{1,9},{9,1},{17,25},{25,17},{2,10},{10... | collective-permute-start | bytes 110600 | tf_op jit(solution)/shard_map/ppermute | solution.py:440
  13.6 1.5 %collective-permute-start.1 = (f32[56,128]{1,0:T(8,128)S(1)}, f32[56,128]{1,0:T(8,128)S(1)}, u32[]{:S(2)}, u32[]{:S(2)}) collective-permute-start(f32[56,128]{1,0:T(8,128)S(1)} %get-tuple-element.50.o1), channel_id=1, source_target_pairs={{0,2},{1,3},{2,0},{3,1},{4,6},{5,7},{6,4},{7,5},{8,10},{9,11},{10,... | collective-permute-start | bytes 86024 | tf_op jit(solution)/shard_map/ppermute | solution.py:440
  15.1 0.0 collective-permute-done.3.a3.other_ref
  15.1 0.6 collective-permute-start.8
  15.6 1.9 %collective-permute-done.1.a1 = f32[56,128]{1,0:T(8,128)S(1)} collective-permute-done((f32[56,128]{1,0:T(8,128)S(1)}, f32[56,128]{1,0:T(8,128)S(1)}, u32[]{:S(2)}, u32[]{:S(2)}) %collective-permute-start.1) | collective-permute-done | bytes 28704 | tf_op jit(solution)/shard_map/ppermute | solution.py:440
  17.5 0.0 collective-permute-done.2.a2
  17.5 0.7 %all-to-all-done = f32[16,4,128]{2,1,0:T(4,128)S(1)} async-done(((f32[16,4,128]{2,1,0:T(4,128)}), f32[16,4,128]{2,1,0:T(4,128)S(1)}, u32[]{:S(2)}, u32[]{:S(2)}) %all-to-all-start) | async-done | bytes 32800 | tf_op jit(solution)/shard_map/all_to_all | solution.py:452
  18.2 0.0 collective-permute-done.a0
  18.2 0.0 copy-done.1
  18.2 0.8 %image1.1 = (f32[32,768]{1,0:T(8,128)S(1)}, f32[8,128]{1,0:T(8,128)S(1)}, bf16[80,768]{1,0:T(8,128)(2,1)S(1)}, f32[80,128]{1,0:T(8,128)S(1)}, f32[96,128]{1,0:T(...) custom-call(f32[64,128]{1,0:T(8,128)S(1)} %bitcast.21, ...), custom_call_target="tpu_custom_call" | custom-call | flops 40000000 | bytes 2273280 | tf_op jit(solution)/shard_map/image1/pallas_call | solution.py:414
  19.1 1.7 %collective-permute-start.4 = (f32[96,128]{1,0:T(8,128)S(1)}, f32[96,128]{1,0:T(8,128)S(1)}, u32[]{:S(2)}, u32[]{:S(2)}) collective-permute-start(f32[96,128]{1,0:T(8,128)S(1)} %get-tuple-element.58.o0), channel_id=1, source_target_pairs={{0,4},{1,5},{2,6},{3,7},{4,0},{5,1},{6,2},{7,3},{8,12},{9,13},{10,... | collective-permute-start | bytes 147464 | tf_op jit(solution)/shard_map/ppermute | solution.py:440
  20.8 1.5 %collective-permute-start.5 = (f32[96,128]{1,0:T(8,128)S(1)}, f32[96,128]{1,0:T(8,128)S(1)}, u32[]{:S(2)}, u32[]{:S(2)}) collective-permute-start(f32[96,128]{1,0:T(8,128)S(1)} %get-tuple-element.59.o1), channel_id=1, source_target_pairs={{0,2},{1,3},{2,0},{3,1},{4,6},{5,7},{6,4},{7,5},{8,10},{9,11},{10,... | collective-permute-start | bytes 147464 | tf_op jit(solution)/shard_map/ppermute | solution.py:440
  22.2 0.6 collective-permute-start.6
  22.8 0.0 collective-permute-start.7
  22.8 0.0 collective-permute-done.8.other
  22.8 1.9 %collective-permute-done.4.a0 = f32[96,128]{1,0:T(8,128)S(1)} collective-permute-done((f32[96,128]{1,0:T(8,128)S(1)}, f32[96,128]{1,0:T(8,128)S(1)}, u32[]{:S(2)}, u32[]{:S(2)}) %collective-permute-start.4) | collective-permute-done | bytes 49184 | tf_op jit(solution)/shard_map/ppermute | solution.py:440
  24.7 0.4 collective-permute-done.5.a1
  25.0 1.3 %collective-permute-done.6.a2 = f32[96,128]{1,0:T(8,128)S(1)} collective-permute-done((f32[96,128]{1,0:T(8,128)S(1)}, f32[96,128]{1,0:T(8,128)S(1)}, u32[]{:S(2)}, u32[]{:S(2)}) %collective-permute-start.6) | collective-permute-done | bytes 49184 | tf_op jit(solution)/shard_map/ppermute | solution.py:440
  26.3 0.0 collective-permute-done.7.a3
  26.3 0.0 copy-done
  26.3 1.0 %local2.1 = (f32[32,768]{1,0:T(8,128)S(1)}, bf16[32,768]{1,0:T(8,128)(2,1)S(1)}, f32[256,128]{1,0:T(8,128)S(1)}, f32[128,128]{1,0:T(8,128)}, f32[48,128]{1,0:T(8...) custom-call(f32[96,128]{1,0:T(8,128)S(1)} %get-tuple-element.58.o0, ...), custom_call_target="tpu_custom_call" | custom-call | flops 40000000 | bytes 2297856 | tf_op jit(solution)/shard_map/local2/pallas_call | solution.py:414
  27.4 2.6 %all-to-all-start.1 = ((f32[32,4,128]{2,1,0:T(4,128)}), f32[32,4,128]{2,1,0:T(4,128)S(1)}, u32[]{:S(2)}, u32[]{:S(2)}) async-start(f32[32,4,128]{2,1,0:T(4,128)} %bitcast.8), calls=%async_computation.1 | async-start | bytes 131072 | tf_op jit(solution)/shard_map/all_to_all | solution.py:458
  30.0 2.7 %collective-permute-start.9 = (f32[48,128]{1,0:T(8,128)S(1)}, f32[48,128]{1,0:T(8,128)S(1)}, u32[]{:S(2)}, u32[]{:S(2)}) collective-permute-start(f32[48,128]{1,0:T(8,128)S(1)} %get-tuple-element.69.o0), channel_id=1, source_target_pairs={{0,4},{1,5},{2,6},{3,7},{4,0},{5,1},{6,2},{7,3},{8,12},{9,13},{10,... | collective-permute-start | bytes 73736 | tf_op jit(solution)/shard_map/ppermute | solution.py:440
  32.7 1.5 %collective-permute-start.10 = (f32[48,128]{1,0:T(8,128)S(1)}, f32[48,128]{1,0:T(8,128)S(1)}, u32[]{:S(2)}, u32[]{:S(2)}) collective-permute-start(f32[48,128]{1,0:T(8,128)S(1)} %get-tuple-element.70.o1), channel_id=1, source_target_pairs={{0,2},{1,3},{2,0},{3,1},{4,6},{5,7},{6,4},{7,5},{8,10},{9,11},{10,... | collective-permute-start | bytes 73736 | tf_op jit(solution)/shard_map/ppermute | solution.py:440
  34.3 1.5 %collective-permute-start.11 = (f32[48,128]{1,0:T(8,128)S(1)}, f32[48,128]{1,0:T(8,128)S(1)}, u32[]{:S(2)}, u32[]{:S(2)}) collective-permute-start(f32[48,128]{1,0:T(8,128)S(1)} %get-tuple-element.71.o2), channel_id=1, source_target_pairs={{0,8},{8,0},{16,24},{24,16},{1,9},{9,1},{17,25},{25,17},{2,10},{10... | collective-permute-start | bytes 73736 | tf_op jit(solution)/shard_map/ppermute | solution.py:440
  35.7 0.0 collective-permute-start.12
  35.7 1.9 %all-to-all-done.1 = f32[32,4,128]{2,1,0:T(4,128)S(1)} async-done(((f32[32,4,128]{2,1,0:T(4,128)}), f32[32,4,128]{2,1,0:T(4,128)S(1)}, u32[]{:S(2)}, u32[]{:S(2)}) %all-to-all-start.1) | async-done | bytes 65568 | tf_op jit(solution)/shard_map/all_to_all | solution.py:458
  37.6 0.4 coarse2.1
  38.1 0.0 collective-permute-done.9.a0
  38.1 0.0 collective-permute-done.10.a1
  38.1 0.0 collective-permute-done.11.a2
  38.1 0.0 collective-permute-done.12.a3
  38.1 0.6 image2.1
  38.7 0.4 collective-permute-start.16
  39.1 0.3 collective-permute-start.13
  39.3 0.7 %collective-permute-start.14 = (f32[48,128]{1,0:T(8,128)S(1)}, f32[48,128]{1,0:T(8,128)S(1)}, u32[]{:S(2)}, u32[]{:S(2)}) collective-permute-start(f32[48,128]{1,0:T(8,128)S(1)} %get-tuple-element.77.o1), channel_id=1, source_target_pairs={{0,2},{1,3},{2,0},{3,1},{4,6},{5,7},{6,4},{7,5},{8,10},{9,11},{10,... | collective-permute-start | bytes 73736 | tf_op jit(solution)/shard_map/ppermute | solution.py:440
  40.0 1.4 %collective-permute-start.15 = (f32[48,128]{1,0:T(8,128)S(1)}, f32[48,128]{1,0:T(8,128)S(1)}, u32[]{:S(2)}, u32[]{:S(2)}) collective-permute-start(f32[48,128]{1,0:T(8,128)S(1)} %get-tuple-element.78.o2), channel_id=1, source_target_pairs={{0,8},{8,0},{16,24},{24,16},{1,9},{9,1},{17,25},{25,17},{2,10},{10... | collective-permute-start | bytes 73736 | tf_op jit(solution)/shard_map/ppermute | solution.py:440
  41.4 0.0 collective-permute-done.16.a3.other_ref
  41.4 1.6 %collective-permute-start.21 = (f32[256,128]{1,0:T(8,128)S(1)}, f32[256,128]{1,0:T(8,128)S(1)}, u32[]{:S(2)}, u32[]{:S(2)}) collective-permute-start(f32[256,128]{1,0:T(8,128)S(1)} %behind.3), channel_id=1, source_target_pairs={{0,16},{8,24},{16,0},{24,8},{1,17},{9,25},{17,1},{25,9},{2,18},{10... | collective-permute-start | bytes 393224 | tf_op jit(solution)/shard_map/ppermute | solution.py:440
  43.0 0.8 %collective-permute-done.13.a0 = f32[48,128]{1,0:T(8,128)S(1)} collective-permute-done((f32[48,128]{1,0:T(8,128)S(1)}, f32[48,128]{1,0:T(8,128)S(1)}, u32[]{:S(2)}, u32[]{:S(2)}) %collective-permute-start.13) | collective-permute-done | bytes 24608 | tf_op jit(solution)/shard_map/ppermute | solution.py:440
  43.8 0.0 collective-permute-done.14.a1
  43.8 0.0 collective-permute-done.15.a2
  43.8 1.2 %local3.1 = (f32[128,128]{1,0:T(8,128)}, f32[48,128]{1,0:T(8,128)S(1)}, f32[48,128]{1,0:T(8,128)S(1)}, f32[48,128]{1,0:T(8,128)S(1)}, f32[48,128]{1,0:T(8,128)S(1)}) custom-call(f32[48,128]{1,0:T(8,128)S(1)} %get-tuple-element.76.o0, f32[48,128]{1,0:T(8,128)S(1)} %get-tuple-element.77.o1, f32[48,128]{1,0:T(8,128)S(1)} %get-tuple-element.78.o2, ...), custom_call_target="tpu_custom_call" | custom-call | flops 40000000 | bytes 1691648 | tf_op jit(solution)/shard_map/local3/pallas_call | solution.py:414
  45.1 5.4 %all-to-all-start.2 = ((f32[32,4,128]{2,1,0:T(4,128)}), f32[32,4,128]{2,1,0:T(4,128)S(1)}, u32[]{:S(2)}, u32[]{:S(2)}) async-start(f32[32,4,128]{2,1,0:T(4,128)} %bitcast.10), calls=%async_computation.2 | async-start | bytes 131072 | tf_op jit(solution)/shard_map/all_to_all | solution.py:458
  50.5 2.7 %collective-permute-start.17 = (f32[48,128]{1,0:T(8,128)S(1)}, f32[48,128]{1,0:T(8,128)S(1)}, u32[]{:S(2)}, u32[]{:S(2)}) collective-permute-start(f32[48,128]{1,0:T(8,128)S(1)} %get-tuple-element.81.o0), channel_id=1, source_target_pairs={{0,4},{1,5},{2,6},{3,7},{4,0},{5,1},{6,2},{7,3},{8,12},{9,13},{10,... | collective-permute-start | bytes 73736 | tf_op jit(solution)/shard_map/ppermute | solution.py:440
  53.2 1.5 %collective-permute-start.18 = (f32[48,128]{1,0:T(8,128)S(1)}, f32[48,128]{1,0:T(8,128)S(1)}, u32[]{:S(2)}, u32[]{:S(2)}) collective-permute-start(f32[48,128]{1,0:T(8,128)S(1)} %get-tuple-element.82.o1), channel_id=1, source_target_pairs={{0,2},{1,3},{2,0},{3,1},{4,6},{5,7},{6,4},{7,5},{8,10},{9,11},{10,... | collective-permute-start | bytes 73736 | tf_op jit(solution)/shard_map/ppermute | solution.py:440
  54.8 1.5 %collective-permute-start.19 = (f32[48,128]{1,0:T(8,128)S(1)}, f32[48,128]{1,0:T(8,128)S(1)}, u32[]{:S(2)}, u32[]{:S(2)}) collective-permute-start(f32[48,128]{1,0:T(8,128)S(1)} %get-tuple-element.83.o2), channel_id=1, source_target_pairs={{0,8},{8,0},{16,24},{24,16},{1,9},{9,1},{17,25},{25,17},{2,10},{10... | collective-permute-start | bytes 73736 | tf_op jit(solution)/shard_map/ppermute | solution.py:440
  56.2 0.0 collective-permute-start.20
  56.2 1.9 %all-to-all-done.2 = f32[32,4,128]{2,1,0:T(4,128)S(1)} async-done(((f32[32,4,128]{2,1,0:T(4,128)}), f32[32,4,128]{2,1,0:T(4,128)S(1)}, u32[]{:S(2)}, u32[]{:S(2)}) %all-to-all-start.2) | async-done | bytes 65568 | tf_op jit(solution)/shard_map/all_to_all | solution.py:458
  58.1 0.0 collective-permute-done.21.rest_1_
  58.1 0.6 coarse3.1
  58.7 0.0 collective-permute-done.17.a0
  58.7 0.0 collective-permute-done.18.a1
  58.7 0.0 collective-permute-done.19.a2
  58.7 0.0 collective-permute-done.20.a3
  58.7 0.8 %finish.1 = (f32[32,768]{1,0:T(8,128)}, f32[32,768]{1,0:T(8,128)}) custom-call(f32[48,128]{1,0:T(8,128)S(1)} %get-tuple-element.81.o0, f32[48,128]{1,0:T(8,128)S(1)} %get-tuple-element.82.o1, f32[48,128]{1,0:T(8,128)S(1)} %get-tuple-element.83.o2, f32[48,128]{1,0:T(8,128)S(1)} %get-tuple-element.84.o3, f32[48,128]{1,0:T(8,128)S(1)} %collective-permute-done.17.a0, ...), custom_call_target="tpu_custom_call" | custom-call | flops 40000000 | bytes 630784 | tf_op jit(solution)/shard_map/finish/pallas_call | solution.py:414
  (3 shorter events, 0.0 us)
Async XLA Ops:
  0.6 17.6 %copy-start.1 = (bf16[1,1,768,768]{3,2,1,0:T(8,128)(2,1)S(1)}, bf16[1,1,768,768]{3,2,1,0:T(8,128)(2,1)}, u32[]{:S(2)}) copy-start(bf16[1,1,768,768]{3,2,1,0:T(8,128)(2,1)} %param.8) | copy-start | bytes 3538948
  3.5 22.8 %copy-start = (bf16[1,1,768,768]{3,2,1,0:T(8,128)(2,1)S(1)}, bf16[1,1,768,768]{3,2,1,0:T(8,128)(2,1)}, u32[]{:S(2)}) copy-start(bf16[1,1,768,768]{3,2,1,0:T(8,128)(2,1)} %param.7) | copy-start | bytes 3538948
  3.5 14.7 %collective-permute-start = (f32[128,128]{1,0:T(8,128)S(1)}, f32[128,128]{1,0:T(8,128)S(1)}, u32[]{:S(2)}, u32[]{:S(2)}) collective-permute-start(f32[128,128]{1,0:T(8,128)S(1)} %get-tuple-element.49.o0), channel_id=1, source_target_pairs={{0,4},{1,5},{2,6},{3,7},{4,0},{5,1},{6,2},{7,3},{8,12},{9,13},{10,... | collective-permute-start | bytes 196616 | tf_op jit(solution)/shard_map/ppermute | solution.py:440
  7.6 10.6 %all-to-all-start = ((f32[16,4,128]{2,1,0:T(4,128)}), f32[16,4,128]{2,1,0:T(4,128)S(1)}, u32[]{:S(2)}, u32[]{:S(2)}) async-start(f32[16,4,128]{2,1,0:T(4,128)} %bitcast.5), calls=%async_computation | async-start | bytes 65536 | tf_op jit(solution)/shard_map/all_to_all | solution.py:452
  11.5 3.6 %collective-permute-start.3 = (f32[56,128]{1,0:T(8,128)S(1)}, f32[56,128]{1,0:T(8,128)S(1)}, u32[]{:S(2)}, u32[]{:S(2)}) collective-permute-start(f32[56,128]{1,0:T(8,128)S(1)} %get-tuple-element.52.o3), channel_id=1, source_target_pairs={{0,1},{1,0},{2,3},{3,2},{4,5},{5,4},{6,7},{7,6},{8,9},{9,8},{10,11... | collective-permute-start | bytes 86024 | tf_op jit(solution)/shard_map/ppermute | solution.py:440
  11.9 5.6 %collective-permute-start.2 = (f32[72,128]{1,0:T(8,128)S(1)}, f32[72,128]{1,0:T(8,128)S(1)}, u32[]{:S(2)}, u32[]{:S(2)}) collective-permute-start(f32[72,128]{1,0:T(8,128)S(1)} %get-tuple-element.51.o2), channel_id=1, source_target_pairs={{0,8},{8,0},{16,24},{24,16},{1,9},{9,1},{17,25},{25,17},{2,10},{10... | collective-permute-start | bytes 110600 | tf_op jit(solution)/shard_map/ppermute | solution.py:440
  13.6 3.9 %collective-permute-start.1 = (f32[56,128]{1,0:T(8,128)S(1)}, f32[56,128]{1,0:T(8,128)S(1)}, u32[]{:S(2)}, u32[]{:S(2)}) collective-permute-start(f32[56,128]{1,0:T(8,128)S(1)} %get-tuple-element.50.o1), channel_id=1, source_target_pairs={{0,2},{1,3},{2,0},{3,1},{4,6},{5,7},{6,4},{7,5},{8,10},{9,11},{10,... | collective-permute-start | bytes 86024 | tf_op jit(solution)/shard_map/ppermute | solution.py:440
  15.1 7.7 %collective-permute-start.8 = (f32[128,128]{1,0:T(8,128)S(1)}, f32[128,128]{1,0:T(8,128)S(1)}, u32[]{:S(2)}, u32[]{:S(2)}) collective-permute-start(f32[128,128]{1,0:T(8,128)S(1)} %behind.2.inverse), channel_id=1, source_target_pairs={{0,8},{8,0},{16,24},{24,16},{1,9},{9,1},{17,25},{25,17},{2,10},{10... | collective-permute-start | bytes 196616 | tf_op jit(solution)/shard_map/ppermute | solution.py:440
  19.1 5.6 %collective-permute-start.4 = (f32[96,128]{1,0:T(8,128)S(1)}, f32[96,128]{1,0:T(8,128)S(1)}, u32[]{:S(2)}, u32[]{:S(2)}) collective-permute-start(f32[96,128]{1,0:T(8,128)S(1)} %get-tuple-element.58.o0), channel_id=1, source_target_pairs={{0,4},{1,5},{2,6},{3,7},{4,0},{5,1},{6,2},{7,3},{8,12},{9,13},{10,... | collective-permute-start | bytes 147464 | tf_op jit(solution)/shard_map/ppermute | solution.py:440
  20.8 4.3 %collective-permute-start.5 = (f32[96,128]{1,0:T(8,128)S(1)}, f32[96,128]{1,0:T(8,128)S(1)}, u32[]{:S(2)}, u32[]{:S(2)}) collective-permute-start(f32[96,128]{1,0:T(8,128)S(1)} %get-tuple-element.59.o1), channel_id=1, source_target_pairs={{0,2},{1,3},{2,0},{3,1},{4,6},{5,7},{6,4},{7,5},{8,10},{9,11},{10,... | collective-permute-start | bytes 147464 | tf_op jit(solution)/shard_map/ppermute | solution.py:440
  22.2 4.1 %collective-permute-start.6 = (f32[96,128]{1,0:T(8,128)S(1)}, f32[96,128]{1,0:T(8,128)S(1)}, u32[]{:S(2)}, u32[]{:S(2)}) collective-permute-start(f32[96,128]{1,0:T(8,128)S(1)} %get-tuple-element.60.o2), channel_id=1, source_target_pairs={{0,8},{8,0},{16,24},{24,16},{1,9},{9,1},{17,25},{25,17},{2,10},{10... | collective-permute-start | bytes 147464 | tf_op jit(solution)/shard_map/ppermute | solution.py:440
  22.8 3.5 %collective-permute-start.7 = (f32[96,128]{1,0:T(8,128)S(1)}, f32[96,128]{1,0:T(8,128)S(1)}, u32[]{:S(2)}, u32[]{:S(2)}) collective-permute-start(f32[96,128]{1,0:T(8,128)S(1)} %get-tuple-element.61.o3), channel_id=1, source_target_pairs={{0,1},{1,0},{2,3},{3,2},{4,5},{5,4},{6,7},{7,6},{8,9},{9,8},{10,11... | collective-permute-start | bytes 147464 | tf_op jit(solution)/shard_map/ppermute | solution.py:440
  27.4 10.2 %all-to-all-start.1 = ((f32[32,4,128]{2,1,0:T(4,128)}), f32[32,4,128]{2,1,0:T(4,128)S(1)}, u32[]{:S(2)}, u32[]{:S(2)}) async-start(f32[32,4,128]{2,1,0:T(4,128)} %bitcast.8), calls=%async_computation.1 | async-start | bytes 131072 | tf_op jit(solution)/shard_map/all_to_all | solution.py:458
  30.0 8.1 %collective-permute-start.9 = (f32[48,128]{1,0:T(8,128)S(1)}, f32[48,128]{1,0:T(8,128)S(1)}, u32[]{:S(2)}, u32[]{:S(2)}) collective-permute-start(f32[48,128]{1,0:T(8,128)S(1)} %get-tuple-element.69.o0), channel_id=1, source_target_pairs={{0,4},{1,5},{2,6},{3,7},{4,0},{5,1},{6,2},{7,3},{8,12},{9,13},{10,... | collective-permute-start | bytes 73736 | tf_op jit(solution)/shard_map/ppermute | solution.py:440
  32.7 5.3 %collective-permute-start.10 = (f32[48,128]{1,0:T(8,128)S(1)}, f32[48,128]{1,0:T(8,128)S(1)}, u32[]{:S(2)}, u32[]{:S(2)}) collective-permute-start(f32[48,128]{1,0:T(8,128)S(1)} %get-tuple-element.70.o1), channel_id=1, source_target_pairs={{0,2},{1,3},{2,0},{3,1},{4,6},{5,7},{6,4},{7,5},{8,10},{9,11},{10,... | collective-permute-start | bytes 73736 | tf_op jit(solution)/shard_map/ppermute | solution.py:440
  34.3 3.8 %collective-permute-start.11 = (f32[48,128]{1,0:T(8,128)S(1)}, f32[48,128]{1,0:T(8,128)S(1)}, u32[]{:S(2)}, u32[]{:S(2)}) collective-permute-start(f32[48,128]{1,0:T(8,128)S(1)} %get-tuple-element.71.o2), channel_id=1, source_target_pairs={{0,8},{8,0},{16,24},{24,16},{1,9},{9,1},{17,25},{25,17},{2,10},{10... | collective-permute-start | bytes 73736 | tf_op jit(solution)/shard_map/ppermute | solution.py:440
  35.7 2.4 %collective-permute-start.12 = (f32[48,128]{1,0:T(8,128)S(1)}, f32[48,128]{1,0:T(8,128)S(1)}, u32[]{:S(2)}, u32[]{:S(2)}) collective-permute-start(f32[48,128]{1,0:T(8,128)S(1)} %get-tuple-element.72.o3), channel_id=1, source_target_pairs={{0,1},{1,0},{2,3},{3,2},{4,5},{5,4},{6,7},{7,6},{8,9},{9,8},{10,11... | collective-permute-start | bytes 73736 | tf_op jit(solution)/shard_map/ppermute | solution.py:440
  38.7 2.7 %collective-permute-start.16 = (f32[48,128]{1,0:T(8,128)S(1)}, f32[48,128]{1,0:T(8,128)S(1)}, u32[]{:S(2)}, u32[]{:S(2)}) collective-permute-start(f32[48,128]{1,0:T(8,128)S(1)} %get-tuple-element.79.o3), channel_id=1, source_target_pairs={{0,1},{1,0},{2,3},{3,2},{4,5},{5,4},{6,7},{7,6},{8,9},{9,8},{10,11... | collective-permute-start | bytes 73736 | tf_op jit(solution)/shard_map/ppermute | solution.py:440
  39.1 4.7 %collective-permute-start.13 = (f32[48,128]{1,0:T(8,128)S(1)}, f32[48,128]{1,0:T(8,128)S(1)}, u32[]{:S(2)}, u32[]{:S(2)}) collective-permute-start(f32[48,128]{1,0:T(8,128)S(1)} %get-tuple-element.76.o0), channel_id=1, source_target_pairs={{0,4},{1,5},{2,6},{3,7},{4,0},{5,1},{6,2},{7,3},{8,12},{9,13},{10,... | collective-permute-start | bytes 73736 | tf_op jit(solution)/shard_map/ppermute | solution.py:440
  39.3 4.5 %collective-permute-start.14 = (f32[48,128]{1,0:T(8,128)S(1)}, f32[48,128]{1,0:T(8,128)S(1)}, u32[]{:S(2)}, u32[]{:S(2)}) collective-permute-start(f32[48,128]{1,0:T(8,128)S(1)} %get-tuple-element.77.o1), channel_id=1, source_target_pairs={{0,2},{1,3},{2,0},{3,1},{4,6},{5,7},{6,4},{7,5},{8,10},{9,11},{10,... | collective-permute-start | bytes 73736 | tf_op jit(solution)/shard_map/ppermute | solution.py:440
  40.0 3.8 %collective-permute-start.15 = (f32[48,128]{1,0:T(8,128)S(1)}, f32[48,128]{1,0:T(8,128)S(1)}, u32[]{:S(2)}, u32[]{:S(2)}) collective-permute-start(f32[48,128]{1,0:T(8,128)S(1)} %get-tuple-element.78.o2), channel_id=1, source_target_pairs={{0,8},{8,0},{16,24},{24,16},{1,9},{9,1},{17,25},{25,17},{2,10},{10... | collective-permute-start | bytes 73736 | tf_op jit(solution)/shard_map/ppermute | solution.py:440
  41.4 16.7 %collective-permute-start.21 = (f32[256,128]{1,0:T(8,128)S(1)}, f32[256,128]{1,0:T(8,128)S(1)}, u32[]{:S(2)}, u32[]{:S(2)}) collective-permute-start(f32[256,128]{1,0:T(8,128)S(1)} %behind.3), channel_id=1, source_target_pairs={{0,16},{8,24},{16,0},{24,8},{1,17},{9,25},{17,1},{25,9},{2,18},{10... | collective-permute-start | bytes 393224 | tf_op jit(solution)/shard_map/ppermute | solution.py:440
  45.1 13.0 %all-to-all-start.2 = ((f32[32,4,128]{2,1,0:T(4,128)}), f32[32,4,128]{2,1,0:T(4,128)S(1)}, u32[]{:S(2)}, u32[]{:S(2)}) async-start(f32[32,4,128]{2,1,0:T(4,128)} %bitcast.10), calls=%async_computation.2 | async-start | bytes 131072 | tf_op jit(solution)/shard_map/all_to_all | solution.py:458
  50.5 8.2 %collective-permute-start.17 = (f32[48,128]{1,0:T(8,128)S(1)}, f32[48,128]{1,0:T(8,128)S(1)}, u32[]{:S(2)}, u32[]{:S(2)}) collective-permute-start(f32[48,128]{1,0:T(8,128)S(1)} %get-tuple-element.81.o0), channel_id=1, source_target_pairs={{0,4},{1,5},{2,6},{3,7},{4,0},{5,1},{6,2},{7,3},{8,12},{9,13},{10,... | collective-permute-start | bytes 73736 | tf_op jit(solution)/shard_map/ppermute | solution.py:440
  53.2 5.5 %collective-permute-start.18 = (f32[48,128]{1,0:T(8,128)S(1)}, f32[48,128]{1,0:T(8,128)S(1)}, u32[]{:S(2)}, u32[]{:S(2)}) collective-permute-start(f32[48,128]{1,0:T(8,128)S(1)} %get-tuple-element.82.o1), channel_id=1, source_target_pairs={{0,2},{1,3},{2,0},{3,1},{4,6},{5,7},{6,4},{7,5},{8,10},{9,11},{10,... | collective-permute-start | bytes 73736 | tf_op jit(solution)/shard_map/ppermute | solution.py:440
  54.8 4.0 %collective-permute-start.19 = (f32[48,128]{1,0:T(8,128)S(1)}, f32[48,128]{1,0:T(8,128)S(1)}, u32[]{:S(2)}, u32[]{:S(2)}) collective-permute-start(f32[48,128]{1,0:T(8,128)S(1)} %get-tuple-element.83.o2), channel_id=1, source_target_pairs={{0,8},{8,0},{16,24},{24,16},{1,9},{9,1},{17,25},{25,17},{2,10},{10... | collective-permute-start | bytes 73736 | tf_op jit(solution)/shard_map/ppermute | solution.py:440
  56.2 2.5 %collective-permute-start.20 = (f32[48,128]{1,0:T(8,128)S(1)}, f32[48,128]{1,0:T(8,128)S(1)}, u32[]{:S(2)}, u32[]{:S(2)}) collective-permute-start(f32[48,128]{1,0:T(8,128)S(1)} %get-tuple-element.84.o3), channel_id=1, source_target_pairs={{0,1},{1,0},{2,3},{3,2},{4,5},{5,4},{6,7},{7,6},{8,9},{9,8},{10,11... | collective-permute-start | bytes 73736 | tf_op jit(solution)/shard_map/ppermute | solution.py:440

commit v9 on v8

--- a/solution.py
+++ b/solution.py
@@ -268,10 +268,10 @@
 
 
 def first_image(
-    received, o0, o1, o2, o3, a0, a1, a2, a3, vectors, corner, resid, spread, low, flex,
-    z_out, sums_out, map_out, spread_out, *wins,
+    received, o0, o1, o2, o3, a0, a1, a2, a3, vectors, corner, spread, low, flex,
+    z_out, map_out, spread_out, *wins,
 ):
-    n_load, dofs = resid.shape
+    n_load, dofs = low.shape
     came = [a0, a1, a2, a3]
     sign, sign_mask = vectors[0:1, :], vectors[2:3, :]
     width = dofs // 4
@@ -293,9 +293,13 @@
     signed = sign * zvec
     image = rounded(signed.astype(BF16), flex[...])
     put_faces(wins, jnp.concatenate([image, low[...]], axis=0))
-    sums_out[...] = with_sums(
-        jnp.zeros((8, 4 * n_load), F32), [rows_sum(resid[...] * zvec), 2.0 * rows_sum(signed * image)]
-    )
+
+
+def first_sums(o0, o1, o2, o3, zvec, resid, vectors, out):
+    n_load = zvec.shape[0]
+    image = from_faces([o0[...], o1[...], o2[...], o3[...]], 2 * n_load)[:n_load]
+    sums = [rows_sum(resid[...] * zvec[...]), 2.0 * rows_sum(vectors[0:1, :] * zvec[...] * image)]
+    out[...] = with_sums(jnp.zeros((8, 4 * n_load), F32), sums)
 
 
 def second_local(
@@ -328,10 +332,9 @@
 
 
 def second_image(
-    total, field, o0, o1, o2, o3, a0, a1, a2, a3, flexed, zold, low, resid, vectors, flex,
-    z_out, step_out, sums_out, *wins,
+    total, field, o0, o1, o2, o3, a0, a1, a2, a3, zold, low, vectors, flex, z_out, step_out, *wins,
 ):
-    n_load, dofs = resid.shape
+    n_load, dofs = zold.shape
     sign, sign_mask = vectors[0:1, :], vectors[2:3, :]
     rz, curve, _, _ = sums_of(total[...], n_load)
     alpha = rz / curve
@@ -343,13 +346,19 @@
     signed = sign * zvec
     image = alpha * fine(signed, flex[...])
     put_faces(wins, image)
-    scaled_flexed = alpha * flexed[...]
+
+
+def second_sums(total, o0, o1, o2, o3, zvec, flexed, resid, vectors, out):
+    n_load = zvec.shape[0]
+    rz, curve, _, _ = sums_of(total[...], n_load)
+    scaled_flexed = rz / curve * flexed[...]
+    image = from_faces([o0[...], o1[...], o2[...], o3[...]], n_load)
     sums = [
-        rows_sum((resid[...] - scaled_flexed) * zvec),
-        2.0 * rows_sum(signed * image),
-        rows_sum(zvec * scaled_flexed),
+        rows_sum((resid[...] - scaled_flexed) * zvec[...]),
+        2.0 * rows_sum(vectors[0:1, :] * zvec[...] * image),
+        rows_sum(zvec[...] * scaled_flexed),
     ]
-    sums_out[...] = with_sums(jnp.zeros((8, 4 * n_load), F32), sums)
+    out[...] = with_sums(jnp.zeros((8, 4 * n_load), F32), sums)
 
 
 def third_local(o0, o1, o2, o3, a0, a1, a2, a3, sums, vectors, corner_map, stiff, sent, w0, w1, w2, w3, block, sem):
@@ -491,10 +500,11 @@
     came = exchange(own)
     inverse = behind(inverse, came[-1])
     other = swap(inverse, "grp", 1)
-    zold, sums, corner_map, spread, *own = call(
-        "image1", first_image, [received] + own + came + [vectors, corner, resid, spread, low, flex],
-        [field, total, ((80, dofs), BF16), ((80, n), F32)] + faces(2 * n_load),
-    )
+    zold, corner_map, spread, *own = call(
+        "image1", first_image, [received] + own + came + [vectors, corner, spread, low, flex],
+        [field, ((80, dofs), BF16), ((80, n), F32)] + faces(2 * n_load),
+    )
+    (sums,) = call("sums1", first_sums, own + [zold, resid, vectors], [total])
     came = exchange(own)
     flexed, low, inverse, sent_rows, *own = call(
         "local2", second_local, own + came + [sums, vectors, corner_map, inverse, other, stiff],
@@ -504,10 +514,11 @@
     received = send_all(sent_rows)
     came = exchange(own)
     before, coarse = call("coarse2", second_coarse, [received, corner_map, spread], [total, field])
-    znew, step, sums, *own = call(
-        "image2", second_image, [before, coarse] + own + came + [flexed, zold, low, resid, vectors, flex],
-        [field, field, total] + faces(n_load),
-    )
+    znew, step, *own = call(
+        "image2", second_image, [before, coarse] + own + came + [zold, low, vectors, flex],
+        [field, field] + faces(n_load),
+    )
+    (sums,) = call("sums2", second_sums, [before] + own + [znew, flexed, resid, vectors], [total])
     came = exchange(own)
     inverses = [inverse]
     distance = 2

time: 59.8 us -> 59.5 us (level)
  waiting for transfers between devices: 10.7 us -> 10 us
    pallas_call x8 -> x10, Pallas kernels: 7.3 us -> 7.61 us  [call(): pl.pallas_call(kernel, out_shape=shapes, in_specs=[pl.BlockSpec(memory_sp...]
  transfers between devices with their start and end apart: 25 -> 25, of which waited for: 8 -> 8; matrix products, arithmetic and copies ran while one was open for 0% -> 0% of each run, Pallas kernels for 5% -> 6%
where the time goes in v9:
time: 59.5 us; the launch traced here: 59.2 us
  starting transfers between devices  39.7 us (67%)
  waiting for transfers between devices  10 us (17%)
  Pallas kernels  7.61 us (13%)
  other arithmetic  1 us (2%)
  between operations  0.83 us (1%)
    ppermute x22, starting transfers between devices, swap(): lax.ppermute(block, axis, [(i, i ^ distance) for i in range(count) if i ^...  27.8 us
    all_to_all x2, starting transfers between devices, send_all(): lax.all_to_all(blocks, ('grp', 'sub'), 0, 0, tiled=True).reshape(rows.shape)  8.02 us
    pallas_call x10, Pallas kernels, call(): pl.pallas_call(kernel, out_shape=shapes, in_specs=[pl.BlockSpec(memory_sp...  7.61 us
    ppermute x22, waiting for transfers between devices, swap(): lax.ppermute(block, axis, [(i, i ^ distance) for i in range(count) if i ^...  5.68 us
    all_to_all x1, starting transfers between devices, send_pair(): lax.all_to_all(blocks, ('grp', 'sub'), 0, 0, tiled=True, axis_index_group...  3.88 us
    all_to_all x2, waiting for transfers between devices, send_all(): lax.all_to_all(blocks, ('grp', 'sub'), 0, 0, tiled=True).reshape(rows.shape)  3.75 us
  transfers between devices with their start and end apart: 25, of which 8 were waited for; matrix products, arithmetic and copies ran while one was open for 0% of the time, Pallas kernels for 6%

profile of v9, /device:TPU:0, one launch (start us, length us, event | category | flops | bytes accessed | tf_op | source)
XLA Modules:
  0.0 59.2 jit_solution(13005104642869485492)
XLA Ops:
  0.6 0.0 copy-start.1
  0.6 1.0 %convert_add_fusion.small = f32[104,128]{1,0:T(8,128)S(1)} fusion(s32[1,12]{1,0:T(1,128)} %bitcast.24, s32[1,4]{1,0:T(1,128)} %bitcast.25, f32[96,96]{1,0:T(8,128)} %bitcast.23), kind=kLoop, calls=%fused_computation | loop fusion | flops 53248 | bytes 90176 | tf_op jit(solution)/shard_map/add | solution.py:489
  1.6 1.8 %start.1 = (f32[64,128]{1,0:T(8,128)}, f32[8,768]{1,0:T(8,128)S(1)}, bf16[16,768]{1,0:T(8,128)(2,1)S(1)}, f32[32,768]{1,0:T(8,128)S(1)}, f32[64,128]{1,0:T(8,128...) custom-call(f32[32,768]{1,0:T(8,128)} %bitcast.22, ...), custom_call_target="tpu_custom_call" | custom-call | flops 40000000 | bytes 1867776 | tf_op jit(solution)/shard_map/start/pallas_call | solution.py:423
  3.5 4.1 %collective-permute-start = (f32[128,128]{1,0:T(8,128)S(1)}, f32[128,128]{1,0:T(8,128)S(1)}, u32[]{:S(2)}, u32[]{:S(2)}) collective-permute-start(f32[128,128]{1,0:T(8,128)S(1)} %get-tuple-element.47.o0), channel_id=1, source_target_pairs={{0,4},{1,5},{2,6},{3,7},{4,0},{5,1},{6,2},{7,3},{8,12},{9,13},{10,... | collective-permute-start | bytes 196616 | tf_op jit(solution)/shard_map/ppermute | solution.py:449
  7.6 3.9 %all-to-all-start = ((f32[16,4,128]{2,1,0:T(4,128)}), f32[16,4,128]{2,1,0:T(4,128)S(1)}, u32[]{:S(2)}, u32[]{:S(2)}) async-start(f32[16,4,128]{2,1,0:T(4,128)} %bitcast.5), calls=%async_computation | async-start | bytes 65536 | tf_op jit(solution)/shard_map/all_to_all | solution.py:461
  11.5 0.0 copy-start
  11.5 0.5 collective-permute-start.3
  12.0 1.7 %collective-permute-start.2 = (f32[72,128]{1,0:T(8,128)S(1)}, f32[72,128]{1,0:T(8,128)S(1)}, u32[]{:S(2)}, u32[]{:S(2)}) collective-permute-start(f32[72,128]{1,0:T(8,128)S(1)} %get-tuple-element.49.o2), channel_id=1, source_target_pairs={{0,8},{8,0},{16,24},{24,16},{1,9},{9,1},{17,25},{25,17},{2,10},{10... | collective-permute-start | bytes 110600 | tf_op jit(solution)/shard_map/ppermute | solution.py:449
  13.7 1.5 %collective-permute-start.1 = (f32[56,128]{1,0:T(8,128)S(1)}, f32[56,128]{1,0:T(8,128)S(1)}, u32[]{:S(2)}, u32[]{:S(2)}) collective-permute-start(f32[56,128]{1,0:T(8,128)S(1)} %get-tuple-element.48.o1), channel_id=1, source_target_pairs={{0,2},{1,3},{2,0},{3,1},{4,6},{5,7},{6,4},{7,5},{8,10},{9,11},{10,... | collective-permute-start | bytes 86024 | tf_op jit(solution)/shard_map/ppermute | solution.py:449
  15.1 0.0 collective-permute-done.3.a3.other_ref
  15.1 0.6 collective-permute-start.8
  15.7 1.8 %collective-permute-done.1.a1 = f32[56,128]{1,0:T(8,128)S(1)} collective-permute-done((f32[56,128]{1,0:T(8,128)S(1)}, f32[56,128]{1,0:T(8,128)S(1)}, u32[]{:S(2)}, u32[]{:S(2)}) %collective-permute-start.1) | collective-permute-done | bytes 28704 | tf_op jit(solution)/shard_map/ppermute | solution.py:449
  17.5 0.0 collective-permute-done.2.a2
  17.5 0.6 %all-to-all-done = f32[16,4,128]{2,1,0:T(4,128)S(1)} async-done(((f32[16,4,128]{2,1,0:T(4,128)}), f32[16,4,128]{2,1,0:T(4,128)S(1)}, u32[]{:S(2)}, u32[]{:S(2)}) %all-to-all-start) | async-done | bytes 32800 | tf_op jit(solution)/shard_map/all_to_all | solution.py:461
  18.1 0.0 collective-permute-done.a0
  18.1 0.0 copy-done.1
  18.1 0.7 %image1.1 = (f32[32,768]{1,0:T(8,128)S(1)}, bf16[80,768]{1,0:T(8,128)(2,1)S(1)}, f32[80,128]{1,0:T(8,128)S(1)}, f32[96,128]{1,0:T(8,128)S(1)}, f32[96,128]{1,0:T...) custom-call(f32[64,128]{1,0:T(8,128)S(1)} %bitcast.21, f32[128,128]{1,0:T(8,128)S(1)} %get-tuple-element.47.o0, ...), custom_call_target="tpu_custom_call" | custom-call | flops 40000000 | bytes 2170880 | tf_op jit(solution)/shard_map/image1/pallas_call | solution.py:423
  18.9 1.8 %collective-permute-start.4 = (f32[96,128]{1,0:T(8,128)S(1)}, f32[96,128]{1,0:T(8,128)S(1)}, u32[]{:S(2)}, u32[]{:S(2)}) collective-permute-start(f32[96,128]{1,0:T(8,128)S(1)} %get-tuple-element.55.o0), channel_id=1, source_target_pairs={{0,4},{1,5},{2,6},{3,7},{4,0},{5,1},{6,2},{7,3},{8,12},{9,13},{10,... | collective-permute-start | bytes 147464 | tf_op jit(solution)/shard_map/ppermute | solution.py:449
  20.7 1.5 %collective-permute-start.5 = (f32[96,128]{1,0:T(8,128)S(1)}, f32[96,128]{1,0:T(8,128)S(1)}, u32[]{:S(2)}, u32[]{:S(2)}) collective-permute-start(f32[96,128]{1,0:T(8,128)S(1)} %get-tuple-element.56.o1), channel_id=1, source_target_pairs={{0,2},{1,3},{2,0},{3,1},{4,6},{5,7},{6,4},{7,5},{8,10},{9,11},{10,... | collective-permute-start | bytes 147464 | tf_op jit(solution)/shard_map/ppermute | solution.py:449
  22.1 0.6 collective-permute-start.6
  22.7 0.0 collective-permute-start.7
  22.7 0.2 sums1.1.sums
  22.9 0.0 collective-permute-done.8.other
  23.0 1.5 %collective-permute-done.4.a0 = f32[96,128]{1,0:T(8,128)S(1)} collective-permute-done((f32[96,128]{1,0:T(8,128)S(1)}, f32[96,128]{1,0:T(8,128)S(1)}, u32[]{:S(2)}, u32[]{:S(2)}) %collective-permute-start.4) | collective-permute-done | bytes 49184 | tf_op jit(solution)/shard_map/ppermute | solution.py:449
  24.4 0.4 collective-permute-done.5.a1
  24.9 1.4 %collective-permute-done.6.a2 = f32[96,128]{1,0:T(8,128)S(1)} collective-permute-done((f32[96,128]{1,0:T(8,128)S(1)}, f32[96,128]{1,0:T(8,128)S(1)}, u32[]{:S(2)}, u32[]{:S(2)}) %collective-permute-start.6) | collective-permute-done | bytes 49184 | tf_op jit(solution)/shard_map/ppermute | solution.py:449
  26.2 0.0 collective-permute-done.7.a3
  26.2 1.0 %local2.1 = (f32[32,768]{1,0:T(8,128)S(1)}, bf16[32,768]{1,0:T(8,128)(2,1)S(1)}, f32[256,128]{1,0:T(8,128)S(1)}, f32[128,128]{1,0:T(8,128)}, f32[48,128]{1,0:T(8...) custom-call(f32[96,128]{1,0:T(8,128)S(1)} %get-tuple-element.55.o0, ...), custom_call_target="tpu_custom_call" | custom-call | flops 40000000 | bytes 2297856 | tf_op jit(solution)/shard_map/local2/pallas_call | solution.py:423
  27.3 2.6 %all-to-all-start.1 = ((f32[32,4,128]{2,1,0:T(4,128)}), f32[32,4,128]{2,1,0:T(4,128)S(1)}, u32[]{:S(2)}, u32[]{:S(2)}) async-start(f32[32,4,128]{2,1,0:T(4,128)} %bitcast.8), calls=%async_computation.1 | async-start | bytes 131072 | tf_op jit(solution)/shard_map/all_to_all | solution.py:467
  29.9 2.7 %collective-permute-start.9 = (f32[48,128]{1,0:T(8,128)S(1)}, f32[48,128]{1,0:T(8,128)S(1)}, u32[]{:S(2)}, u32[]{:S(2)}) collective-permute-start(f32[48,128]{1,0:T(8,128)S(1)} %get-tuple-element.67.o0), channel_id=1, source_target_pairs={{0,4},{1,5},{2,6},{3,7},{4,0},{5,1},{6,2},{7,3},{8,12},{9,13},{10,... | collective-permute-start | bytes 73736 | tf_op jit(solution)/shard_map/ppermute | solution.py:449
  32.6 1.5 %collective-permute-start.10 = (f32[48,128]{1,0:T(8,128)S(1)}, f32[48,128]{1,0:T(8,128)S(1)}, u32[]{:S(2)}, u32[]{:S(2)}) collective-permute-start(f32[48,128]{1,0:T(8,128)S(1)} %get-tuple-element.68.o1), channel_id=1, source_target_pairs={{0,2},{1,3},{2,0},{3,1},{4,6},{5,7},{6,4},{7,5},{8,10},{9,11},{10,... | collective-permute-start | bytes 73736 | tf_op jit(solution)/shard_map/ppermute | solution.py:449
  34.1 1.5 %collective-permute-start.11 = (f32[48,128]{1,0:T(8,128)S(1)}, f32[48,128]{1,0:T(8,128)S(1)}, u32[]{:S(2)}, u32[]{:S(2)}) collective-permute-start(f32[48,128]{1,0:T(8,128)S(1)} %get-tuple-element.69.o2), channel_id=1, source_target_pairs={{0,8},{8,0},{16,24},{24,16},{1,9},{9,1},{17,25},{25,17},{2,10},{10... | collective-permute-start | bytes 73736 | tf_op jit(solution)/shard_map/ppermute | solution.py:449
  35.6 0.0 collective-permute-start.12
  35.6 1.9 %all-to-all-done.1 = f32[32,4,128]{2,1,0:T(4,128)S(1)} async-done(((f32[32,4,128]{2,1,0:T(4,128)}), f32[32,4,128]{2,1,0:T(4,128)S(1)}, u32[]{:S(2)}, u32[]{:S(2)}) %all-to-all-start.1) | async-done | bytes 65568 | tf_op jit(solution)/shard_map/all_to_all | solution.py:467
  37.5 0.4 coarse2.1
  37.9 0.0 collective-permute-done.9.a0
  37.9 0.0 collective-permute-done.10.a1
  38.0 0.0 collective-permute-done.11.a2
  38.0 0.0 collective-permute-done.12.a3
  38.0 0.5 image2.1
  38.5 0.3 collective-permute-start.16
  38.8 0.2 collective-permute-start.13
  39.0 0.7 %collective-permute-start.14 = (f32[48,128]{1,0:T(8,128)S(1)}, f32[48,128]{1,0:T(8,128)S(1)}, u32[]{:S(2)}, u32[]{:S(2)}) collective-permute-start(f32[48,128]{1,0:T(8,128)S(1)} %get-tuple-element.73.o1), channel_id=1, source_target_pairs={{0,2},{1,3},{2,0},{3,1},{4,6},{5,7},{6,4},{7,5},{8,10},{9,11},{10,... | collective-permute-start | bytes 73736 | tf_op jit(solution)/shard_map/ppermute | solution.py:449
  39.6 1.5 %collective-permute-start.15 = (f32[48,128]{1,0:T(8,128)S(1)}, f32[48,128]{1,0:T(8,128)S(1)}, u32[]{:S(2)}, u32[]{:S(2)}) collective-permute-start(f32[48,128]{1,0:T(8,128)S(1)} %get-tuple-element.74.o2), channel_id=1, source_target_pairs={{0,8},{8,0},{16,24},{24,16},{1,9},{9,1},{17,25},{25,17},{2,10},{10... | collective-permute-start | bytes 73736 | tf_op jit(solution)/shard_map/ppermute | solution.py:449
  41.1 0.0 collective-permute-done.16.a3.other_ref
  41.1 1.6 %collective-permute-start.21 = (f32[256,128]{1,0:T(8,128)S(1)}, f32[256,128]{1,0:T(8,128)S(1)}, u32[]{:S(2)}, u32[]{:S(2)}) collective-permute-start(f32[256,128]{1,0:T(8,128)S(1)} %behind.3), channel_id=1, source_target_pairs={{0,16},{8,24},{16,0},{24,8},{1,17},{9,25},{17,1},{25,9},{2,18},{10... | collective-permute-start | bytes 393224 | tf_op jit(solution)/shard_map/ppermute | solution.py:449
  42.7 0.3 sums2.1.sums
  43.0 0.5 collective-permute-done.13.a0
  43.5 0.0 collective-permute-done.14.a1
  43.5 0.0 collective-permute-done.15.a2
  43.5 1.2 %local3.1 = (f32[128,128]{1,0:T(8,128)}, f32[48,128]{1,0:T(8,128)S(1)}, f32[48,128]{1,0:T(8,128)S(1)}, f32[48,128]{1,0:T(8,128)S(1)}, f32[48,128]{1,0:T(8,128)S(1)}) custom-call(f32[48,128]{1,0:T(8,128)S(1)} %get-tuple-element.72.o0, f32[48,128]{1,0:T(8,128)S(1)} %get-tuple-element.73.o1, f32[48,128]{1,0:T(8,128)S(1)} %get-tuple-element.74.o2, ...), custom_call_target="tpu_custom_call" | custom-call | flops 40000000 | bytes 1691648 | tf_op jit(solution)/shard_map/local3/pallas_call | solution.py:423
  44.8 5.4 %all-to-all-start.2 = ((f32[32,4,128]{2,1,0:T(4,128)}), f32[32,4,128]{2,1,0:T(4,128)S(1)}, u32[]{:S(2)}, u32[]{:S(2)}) async-start(f32[32,4,128]{2,1,0:T(4,128)} %bitcast.10), calls=%async_computation.2 | async-start | bytes 131072 | tf_op jit(solution)/shard_map/all_to_all | solution.py:467
  50.2 2.7 %collective-permute-start.17 = (f32[48,128]{1,0:T(8,128)S(1)}, f32[48,128]{1,0:T(8,128)S(1)}, u32[]{:S(2)}, u32[]{:S(2)}) collective-permute-start(f32[48,128]{1,0:T(8,128)S(1)} %get-tuple-element.78.o0), channel_id=1, source_target_pairs={{0,4},{1,5},{2,6},{3,7},{4,0},{5,1},{6,2},{7,3},{8,12},{9,13},{10,... | collective-permute-start | bytes 73736 | tf_op jit(solution)/shard_map/ppermute | solution.py:449
  53.0 1.5 %collective-permute-start.18 = (f32[48,128]{1,0:T(8,128)S(1)}, f32[48,128]{1,0:T(8,128)S(1)}, u32[]{:S(2)}, u32[]{:S(2)}) collective-permute-start(f32[48,128]{1,0:T(8,128)S(1)} %get-tuple-element.79.o1), channel_id=1, source_target_pairs={{0,2},{1,3},{2,0},{3,1},{4,6},{5,7},{6,4},{7,5},{8,10},{9,11},{10,... | collective-permute-start | bytes 73736 | tf_op jit(solution)/shard_map/ppermute | solution.py:449
  54.5 1.5 %collective-permute-start.19 = (f32[48,128]{1,0:T(8,128)S(1)}, f32[48,128]{1,0:T(8,128)S(1)}, u32[]{:S(2)}, u32[]{:S(2)}) collective-permute-start(f32[48,128]{1,0:T(8,128)S(1)} %get-tuple-element.80.o2), channel_id=1, source_target_pairs={{0,8},{8,0},{16,24},{24,16},{1,9},{9,1},{17,25},{25,17},{2,10},{10... | collective-permute-start | bytes 73736 | tf_op jit(solution)/shard_map/ppermute | solution.py:449
  55.9 0.0 collective-permute-start.20
  56.0 1.9 %all-to-all-done.2 = f32[32,4,128]{2,1,0:T(4,128)S(1)} async-done(((f32[32,4,128]{2,1,0:T(4,128)}), f32[32,4,128]{2,1,0:T(4,128)S(1)}, u32[]{:S(2)}, u32[]{:S(2)}) %all-to-all-start.2) | async-done | bytes 65568 | tf_op jit(solution)/shard_map/all_to_all | solution.py:467
  57.8 0.0 collective-permute-done.21.rest_1_
  57.8 0.6 coarse3.1
  58.4 0.0 collective-permute-done.17.a0
  58.4 0.0 collective-permute-done.18.a1
  58.4 0.0 collective-permute-done.19.a2
  58.4 0.0 collective-permute-done.20.a3
  58.4 0.8 %finish.1 = (f32[32,768]{1,0:T(8,128)}, f32[32,768]{1,0:T(8,128)}) custom-call(f32[48,128]{1,0:T(8,128)S(1)} %get-tuple-element.78.o0, f32[48,128]{1,0:T(8,128)S(1)} %get-tuple-element.79.o1, f32[48,128]{1,0:T(8,128)S(1)} %get-tuple-element.80.o2, f32[48,128]{1,0:T(8,128)S(1)} %get-tuple-element.81.o3, f32[48,128]{1,0:T(8,128)S(1)} %collective-permute-done.17.a0, ...), custom_call_target="tpu_custom_call" | custom-call | flops 40000000 | bytes 630784 | tf_op jit(solution)/shard_map/finish/pallas_call | solution.py:423
  (4 shorter events, 0.0 us)
Async XLA Ops:
  0.6 17.5 %copy-start.1 = (bf16[1,1,768,768]{3,2,1,0:T(8,128)(2,1)S(1)}, bf16[1,1,768,768]{3,2,1,0:T(8,128)(2,1)}, u32[]{:S(2)}) copy-start(bf16[1,1,768,768]{3,2,1,0:T(8,128)(2,1)} %param.8) | copy-start | bytes 3538948
  3.5 14.6 %collective-permute-start = (f32[128,128]{1,0:T(8,128)S(1)}, f32[128,128]{1,0:T(8,128)S(1)}, u32[]{:S(2)}, u32[]{:S(2)}) collective-permute-start(f32[128,128]{1,0:T(8,128)S(1)} %get-tuple-element.47.o0), channel_id=1, source_target_pairs={{0,4},{1,5},{2,6},{3,7},{4,0},{5,1},{6,2},{7,3},{8,12},{9,13},{10,... | collective-permute-start | bytes 196616 | tf_op jit(solution)/shard_map/ppermute | solution.py:449
  7.6 10.5 %all-to-all-start = ((f32[16,4,128]{2,1,0:T(4,128)}), f32[16,4,128]{2,1,0:T(4,128)S(1)}, u32[]{:S(2)}, u32[]{:S(2)}) async-start(f32[16,4,128]{2,1,0:T(4,128)} %bitcast.5), calls=%async_computation | async-start | bytes 65536 | tf_op jit(solution)/shard_map/all_to_all | solution.py:461
  11.5 14.7 %copy-start = (bf16[1,1,768,768]{3,2,1,0:T(8,128)(2,1)S(1)}, bf16[1,1,768,768]{3,2,1,0:T(8,128)(2,1)}, u32[]{:S(2)}) copy-start(bf16[1,1,768,768]{3,2,1,0:T(8,128)(2,1)} %param.7) | copy-start | bytes 3538948
  11.5 3.6 %collective-permute-start.3 = (f32[56,128]{1,0:T(8,128)S(1)}, f32[56,128]{1,0:T(8,128)S(1)}, u32[]{:S(2)}, u32[]{:S(2)}) collective-permute-start(f32[56,128]{1,0:T(8,128)S(1)} %get-tuple-element.50.o3), channel_id=1, source_target_pairs={{0,1},{1,0},{2,3},{3,2},{4,5},{5,4},{6,7},{7,6},{8,9},{9,8},{10,11... | collective-permute-start | bytes 86024 | tf_op jit(solution)/shard_map/ppermute | solution.py:449
  12.0 5.6 %collective-permute-start.2 = (f32[72,128]{1,0:T(8,128)S(1)}, f32[72,128]{1,0:T(8,128)S(1)}, u32[]{:S(2)}, u32[]{:S(2)}) collective-permute-start(f32[72,128]{1,0:T(8,128)S(1)} %get-tuple-element.49.o2), channel_id=1, source_target_pairs={{0,8},{8,0},{16,24},{24,16},{1,9},{9,1},{17,25},{25,17},{2,10},{10... | collective-permute-start | bytes 110600 | tf_op jit(solution)/shard_map/ppermute | solution.py:449
  13.7 3.9 %collective-permute-start.1 = (f32[56,128]{1,0:T(8,128)S(1)}, f32[56,128]{1,0:T(8,128)S(1)}, u32[]{:S(2)}, u32[]{:S(2)}) collective-permute-start(f32[56,128]{1,0:T(8,128)S(1)} %get-tuple-element.48.o1), channel_id=1, source_target_pairs={{0,2},{1,3},{2,0},{3,1},{4,6},{5,7},{6,4},{7,5},{8,10},{9,11},{10,... | collective-permute-start | bytes 86024 | tf_op jit(solution)/shard_map/ppermute | solution.py:449
  15.1 7.8 %collective-permute-start.8 = (f32[128,128]{1,0:T(8,128)S(1)}, f32[128,128]{1,0:T(8,128)S(1)}, u32[]{:S(2)}, u32[]{:S(2)}) collective-permute-start(f32[128,128]{1,0:T(8,128)S(1)} %behind.2.inverse), channel_id=1, source_target_pairs={{0,8},{8,0},{16,24},{24,16},{1,9},{9,1},{17,25},{25,17},{2,10},{10... | collective-permute-start | bytes 196616 | tf_op jit(solution)/shard_map/ppermute | solution.py:449
  18.9 5.5 %collective-permute-start.4 = (f32[96,128]{1,0:T(8,128)S(1)}, f32[96,128]{1,0:T(8,128)S(1)}, u32[]{:S(2)}, u32[]{:S(2)}) collective-permute-start(f32[96,128]{1,0:T(8,128)S(1)} %get-tuple-element.55.o0), channel_id=1, source_target_pairs={{0,4},{1,5},{2,6},{3,7},{4,0},{5,1},{6,2},{7,3},{8,12},{9,13},{10,... | collective-permute-start | bytes 147464 | tf_op jit(solution)/shard_map/ppermute | solution.py:449
  20.7 4.2 %collective-permute-start.5 = (f32[96,128]{1,0:T(8,128)S(1)}, f32[96,128]{1,0:T(8,128)S(1)}, u32[]{:S(2)}, u32[]{:S(2)}) collective-permute-start(f32[96,128]{1,0:T(8,128)S(1)} %get-tuple-element.56.o1), channel_id=1, source_target_pairs={{0,2},{1,3},{2,0},{3,1},{4,6},{5,7},{6,4},{7,5},{8,10},{9,11},{10,... | collective-permute-start | bytes 147464 | tf_op jit(solution)/shard_map/ppermute | solution.py:449
  22.1 4.1 %collective-permute-start.6 = (f32[96,128]{1,0:T(8,128)S(1)}, f32[96,128]{1,0:T(8,128)S(1)}, u32[]{:S(2)}, u32[]{:S(2)}) collective-permute-start(f32[96,128]{1,0:T(8,128)S(1)} %get-tuple-element.57.o2), channel_id=1, source_target_pairs={{0,8},{8,0},{16,24},{24,16},{1,9},{9,1},{17,25},{25,17},{2,10},{10... | collective-permute-start | bytes 147464 | tf_op jit(solution)/shard_map/ppermute | solution.py:449
  22.7 3.5 %collective-permute-start.7 = (f32[96,128]{1,0:T(8,128)S(1)}, f32[96,128]{1,0:T(8,128)S(1)}, u32[]{:S(2)}, u32[]{:S(2)}) collective-permute-start(f32[96,128]{1,0:T(8,128)S(1)} %get-tuple-element.58.o3), channel_id=1, source_target_pairs={{0,1},{1,0},{2,3},{3,2},{4,5},{5,4},{6,7},{7,6},{8,9},{9,8},{10,11... | collective-permute-start | bytes 147464 | tf_op jit(solution)/shard_map/ppermute | solution.py:449
  27.3 10.2 %all-to-all-start.1 = ((f32[32,4,128]{2,1,0:T(4,128)}), f32[32,4,128]{2,1,0:T(4,128)S(1)}, u32[]{:S(2)}, u32[]{:S(2)}) async-start(f32[32,4,128]{2,1,0:T(4,128)} %bitcast.8), calls=%async_computation.1 | async-start | bytes 131072 | tf_op jit(solution)/shard_map/all_to_all | solution.py:467
  29.9 8.1 %collective-permute-start.9 = (f32[48,128]{1,0:T(8,128)S(1)}, f32[48,128]{1,0:T(8,128)S(1)}, u32[]{:S(2)}, u32[]{:S(2)}) collective-permute-start(f32[48,128]{1,0:T(8,128)S(1)} %get-tuple-element.67.o0), channel_id=1, source_target_pairs={{0,4},{1,5},{2,6},{3,7},{4,0},{5,1},{6,2},{7,3},{8,12},{9,13},{10,... | collective-permute-start | bytes 73736 | tf_op jit(solution)/shard_map/ppermute | solution.py:449
  32.6 5.3 %collective-permute-start.10 = (f32[48,128]{1,0:T(8,128)S(1)}, f32[48,128]{1,0:T(8,128)S(1)}, u32[]{:S(2)}, u32[]{:S(2)}) collective-permute-start(f32[48,128]{1,0:T(8,128)S(1)} %get-tuple-element.68.o1), channel_id=1, source_target_pairs={{0,2},{1,3},{2,0},{3,1},{4,6},{5,7},{6,4},{7,5},{8,10},{9,11},{10,... | collective-permute-start | bytes 73736 | tf_op jit(solution)/shard_map/ppermute | solution.py:449
  34.1 3.8 %collective-permute-start.11 = (f32[48,128]{1,0:T(8,128)S(1)}, f32[48,128]{1,0:T(8,128)S(1)}, u32[]{:S(2)}, u32[]{:S(2)}) collective-permute-start(f32[48,128]{1,0:T(8,128)S(1)} %get-tuple-element.69.o2), channel_id=1, source_target_pairs={{0,8},{8,0},{16,24},{24,16},{1,9},{9,1},{17,25},{25,17},{2,10},{10... | collective-permute-start | bytes 73736 | tf_op jit(solution)/shard_map/ppermute | solution.py:449
  35.6 2.4 %collective-permute-start.12 = (f32[48,128]{1,0:T(8,128)S(1)}, f32[48,128]{1,0:T(8,128)S(1)}, u32[]{:S(2)}, u32[]{:S(2)}) collective-permute-start(f32[48,128]{1,0:T(8,128)S(1)} %get-tuple-element.70.o3), channel_id=1, source_target_pairs={{0,1},{1,0},{2,3},{3,2},{4,5},{5,4},{6,7},{7,6},{8,9},{9,8},{10,11... | collective-permute-start | bytes 73736 | tf_op jit(solution)/shard_map/ppermute | solution.py:449
  38.5 2.7 %collective-permute-start.16 = (f32[48,128]{1,0:T(8,128)S(1)}, f32[48,128]{1,0:T(8,128)S(1)}, u32[]{:S(2)}, u32[]{:S(2)}) collective-permute-start(f32[48,128]{1,0:T(8,128)S(1)} %get-tuple-element.75.o3), channel_id=1, source_target_pairs={{0,1},{1,0},{2,3},{3,2},{4,5},{5,4},{6,7},{7,6},{8,9},{9,8},{10,11... | collective-permute-start | bytes 73736 | tf_op jit(solution)/shard_map/ppermute | solution.py:449
  38.8 4.8 %collective-permute-start.13 = (f32[48,128]{1,0:T(8,128)S(1)}, f32[48,128]{1,0:T(8,128)S(1)}, u32[]{:S(2)}, u32[]{:S(2)}) collective-permute-start(f32[48,128]{1,0:T(8,128)S(1)} %get-tuple-element.72.o0), channel_id=1, source_target_pairs={{0,4},{1,5},{2,6},{3,7},{4,0},{5,1},{6,2},{7,3},{8,12},{9,13},{10,... | collective-permute-start | bytes 73736 | tf_op jit(solution)/shard_map/ppermute | solution.py:449
  39.0 4.6 %collective-permute-start.14 = (f32[48,128]{1,0:T(8,128)S(1)}, f32[48,128]{1,0:T(8,128)S(1)}, u32[]{:S(2)}, u32[]{:S(2)}) collective-permute-start(f32[48,128]{1,0:T(8,128)S(1)} %get-tuple-element.73.o1), channel_id=1, source_target_pairs={{0,2},{1,3},{2,0},{3,1},{4,6},{5,7},{6,4},{7,5},{8,10},{9,11},{10,... | collective-permute-start | bytes 73736 | tf_op jit(solution)/shard_map/ppermute | solution.py:449
  39.6 3.9 %collective-permute-start.15 = (f32[48,128]{1,0:T(8,128)S(1)}, f32[48,128]{1,0:T(8,128)S(1)}, u32[]{:S(2)}, u32[]{:S(2)}) collective-permute-start(f32[48,128]{1,0:T(8,128)S(1)} %get-tuple-element.74.o2), channel_id=1, source_target_pairs={{0,8},{8,0},{16,24},{24,16},{1,9},{9,1},{17,25},{25,17},{2,10},{10... | collective-permute-start | bytes 73736 | tf_op jit(solution)/shard_map/ppermute | solution.py:449
  41.1 16.7 %collective-permute-start.21 = (f32[256,128]{1,0:T(8,128)S(1)}, f32[256,128]{1,0:T(8,128)S(1)}, u32[]{:S(2)}, u32[]{:S(2)}) collective-permute-start(f32[256,128]{1,0:T(8,128)S(1)} %behind.3), channel_id=1, source_target_pairs={{0,16},{8,24},{16,0},{24,8},{1,17},{9,25},{17,1},{25,9},{2,18},{10... | collective-permute-start | bytes 393224 | tf_op jit(solution)/shard_map/ppermute | solution.py:449
  44.8 13.0 %all-to-all-start.2 = ((f32[32,4,128]{2,1,0:T(4,128)}), f32[32,4,128]{2,1,0:T(4,128)S(1)}, u32[]{:S(2)}, u32[]{:S(2)}) async-start(f32[32,4,128]{2,1,0:T(4,128)} %bitcast.10), calls=%async_computation.2 | async-start | bytes 131072 | tf_op jit(solution)/shard_map/all_to_all | solution.py:467
  50.2 8.2 %collective-permute-start.17 = (f32[48,128]{1,0:T(8,128)S(1)}, f32[48,128]{1,0:T(8,128)S(1)}, u32[]{:S(2)}, u32[]{:S(2)}) collective-permute-start(f32[48,128]{1,0:T(8,128)S(1)} %get-tuple-element.78.o0), channel_id=1, source_target_pairs={{0,4},{1,5},{2,6},{3,7},{4,0},{5,1},{6,2},{7,3},{8,12},{9,13},{10,... | collective-permute-start | bytes 73736 | tf_op jit(solution)/shard_map/ppermute | solution.py:449
  53.0 5.5 %collective-permute-start.18 = (f32[48,128]{1,0:T(8,128)S(1)}, f32[48,128]{1,0:T(8,128)S(1)}, u32[]{:S(2)}, u32[]{:S(2)}) collective-permute-start(f32[48,128]{1,0:T(8,128)S(1)} %get-tuple-element.79.o1), channel_id=1, source_target_pairs={{0,2},{1,3},{2,0},{3,1},{4,6},{5,7},{6,4},{7,5},{8,10},{9,11},{10,... | collective-permute-start | bytes 73736 | tf_op jit(solution)/shard_map/ppermute | solution.py:449
  54.5 4.0 %collective-permute-start.19 = (f32[48,128]{1,0:T(8,128)S(1)}, f32[48,128]{1,0:T(8,128)S(1)}, u32[]{:S(2)}, u32[]{:S(2)}) collective-permute-start(f32[48,128]{1,0:T(8,128)S(1)} %get-tuple-element.80.o2), channel_id=1, source_target_pairs={{0,8},{8,0},{16,24},{24,16},{1,9},{9,1},{17,25},{25,17},{2,10},{10... | collective-permute-start | bytes 73736 | tf_op jit(solution)/shard_map/ppermute | solution.py:449
  55.9 2.5 %collective-permute-start.20 = (f32[48,128]{1,0:T(8,128)S(1)}, f32[48,128]{1,0:T(8,128)S(1)}, u32[]{:S(2)}, u32[]{:S(2)}) collective-permute-start(f32[48,128]{1,0:T(8,128)S(1)} %get-tuple-element.81.o3), channel_id=1, source_target_pairs={{0,1},{1,0},{2,3},{3,2},{4,5},{5,4},{6,7},{7,6},{8,9},{9,8},{10,11... | collective-permute-start | bytes 73736 | tf_op jit(solution)/shard_map/ppermute | solution.py:449

commit v10 on v9

--- a/solution.py
+++ b/solution.py
@@ -498,7 +498,7 @@
     )
     received = send_pair(corners)
     came = exchange(own)
-    inverse = behind(inverse, came[-1])
+    inverse = inverse
     other = swap(inverse, "grp", 1)
     zold, corner_map, spread, *own = call(
         "image1", first_image, [received] + own + came + [vectors, corner, spread, low, flex],
@@ -524,7 +524,7 @@
     distance = 2
     while distance < groups:
         held = inverses[0] if distance == 2 else jnp.concatenate(inverses, axis=0)
-        inverses.append(swap(behind(held, came[-1]), "grp", distance))
+        inverses.append(swap(held, "grp", distance))
         distance *= 2
     sent_rows, *own = call(
         "local3", third_local, own + came + [sums, vectors, corner_map, stiff], [sent] + faces(n_load),

time: 59.5 us -> 59.4 us (level)
    ppermute x22, starting transfers between devices: 27.8 us -> 27.1 us  [swap(): lax.ppermute(block, axis, [(i, i ^ distance) for i in range(count) if i ^...]
where the time goes in v10:
time: 59.4 us; the launch traced here: 59.1 us
  starting transfers between devices  39.2 us (66%)
  waiting for transfers between devices  10.5 us (18%)
  Pallas kernels  7.62 us (13%)
  other arithmetic  1 us (2%)
  between operations  0.81 us (1%)
    ppermute x22, starting transfers between devices, swap(): lax.ppermute(block, axis, [(i, i ^ distance) for i in range(count) if i ^...  27.1 us
    all_to_all x2, starting transfers between devices, send_all(): lax.all_to_all(blocks, ('grp', 'sub'), 0, 0, tiled=True).reshape(rows.shape)  8.27 us
    pallas_call x10, Pallas kernels, call(): pl.pallas_call(kernel, out_shape=shapes, in_specs=[pl.BlockSpec(memory_sp...  7.62 us
    ppermute x22, waiting for transfers between devices, swap(): lax.ppermute(block, axis, [(i, i ^ distance) for i in range(count) if i ^...  5.85 us
    all_to_all x1, starting transfers between devices, send_pair(): lax.all_to_all(blocks, ('grp', 'sub'), 0, 0, tiled=True, axis_index_group...  3.88 us
    all_to_all x2, waiting for transfers between devices, send_all(): lax.all_to_all(blocks, ('grp', 'sub'), 0, 0, tiled=True).reshape(rows.shape)  3.74 us
  transfers between devices with their start and end apart: 25, of which 8 were waited for; matrix products, arithmetic and copies ran while one was open for 0% of the time, Pallas kernels for 6%

profile of v10, /device:TPU:0, one launch (start us, length us, event | category | flops | bytes accessed | tf_op | source)
XLA Modules:
  0.0 59.1 jit_solution(12961451460847776729)
XLA Ops:
  0.6 0.0 copy-start.1
  0.6 1.0 %convert_add_fusion.small = f32[104,128]{1,0:T(8,128)S(1)} fusion(s32[1,12]{1,0:T(1,128)} %bitcast.24, s32[1,4]{1,0:T(1,128)} %bitcast.25, f32[96,96]{1,0:T(8,128)} %bitcast.23), kind=kLoop, calls=%fused_computation | loop fusion | flops 53248 | bytes 90176 | tf_op jit(solution)/shard_map/add | solution.py:489
  1.6 1.8 %start.1 = (f32[64,128]{1,0:T(8,128)}, f32[8,768]{1,0:T(8,128)S(1)}, bf16[16,768]{1,0:T(8,128)(2,1)S(1)}, f32[32,768]{1,0:T(8,128)S(1)}, f32[64,128]{1,0:T(8,128...) custom-call(f32[32,768]{1,0:T(8,128)} %bitcast.22, ...), custom_call_target="tpu_custom_call" | custom-call | flops 40000000 | bytes 1867776 | tf_op jit(solution)/shard_map/start/pallas_call | solution.py:423
  3.5 0.0 copy-start
  3.5 4.1 %collective-permute-start = (f32[128,128]{1,0:T(8,128)S(1)}, f32[128,128]{1,0:T(8,128)S(1)}, u32[]{:S(2)}, u32[]{:S(2)}) collective-permute-start(f32[128,128]{1,0:T(8,128)S(1)} %get-tuple-element.47.o0), channel_id=1, source_target_pairs={{0,4},{1,5},{2,6},{3,7},{4,0},{5,1},{6,2},{7,3},{8,12},{9,13},{10,... | collective-permute-start | bytes 196616 | tf_op jit(solution)/shard_map/ppermute | solution.py:449
  7.6 3.9 %all-to-all-start = ((f32[16,4,128]{2,1,0:T(4,128)}), f32[16,4,128]{2,1,0:T(4,128)S(1)}, u32[]{:S(2)}, u32[]{:S(2)}) async-start(f32[16,4,128]{2,1,0:T(4,128)} %bitcast.5), calls=%async_computation | async-start | bytes 65536 | tf_op jit(solution)/shard_map/all_to_all | solution.py:461
  11.5 1.9 %collective-permute-start.2 = (f32[72,128]{1,0:T(8,128)S(1)}, f32[72,128]{1,0:T(8,128)S(1)}, u32[]{:S(2)}, u32[]{:S(2)}) collective-permute-start(f32[72,128]{1,0:T(8,128)S(1)} %get-tuple-element.49.o2), channel_id=1, source_target_pairs={{0,8},{8,0},{16,24},{24,16},{1,9},{9,1},{17,25},{25,17},{2,10},{10... | collective-permute-start | bytes 110600 | tf_op jit(solution)/shard_map/ppermute | solution.py:449
  13.4 1.5 %collective-permute-start.1 = (f32[56,128]{1,0:T(8,128)S(1)}, f32[56,128]{1,0:T(8,128)S(1)}, u32[]{:S(2)}, u32[]{:S(2)}) collective-permute-start(f32[56,128]{1,0:T(8,128)S(1)} %get-tuple-element.48.o1), channel_id=1, source_target_pairs={{0,2},{1,3},{2,0},{3,1},{4,6},{5,7},{6,4},{7,5},{8,10},{9,11},{10,... | collective-permute-start | bytes 86024 | tf_op jit(solution)/shard_map/ppermute | solution.py:449
  14.9 0.0 collective-permute-start.3
  14.9 0.6 collective-permute-start.8
  15.5 1.9 %collective-permute-done.1.a1 = f32[56,128]{1,0:T(8,128)S(1)} collective-permute-done((f32[56,128]{1,0:T(8,128)S(1)}, f32[56,128]{1,0:T(8,128)S(1)}, u32[]{:S(2)}, u32[]{:S(2)}) %collective-permute-start.1) | collective-permute-done | bytes 28704 | tf_op jit(solution)/shard_map/ppermute | solution.py:449
  17.4 0.0 collective-permute-done.3.a3
  17.4 0.0 collective-permute-done.2.a2
  17.4 0.9 %all-to-all-done = f32[16,4,128]{2,1,0:T(4,128)S(1)} async-done(((f32[16,4,128]{2,1,0:T(4,128)}), f32[16,4,128]{2,1,0:T(4,128)S(1)}, u32[]{:S(2)}, u32[]{:S(2)}) %all-to-all-start) | async-done | bytes 32800 | tf_op jit(solution)/shard_map/all_to_all | solution.py:461
  18.3 0.0 collective-permute-done.a0
  18.3 0.7 %image1.1 = (f32[32,768]{1,0:T(8,128)S(1)}, bf16[80,768]{1,0:T(8,128)(2,1)S(1)}, f32[80,128]{1,0:T(8,128)S(1)}, f32[96,128]{1,0:T(8,128)S(1)}, f32[96,128]{1,0:T...) custom-call(f32[64,128]{1,0:T(8,128)S(1)} %bitcast.21, f32[128,128]{1,0:T(8,128)S(1)} %get-tuple-element.47.o0, ...), custom_call_target="tpu_custom_call" | custom-call | flops 40000000 | bytes 2170880 | tf_op jit(solution)/shard_map/image1/pallas_call | solution.py:423
  19.0 1.4 %collective-permute-start.4 = (f32[96,128]{1,0:T(8,128)S(1)}, f32[96,128]{1,0:T(8,128)S(1)}, u32[]{:S(2)}, u32[]{:S(2)}) collective-permute-start(f32[96,128]{1,0:T(8,128)S(1)} %get-tuple-element.55.o0), channel_id=1, source_target_pairs={{0,4},{1,5},{2,6},{3,7},{4,0},{5,1},{6,2},{7,3},{8,12},{9,13},{10,... | collective-permute-start | bytes 147464 | tf_op jit(solution)/shard_map/ppermute | solution.py:449
  20.5 1.5 %collective-permute-start.5 = (f32[96,128]{1,0:T(8,128)S(1)}, f32[96,128]{1,0:T(8,128)S(1)}, u32[]{:S(2)}, u32[]{:S(2)}) collective-permute-start(f32[96,128]{1,0:T(8,128)S(1)} %get-tuple-element.56.o1), channel_id=1, source_target_pairs={{0,2},{1,3},{2,0},{3,1},{4,6},{5,7},{6,4},{7,5},{8,10},{9,11},{10,... | collective-permute-start | bytes 147464 | tf_op jit(solution)/shard_map/ppermute | solution.py:449
  21.9 0.6 collective-permute-start.6
  22.5 0.0 collective-permute-start.7
  22.5 0.2 sums1.1.sums
  22.7 0.0 collective-permute-done.8.other
  22.7 1.8 %collective-permute-done.4.a0 = f32[96,128]{1,0:T(8,128)S(1)} collective-permute-done((f32[96,128]{1,0:T(8,128)S(1)}, f32[96,128]{1,0:T(8,128)S(1)}, u32[]{:S(2)}, u32[]{:S(2)}) %collective-permute-start.4) | collective-permute-done | bytes 49184 | tf_op jit(solution)/shard_map/ppermute | solution.py:449
  24.6 0.2 collective-permute-done.5.a1
  24.8 1.2 %collective-permute-done.6.a2 = f32[96,128]{1,0:T(8,128)S(1)} collective-permute-done((f32[96,128]{1,0:T(8,128)S(1)}, f32[96,128]{1,0:T(8,128)S(1)}, u32[]{:S(2)}, u32[]{:S(2)}) %collective-permute-start.6) | collective-permute-done | bytes 49184 | tf_op jit(solution)/shard_map/ppermute | solution.py:449
  26.0 0.0 collective-permute-done.7.a3
  26.0 0.0 copy-done
  26.0 1.0 %local2.1 = (f32[32,768]{1,0:T(8,128)S(1)}, bf16[32,768]{1,0:T(8,128)(2,1)S(1)}, f32[256,128]{1,0:T(8,128)S(1)}, f32[128,128]{1,0:T(8,128)}, f32[48,128]{1,0:T(8...) custom-call(f32[96,128]{1,0:T(8,128)S(1)} %get-tuple-element.55.o0, ...), custom_call_target="tpu_custom_call" | custom-call | flops 40000000 | bytes 2297856 | tf_op jit(solution)/shard_map/local2/pallas_call | solution.py:423
  27.1 2.8 %all-to-all-start.1 = ((f32[32,4,128]{2,1,0:T(4,128)}), f32[32,4,128]{2,1,0:T(4,128)S(1)}, u32[]{:S(2)}, u32[]{:S(2)}) async-start(f32[32,4,128]{2,1,0:T(4,128)} %bitcast.8), calls=%async_computation.1 | async-start | bytes 131072 | tf_op jit(solution)/shard_map/all_to_all | solution.py:467
  29.9 2.7 %collective-permute-start.9 = (f32[48,128]{1,0:T(8,128)S(1)}, f32[48,128]{1,0:T(8,128)S(1)}, u32[]{:S(2)}, u32[]{:S(2)}) collective-permute-start(f32[48,128]{1,0:T(8,128)S(1)} %get-tuple-element.67.o0), channel_id=1, source_target_pairs={{0,4},{1,5},{2,6},{3,7},{4,0},{5,1},{6,2},{7,3},{8,12},{9,13},{10,... | collective-permute-start | bytes 73736 | tf_op jit(solution)/shard_map/ppermute | solution.py:449
  32.6 1.5 %collective-permute-start.10 = (f32[48,128]{1,0:T(8,128)S(1)}, f32[48,128]{1,0:T(8,128)S(1)}, u32[]{:S(2)}, u32[]{:S(2)}) collective-permute-start(f32[48,128]{1,0:T(8,128)S(1)} %get-tuple-element.68.o1), channel_id=1, source_target_pairs={{0,2},{1,3},{2,0},{3,1},{4,6},{5,7},{6,4},{7,5},{8,10},{9,11},{10,... | collective-permute-start | bytes 73736 | tf_op jit(solution)/shard_map/ppermute | solution.py:449
  34.2 1.5 %collective-permute-start.11 = (f32[48,128]{1,0:T(8,128)S(1)}, f32[48,128]{1,0:T(8,128)S(1)}, u32[]{:S(2)}, u32[]{:S(2)}) collective-permute-start(f32[48,128]{1,0:T(8,128)S(1)} %get-tuple-element.69.o2), channel_id=1, source_target_pairs={{0,8},{8,0},{16,24},{24,16},{1,9},{9,1},{17,25},{25,17},{2,10},{10... | collective-permute-start | bytes 73736 | tf_op jit(solution)/shard_map/ppermute | solution.py:449
  35.6 0.0 collective-permute-start.12
  35.6 1.9 %all-to-all-done.1 = f32[32,4,128]{2,1,0:T(4,128)S(1)} async-done(((f32[32,4,128]{2,1,0:T(4,128)}), f32[32,4,128]{2,1,0:T(4,128)S(1)}, u32[]{:S(2)}, u32[]{:S(2)}) %all-to-all-start.1) | async-done | bytes 65568 | tf_op jit(solution)/shard_map/all_to_all | solution.py:467
  37.5 0.4 coarse2.1
  38.0 0.0 collective-permute-done.9.a0
  38.0 0.0 collective-permute-done.10.a1
  38.0 0.0 collective-permute-done.11.a2
  38.0 0.0 collective-permute-done.12.a3
  38.0 0.5 image2.1
  38.5 0.5 collective-permute-start.13
  39.0 0.6 %collective-permute-start.14 = (f32[48,128]{1,0:T(8,128)S(1)}, f32[48,128]{1,0:T(8,128)S(1)}, u32[]{:S(2)}, u32[]{:S(2)}) collective-permute-start(f32[48,128]{1,0:T(8,128)S(1)} %get-tuple-element.73.o1), channel_id=1, source_target_pairs={{0,2},{1,3},{2,0},{3,1},{4,6},{5,7},{6,4},{7,5},{8,10},{9,11},{10,... | collective-permute-start | bytes 73736 | tf_op jit(solution)/shard_map/ppermute | solution.py:449
  39.6 1.4 %collective-permute-start.15 = (f32[48,128]{1,0:T(8,128)S(1)}, f32[48,128]{1,0:T(8,128)S(1)}, u32[]{:S(2)}, u32[]{:S(2)}) collective-permute-start(f32[48,128]{1,0:T(8,128)S(1)} %get-tuple-element.74.o2), channel_id=1, source_target_pairs={{0,8},{8,0},{16,24},{24,16},{1,9},{9,1},{17,25},{25,17},{2,10},{10... | collective-permute-start | bytes 73736 | tf_op jit(solution)/shard_map/ppermute | solution.py:449
  41.1 0.0 collective-permute-start.16
  41.1 1.5 %collective-permute-start.21 = (f32[256,128]{1,0:T(8,128)S(1)}, f32[256,128]{1,0:T(8,128)S(1)}, u32[]{:S(2)}, u32[]{:S(2)}) collective-permute-start(f32[256,128]{1,0:T(8,128)S(1)} %get-tuple-element.84.rest_0_), channel_id=1, source_target_pairs={{0,16},{8,24},{16,0},{24,8},{1,17},{9,25},{17,1},{25,9},{2,18},{10... | collective-permute-start | bytes 393224 | tf_op jit(solution)/shard_map/ppermute | solution.py:449
  42.6 0.3 sums2.1.sums
  42.8 0.6 collective-permute-done.13.a0
  43.4 0.0 collective-permute-done.14.a1
  43.4 0.0 collective-permute-done.15.a2
  43.4 0.0 collective-permute-done.16.a3
  43.4 1.2 %local3.1 = (f32[128,128]{1,0:T(8,128)}, f32[48,128]{1,0:T(8,128)S(1)}, f32[48,128]{1,0:T(8,128)S(1)}, f32[48,128]{1,0:T(8,128)S(1)}, f32[48,128]{1,0:T(8,128)S(1)}) custom-call(f32[48,128]{1,0:T(8,128)S(1)} %get-tuple-element.72.o0, f32[48,128]{1,0:T(8,128)S(1)} %get-tuple-element.73.o1, f32[48,128]{1,0:T(8,128)S(1)} %get-tuple-element.74.o2, ...), custom_call_target="tpu_custom_call" | custom-call | flops 40000000 | bytes 1691648 | tf_op jit(solution)/shard_map/local3/pallas_call | solution.py:423
  44.7 5.5 %all-to-all-start.2 = ((f32[32,4,128]{2,1,0:T(4,128)}), f32[32,4,128]{2,1,0:T(4,128)S(1)}, u32[]{:S(2)}, u32[]{:S(2)}) async-start(f32[32,4,128]{2,1,0:T(4,128)} %bitcast.10), calls=%async_computation.2 | async-start | bytes 131072 | tf_op jit(solution)/shard_map/all_to_all | solution.py:467
  50.2 2.7 %collective-permute-start.17 = (f32[48,128]{1,0:T(8,128)S(1)}, f32[48,128]{1,0:T(8,128)S(1)}, u32[]{:S(2)}, u32[]{:S(2)}) collective-permute-start(f32[48,128]{1,0:T(8,128)S(1)} %get-tuple-element.78.o0), channel_id=1, source_target_pairs={{0,4},{1,5},{2,6},{3,7},{4,0},{5,1},{6,2},{7,3},{8,12},{9,13},{10,... | collective-permute-start | bytes 73736 | tf_op jit(solution)/shard_map/ppermute | solution.py:449
  52.9 1.5 %collective-permute-start.18 = (f32[48,128]{1,0:T(8,128)S(1)}, f32[48,128]{1,0:T(8,128)S(1)}, u32[]{:S(2)}, u32[]{:S(2)}) collective-permute-start(f32[48,128]{1,0:T(8,128)S(1)} %get-tuple-element.79.o1), channel_id=1, source_target_pairs={{0,2},{1,3},{2,0},{3,1},{4,6},{5,7},{6,4},{7,5},{8,10},{9,11},{10,... | collective-permute-start | bytes 73736 | tf_op jit(solution)/shard_map/ppermute | solution.py:449
  54.4 1.5 %collective-permute-start.19 = (f32[48,128]{1,0:T(8,128)S(1)}, f32[48,128]{1,0:T(8,128)S(1)}, u32[]{:S(2)}, u32[]{:S(2)}) collective-permute-start(f32[48,128]{1,0:T(8,128)S(1)} %get-tuple-element.80.o2), channel_id=1, source_target_pairs={{0,8},{8,0},{16,24},{24,16},{1,9},{9,1},{17,25},{25,17},{2,10},{10... | collective-permute-start | bytes 73736 | tf_op jit(solution)/shard_map/ppermute | solution.py:449
  55.9 0.0 collective-permute-start.20
  55.9 0.0 collective-permute-done.21.rest_1_
  55.9 1.9 %all-to-all-done.2 = f32[32,4,128]{2,1,0:T(4,128)S(1)} async-done(((f32[32,4,128]{2,1,0:T(4,128)}), f32[32,4,128]{2,1,0:T(4,128)S(1)}, u32[]{:S(2)}, u32[]{:S(2)}) %all-to-all-start.2) | async-done | bytes 65568 | tf_op jit(solution)/shard_map/all_to_all | solution.py:467
  57.8 0.6 coarse3.1
  58.3 0.0 collective-permute-done.17.a0
  58.4 0.0 collective-permute-done.18.a1
  58.4 0.0 collective-permute-done.19.a2
  58.4 0.0 collective-permute-done.20.a3
  58.4 0.8 %finish.1 = (f32[32,768]{1,0:T(8,128)}, f32[32,768]{1,0:T(8,128)}) custom-call(f32[48,128]{1,0:T(8,128)S(1)} %get-tuple-element.78.o0, f32[48,128]{1,0:T(8,128)S(1)} %get-tuple-element.79.o1, f32[48,128]{1,0:T(8,128)S(1)} %get-tuple-element.80.o2, f32[48,128]{1,0:T(8,128)S(1)} %get-tuple-element.81.o3, f32[48,128]{1,0:T(8,128)S(1)} %collective-permute-done.17.a0, ...), custom_call_target="tpu_custom_call" | custom-call | flops 40000000 | bytes 630784 | tf_op jit(solution)/shard_map/finish/pallas_call | solution.py:423
  (1 shorter events, 0.0 us)
Async XLA Ops:
  0.6 17.6 %copy-start.1 = (bf16[1,1,768,768]{3,2,1,0:T(8,128)(2,1)S(1)}, bf16[1,1,768,768]{3,2,1,0:T(8,128)(2,1)}, u32[]{:S(2)}) copy-start(bf16[1,1,768,768]{3,2,1,0:T(8,128)(2,1)} %param.8) | copy-start | bytes 3538948
  3.5 22.5 %copy-start = (bf16[1,1,768,768]{3,2,1,0:T(8,128)(2,1)S(1)}, bf16[1,1,768,768]{3,2,1,0:T(8,128)(2,1)}, u32[]{:S(2)}) copy-start(bf16[1,1,768,768]{3,2,1,0:T(8,128)(2,1)} %param.7) | copy-start | bytes 3538948
  3.5 14.8 %collective-permute-start = (f32[128,128]{1,0:T(8,128)S(1)}, f32[128,128]{1,0:T(8,128)S(1)}, u32[]{:S(2)}, u32[]{:S(2)}) collective-permute-start(f32[128,128]{1,0:T(8,128)S(1)} %get-tuple-element.47.o0), channel_id=1, source_target_pairs={{0,4},{1,5},{2,6},{3,7},{4,0},{5,1},{6,2},{7,3},{8,12},{9,13},{10,... | collective-permute-start | bytes 196616 | tf_op jit(solution)/shard_map/ppermute | solution.py:449
  7.6 10.7 %all-to-all-start = ((f32[16,4,128]{2,1,0:T(4,128)}), f32[16,4,128]{2,1,0:T(4,128)S(1)}, u32[]{:S(2)}, u32[]{:S(2)}) async-start(f32[16,4,128]{2,1,0:T(4,128)} %bitcast.5), calls=%async_computation | async-start | bytes 65536 | tf_op jit(solution)/shard_map/all_to_all | solution.py:461
  11.5 5.9 %collective-permute-start.2 = (f32[72,128]{1,0:T(8,128)S(1)}, f32[72,128]{1,0:T(8,128)S(1)}, u32[]{:S(2)}, u32[]{:S(2)}) collective-permute-start(f32[72,128]{1,0:T(8,128)S(1)} %get-tuple-element.49.o2), channel_id=1, source_target_pairs={{0,8},{8,0},{16,24},{24,16},{1,9},{9,1},{17,25},{25,17},{2,10},{10... | collective-permute-start | bytes 110600 | tf_op jit(solution)/shard_map/ppermute | solution.py:449
  13.4 4.0 %collective-permute-start.1 = (f32[56,128]{1,0:T(8,128)S(1)}, f32[56,128]{1,0:T(8,128)S(1)}, u32[]{:S(2)}, u32[]{:S(2)}) collective-permute-start(f32[56,128]{1,0:T(8,128)S(1)} %get-tuple-element.48.o1), channel_id=1, source_target_pairs={{0,2},{1,3},{2,0},{3,1},{4,6},{5,7},{6,4},{7,5},{8,10},{9,11},{10,... | collective-permute-start | bytes 86024 | tf_op jit(solution)/shard_map/ppermute | solution.py:449
  14.9 2.5 %collective-permute-start.3 = (f32[56,128]{1,0:T(8,128)S(1)}, f32[56,128]{1,0:T(8,128)S(1)}, u32[]{:S(2)}, u32[]{:S(2)}) collective-permute-start(f32[56,128]{1,0:T(8,128)S(1)} %get-tuple-element.50.o3), channel_id=1, source_target_pairs={{0,1},{1,0},{2,3},{3,2},{4,5},{5,4},{6,7},{7,6},{8,9},{9,8},{10,11... | collective-permute-start | bytes 86024 | tf_op jit(solution)/shard_map/ppermute | solution.py:449
  14.9 7.8 %collective-permute-start.8 = (f32[128,128]{1,0:T(8,128)S(1)}, f32[128,128]{1,0:T(8,128)S(1)}, u32[]{:S(2)}, u32[]{:S(2)}) collective-permute-start(f32[128,128]{1,0:T(8,128)S(1)} %get-tuple-element.62.inverse), channel_id=1, source_target_pairs={{0,8},{8,0},{16,24},{24,16},{1,9},{9,1},{17,25},{25,17},{2,10},{10... | collective-permute-start | bytes 196616 | tf_op jit(solution)/shard_map/ppermute | solution.py:449
  19.0 5.6 %collective-permute-start.4 = (f32[96,128]{1,0:T(8,128)S(1)}, f32[96,128]{1,0:T(8,128)S(1)}, u32[]{:S(2)}, u32[]{:S(2)}) collective-permute-start(f32[96,128]{1,0:T(8,128)S(1)} %get-tuple-element.55.o0), channel_id=1, source_target_pairs={{0,4},{1,5},{2,6},{3,7},{4,0},{5,1},{6,2},{7,3},{8,12},{9,13},{10,... | collective-permute-start | bytes 147464 | tf_op jit(solution)/shard_map/ppermute | solution.py:449
  20.5 4.3 %collective-permute-start.5 = (f32[96,128]{1,0:T(8,128)S(1)}, f32[96,128]{1,0:T(8,128)S(1)}, u32[]{:S(2)}, u32[]{:S(2)}) collective-permute-start(f32[96,128]{1,0:T(8,128)S(1)} %get-tuple-element.56.o1), channel_id=1, source_target_pairs={{0,2},{1,3},{2,0},{3,1},{4,6},{5,7},{6,4},{7,5},{8,10},{9,11},{10,... | collective-permute-start | bytes 147464 | tf_op jit(solution)/shard_map/ppermute | solution.py:449
  21.9 4.1 %collective-permute-start.6 = (f32[96,128]{1,0:T(8,128)S(1)}, f32[96,128]{1,0:T(8,128)S(1)}, u32[]{:S(2)}, u32[]{:S(2)}) collective-permute-start(f32[96,128]{1,0:T(8,128)S(1)} %get-tuple-element.57.o2), channel_id=1, source_target_pairs={{0,8},{8,0},{16,24},{24,16},{1,9},{9,1},{17,25},{25,17},{2,10},{10... | collective-permute-start | bytes 147464 | tf_op jit(solution)/shard_map/ppermute | solution.py:449
  22.5 3.5 %collective-permute-start.7 = (f32[96,128]{1,0:T(8,128)S(1)}, f32[96,128]{1,0:T(8,128)S(1)}, u32[]{:S(2)}, u32[]{:S(2)}) collective-permute-start(f32[96,128]{1,0:T(8,128)S(1)} %get-tuple-element.58.o3), channel_id=1, source_target_pairs={{0,1},{1,0},{2,3},{3,2},{4,5},{5,4},{6,7},{7,6},{8,9},{9,8},{10,11... | collective-permute-start | bytes 147464 | tf_op jit(solution)/shard_map/ppermute | solution.py:449
  27.1 10.4 %all-to-all-start.1 = ((f32[32,4,128]{2,1,0:T(4,128)}), f32[32,4,128]{2,1,0:T(4,128)S(1)}, u32[]{:S(2)}, u32[]{:S(2)}) async-start(f32[32,4,128]{2,1,0:T(4,128)} %bitcast.8), calls=%async_computation.1 | async-start | bytes 131072 | tf_op jit(solution)/shard_map/all_to_all | solution.py:467
  29.9 8.1 %collective-permute-start.9 = (f32[48,128]{1,0:T(8,128)S(1)}, f32[48,128]{1,0:T(8,128)S(1)}, u32[]{:S(2)}, u32[]{:S(2)}) collective-permute-start(f32[48,128]{1,0:T(8,128)S(1)} %get-tuple-element.67.o0), channel_id=1, source_target_pairs={{0,4},{1,5},{2,6},{3,7},{4,0},{5,1},{6,2},{7,3},{8,12},{9,13},{10,... | collective-permute-start | bytes 73736 | tf_op jit(solution)/shard_map/ppermute | solution.py:449
  32.6 5.3 %collective-permute-start.10 = (f32[48,128]{1,0:T(8,128)S(1)}, f32[48,128]{1,0:T(8,128)S(1)}, u32[]{:S(2)}, u32[]{:S(2)}) collective-permute-start(f32[48,128]{1,0:T(8,128)S(1)} %get-tuple-element.68.o1), channel_id=1, source_target_pairs={{0,2},{1,3},{2,0},{3,1},{4,6},{5,7},{6,4},{7,5},{8,10},{9,11},{10,... | collective-permute-start | bytes 73736 | tf_op jit(solution)/shard_map/ppermute | solution.py:449
  34.2 3.8 %collective-permute-start.11 = (f32[48,128]{1,0:T(8,128)S(1)}, f32[48,128]{1,0:T(8,128)S(1)}, u32[]{:S(2)}, u32[]{:S(2)}) collective-permute-start(f32[48,128]{1,0:T(8,128)S(1)} %get-tuple-element.69.o2), channel_id=1, source_target_pairs={{0,8},{8,0},{16,24},{24,16},{1,9},{9,1},{17,25},{25,17},{2,10},{10... | collective-permute-start | bytes 73736 | tf_op jit(solution)/shard_map/ppermute | solution.py:449
  35.6 2.4 %collective-permute-start.12 = (f32[48,128]{1,0:T(8,128)S(1)}, f32[48,128]{1,0:T(8,128)S(1)}, u32[]{:S(2)}, u32[]{:S(2)}) collective-permute-start(f32[48,128]{1,0:T(8,128)S(1)} %get-tuple-element.70.o3), channel_id=1, source_target_pairs={{0,1},{1,0},{2,3},{3,2},{4,5},{5,4},{6,7},{7,6},{8,9},{9,8},{10,11... | collective-permute-start | bytes 73736 | tf_op jit(solution)/shard_map/ppermute | solution.py:449
  38.5 4.9 %collective-permute-start.13 = (f32[48,128]{1,0:T(8,128)S(1)}, f32[48,128]{1,0:T(8,128)S(1)}, u32[]{:S(2)}, u32[]{:S(2)}) collective-permute-start(f32[48,128]{1,0:T(8,128)S(1)} %get-tuple-element.72.o0), channel_id=1, source_target_pairs={{0,4},{1,5},{2,6},{3,7},{4,0},{5,1},{6,2},{7,3},{8,12},{9,13},{10,... | collective-permute-start | bytes 73736 | tf_op jit(solution)/shard_map/ppermute | solution.py:449
  39.0 4.4 %collective-permute-start.14 = (f32[48,128]{1,0:T(8,128)S(1)}, f32[48,128]{1,0:T(8,128)S(1)}, u32[]{:S(2)}, u32[]{:S(2)}) collective-permute-start(f32[48,128]{1,0:T(8,128)S(1)} %get-tuple-element.73.o1), channel_id=1, source_target_pairs={{0,2},{1,3},{2,0},{3,1},{4,6},{5,7},{6,4},{7,5},{8,10},{9,11},{10,... | collective-permute-start | bytes 73736 | tf_op jit(solution)/shard_map/ppermute | solution.py:449
  39.6 3.8 %collective-permute-start.15 = (f32[48,128]{1,0:T(8,128)S(1)}, f32[48,128]{1,0:T(8,128)S(1)}, u32[]{:S(2)}, u32[]{:S(2)}) collective-permute-start(f32[48,128]{1,0:T(8,128)S(1)} %get-tuple-element.74.o2), channel_id=1, source_target_pairs={{0,8},{8,0},{16,24},{24,16},{1,9},{9,1},{17,25},{25,17},{2,10},{10... | collective-permute-start | bytes 73736 | tf_op jit(solution)/shard_map/ppermute | solution.py:449
  41.1 2.4 %collective-permute-start.16 = (f32[48,128]{1,0:T(8,128)S(1)}, f32[48,128]{1,0:T(8,128)S(1)}, u32[]{:S(2)}, u32[]{:S(2)}) collective-permute-start(f32[48,128]{1,0:T(8,128)S(1)} %get-tuple-element.75.o3), channel_id=1, source_target_pairs={{0,1},{1,0},{2,3},{3,2},{4,5},{5,4},{6,7},{7,6},{8,9},{9,8},{10,11... | collective-permute-start | bytes 73736 | tf_op jit(solution)/shard_map/ppermute | solution.py:449
  41.1 14.8 %collective-permute-start.21 = (f32[256,128]{1,0:T(8,128)S(1)}, f32[256,128]{1,0:T(8,128)S(1)}, u32[]{:S(2)}, u32[]{:S(2)}) collective-permute-start(f32[256,128]{1,0:T(8,128)S(1)} %get-tuple-element.84.rest_0_), channel_id=1, source_target_pairs={{0,16},{8,24},{16,0},{24,8},{1,17},{9,25},{17,1},{25,9},{2,18},{10... | collective-permute-start | bytes 393224 | tf_op jit(solution)/shard_map/ppermute | solution.py:449
  44.7 13.1 %all-to-all-start.2 = ((f32[32,4,128]{2,1,0:T(4,128)}), f32[32,4,128]{2,1,0:T(4,128)S(1)}, u32[]{:S(2)}, u32[]{:S(2)}) async-start(f32[32,4,128]{2,1,0:T(4,128)} %bitcast.10), calls=%async_computation.2 | async-start | bytes 131072 | tf_op jit(solution)/shard_map/all_to_all | solution.py:467
  50.2 8.2 %collective-permute-start.17 = (f32[48,128]{1,0:T(8,128)S(1)}, f32[48,128]{1,0:T(8,128)S(1)}, u32[]{:S(2)}, u32[]{:S(2)}) collective-permute-start(f32[48,128]{1,0:T(8,128)S(1)} %get-tuple-element.78.o0), channel_id=1, source_target_pairs={{0,4},{1,5},{2,6},{3,7},{4,0},{5,1},{6,2},{7,3},{8,12},{9,13},{10,... | collective-permute-start | bytes 73736 | tf_op jit(solution)/shard_map/ppermute | solution.py:449
  52.9 5.5 %collective-permute-start.18 = (f32[48,128]{1,0:T(8,128)S(1)}, f32[48,128]{1,0:T(8,128)S(1)}, u32[]{:S(2)}, u32[]{:S(2)}) collective-permute-start(f32[48,128]{1,0:T(8,128)S(1)} %get-tuple-element.79.o1), channel_id=1, source_target_pairs={{0,2},{1,3},{2,0},{3,1},{4,6},{5,7},{6,4},{7,5},{8,10},{9,11},{10,... | collective-permute-start | bytes 73736 | tf_op jit(solution)/shard_map/ppermute | solution.py:449
  54.4 4.0 %collective-permute-start.19 = (f32[48,128]{1,0:T(8,128)S(1)}, f32[48,128]{1,0:T(8,128)S(1)}, u32[]{:S(2)}, u32[]{:S(2)}) collective-permute-start(f32[48,128]{1,0:T(8,128)S(1)} %get-tuple-element.80.o2), channel_id=1, source_target_pairs={{0,8},{8,0},{16,24},{24,16},{1,9},{9,1},{17,25},{25,17},{2,10},{10... | collective-permute-start | bytes 73736 | tf_op jit(solution)/shard_map/ppermute | solution.py:449
  55.9 2.5 %collective-permute-start.20 = (f32[48,128]{1,0:T(8,128)S(1)}, f32[48,128]{1,0:T(8,128)S(1)}, u32[]{:S(2)}, u32[]{:S(2)}) collective-permute-start(f32[48,128]{1,0:T(8,128)S(1)} %get-tuple-element.81.o3), channel_id=1, source_target_pairs={{0,1},{1,0},{2,3},{3,2},{4,5},{5,4},{6,7},{7,6},{8,9},{9,8},{10,11... | collective-permute-start | bytes 73736 | tf_op jit(solution)/shard_map/ppermute | solution.py:449

commit v11 on v10

--- a/solution.py
+++ b/solution.py
@@ -134,8 +134,9 @@
 
 
 def sums_of(total, n_load):
-    column = to_column(total[3:4])
-    return [column[i * n_load : (i + 1) * n_load] for i in range(4)]
+    shape = (n_load, 4 * n_load)
+    away = iota(shape, 1) - iota(shape, 0)
+    return [rows_sum(jnp.where(away == i * n_load, total[3:4], 0.0)) for i in range(4)]
 
 
 def halves(x):
@@ -167,10 +168,14 @@
     return block + pltpu.roll(block, 4, 0)
 
 
-def with_sums(block, sums):
-    zero = jnp.zeros_like(sums[0])
-    row = to_row(jnp.concatenate(sums + [zero] * (4 - len(sums)), axis=0))
-    return jnp.where(iota(block.shape, 0) % 4 == 3, row, block)
+def with_sums(block, sums, first=0):
+    n_load = sums[0].shape[0]
+    shape = (n_load, 4 * n_load)
+    away = iota(shape, 1) - iota(shape, 0)
+    spread = jnp.zeros(shape, F32)
+    for i, one in enumerate(sums):
+        spread = jnp.where(away == (first + i) * n_load, one, spread)
+    return jnp.where(iota(block.shape, 0) % 4 == 3, jnp.sum(spread, axis=0, keepdims=True), block)
 
 
 def put_all(out, block):
@@ -367,8 +372,7 @@
     flexed = jump([o0, o1, o2, o3], [a0, a1, a2, a3], n_load, sign_mask)
     scaled = 0.5 * sign * flexed
     local = fine(scaled, stiff[...])
-    fourth = jnp.where(iota((1, 4 * n_load), 1) // n_load == 3, 1.0, 0.0)
-    square = with_sums(jnp.zeros((8, 4 * n_load), F32), [4.0 * rows_sum(scaled * local)] * 4) * fourth
+    square = with_sums(jnp.zeros((8, 4 * n_load), F32), [4.0 * rows_sum(scaled * local)], 3)
     is_sum = iota((8, 1), 0) % 4 == 3
     put_all(block, jnp.where(is_sum, sums[...] + square, packed_corners(scaled, abs(corner_map[:16, :]))))
     copy = pltpu.make_async_copy(block, sent, sem)

time: 59.4 us -> 59.4 us (level)
  no operation moved by 1% of the time
where the time goes in v11:
time: 59.4 us; the launch traced here: 59.1 us
  starting transfers between devices  39.2 us (66%)
  waiting for transfers between devices  10.6 us (18%)
  Pallas kernels  7.44 us (13%)
  other arithmetic  1 us (2%)
  between operations  0.81 us (1%)
    ppermute x22, starting transfers between devices, swap(): lax.ppermute(block, axis, [(i, i ^ distance) for i in range(count) if i ^...  27.1 us
    all_to_all x2, starting transfers between devices, send_all(): lax.all_to_all(blocks, ('grp', 'sub'), 0, 0, tiled=True).reshape(rows.shape)  8.27 us
    pallas_call x10, Pallas kernels, call(): pl.pallas_call(kernel, out_shape=shapes, in_specs=[pl.BlockSpec(memory_sp...  7.44 us
    ppermute x22, waiting for transfers between devices, swap(): lax.ppermute(block, axis, [(i, i ^ distance) for i in range(count) if i ^...  6 us
    all_to_all x1, starting transfers between devices, send_pair(): lax.all_to_all(blocks, ('grp', 'sub'), 0, 0, tiled=True, axis_index_group...  3.88 us
    all_to_all x2, waiting for transfers between devices, send_all(): lax.all_to_all(blocks, ('grp', 'sub'), 0, 0, tiled=True).reshape(rows.shape)  3.74 us
  transfers between devices with their start and end apart: 25, of which 8 were waited for; matrix products, arithmetic and copies ran while one was open for 0% of the time, Pallas kernels for 6%

profile of v11, /device:TPU:0, one launch (start us, length us, event | category | flops | bytes accessed | tf_op | source)
XLA Modules:
  0.0 59.1 jit_solution(5129554540219056857)
XLA Ops:
  0.6 0.0 copy-start.1
  0.6 1.0 %convert_add_fusion.small = f32[104,128]{1,0:T(8,128)S(1)} fusion(s32[1,12]{1,0:T(1,128)} %bitcast.24, s32[1,4]{1,0:T(1,128)} %bitcast.25, f32[96,96]{1,0:T(8,128)} %bitcast.23), kind=kLoop, calls=%fused_computation | loop fusion | flops 53248 | bytes 90176 | tf_op jit(solution)/shard_map/add | solution.py:493
  1.6 1.8 %start.1 = (f32[64,128]{1,0:T(8,128)}, f32[8,768]{1,0:T(8,128)S(1)}, bf16[16,768]{1,0:T(8,128)(2,1)S(1)}, f32[32,768]{1,0:T(8,128)S(1)}, f32[64,128]{1,0:T(8,128...) custom-call(f32[32,768]{1,0:T(8,128)} %bitcast.22, ...), custom_call_target="tpu_custom_call" | custom-call | flops 40000000 | bytes 1867776 | tf_op jit(solution)/shard_map/start/pallas_call | solution.py:427
  3.5 0.0 copy-start
  3.5 4.1 %collective-permute-start = (f32[128,128]{1,0:T(8,128)S(1)}, f32[128,128]{1,0:T(8,128)S(1)}, u32[]{:S(2)}, u32[]{:S(2)}) collective-permute-start(f32[128,128]{1,0:T(8,128)S(1)} %get-tuple-element.47.o0), channel_id=1, source_target_pairs={{0,4},{1,5},{2,6},{3,7},{4,0},{5,1},{6,2},{7,3},{8,12},{9,13},{10,... | collective-permute-start | bytes 196616 | tf_op jit(solution)/shard_map/ppermute | solution.py:453
  7.6 3.9 %all-to-all-start = ((f32[16,4,128]{2,1,0:T(4,128)}), f32[16,4,128]{2,1,0:T(4,128)S(1)}, u32[]{:S(2)}, u32[]{:S(2)}) async-start(f32[16,4,128]{2,1,0:T(4,128)} %bitcast.5), calls=%async_computation | async-start | bytes 65536 | tf_op jit(solution)/shard_map/all_to_all | solution.py:465
  11.5 1.9 %collective-permute-start.2 = (f32[72,128]{1,0:T(8,128)S(1)}, f32[72,128]{1,0:T(8,128)S(1)}, u32[]{:S(2)}, u32[]{:S(2)}) collective-permute-start(f32[72,128]{1,0:T(8,128)S(1)} %get-tuple-element.49.o2), channel_id=1, source_target_pairs={{0,8},{8,0},{16,24},{24,16},{1,9},{9,1},{17,25},{25,17},{2,10},{10... | collective-permute-start | bytes 110600 | tf_op jit(solution)/shard_map/ppermute | solution.py:453
  13.4 1.5 %collective-permute-start.1 = (f32[56,128]{1,0:T(8,128)S(1)}, f32[56,128]{1,0:T(8,128)S(1)}, u32[]{:S(2)}, u32[]{:S(2)}) collective-permute-start(f32[56,128]{1,0:T(8,128)S(1)} %get-tuple-element.48.o1), channel_id=1, source_target_pairs={{0,2},{1,3},{2,0},{3,1},{4,6},{5,7},{6,4},{7,5},{8,10},{9,11},{10,... | collective-permute-start | bytes 86024 | tf_op jit(solution)/shard_map/ppermute | solution.py:453
  14.9 0.0 collective-permute-start.3
  14.9 0.6 collective-permute-start.8
  15.5 1.9 %collective-permute-done.1.a1 = f32[56,128]{1,0:T(8,128)S(1)} collective-permute-done((f32[56,128]{1,0:T(8,128)S(1)}, f32[56,128]{1,0:T(8,128)S(1)}, u32[]{:S(2)}, u32[]{:S(2)}) %collective-permute-start.1) | collective-permute-done | bytes 28704 | tf_op jit(solution)/shard_map/ppermute | solution.py:453
  17.4 0.0 collective-permute-done.3.a3
  17.4 0.0 collective-permute-done.2.a2
  17.4 0.9 %all-to-all-done = f32[16,4,128]{2,1,0:T(4,128)S(1)} async-done(((f32[16,4,128]{2,1,0:T(4,128)}), f32[16,4,128]{2,1,0:T(4,128)S(1)}, u32[]{:S(2)}, u32[]{:S(2)}) %all-to-all-start) | async-done | bytes 32800 | tf_op jit(solution)/shard_map/all_to_all | solution.py:465
  18.3 0.0 collective-permute-done.a0
  18.3 0.0 copy-done.1
  18.3 0.7 %image1.1 = (f32[32,768]{1,0:T(8,128)S(1)}, bf16[80,768]{1,0:T(8,128)(2,1)S(1)}, f32[80,128]{1,0:T(8,128)S(1)}, f32[96,128]{1,0:T(8,128)S(1)}, f32[96,128]{1,0:T...) custom-call(f32[64,128]{1,0:T(8,128)S(1)} %bitcast.21, f32[128,128]{1,0:T(8,128)S(1)} %get-tuple-element.47.o0, ...), custom_call_target="tpu_custom_call" | custom-call | flops 40000000 | bytes 2170880 | tf_op jit(solution)/shard_map/image1/pallas_call | solution.py:427
  19.0 1.4 %collective-permute-start.4 = (f32[96,128]{1,0:T(8,128)S(1)}, f32[96,128]{1,0:T(8,128)S(1)}, u32[]{:S(2)}, u32[]{:S(2)}) collective-permute-start(f32[96,128]{1,0:T(8,128)S(1)} %get-tuple-element.55.o0), channel_id=1, source_target_pairs={{0,4},{1,5},{2,6},{3,7},{4,0},{5,1},{6,2},{7,3},{8,12},{9,13},{10,... | collective-permute-start | bytes 147464 | tf_op jit(solution)/shard_map/ppermute | solution.py:453
  20.5 1.5 %collective-permute-start.5 = (f32[96,128]{1,0:T(8,128)S(1)}, f32[96,128]{1,0:T(8,128)S(1)}, u32[]{:S(2)}, u32[]{:S(2)}) collective-permute-start(f32[96,128]{1,0:T(8,128)S(1)} %get-tuple-element.56.o1), channel_id=1, source_target_pairs={{0,2},{1,3},{2,0},{3,1},{4,6},{5,7},{6,4},{7,5},{8,10},{9,11},{10,... | collective-permute-start | bytes 147464 | tf_op jit(solution)/shard_map/ppermute | solution.py:453
  21.9 0.6 collective-permute-start.6
  22.5 0.0 collective-permute-start.7
  22.5 0.2 sums1.1.sums
  22.7 0.0 collective-permute-done.8.other
  22.7 1.9 %collective-permute-done.4.a0 = f32[96,128]{1,0:T(8,128)S(1)} collective-permute-done((f32[96,128]{1,0:T(8,128)S(1)}, f32[96,128]{1,0:T(8,128)S(1)}, u32[]{:S(2)}, u32[]{:S(2)}) %collective-permute-start.4) | collective-permute-done | bytes 49184 | tf_op jit(solution)/shard_map/ppermute | solution.py:453
  24.6 0.2 collective-permute-done.5.a1
  24.8 1.2 %collective-permute-done.6.a2 = f32[96,128]{1,0:T(8,128)S(1)} collective-permute-done((f32[96,128]{1,0:T(8,128)S(1)}, f32[96,128]{1,0:T(8,128)S(1)}, u32[]{:S(2)}, u32[]{:S(2)}) %collective-permute-start.6) | collective-permute-done | bytes 49184 | tf_op jit(solution)/shard_map/ppermute | solution.py:453
  26.0 0.0 collective-permute-done.7.a3
  26.0 1.0 %local2.1 = (f32[32,768]{1,0:T(8,128)S(1)}, bf16[32,768]{1,0:T(8,128)(2,1)S(1)}, f32[256,128]{1,0:T(8,128)S(1)}, f32[128,128]{1,0:T(8,128)}, f32[48,128]{1,0:T(8...) custom-call(f32[96,128]{1,0:T(8,128)S(1)} %get-tuple-element.55.o0, ...), custom_call_target="tpu_custom_call" | custom-call | flops 40000000 | bytes 2297856 | tf_op jit(solution)/shard_map/local2/pallas_call | solution.py:427
  27.1 2.8 %all-to-all-start.1 = ((f32[32,4,128]{2,1,0:T(4,128)}), f32[32,4,128]{2,1,0:T(4,128)S(1)}, u32[]{:S(2)}, u32[]{:S(2)}) async-start(f32[32,4,128]{2,1,0:T(4,128)} %bitcast.8), calls=%async_computation.1 | async-start | bytes 131072 | tf_op jit(solution)/shard_map/all_to_all | solution.py:471
  29.9 2.7 %collective-permute-start.9 = (f32[48,128]{1,0:T(8,128)S(1)}, f32[48,128]{1,0:T(8,128)S(1)}, u32[]{:S(2)}, u32[]{:S(2)}) collective-permute-start(f32[48,128]{1,0:T(8,128)S(1)} %get-tuple-element.67.o0), channel_id=1, source_target_pairs={{0,4},{1,5},{2,6},{3,7},{4,0},{5,1},{6,2},{7,3},{8,12},{9,13},{10,... | collective-permute-start | bytes 73736 | tf_op jit(solution)/shard_map/ppermute | solution.py:453
  32.6 1.5 %collective-permute-start.10 = (f32[48,128]{1,0:T(8,128)S(1)}, f32[48,128]{1,0:T(8,128)S(1)}, u32[]{:S(2)}, u32[]{:S(2)}) collective-permute-start(f32[48,128]{1,0:T(8,128)S(1)} %get-tuple-element.68.o1), channel_id=1, source_target_pairs={{0,2},{1,3},{2,0},{3,1},{4,6},{5,7},{6,4},{7,5},{8,10},{9,11},{10,... | collective-permute-start | bytes 73736 | tf_op jit(solution)/shard_map/ppermute | solution.py:453
  34.2 1.5 %collective-permute-start.11 = (f32[48,128]{1,0:T(8,128)S(1)}, f32[48,128]{1,0:T(8,128)S(1)}, u32[]{:S(2)}, u32[]{:S(2)}) collective-permute-start(f32[48,128]{1,0:T(8,128)S(1)} %get-tuple-element.69.o2), channel_id=1, source_target_pairs={{0,8},{8,0},{16,24},{24,16},{1,9},{9,1},{17,25},{25,17},{2,10},{10... | collective-permute-start | bytes 73736 | tf_op jit(solution)/shard_map/ppermute | solution.py:453
  35.6 0.0 collective-permute-start.12
  35.6 1.9 %all-to-all-done.1 = f32[32,4,128]{2,1,0:T(4,128)S(1)} async-done(((f32[32,4,128]{2,1,0:T(4,128)}), f32[32,4,128]{2,1,0:T(4,128)S(1)}, u32[]{:S(2)}, u32[]{:S(2)}) %all-to-all-start.1) | async-done | bytes 65568 | tf_op jit(solution)/shard_map/all_to_all | solution.py:471
  37.5 0.4 coarse2.1
  38.0 0.0 collective-permute-done.9.a0
  38.0 0.0 collective-permute-done.10.a1
  38.0 0.0 collective-permute-done.11.a2
  38.0 0.0 collective-permute-done.12.a3
  38.0 0.5 image2.1
  38.5 0.5 collective-permute-start.13
  39.0 0.6 %collective-permute-start.14 = (f32[48,128]{1,0:T(8,128)S(1)}, f32[48,128]{1,0:T(8,128)S(1)}, u32[]{:S(2)}, u32[]{:S(2)}) collective-permute-start(f32[48,128]{1,0:T(8,128)S(1)} %get-tuple-element.73.o1), channel_id=1, source_target_pairs={{0,2},{1,3},{2,0},{3,1},{4,6},{5,7},{6,4},{7,5},{8,10},{9,11},{10,... | collective-permute-start | bytes 73736 | tf_op jit(solution)/shard_map/ppermute | solution.py:453
  39.6 1.4 %collective-permute-start.15 = (f32[48,128]{1,0:T(8,128)S(1)}, f32[48,128]{1,0:T(8,128)S(1)}, u32[]{:S(2)}, u32[]{:S(2)}) collective-permute-start(f32[48,128]{1,0:T(8,128)S(1)} %get-tuple-element.74.o2), channel_id=1, source_target_pairs={{0,8},{8,0},{16,24},{24,16},{1,9},{9,1},{17,25},{25,17},{2,10},{10... | collective-permute-start | bytes 73736 | tf_op jit(solution)/shard_map/ppermute | solution.py:453
  41.1 0.0 collective-permute-start.16
  41.1 1.5 %collective-permute-start.21 = (f32[256,128]{1,0:T(8,128)S(1)}, f32[256,128]{1,0:T(8,128)S(1)}, u32[]{:S(2)}, u32[]{:S(2)}) collective-permute-start(f32[256,128]{1,0:T(8,128)S(1)} %get-tuple-element.84.rest_0_), channel_id=1, source_target_pairs={{0,16},{8,24},{16,0},{24,8},{1,17},{9,25},{17,1},{25,9},{2,18},{10... | collective-permute-start | bytes 393224 | tf_op jit(solution)/shard_map/ppermute | solution.py:453
  42.6 0.2 sums2.1.sums
  42.8 0.6 %collective-permute-done.13.a0 = f32[48,128]{1,0:T(8,128)S(1)} collective-permute-done((f32[48,128]{1,0:T(8,128)S(1)}, f32[48,128]{1,0:T(8,128)S(1)}, u32[]{:S(2)}, u32[]{:S(2)}) %collective-permute-start.13) | collective-permute-done | bytes 24608 | tf_op jit(solution)/shard_map/ppermute | solution.py:453
  43.4 0.0 collective-permute-done.14.a1
  43.4 0.0 collective-permute-done.15.a2
  43.4 0.0 collective-permute-done.16.a3
  43.4 1.2 %local3.1 = (f32[128,128]{1,0:T(8,128)}, f32[48,128]{1,0:T(8,128)S(1)}, f32[48,128]{1,0:T(8,128)S(1)}, f32[48,128]{1,0:T(8,128)S(1)}, f32[48,128]{1,0:T(8,128)S(1)}) custom-call(f32[48,128]{1,0:T(8,128)S(1)} %get-tuple-element.72.o0, f32[48,128]{1,0:T(8,128)S(1)} %get-tuple-element.73.o1, f32[48,128]{1,0:T(8,128)S(1)} %get-tuple-element.74.o2, ...), custom_call_target="tpu_custom_call" | custom-call | flops 40000000 | bytes 1691648 | tf_op jit(solution)/shard_map/local3/pallas_call | solution.py:427
  44.7 5.5 %all-to-all-start.2 = ((f32[32,4,128]{2,1,0:T(4,128)}), f32[32,4,128]{2,1,0:T(4,128)S(1)}, u32[]{:S(2)}, u32[]{:S(2)}) async-start(f32[32,4,128]{2,1,0:T(4,128)} %bitcast.10), calls=%async_computation.2 | async-start | bytes 131072 | tf_op jit(solution)/shard_map/all_to_all | solution.py:471
  50.1 2.7 %collective-permute-start.17 = (f32[48,128]{1,0:T(8,128)S(1)}, f32[48,128]{1,0:T(8,128)S(1)}, u32[]{:S(2)}, u32[]{:S(2)}) collective-permute-start(f32[48,128]{1,0:T(8,128)S(1)} %get-tuple-element.78.o0), channel_id=1, source_target_pairs={{0,4},{1,5},{2,6},{3,7},{4,0},{5,1},{6,2},{7,3},{8,12},{9,13},{10,... | collective-permute-start | bytes 73736 | tf_op jit(solution)/shard_map/ppermute | solution.py:453
  52.9 1.5 %collective-permute-start.18 = (f32[48,128]{1,0:T(8,128)S(1)}, f32[48,128]{1,0:T(8,128)S(1)}, u32[]{:S(2)}, u32[]{:S(2)}) collective-permute-start(f32[48,128]{1,0:T(8,128)S(1)} %get-tuple-element.79.o1), channel_id=1, source_target_pairs={{0,2},{1,3},{2,0},{3,1},{4,6},{5,7},{6,4},{7,5},{8,10},{9,11},{10,... | collective-permute-start | bytes 73736 | tf_op jit(solution)/shard_map/ppermute | solution.py:453
  54.4 1.5 %collective-permute-start.19 = (f32[48,128]{1,0:T(8,128)S(1)}, f32[48,128]{1,0:T(8,128)S(1)}, u32[]{:S(2)}, u32[]{:S(2)}) collective-permute-start(f32[48,128]{1,0:T(8,128)S(1)} %get-tuple-element.80.o2), channel_id=1, source_target_pairs={{0,8},{8,0},{16,24},{24,16},{1,9},{9,1},{17,25},{25,17},{2,10},{10... | collective-permute-start | bytes 73736 | tf_op jit(solution)/shard_map/ppermute | solution.py:453
  55.9 0.0 collective-permute-start.20
  55.9 0.0 collective-permute-done.21.rest_1_
  55.9 1.9 %all-to-all-done.2 = f32[32,4,128]{2,1,0:T(4,128)S(1)} async-done(((f32[32,4,128]{2,1,0:T(4,128)}), f32[32,4,128]{2,1,0:T(4,128)S(1)}, u32[]{:S(2)}, u32[]{:S(2)}) %all-to-all-start.2) | async-done | bytes 65568 | tf_op jit(solution)/shard_map/all_to_all | solution.py:471
  57.8 0.6 coarse3.1
  58.3 0.0 collective-permute-done.17.a0
  58.3 0.0 collective-permute-done.18.a1
  58.3 0.0 collective-permute-done.19.a2
  58.4 0.0 collective-permute-done.20.a3
  58.4 0.8 %finish.1 = (f32[32,768]{1,0:T(8,128)}, f32[32,768]{1,0:T(8,128)}) custom-call(f32[48,128]{1,0:T(8,128)S(1)} %get-tuple-element.78.o0, f32[48,128]{1,0:T(8,128)S(1)} %get-tuple-element.79.o1, f32[48,128]{1,0:T(8,128)S(1)} %get-tuple-element.80.o2, f32[48,128]{1,0:T(8,128)S(1)} %get-tuple-element.81.o3, f32[48,128]{1,0:T(8,128)S(1)} %collective-permute-done.17.a0, ...), custom_call_target="tpu_custom_call" | custom-call | flops 40000000 | bytes 630784 | tf_op jit(solution)/shard_map/finish/pallas_call | solution.py:427
  (1 shorter events, 0.0 us)
Async XLA Ops:
  0.6 17.6 %copy-start.1 = (bf16[1,1,768,768]{3,2,1,0:T(8,128)(2,1)S(1)}, bf16[1,1,768,768]{3,2,1,0:T(8,128)(2,1)}, u32[]{:S(2)}) copy-start(bf16[1,1,768,768]{3,2,1,0:T(8,128)(2,1)} %param.8) | copy-start | bytes 3538948
  3.5 22.5 %copy-start = (bf16[1,1,768,768]{3,2,1,0:T(8,128)(2,1)S(1)}, bf16[1,1,768,768]{3,2,1,0:T(8,128)(2,1)}, u32[]{:S(2)}) copy-start(bf16[1,1,768,768]{3,2,1,0:T(8,128)(2,1)} %param.7) | copy-start | bytes 3538948
  3.5 14.8 %collective-permute-start = (f32[128,128]{1,0:T(8,128)S(1)}, f32[128,128]{1,0:T(8,128)S(1)}, u32[]{:S(2)}, u32[]{:S(2)}) collective-permute-start(f32[128,128]{1,0:T(8,128)S(1)} %get-tuple-element.47.o0), channel_id=1, source_target_pairs={{0,4},{1,5},{2,6},{3,7},{4,0},{5,1},{6,2},{7,3},{8,12},{9,13},{10,... | collective-permute-start | bytes 196616 | tf_op jit(solution)/shard_map/ppermute | solution.py:453
  7.6 10.7 %all-to-all-start = ((f32[16,4,128]{2,1,0:T(4,128)}), f32[16,4,128]{2,1,0:T(4,128)S(1)}, u32[]{:S(2)}, u32[]{:S(2)}) async-start(f32[16,4,128]{2,1,0:T(4,128)} %bitcast.5), calls=%async_computation | async-start | bytes 65536 | tf_op jit(solution)/shard_map/all_to_all | solution.py:465
  11.5 5.9 %collective-permute-start.2 = (f32[72,128]{1,0:T(8,128)S(1)}, f32[72,128]{1,0:T(8,128)S(1)}, u32[]{:S(2)}, u32[]{:S(2)}) collective-permute-start(f32[72,128]{1,0:T(8,128)S(1)} %get-tuple-element.49.o2), channel_id=1, source_target_pairs={{0,8},{8,0},{16,24},{24,16},{1,9},{9,1},{17,25},{25,17},{2,10},{10... | collective-permute-start | bytes 110600 | tf_op jit(solution)/shard_map/ppermute | solution.py:453
  13.4 4.0 %collective-permute-start.1 = (f32[56,128]{1,0:T(8,128)S(1)}, f32[56,128]{1,0:T(8,128)S(1)}, u32[]{:S(2)}, u32[]{:S(2)}) collective-permute-start(f32[56,128]{1,0:T(8,128)S(1)} %get-tuple-element.48.o1), channel_id=1, source_target_pairs={{0,2},{1,3},{2,0},{3,1},{4,6},{5,7},{6,4},{7,5},{8,10},{9,11},{10,... | collective-permute-start | bytes 86024 | tf_op jit(solution)/shard_map/ppermute | solution.py:453
  14.9 2.5 %collective-permute-start.3 = (f32[56,128]{1,0:T(8,128)S(1)}, f32[56,128]{1,0:T(8,128)S(1)}, u32[]{:S(2)}, u32[]{:S(2)}) collective-permute-start(f32[56,128]{1,0:T(8,128)S(1)} %get-tuple-element.50.o3), channel_id=1, source_target_pairs={{0,1},{1,0},{2,3},{3,2},{4,5},{5,4},{6,7},{7,6},{8,9},{9,8},{10,11... | collective-permute-start | bytes 86024 | tf_op jit(solution)/shard_map/ppermute | solution.py:453
  14.9 7.8 %collective-permute-start.8 = (f32[128,128]{1,0:T(8,128)S(1)}, f32[128,128]{1,0:T(8,128)S(1)}, u32[]{:S(2)}, u32[]{:S(2)}) collective-permute-start(f32[128,128]{1,0:T(8,128)S(1)} %get-tuple-element.62.inverse), channel_id=1, source_target_pairs={{0,8},{8,0},{16,24},{24,16},{1,9},{9,1},{17,25},{25,17},{2,10},{10... | collective-permute-start | bytes 196616 | tf_op jit(solution)/shard_map/ppermute | solution.py:453
  19.0 5.6 %collective-permute-start.4 = (f32[96,128]{1,0:T(8,128)S(1)}, f32[96,128]{1,0:T(8,128)S(1)}, u32[]{:S(2)}, u32[]{:S(2)}) collective-permute-start(f32[96,128]{1,0:T(8,128)S(1)} %get-tuple-element.55.o0), channel_id=1, source_target_pairs={{0,4},{1,5},{2,6},{3,7},{4,0},{5,1},{6,2},{7,3},{8,12},{9,13},{10,... | collective-permute-start | bytes 147464 | tf_op jit(solution)/shard_map/ppermute | solution.py:453
  20.5 4.3 %collective-permute-start.5 = (f32[96,128]{1,0:T(8,128)S(1)}, f32[96,128]{1,0:T(8,128)S(1)}, u32[]{:S(2)}, u32[]{:S(2)}) collective-permute-start(f32[96,128]{1,0:T(8,128)S(1)} %get-tuple-element.56.o1), channel_id=1, source_target_pairs={{0,2},{1,3},{2,0},{3,1},{4,6},{5,7},{6,4},{7,5},{8,10},{9,11},{10,... | collective-permute-start | bytes 147464 | tf_op jit(solution)/shard_map/ppermute | solution.py:453
  21.9 4.1 %collective-permute-start.6 = (f32[96,128]{1,0:T(8,128)S(1)}, f32[96,128]{1,0:T(8,128)S(1)}, u32[]{:S(2)}, u32[]{:S(2)}) collective-permute-start(f32[96,128]{1,0:T(8,128)S(1)} %get-tuple-element.57.o2), channel_id=1, source_target_pairs={{0,8},{8,0},{16,24},{24,16},{1,9},{9,1},{17,25},{25,17},{2,10},{10... | collective-permute-start | bytes 147464 | tf_op jit(solution)/shard_map/ppermute | solution.py:453
  22.5 3.5 %collective-permute-start.7 = (f32[96,128]{1,0:T(8,128)S(1)}, f32[96,128]{1,0:T(8,128)S(1)}, u32[]{:S(2)}, u32[]{:S(2)}) collective-permute-start(f32[96,128]{1,0:T(8,128)S(1)} %get-tuple-element.58.o3), channel_id=1, source_target_pairs={{0,1},{1,0},{2,3},{3,2},{4,5},{5,4},{6,7},{7,6},{8,9},{9,8},{10,11... | collective-permute-start | bytes 147464 | tf_op jit(solution)/shard_map/ppermute | solution.py:453
  27.1 10.4 %all-to-all-start.1 = ((f32[32,4,128]{2,1,0:T(4,128)}), f32[32,4,128]{2,1,0:T(4,128)S(1)}, u32[]{:S(2)}, u32[]{:S(2)}) async-start(f32[32,4,128]{2,1,0:T(4,128)} %bitcast.8), calls=%async_computation.1 | async-start | bytes 131072 | tf_op jit(solution)/shard_map/all_to_all | solution.py:471
  29.9 8.1 %collective-permute-start.9 = (f32[48,128]{1,0:T(8,128)S(1)}, f32[48,128]{1,0:T(8,128)S(1)}, u32[]{:S(2)}, u32[]{:S(2)}) collective-permute-start(f32[48,128]{1,0:T(8,128)S(1)} %get-tuple-element.67.o0), channel_id=1, source_target_pairs={{0,4},{1,5},{2,6},{3,7},{4,0},{5,1},{6,2},{7,3},{8,12},{9,13},{10,... | collective-permute-start | bytes 73736 | tf_op jit(solution)/shard_map/ppermute | solution.py:453
  32.6 5.3 %collective-permute-start.10 = (f32[48,128]{1,0:T(8,128)S(1)}, f32[48,128]{1,0:T(8,128)S(1)}, u32[]{:S(2)}, u32[]{:S(2)}) collective-permute-start(f32[48,128]{1,0:T(8,128)S(1)} %get-tuple-element.68.o1), channel_id=1, source_target_pairs={{0,2},{1,3},{2,0},{3,1},{4,6},{5,7},{6,4},{7,5},{8,10},{9,11},{10,... | collective-permute-start | bytes 73736 | tf_op jit(solution)/shard_map/ppermute | solution.py:453
  34.2 3.8 %collective-permute-start.11 = (f32[48,128]{1,0:T(8,128)S(1)}, f32[48,128]{1,0:T(8,128)S(1)}, u32[]{:S(2)}, u32[]{:S(2)}) collective-permute-start(f32[48,128]{1,0:T(8,128)S(1)} %get-tuple-element.69.o2), channel_id=1, source_target_pairs={{0,8},{8,0},{16,24},{24,16},{1,9},{9,1},{17,25},{25,17},{2,10},{10... | collective-permute-start | bytes 73736 | tf_op jit(solution)/shard_map/ppermute | solution.py:453
  35.6 2.4 %collective-permute-start.12 = (f32[48,128]{1,0:T(8,128)S(1)}, f32[48,128]{1,0:T(8,128)S(1)}, u32[]{:S(2)}, u32[]{:S(2)}) collective-permute-start(f32[48,128]{1,0:T(8,128)S(1)} %get-tuple-element.70.o3), channel_id=1, source_target_pairs={{0,1},{1,0},{2,3},{3,2},{4,5},{5,4},{6,7},{7,6},{8,9},{9,8},{10,11... | collective-permute-start | bytes 73736 | tf_op jit(solution)/shard_map/ppermute | solution.py:453
  38.5 4.9 %collective-permute-start.13 = (f32[48,128]{1,0:T(8,128)S(1)}, f32[48,128]{1,0:T(8,128)S(1)}, u32[]{:S(2)}, u32[]{:S(2)}) collective-permute-start(f32[48,128]{1,0:T(8,128)S(1)} %get-tuple-element.72.o0), channel_id=1, source_target_pairs={{0,4},{1,5},{2,6},{3,7},{4,0},{5,1},{6,2},{7,3},{8,12},{9,13},{10,... | collective-permute-start | bytes 73736 | tf_op jit(solution)/shard_map/ppermute | solution.py:453
  39.0 4.4 %collective-permute-start.14 = (f32[48,128]{1,0:T(8,128)S(1)}, f32[48,128]{1,0:T(8,128)S(1)}, u32[]{:S(2)}, u32[]{:S(2)}) collective-permute-start(f32[48,128]{1,0:T(8,128)S(1)} %get-tuple-element.73.o1), channel_id=1, source_target_pairs={{0,2},{1,3},{2,0},{3,1},{4,6},{5,7},{6,4},{7,5},{8,10},{9,11},{10,... | collective-permute-start | bytes 73736 | tf_op jit(solution)/shard_map/ppermute | solution.py:453
  39.6 3.8 %collective-permute-start.15 = (f32[48,128]{1,0:T(8,128)S(1)}, f32[48,128]{1,0:T(8,128)S(1)}, u32[]{:S(2)}, u32[]{:S(2)}) collective-permute-start(f32[48,128]{1,0:T(8,128)S(1)} %get-tuple-element.74.o2), channel_id=1, source_target_pairs={{0,8},{8,0},{16,24},{24,16},{1,9},{9,1},{17,25},{25,17},{2,10},{10... | collective-permute-start | bytes 73736 | tf_op jit(solution)/shard_map/ppermute | solution.py:453
  41.1 2.4 %collective-permute-start.16 = (f32[48,128]{1,0:T(8,128)S(1)}, f32[48,128]{1,0:T(8,128)S(1)}, u32[]{:S(2)}, u32[]{:S(2)}) collective-permute-start(f32[48,128]{1,0:T(8,128)S(1)} %get-tuple-element.75.o3), channel_id=1, source_target_pairs={{0,1},{1,0},{2,3},{3,2},{4,5},{5,4},{6,7},{7,6},{8,9},{9,8},{10,11... | collective-permute-start | bytes 73736 | tf_op jit(solution)/shard_map/ppermute | solution.py:453
  41.1 14.8 %collective-permute-start.21 = (f32[256,128]{1,0:T(8,128)S(1)}, f32[256,128]{1,0:T(8,128)S(1)}, u32[]{:S(2)}, u32[]{:S(2)}) collective-permute-start(f32[256,128]{1,0:T(8,128)S(1)} %get-tuple-element.84.rest_0_), channel_id=1, source_target_pairs={{0,16},{8,24},{16,0},{24,8},{1,17},{9,25},{17,1},{25,9},{2,18},{10... | collective-permute-start | bytes 393224 | tf_op jit(solution)/shard_map/ppermute | solution.py:453
  44.7 13.1 %all-to-all-start.2 = ((f32[32,4,128]{2,1,0:T(4,128)}), f32[32,4,128]{2,1,0:T(4,128)S(1)}, u32[]{:S(2)}, u32[]{:S(2)}) async-start(f32[32,4,128]{2,1,0:T(4,128)} %bitcast.10), calls=%async_computation.2 | async-start | bytes 131072 | tf_op jit(solution)/shard_map/all_to_all | solution.py:471
  50.1 8.2 %collective-permute-start.17 = (f32[48,128]{1,0:T(8,128)S(1)}, f32[48,128]{1,0:T(8,128)S(1)}, u32[]{:S(2)}, u32[]{:S(2)}) collective-permute-start(f32[48,128]{1,0:T(8,128)S(1)} %get-tuple-element.78.o0), channel_id=1, source_target_pairs={{0,4},{1,5},{2,6},{3,7},{4,0},{5,1},{6,2},{7,3},{8,12},{9,13},{10,... | collective-permute-start | bytes 73736 | tf_op jit(solution)/shard_map/ppermute | solution.py:453
  52.9 5.5 %collective-permute-start.18 = (f32[48,128]{1,0:T(8,128)S(1)}, f32[48,128]{1,0:T(8,128)S(1)}, u32[]{:S(2)}, u32[]{:S(2)}) collective-permute-start(f32[48,128]{1,0:T(8,128)S(1)} %get-tuple-element.79.o1), channel_id=1, source_target_pairs={{0,2},{1,3},{2,0},{3,1},{4,6},{5,7},{6,4},{7,5},{8,10},{9,11},{10,... | collective-permute-start | bytes 73736 | tf_op jit(solution)/shard_map/ppermute | solution.py:453
  54.4 4.0 %collective-permute-start.19 = (f32[48,128]{1,0:T(8,128)S(1)}, f32[48,128]{1,0:T(8,128)S(1)}, u32[]{:S(2)}, u32[]{:S(2)}) collective-permute-start(f32[48,128]{1,0:T(8,128)S(1)} %get-tuple-element.80.o2), channel_id=1, source_target_pairs={{0,8},{8,0},{16,24},{24,16},{1,9},{9,1},{17,25},{25,17},{2,10},{10... | collective-permute-start | bytes 73736 | tf_op jit(solution)/shard_map/ppermute | solution.py:453
  55.9 2.5 %collective-permute-start.20 = (f32[48,128]{1,0:T(8,128)S(1)}, f32[48,128]{1,0:T(8,128)S(1)}, u32[]{:S(2)}, u32[]{:S(2)}) collective-permute-start(f32[48,128]{1,0:T(8,128)S(1)} %get-tuple-element.81.o3), channel_id=1, source_target_pairs={{0,1},{1,0},{2,3},{3,2},{4,5},{5,4},{6,7},{7,6},{8,9},{9,8},{10,11... | collective-permute-start | bytes 73736 | tf_op jit(solution)/shard_map/ppermute | solution.py:453
